TPU v7x, 32 devices: a whole 2x2x4 slice. The times are simulated.
32 devices in a mesh: section: 2 (over x), tensor: 4 (over y, core), dp: 4 (over z).
Axes of the slice: x: 2, y: 2, z: 4, core: 2. Of those that a mesh axis runs over, the one named last changes fastest.
Arguments:
- ends_in: bfloat16 [2, 14336, 768], P('section', 'dp', 'tensor'), may hold values from -6 to 6
- ln_gain: bfloat16 [2, 2, 768], P('section', None, 'tensor'), may hold values from 0.5 to 1.5
- ln_shift: bfloat16 [2, 2, 768], P('section', None, 'tensor'), may hold values from -1.796875 to 1.796875
- w_qkv: bfloat16 [2, 768, 3, 768], P('section', None, None, 'tensor'), may hold values from -0.21875 to 0.21875
- b_qv: bfloat16 [2, 2, 768], P('section', None, 'tensor'), may hold values from -1.1953125 to 1.1953125
- w_out: bfloat16 [2, 768, 768], P('section', 'tensor'), may hold values from -1.75 to 1.75
- b_out: bfloat16 [2, 768], P('section', 'tensor'), may hold values from -1.796875 to 1.796875
- w_fc1: bfloat16 [2, 768, 3072], P('section', None, 'tensor'), may hold values from -0.21875 to 0.21875
- b_fc1: bfloat16 [2, 3072], P('section', 'tensor'), may hold values from -1.796875 to 1.796875
- w_fc2: bfloat16 [2, 3072, 768], P('section', 'tensor'), may hold values from -0.109375 to 0.109375
- b_fc2: bfloat16 [2, 768], P('section', 'tensor'), may hold values from -1.796875 to 1.796875
Outputs:
- ends_out: float32 [2, 14336, 768], P('section', 'dp', 'tensor')
- grad_ln_gain: float32 [2, 2, 768], P('section', None, 'tensor')
- grad_ln_shift: float32 [2, 2, 768], P('section', None, 'tensor')
- grad_w_qkv: float32 [2, 768, 3, 768], P('section', None, None, 'tensor')
- grad_b_qv: float32 [2, 2, 768], P('section', None, 'tensor')
- grad_w_out: float32 [2, 768, 768], P('section', 'tensor')
- grad_b_out: float32 [2, 768], P('section', 'tensor')
- grad_w_fc1: float32 [2, 768, 3072], P('section', None, 'tensor')
- grad_b_fc1: float32 [2, 3072], P('section', 'tensor')
- grad_w_fc2: float32 [2, 3072, 768], P('section', 'tensor')
- grad_b_fc2: float32 [2, 768], P('section', 'tensor')
All inputs are finite; a program needn't handle non-finite values.
Results may differ from a plain program's by a relative error of at most 0.015.
Values may be sent and summed in bfloat16 or wider, within the bound.
No kernel may reach another device: no remote copies, remote signals or barrier semaphores. Data moves between devices by JAX's collectives and lax.ppermute only.
A program may use at most 256 MiB of HBM per device.

v0:
```python
import jax
import jax.numpy as jnp
from jax import lax
from jax.sharding import PartitionSpec as P

D = 768
HD = 64
FRAMES = 448
MICRO = 2


EPSILON = 1e-05


def as_sent(value):
    return jax.tree.map(lambda a: a.astype(jnp.bfloat16) if a.dtype == jnp.float32 else a, value)


def from_behind(block, axis, distance):
    devices = range(lax.axis_size(axis))
    route = [(i - distance, i) for i in devices if i - distance in devices]
    return lax.ppermute(block, axis, route)


def gelu_exact(points):
    return jax.nn.gelu(points, approximate=False)


def add_trees(left_tree, right_tree):
    return jax.tree.map(jnp.add, left_tree, right_tree)


def norm_forward(values, norm_gain, norm_shift):
    firsts = (jnp.sum(values, axis=1), jnp.sum(values * values, axis=1))
    center = firsts[0] / D
    inv_std = lax.rsqrt(firsts[1] / D - center * center + EPSILON)
    normed = (values - center[:, None]) * inv_std[:, None]
    rounded = (normed * norm_gain.astype(jnp.float32) + norm_shift.astype(jnp.float32)).astype(
        jnp.bfloat16
    )
    return (rounded, normed, inv_std)


def norm_backward(upstream, normed, inv_std, norm_gain):
    d_gain = jnp.sum(upstream * normed, axis=0)
    d_shift = jnp.sum(upstream, axis=0)
    scaled = upstream * norm_gain.astype(jnp.float32)
    totals = (jnp.sum(scaled, axis=1), jnp.sum(scaled * normed, axis=1))
    d_input = inv_std[:, None] * (
        scaled - totals[0][:, None] / D - normed * (totals[1][:, None] / D)
    )
    return (d_input, d_gain, d_shift)


def branch_grad(upstream):
    rounded = upstream.astype(jnp.bfloat16)
    return rounded


def split_heads(flat_rows):
    row_count, head_cols = flat_rows.shape
    return flat_rows.reshape(row_count // FRAMES, FRAMES, head_cols // HD, HD)


def layer_forward(values, weights):
    norm_gain, norm_shift, w_qkv, b_qv, w_out, b_out, w_fc1, b_fc1, w_fc2, b_fc2 = weights
    row_count = values.shape[0]
    head_cols = w_qkv.shape[2]
    score_scale = float(HD) ** (-0.5)
    normed_in, normed_one, scale_one = norm_forward(values, norm_gain[0], norm_shift[0])
    qkv_bias = jnp.stack([b_qv[0], jnp.zeros_like(b_qv[0]), b_qv[1]]).astype(jnp.float32)
    projected = jnp.dot(
        normed_in, w_qkv.reshape(D, 3 * head_cols), preferred_element_type=jnp.float32
    )
    projected = (projected.reshape(row_count, 3, head_cols) + qkv_bias).astype(jnp.bfloat16)
    queries = split_heads(projected[:, 0])
    key_heads = split_heads(projected[:, 1])
    value_heads = split_heads(projected[:, 2])
    scores = (
        jnp.einsum("cqhd,ckhd->chqk", queries, key_heads, preferred_element_type=jnp.float32)
        * score_scale
    )
    row_max = jnp.max(scores, axis=-1, keepdims=True)
    exp_scores = jnp.exp(scores - row_max)
    row_total = jnp.sum(exp_scores, axis=-1, keepdims=True)
    soft_weights = (exp_scores / row_total).astype(jnp.bfloat16)
    logsum = row_max + jnp.log(row_total)
    attended = jnp.einsum(
        "chqk,ckhd->cqhd", soft_weights, value_heads, preferred_element_type=jnp.float32
    )
    attended = attended.astype(jnp.bfloat16).reshape(row_count, head_cols)
    hidden = (
        values
        + jnp.dot(attended, w_out, preferred_element_type=jnp.float32)
        + b_out.astype(jnp.float32)
    )
    normed_mid, normed_two, scale_two = norm_forward(hidden, norm_gain[1], norm_shift[1])
    fc_inner = jnp.dot(normed_mid, w_fc1, preferred_element_type=jnp.float32) + b_fc1.astype(
        jnp.float32
    )
    active = gelu_exact(fc_inner).astype(jnp.bfloat16)
    output = (
        hidden
        + jnp.dot(active, w_fc2, preferred_element_type=jnp.float32)
        + b_fc2.astype(jnp.float32)
    )
    stored = (
        normed_in,
        normed_one,
        scale_one,
        queries,
        key_heads,
        value_heads,
        logsum,
        attended,
        normed_mid,
        normed_two,
        scale_two,
        fc_inner,
        active,
    )
    return (output, stored)


def layer_backward(stored, weights, upstream):
    norm_gain, norm_shift, w_qkv, b_qv, w_out, b_out, w_fc1, b_fc1, w_fc2, b_fc2 = weights
    (
        normed_in,
        normed_one,
        scale_one,
        queries,
        key_heads,
        value_heads,
        logsum,
        attended,
        normed_mid,
        normed_two,
        scale_two,
        fc_inner,
        active,
    ) = stored
    row_count, head_cols = attended.shape
    score_scale = float(HD) ** (-0.5)
    mlp_grad = branch_grad(upstream)
    d_b_fc2 = jnp.sum(upstream, axis=0)
    d_w_fc2 = jnp.einsum("rf,rd->fd", active, mlp_grad, preferred_element_type=jnp.float32)
    d_active = jnp.einsum("rd,fd->rf", mlp_grad, w_fc2, preferred_element_type=jnp.float32)
    d_inner = jax.vjp(gelu_exact, fc_inner)[1](d_active)[0].astype(jnp.bfloat16)
    d_b_fc1 = jnp.sum(d_inner, axis=0, dtype=jnp.float32)
    d_w_fc1 = jnp.einsum("rd,rf->df", normed_mid, d_inner, preferred_element_type=jnp.float32)
    d_mid = jnp.einsum("rf,df->rd", d_inner, w_fc1, preferred_element_type=jnp.float32)
    d_hidden_norm, d_gain_two, d_shift_two = norm_backward(
        d_mid, normed_two, scale_two, norm_gain[1]
    )
    d_hidden = upstream + d_hidden_norm
    attn_grad = branch_grad(d_hidden)
    d_b_out = jnp.sum(d_hidden, axis=0)
    d_w_out = jnp.einsum("rc,rd->cd", attended, attn_grad, preferred_element_type=jnp.float32)
    d_attended = jnp.einsum("rd,cd->rc", attn_grad, w_out, preferred_element_type=jnp.float32)
    d_attended = split_heads(d_attended.astype(jnp.bfloat16))
    scores = (
        jnp.einsum("cqhd,ckhd->chqk", queries, key_heads, preferred_element_type=jnp.float32)
        * score_scale
    )
    soft_full = jnp.exp(scores - logsum)
    d_values = jnp.einsum(
        "chqk,cqhd->ckhd",
        soft_full.astype(jnp.bfloat16),
        d_attended,
        preferred_element_type=jnp.float32,
    ).astype(jnp.bfloat16)
    d_soft = jnp.einsum(
        "cqhd,ckhd->chqk", d_attended, value_heads, preferred_element_type=jnp.float32
    )
    d_scores = soft_full * (d_soft - jnp.sum(soft_full * d_soft, axis=-1, keepdims=True))
    d_scores = d_scores.astype(jnp.bfloat16)
    d_queries = (
        jnp.einsum("chqk,ckhd->cqhd", d_scores, key_heads, preferred_element_type=jnp.float32)
        * score_scale
    )
    d_keys = (
        jnp.einsum("chqk,cqhd->ckhd", d_scores, queries, preferred_element_type=jnp.float32)
        * score_scale
    )
    d_queries = d_queries.astype(jnp.bfloat16).reshape(row_count, head_cols)
    d_keys = d_keys.astype(jnp.bfloat16).reshape(row_count, head_cols)
    d_values = d_values.reshape(row_count, head_cols)
    d_mixed = jnp.stack([d_queries, d_keys, d_values], axis=1).reshape(row_count, 3 * head_cols)
    d_b_qv = jnp.stack(
        [
            jnp.sum(d_queries, axis=0, dtype=jnp.float32),
            jnp.sum(d_values, axis=0, dtype=jnp.float32),
        ]
    )
    d_w_qkv = jnp.einsum("rd,rk->dk", normed_in, d_mixed, preferred_element_type=jnp.float32)
    d_w_qkv = d_w_qkv.reshape(D, 3, head_cols)
    d_first = jnp.einsum(
        "rk,dk->rd", d_mixed, w_qkv.reshape(D, 3 * head_cols), preferred_element_type=jnp.float32
    )
    d_stream_norm, d_gain_one, d_shift_one = norm_backward(
        d_first, normed_one, scale_one, norm_gain[0]
    )
    d_stream = d_hidden + d_stream_norm
    layer_grads = (
        jnp.stack([d_gain_one, d_gain_two]),
        jnp.stack([d_shift_one, d_shift_two]),
        d_w_qkv,
        d_b_qv,
        d_w_out,
        d_b_out,
        d_w_fc1,
        d_b_fc1,
        d_w_fc2,
        d_b_fc2,
    )
    return (d_stream, layer_grads)


def reduce_grads(layer_grads):
    layer_grads = (
        lax.psum_scatter(
            layer_grads[0].astype(jnp.bfloat16), "tensor", scatter_dimension=1, tiled=True
        ).astype(jnp.float32),
        lax.psum_scatter(
            layer_grads[1].astype(jnp.bfloat16), "tensor", scatter_dimension=1, tiled=True
        ).astype(jnp.float32),
        lax.psum_scatter(
            layer_grads[2].astype(jnp.bfloat16), "tensor", scatter_dimension=2, tiled=True
        ).astype(jnp.float32),
        lax.psum_scatter(
            layer_grads[3].astype(jnp.bfloat16), "tensor", scatter_dimension=1, tiled=True
        ).astype(jnp.float32),
        lax.psum_scatter(
            layer_grads[4].astype(jnp.bfloat16), "tensor", scatter_dimension=0, tiled=True
        ).astype(jnp.float32),
        lax.psum_scatter(
            layer_grads[5].astype(jnp.bfloat16), "tensor", scatter_dimension=0, tiled=True
        ).astype(jnp.float32),
        lax.psum_scatter(
            layer_grads[6].astype(jnp.bfloat16), "tensor", scatter_dimension=1, tiled=True
        ).astype(jnp.float32),
        lax.psum_scatter(
            layer_grads[7].astype(jnp.bfloat16), "tensor", scatter_dimension=0, tiled=True
        ).astype(jnp.float32),
        lax.psum_scatter(
            layer_grads[8].astype(jnp.bfloat16), "tensor", scatter_dimension=0, tiled=True
        ).astype(jnp.float32),
        lax.psum_scatter(
            layer_grads[9].astype(jnp.bfloat16), "tensor", scatter_dimension=0, tiled=True
        ).astype(jnp.float32),
    )
    return jax.tree.map(lambda part: part.astype(jnp.float32), lax.psum(as_sent(layer_grads), "dp"))


def body(ends_in, ln_gain, ln_shift, w_qkv, b_qv, w_out, b_out, w_fc1, b_fc1, w_fc2, b_fc2):
    weights = (
        ln_gain[0],
        ln_shift[0],
        w_qkv[0],
        b_qv[0],
        w_out[0],
        b_out[0],
        w_fc1[0],
        b_fc1[0],
        w_fc2[0],
        b_fc2[0],
    )
    weights = (
        lax.all_gather(weights[0], "tensor", axis=1, tiled=True),
        lax.all_gather(weights[1], "tensor", axis=1, tiled=True),
        lax.all_gather(weights[2], "tensor", axis=2, tiled=True),
        lax.all_gather(weights[3], "tensor", axis=1, tiled=True),
        lax.all_gather(weights[4], "tensor", axis=0, tiled=True),
        lax.all_gather(weights[5], "tensor", axis=0, tiled=True),
        lax.all_gather(weights[6], "tensor", axis=1, tiled=True),
        lax.all_gather(weights[7], "tensor", axis=0, tiled=True),
        lax.all_gather(weights[8], "tensor", axis=0, tiled=True),
        lax.all_gather(weights[9], "tensor", axis=0, tiled=True),
    )
    rows_all, col_count = (ends_in.shape[1], ends_in.shape[2])
    boundary = ends_in[0].reshape(MICRO, rows_all // MICRO, col_count)
    boundary = lax.all_to_all(boundary, "tensor", split_axis=1, concat_axis=2, tiled=True)
    boundary = boundary.astype(jnp.float32)
    first_section = lax.axis_index("section") == 0
    zero_rows = jnp.zeros((boundary.shape[1], boundary.shape[2]), jnp.float32)
    received = zero_rows
    stored_all = []
    forward_out = []
    for turn_index in range(MICRO + 1):
        own_rows = boundary[turn_index] if turn_index < MICRO else zero_rows
        stream = jnp.where(first_section, own_rows, received)
        result, stored = layer_forward(stream, weights)
        stored_all.append(stored)
        if turn_index >= 1:
            forward_out.append(result)
        if turn_index < MICRO:
            received = from_behind(result.astype(jnp.bfloat16), "section", 1).astype(result.dtype)
    came_back = zero_rows
    local_grads = None
    summed_grads = None
    input_grads = []
    for turn_index in range(MICRO + 1):
        micro_index = MICRO - 1 - turn_index
        own_rows = boundary[micro_index] if micro_index >= 0 else zero_rows
        upstream = jnp.where(first_section, came_back, own_rows)
        d_stream, layer_grads = layer_backward(stored_all[MICRO - turn_index], weights, upstream)
        local_grads = layer_grads if local_grads is None else add_trees(local_grads, layer_grads)
        if turn_index >= 1:
            input_grads.append(d_stream)
        if turn_index < MICRO:
            came_back = from_behind(d_stream.astype(jnp.bfloat16), "section", -1).astype(
                d_stream.dtype
            )
    summed_grads = reduce_grads(local_grads)
    outputs_rows = jnp.stack(forward_out)
    gradient_rows = jnp.stack(input_grads[::-1])
    ends_local = jnp.where(first_section, gradient_rows, outputs_rows)
    ends_local = lax.all_to_all(
        ends_local.astype(jnp.bfloat16), "tensor", split_axis=2, concat_axis=1, tiled=True
    ).astype(ends_local.dtype)
    ends_local = ends_local.reshape(1, rows_all, col_count)
    return (
        ends_local,
        summed_grads[0][None],
        summed_grads[1][None],
        summed_grads[2][None],
        summed_grads[3][None],
        summed_grads[4][None],
        summed_grads[5][None],
        summed_grads[6][None],
        summed_grads[7][None],
        summed_grads[8][None],
        summed_grads[9][None],
    )


def solution(mesh):
    placed = (
        P("section", "dp", "tensor"),
        P("section", None, "tensor"),
        P("section", None, "tensor"),
        P("section", None, None, "tensor"),
        P("section", None, "tensor"),
        P("section", "tensor", None),
        P("section", "tensor"),
        P("section", None, "tensor"),
        P("section", "tensor"),
        P("section", "tensor", None),
        P("section", "tensor"),
    )
    return jax.shard_map(
        body,
        mesh=mesh,
        in_specs=placed,
        out_specs=(
            P("section", "dp", "tensor"),
            P("section", None, "tensor"),
            P("section", None, "tensor"),
            P("section", None, None, "tensor"),
            P("section", None, "tensor"),
            P("section", "tensor", None),
            P("section", "tensor"),
            P("section", None, "tensor"),
            P("section", "tensor"),
            P("section", "tensor", None),
            P("section", "tensor"),
        ),
        check_vma=False,
    )
```

profile of v0, /device:TPU:0, one launch (start us, length us, event | category | flops | bytes accessed | tf_op | source)
XLA Modules:
  0.0 849.1 jit_solution(14154362215883557854)
XLA Ops:
  12.7 5.0 copy.287
  24.3 38.2 %all-reduce.8 = (bf16[768]{0:T(1024)(128)(2,1)S(1)}, bf16[768]{0:T(1024)(128)(2,1)S(1)}) all-reduce(bf16[768]{0:T(1024)(128)(2,1)S(1)} %dynamic-update-slice, bf16[768]{0:T(1024)(128)(2,1)S(1)} %dynamic-update-slice.1), channel_id=7, replica_groups=mesh['section'=2,'tensor'=4,'dp'=4] {'tensor'}, use_global_device_ids=true, to_apply=%add | all-reduce | flops 1536 | bytes 6144
  62.7 6.7 all-gather.3
  69.4 4.7 slice_reduce_fusion.1
  74.5 5.2 all-gather.7
  81.0 6.5 all-gather.1
  87.5 9.2 %all-gather = bf16[1,2,768]{1,0,2:T(2,128)(2,1)S(1)} all-gather(bf16[1,2,192]{1,0,2:T(2,128)(2,1)S(1)} %copy.294), channel_id=2, replica_groups=mesh['section'=2,'tensor'=4,'dp'=4] {'tensor'}, dimensions={2}, use_global_device_ids=true | all-gather | bytes 3840 | tf_op jit(solution)/shard_map/all_gather | solution.py:269
  101.3 4.6 fusion.145
  141.4 17.9 %multiply_convert_fusion.5 = (bf16[448,3072]{1,0:T(8,128)(2,1)}, f32[448,3072]{1,0:T(8,128)}, f32[448,3072]{1,0:T(8,128)}) fusion(f32[3072]{0:T(1024)} %bitcast.387, bf16[1,768,3072]{2,1,0:T(8,128)(2,1)} %all-gather.19.cloned.1.call-done, f32[448,768]{1,0:T(8,128)S(1)} %get-tuple-element.112, f32[768]{0:T(1024)} %get-tuple-element.50, ...), kind=kOutput, calls=%fused_computation.71 | convolution fusion | flops 2206482432 | bytes 19879424 | tf_op jit(solution)/shard_map/dot_general | solution.py:98
  159.4 6.4 add_convert_fusion.15
  165.8 4.6 collective-permute-start
  171.5 13.2 %collective-permute-done = bf16[448,768]{1,0:T(8,128)(2,1)} collective-permute-done((bf16[448,768]{1,0:T(8,128)(2,1)}, bf16[448,768]{1,0:T(8,128)(2,1)}, u32[]{:S(2)}, u32[]{:S(2)}) %collective-permute-start) | collective-permute-done | bytes 688160 | tf_op jit(solution)/shard_map/ppermute | solution.py:22
  204.3 18.4 %multiply_convert_fusion.4 = (bf16[448,3072]{1,0:T(8,128)(2,1)S(1)}, f32[448,3072]{1,0:T(8,128)}, f32[448,3072]{1,0:T(8,128)}) fusion(f32[3072]{0:T(1024)S(1)} %bitcast.388, bf16[1,768,3072]{2,1,0:T(8,128)(2,1)} %all-gather.19.cloned.1.call-done, f32[448,768]{1,0:T(8,128)S(1)} %get-tuple-element.116, f32[448]{0:T(512)S(1)} %get-tuple-element.101, ...), kind=kOutput, calls=%fused_computation.58 | convolution fusion | flops 2206482432 | bytes 19879424 | tf_op jit(solution)/shard_map/dot_general | solution.py:98
  225.1 4.6 collective-permute-start.1
  230.4 13.4 %collective-permute-done.1 = bf16[448,768]{1,0:T(8,128)(2,1)S(1)} collective-permute-done((bf16[448,768]{1,0:T(8,128)(2,1)S(1)}, bf16[448,768]{1,0:T(8,128)(2,1)S(1)}, u32[]{:S(2)}, u32[]{:S(2)}) %collective-permute-start.1) | collective-permute-done | bytes 688160 | tf_op jit(solution)/shard_map/ppermute | solution.py:22
  259.9 18.9 %multiply_convert_fusion.3 = (bf16[448,3072]{1,0:T(8,128)(2,1)}, f32[448,3072]{1,0:T(8,128)}, f32[448,3072]{1,0:T(8,128)}) fusion(f32[3072]{0:T(1024)S(1)} %bitcast.389, bf16[1,768,3072]{2,1,0:T(8,128)(2,1)} %all-gather.19.cloned.1.call-done, f32[448,768]{1,0:T(8,128)S(1)} %get-tuple-element.120, f32[448]{0:T(512)S(1)} %get-tuple-element.97, ...), kind=kOutput, calls=%fused_computation.39 | convolution fusion | flops 2206482432 | bytes 19879424 | tf_op jit(solution)/shard_map/dot_general | solution.py:98
  278.9 9.1 %convert_reduce_fusion.2 = (f32[3072]{0:T(1024)}, bf16[448,3072]{1,0:T(8,128)(2,1)}) fusion(f32[448,3072]{1,0:T(8,128)} %get-tuple-element.76, bf16[1,3072,768]{2,1,0:T(8,128)(2,1)S(1)} %bitcast.399, f32[448,768]{1,0:T(8,128)S(1)} %copy.290, pred[]{:T(512)S(6)} %eq.3, f32[448,3072]{1,0:T(8,128)} %get-tuple-element.121, f32[3072]{0:T(1024)S(1)} %bitcast.390), kind=kOutput, calls=%fused_computation.38 | convolution fusion | flops 2137666560 | bytes 19881984 | tf_op jit(solution)/shard_map/rd,fd->rf/dot_general | solution.py:147
  287.9 5.1 multiply_reduce_fusion.10
  296.2 7.8 convert_reduce_fusion.7
  304.0 8.2 multiply_reduce_fusion.2
  323.8 5.4 multiply_reduce_fusion.11
  333.6 5.1 fusion.85
  338.7 9.3 %collective-permute-done.2 = bf16[448,768]{1,0:T(8,128)(2,1)S(1)} collective-permute-done((bf16[448,768]{1,0:T(8,128)(2,1)S(1)}, bf16[448,768]{1,0:T(8,128)(2,1)S(1)}, u32[]{:S(2)}, u32[]{:S(2)}) %collective-permute-start.2) | collective-permute-done | bytes 688160 | tf_op jit(solution)/shard_map/ppermute | solution.py:22
  348.3 8.0 convert_reduce_fusion.1
  363.7 7.8 convert_reduce_fusion.5
  371.5 8.3 multiply_reduce_fusion.1
  395.3 5.2 multiply_reduce_fusion.9
  404.9 5.0 fusion.83
  409.9 8.3 collective-permute-done.3
  418.3 7.9 convert_reduce_fusion
  432.7 8.1 convert_reduce_fusion.3
  440.8 8.1 multiply_reduce_fusion
  455.7 9.2 %multiply_convert_fusion = bf16[12,448,448]{1,2,0:T(8,128)(2,1)S(1)} fusion(f32[12,448,448]{1,2,0:T(8,128)} %get-tuple-element.132, f32[12,448,448]{1,2,0:T(8,128)} %copy-done, f32[12,448]{1,0:T(8,128)S(1)} %get-tuple-element.131, f32[12,448]{1,0:T(8,128)S(1)} %copy-done.79), kind=kLoop, calls=%fused_computation | loop fusion | flops 12042240 | bytes 24127488 | tf_op jit(solution)/shard_map/convert_element_type | solution.py:176
  470.1 4.7 convert_reduce_fusion.4
  476.3 9.7 %add_convert_fusion.2 = bf16[768,3,768]{0,2,1:T(8,128)(2,1)} fusion(f32[768,3,768]{0,2,1:T(8,128)} %fusion.85, f32[768,3,768]{0,2,1:T(8,128)} %fusion.83, bf16[448,1,768]{2,0,1:T(8,128)(2,1)} %copy.333, bf16[448,1,768]{2,0,1:T(8,128)(2,1)} %copy.332, bf16[448,1,768]{2,0,1:T(8,128)(2,1)S(1)} %copy.331, bf16[1,448,768]{1,2,0:T(8,128)(2,1)S(1)} %copy-done.40), kind=kOutput, calls=%fused_computation.29 | convolution fusion | flops 1596948480 | bytes 20447232 | tf_op jit(solution)/shard_map/rd,rk->dk/dot_general | solution.py:195
  486.1 5.2 fusion.186
  491.4 5.8 fusion.185
  497.2 7.7 add_convert_fusion.1
  510.9 5.1 fusion.201
  516.1 7.3 add_convert_fusion
  524.9 5.9 multiply_reduce_fusion.7
  534.0 43.2 %reduce-scatter.18.cloned.1.call-done = bf16[768,768]{1,0:T(8,128)(2,1)} async-done(((bf16[768,3072]{1,0:T(8,128)(2,1)}), bf16[768,768]{1,0:T(8,128)(2,1)}) %reduce-scatter.18.cloned.1.call-update) | async-done | bytes 1179664 | tf_op jit(solution)/shard_map/reduce_scatter | solution.py:239
  577.2 50.6 %reduce-scatter.20.cloned.1.call-done = bf16[768,768]{1,0:T(8,128)(2,1)} async-done(((bf16[3072,768]{1,0:T(8,128)(2,1)}), bf16[768,768]{1,0:T(8,128)(2,1)}) %reduce-scatter.20.cloned.1.call-update) | async-done | bytes 1179664 | tf_op jit(solution)/shard_map/reduce_scatter | solution.py:245
  627.8 5.6 add_bitcast_fusion
  643.0 25.4 %all-reduce.7 = (bf16[768]{0:T(1024)(128)(2,1)S(1)}, bf16[3072]{0:T(1024)(128)(2,1)S(1)}, bf16[768]{0:T(1024)(128)(2,1)S(1)}) all-reduce(bf16[768]{0:T(1024)(128)(2,1)S(1)} %add_convert_fusion.19, bf16[3072]{0:T(1024)(128)(2,1)S(1)} %add_convert_fusion.17, ...), channel_id=17, replica_groups=mesh['section'=2,'tensor'=4,'dp'=4] {'tensor'}, use_global_device_ids=true, to_apply=%region_64.65.clone | all-reduce | flops 4608 | bytes 18432
  675.1 21.9 %reduce-scatter.26.cloned.1.call-done = bf16[192,2]{1,0:T(8,128)(2,1)} async-done(((bf16[768,2]{1,0:T(8,128)(2,1)}), bf16[192,2]{1,0:T(8,128)(2,1)}) %reduce-scatter.26.cloned.1.call-update) | async-done | bytes 784
  697.8 12.3 %all-reduce.5 = (bf16[1,2,192]{2,1,0:T(2,128)(2,1)S(1)}, bf16[1,2,192]{2,1,0:T(2,128)(2,1)S(1)}, bf16[1,2,192]{2,1,0:T(2,128)(2,1)S(1)}, bf16[1,192]{1,0:T(2,128...) all-reduce(bf16[1,2,192]{2,1,0:T(2,128)(2,1)S(1)} %bitcast.393, ...), channel_id=1, replica_groups=mesh['section'=2,'tensor'=4,'dp'=4] {'dp'}, use_global_device_ids=true, to_apply=%region_40.41 | all-reduce | flops 2304 | bytes 9216 | tf_op jit(solution)/shard_map/psum | solution.py:252
  720.1 114.4 %all-reduce.11.cloned.1.call-done = (bf16[1,768,3,192]{1,3,2,0:T(8,128)(2,1)}, bf16[1,192,768]{2,1,0:T(8,128)(2,1)}, bf16[1,768,768]{2,1,0:T(8,128)(2,1)}, bf16[1,768,768]{2,1,0:T(8,128)(2,1)}) async-done(((bf16[1,768,3,192]{1,3,2,0:T(8,128)(2,1)}, bf16[1,192,768]{2,1,0:T(8,128)(2,1)}, bf16[1,768,768]{2,1,0:T(8,128)(2,1)}, bf16[1,768,768]{2,1,0:T(8,128)(2,1)}), (bf16[1,768,3,192]{1,3,2,0:T(8,128)(2,1)}, ...) | async-done | bytes 3538960 | tf_op jit(solution)/shard_map/psum | solution.py:252
  (575 shorter events, 201.8 us)
Async XLA Ops:
  7.2 114.3 %all-gather.15.cloned.1.call-start = ((), (), s32[]{:S(2)}) async-start(), calls=%async_computation.13 | async-start | bytes 4423680 | tf_op jit(solution)/shard_map/all_gather | solution.py:271
  7.9 130.9 %all-gather.17.cloned.1.call-start = ((), (), s32[]{:S(2)}) async-start(), calls=%async_computation.14 | async-start | bytes 1474560 | tf_op jit(solution)/shard_map/all_gather | solution.py:273
  8.7 132.7 %all-gather.19.cloned.1.call-start = ((), (), s32[]{:S(2)}) async-start(), calls=%async_computation.15 | async-start | bytes 5898240 | tf_op jit(solution)/shard_map/all_gather | solution.py:275
  12.7 49.9 %copy-start.147 = (bf16[1,2,192]{2,1,0:T(2,128)(2,1)S(1)}, bf16[1,2,192]{2,1,0:T(2,128)(2,1)}, u32[]{:S(2)}) copy-start(bf16[1,2,192]{2,1,0:T(2,128)(2,1)} %param.15) | copy-start | bytes 2308
  12.7 61.5 %copy-start.148 = (bf16[1,2,192]{2,1,0:T(2,128)(2,1)S(1)}, bf16[1,2,192]{2,1,0:T(2,128)(2,1)}, u32[]{:S(2)}) copy-start(bf16[1,2,192]{2,1,0:T(2,128)(2,1)} %param.13) | copy-start | bytes 2308
  12.7 61.7 %copy-start.149 = (bf16[1,2,192]{2,1,0:T(2,128)(2,1)S(1)}, bf16[1,2,192]{2,1,0:T(2,128)(2,1)}, u32[]{:S(2)}) copy-start(bf16[1,2,192]{2,1,0:T(2,128)(2,1)} %param.12) | copy-start | bytes 2308
  12.7 61.8 %copy-start.144 = (bf16[1,768]{1,0:T(2,128)(2,1)S(1)}, bf16[1,768]{1,0:T(2,128)(2,1)}, u32[]{:S(2)}) copy-start(bf16[1,768]{1,0:T(2,128)(2,1)} %param.19) | copy-start | bytes 4612
  17.7 88.3 %all-to-all-start = ((bf16[2,1792,192]{2,0,1:T(2,128)(2,1)}), bf16[2,1792,192]{2,0,1:T(2,128)(2,1)S(1)}, u32[]{:S(2)}, u32[]{:S(2)}) async-start(bf16[2,1792,192]{2,0,1:T(2,128)(2,1)} %copy.287), calls=%async_computation | async-start | bytes 3670016 | tf_op jit(solution)/shard_map/all_to_all | solution.py:282
  21.9 137.4 %all-gather.21.cloned.1.call-start = ((), (), s32[]{:S(2)}) async-start(), calls=%async_computation.16 | async-start | bytes 5898240 | tf_op jit(solution)/shard_map/all_gather | solution.py:277
  22.5 511.4 %reduce-scatter.16.cloned.1.call-start = ((), (), s32[]{:S(2)}) async-start(), calls=%async_computation.10 | async-start | bytes 1474560 | tf_op jit(solution)/shard_map/reduce_scatter | solution.py:233
  62.6 76.3 %copy-start.142 = (f32[768]{0:T(1024)}, f32[768]{0:T(1024)S(1)}, u32[]{:S(2)}) copy-start(f32[768]{0:T(1024)S(1)} %convert_element_type.532) | copy-start | bytes 9220
  120.0 18.9 %copy-start.4 = (f32[448,768]{1,0:T(8,128)}, f32[448,768]{1,0:T(8,128)S(1)}, u32[]{:S(2)}) copy-start(f32[448,768]{1,0:T(8,128)S(1)} %copy.292) | copy-start | bytes 4128772
  138.8 20.5 %copy-start.68 = (bf16[12,64,448]{2,1,0:T(8,128)(2,1)}, bf16[12,64,448]{2,1,0:T(8,128)(2,1)S(1)}, u32[]{:S(2)}) copy-start(bf16[12,64,448]{2,1,0:T(8,128)(2,1)S(1)} %fusion.111) | copy-start | bytes 2064388
  165.8 18.8 %collective-permute-start = (bf16[448,768]{1,0:T(8,128)(2,1)}, bf16[448,768]{1,0:T(8,128)(2,1)}, u32[]{:S(2)}, u32[]{:S(2)}) collective-permute-start(bf16[448,768]{1,0:T(8,128)(2,1)} %add_convert_fusion.15), channel_id=1, source_target_pairs={{0,16},{1,17},{2,18},{3,19},{4,20},{5,21},{6,22},{7,23},{8,24},{9,... | collective-permute-start | bytes 2064392 | tf_op jit(solution)/shard_map/ppermute | solution.py:22
  171.5 121.6 %copy-start.6 = (f32[448,768]{1,0:T(8,128)}, f32[448,768]{1,0:T(8,128)S(1)}, u32[]{:S(2)}) copy-start(f32[448,768]{1,0:T(8,128)S(1)} %copy.290) | copy-start | bytes 4128772
  203.2 19.5 %copy-start.64 = (bf16[12,64,448]{2,1,0:T(8,128)(2,1)}, bf16[12,64,448]{2,1,0:T(8,128)(2,1)S(1)}, u32[]{:S(2)}) copy-start(bf16[12,64,448]{2,1,0:T(8,128)(2,1)S(1)} %fusion.110) | copy-start | bytes 2064388
  203.2 19.4 %slice-start.6 = ((s8[4718592]{0:T(1024)(128)(4,1)}), s8[4194304]{0:T(1024)(128)(4,1)S(1)}, s32[]{:S(2)}) async-start(s8[4718592]{0:T(1024)(128)(4,1)} %bitcast.396), calls=%async_computation.27 | async-start | bytes 8388608
  204.2 18.5 %copy-start.58 = (f32[448,768]{1,0:T(8,128)}, f32[448,768]{1,0:T(8,128)S(1)}, u32[]{:S(2)}) copy-start(f32[448,768]{1,0:T(8,128)S(1)} %get-tuple-element.116) | copy-start | bytes 4128772
  204.2 18.4 %copy-start.111 = (f32[448]{0:T(512)}, f32[448]{0:T(512)S(1)}, u32[]{:S(2)}) copy-start(f32[448]{0:T(512)S(1)} %get-tuple-element.100) | copy-start | bytes 5380
  204.2 18.4 %copy-start.140 = (f32[768]{0:T(1024)S(1)}, f32[768]{0:T(1024)}, u32[]{:S(2)}) copy-start(f32[768]{0:T(1024)} %convert_element_type.533) | copy-start | bytes 9220
  222.7 21.5 %copy-start.152 = (bf16[1,768,3,768]{1,3,2,0:T(8,128)(2,1)S(1)}, bf16[1,768,3,768]{1,3,2,0:T(8,128)(2,1)}, u32[]{:S(2)}) copy-start(bf16[1,768,3,768]{1,3,2,0:T(8,128)(2,1)} %all-gather.15.cloned.1.call-done) | copy-start | bytes 10616836
  225.1 19.1 %copy-start.77 = (bf16[448,768]{1,0:T(8,128)(2,1)}, bf16[448,768]{1,0:T(8,128)(2,1)S(1)}, u32[]{:S(2)}) copy-start(bf16[448,768]{1,0:T(8,128)(2,1)S(1)} %add_add_fusion) | copy-start | bytes 2064388
  225.1 18.8 %collective-permute-start.1 = (bf16[448,768]{1,0:T(8,128)(2,1)S(1)}, bf16[448,768]{1,0:T(8,128)(2,1)S(1)}, u32[]{:S(2)}, u32[]{:S(2)}) collective-permute-start(bf16[448,768]{1,0:T(8,128)(2,1)S(1)} %add_add_fusion), channel_id=1, source_target_pairs={{0,16},{1,17},{2,18},{3,19},{4,20},{5,21},{6,22},{7,23},{8,24},{9,... | collective-permute-start | bytes 2064392 | tf_op jit(solution)/shard_map/ppermute | solution.py:22
  254.0 41.4 %copy-start.80 = (f32[12,448]{1,0:T(8,128)}, f32[12,448]{1,0:T(8,128)S(1)}, u32[]{:S(2)}) copy-start(f32[12,448]{1,0:T(8,128)S(1)} %log_add_fusion.2) | copy-start | bytes 64516
  258.8 20.0 %copy-start.66 = (bf16[12,64,448]{2,1,0:T(8,128)(2,1)}, bf16[12,64,448]{2,1,0:T(8,128)(2,1)S(1)}, u32[]{:S(2)}) copy-start(bf16[12,64,448]{2,1,0:T(8,128)(2,1)S(1)} %fusion.109) | copy-start | bytes 2064388
  258.9 20.0 %slice-start.8 = ((s8[4718592]{0:T(1024)(128)(4,1)}), s8[4194304]{0:T(1024)(128)(4,1)S(1)}, s32[]{:S(2)}) async-start(s8[4718592]{0:T(1024)(128)(4,1)} %bitcast.398), calls=%async_computation.29 | async-start | bytes 8388608
  258.9 29.1 %slice-start.14 = ((s8[4718592]{0:T(1024)(128)(4,1)}), s8[4194304]{0:T(1024)(128)(4,1)S(1)}, s32[]{:S(2)}) async-start(s8[4718592]{0:T(1024)(128)(4,1)} %bitcast.404), calls=%async_computation.35 | async-start | bytes 8388608
  259.9 33.2 %copy-start.56 = (f32[448,768]{1,0:T(8,128)}, f32[448,768]{1,0:T(8,128)S(1)}, u32[]{:S(2)}) copy-start(f32[448,768]{1,0:T(8,128)S(1)} %get-tuple-element.120) | copy-start | bytes 4128772
  259.9 33.2 %copy-start.117 = (f32[448]{0:T(512)}, f32[448]{0:T(512)S(1)}, u32[]{:S(2)}) copy-start(f32[448]{0:T(512)S(1)} %get-tuple-element.96) | copy-start | bytes 5380
  259.9 33.2 %copy-start.119 = (f32[448]{0:T(512)}, f32[448]{0:T(512)S(1)}, u32[]{:S(2)}) copy-start(f32[448]{0:T(512)S(1)} %get-tuple-element.97) | copy-start | bytes 5380
  259.9 18.9 %slice-start.9 = ((s8[4718592]{0:T(1024)(128)(4,1)}), s8[524288]{0:T(1024)(128)(4,1)S(1)}, s32[]{:S(2)}) async-start(s8[4718592]{0:T(1024)(128)(4,1)} %bitcast.398), calls=%async_computation.30 | async-start | bytes 1048576
  259.9 28.0 %slice-start.15 = ((s8[4718592]{0:T(1024)(128)(4,1)}), s8[524288]{0:T(1024)(128)(4,1)S(1)}, s32[]{:S(2)}) async-start(s8[4718592]{0:T(1024)(128)(4,1)} %bitcast.404), calls=%async_computation.36 | async-start | bytes 1048576
  329.2 19.0 %slice-start.10 = ((s8[4718592]{0:T(1024)(128)(4,1)}), s8[4194304]{0:T(1024)(128)(4,1)S(1)}, s32[]{:S(2)}) async-start(s8[4718592]{0:T(1024)(128)(4,1)} %bitcast.400), calls=%async_computation.31 | async-start | bytes 8388608
  329.8 18.2 %collective-permute-start.2 = (bf16[448,768]{1,0:T(8,128)(2,1)S(1)}, bf16[448,768]{1,0:T(8,128)(2,1)S(1)}, u32[]{:S(2)}, u32[]{:S(2)}) collective-permute-start(bf16[448,768]{1,0:T(8,128)(2,1)S(1)} %add_convert_fusion.10), channel_id=1, source_target_pairs={{16,0},{17,1},{18,2},{19,3},{20,4},{21,5},{22,6},{23,7},{24,8},{25... | collective-permute-start | bytes 2064392 | tf_op jit(solution)/shard_map/ppermute | solution.py:22
  333.6 22.7 %slice-start.16 = ((s8[4718592]{0:T(1024)(128)(4,1)}), s8[4194304]{0:T(1024)(128)(4,1)S(1)}, s32[]{:S(2)}) async-start(s8[4718592]{0:T(1024)(128)(4,1)} %bitcast.406), calls=%async_computation.37 | async-start | bytes 8388608
  401.1 17.2 %collective-permute-start.3 = (bf16[448,768]{1,0:T(8,128)(2,1)S(1)}, bf16[448,768]{1,0:T(8,128)(2,1)S(1)}, u32[]{:S(2)}, u32[]{:S(2)}) collective-permute-start(bf16[448,768]{1,0:T(8,128)(2,1)S(1)} %multiply_add_fusion.1), channel_id=1, source_target_pairs={{16,0},{17,1},{18,2},{19,3},{20,4},{21,5},{22,6},{23,7},{24,8},{25... | collective-permute-start | bytes 2064392 | tf_op jit(solution)/shard_map/ppermute | solution.py:22
  404.8 21.4 %slice-start.18 = ((s8[4718592]{0:T(1024)(128)(4,1)}), s8[4194304]{0:T(1024)(128)(4,1)S(1)}, s32[]{:S(2)}) async-start(s8[4718592]{0:T(1024)(128)(4,1)} %bitcast.408), calls=%async_computation.39 | async-start | bytes 8388608
  430.7 20.5 %copy-start.10 = (f32[448,768]{1,0:T(8,128)}, f32[448,768]{1,0:T(8,128)S(1)}, u32[]{:S(2)}) copy-start(f32[448,768]{1,0:T(8,128)S(1)} %get-tuple-element.74) | copy-start | bytes 4128772
  455.6 78.3 %reduce-scatter.14.cloned.1.call-start = ((), (), s32[]{:S(2)}) async-start(), calls=%async_computation.9 | async-start | bytes 4423680 | tf_op jit(solution)/shard_map/reduce_scatter | solution.py:227
  486.0 91.2 %reduce-scatter.18.cloned.1.call-start = ((), (), s32[]{:S(2)}) async-start(), calls=%async_computation.11 | async-start | bytes 5898240 | tf_op jit(solution)/shard_map/reduce_scatter | solution.py:239
  504.9 122.9 %reduce-scatter.20.cloned.1.call-start = ((), (), s32[]{:S(2)}) async-start(), calls=%async_computation.12 | async-start | bytes 5898240 | tf_op jit(solution)/shard_map/reduce_scatter | solution.py:245
  523.5 145.2 %reduce-scatter.22.cloned.1.call-start = ((), (), s32[]{:S(2)}) async-start(), calls=%async_computation.17 | async-start | bytes 245760
  530.9 96.9 %copy-start.57 = (f32[448,768]{1,0:T(8,128)S(1)}, f32[448,768]{1,0:T(8,128)}, u32[]{:S(2)}) copy-start(f32[448,768]{1,0:T(8,128)} %copy-done.56) | copy-start | bytes 4128772
  530.9 96.9 %copy-start.141 = (f32[768]{0:T(1024)S(1)}, f32[768]{0:T(1024)}, u32[]{:S(2)}) copy-start(f32[768]{0:T(1024)} %convert_element_type.533) | copy-start | bytes 9220
  531.8 142.4 %reduce-scatter.24.cloned.1.call-start = ((), (), s32[]{:S(2)}) async-start(), calls=%async_computation.18 | async-start | bytes 245760
  532.9 164.1 %reduce-scatter.26.cloned.1.call-start = ((), (), s32[]{:S(2)}) async-start(), calls=%async_computation.19 | async-start | bytes 245760
  533.9 300.6 %all-reduce.11.cloned.1.call-start = ((), (), s32[]{:S(2)}) async-start(), calls=%async_computation.20 | async-start | bytes 7077888 | tf_op jit(solution)/shard_map/psum | solution.py:252
  638.1 75.5 %all-to-all-start.1 = ((bf16[2,448,768]{1,0,2:T(2,128)(2,1)}), bf16[2,448,768]{1,0,2:T(2,128)(2,1)S(1)}, u32[]{:S(2)}, u32[]{:S(2)}) async-start(bf16[2,448,768]{1,0,2:T(2,128)(2,1)} %copy.334), calls=%async_computation.1 | async-start | bytes 3145728 | tf_op jit(solution)/shard_map/all_to_all | solution.py:318
  (151 other events, 943.9 us)
Sparse Core Ops, SparseCore 0:
  9.6 49.6 all-gather.14
  60.8 16.8 all-gather.16
  79.3 39.5 all-gather.18
  120.3 37.4 all-gather.20
  455.8 25.9 reduce-scatter.15
  486.1 40.6 reduce-scatter.13
  529.3 47.8 reduce-scatter.17
  579.9 47.8 reduce-scatter.19
  630.8 20.7 reduce-scatter.21
  654.4 19.7 reduce-scatter.23
  677.2 19.7 reduce-scatter.25
  699.5 134.9 all-reduce.10
where the time goes:
time: 857 us; the launch traced here: 849 us
  waiting for transfers between devices  282 us (33%)
  matrix products  280 us (33%)
  blocking collectives  103 us (12%)
  local copies, waits for them, and re-layouts  86.1 us (10%)
  other arithmetic  57.6 us (7%)
  starting transfers between devices  21 us (2%)
  between operations  18.9 us (2%)
    psum x1, waiting for transfers between devices, reduce_grads(): lax.psum(as_sent(layer_grads), 'dp')  114 us
    unnamed x2, blocking collectives  63.6 us
    dot_general x3, matrix products, layer_forward(): jnp.dot(normed_mid, w_fc1, preferred_element_type=jnp.float32)  55.2 us
    reduce_scatter x1, waiting for transfers between devices, reduce_grads(): lax.psum_scatter(layer_grads[8].astype(jnp.bfloat16), 'tensor', scatter_d...  50.6 us
    ppermute x4, waiting for transfers between devices, from_behind(): return lax.ppermute(block, axis, route)  44.2 us
    reduce_scatter x1, waiting for transfers between devices, reduce_grads(): lax.psum_scatter(layer_grads[6].astype(jnp.bfloat16), 'tensor', scatter_d...  43.2 us
    unnamed x15, waiting for transfers between devices  29.2 us
    dot_general x3, matrix products, layer_backward(): jnp.einsum('rd,fd->rf', mlp_grad, w_fc2, preferred_element_type=jnp.float32)  25 us
  transfers between devices with their start and end apart: 18, of which 9 were waited for; matrix products, arithmetic and copies ran while one was open for 22% of the time, Pallas kernels for 0%

commit v1 on v0

v1 whole, which is shorter than its diff:
```python
import jax
import jax.numpy as jnp
from jax import lax
from jax.experimental import pallas as pl
from jax.experimental.pallas import tpu as pltpu
from jax.sharding import PartitionSpec as P

D = 768
HD = 64
FRAMES = 448
SHARDS = 4
HEADS_SHARD = 3
FEATS = HEADS_SHARD * HD
QKV = 3 * FEATS
FF_SHARD = 768
HALF = D // 2
EPSILON = 1e-05
SCALE = float(HD) ** (-0.5)
VMEM_LIMIT = 48 * 1024 * 1024
GAIN1, GAIN2, SHIFT1, SHIFT2, BIAS_Q, BIAS_V, BIAS_OUT, BIAS_FC2 = range(8)
BACK_ORDER = (3, 1, 2, 0)
F32 = jnp.float32
BF16 = jnp.bfloat16


def matmul(left, right, left_dim=1, right_dim=0):
    return lax.dot_general(
        left, right, (((left_dim,), (right_dim,)), ((), ())), preferred_element_type=F32
    )


def normalize(values):
    center = jnp.mean(values, axis=0, keepdims=True)
    moved = values - center
    inv_std = lax.rsqrt(jnp.mean(moved * moved, axis=0, keepdims=True) + EPSILON)
    return moved * inv_std, inv_std


def norm_backward(upstream, normed, inv_std, gain):
    scaled = upstream * gain
    mean_one = jnp.mean(scaled, axis=0, keepdims=True)
    mean_two = jnp.mean(scaled * normed, axis=0, keepdims=True)
    return inv_std * (scaled - mean_one - normed * mean_two)


def row_sums(values):
    return jnp.sum(values, axis=1, keepdims=True)


def columns(parts, lanes):
    lane = lax.broadcasted_iota(jnp.int32, (parts[0].shape[0], lanes), 1)
    total = jnp.zeros((parts[0].shape[0], lanes), F32)
    for index, part in enumerate(parts):
        total = jnp.where(lane == index, part, total)
    return total


def piece_copies(info, pieces, held, sems):
    own, other, near, far, other_near, other_far = pieces
    first = pl.multiple_of(info[4] * HALF, HALF)
    second = pl.multiple_of((1 - info[4]) * HALF, HALF)
    routes = (
        (own, held.at[0]),
        (other, held.at[1]),
        (near, held.at[2, pl.ds(first, HALF)]),
        (far, held.at[2, pl.ds(second, HALF)]),
        (other_near, held.at[3, pl.ds(first, HALF)]),
        (other_far, held.at[3, pl.ds(second, HALF)]),
    )
    copies = [
        pltpu.make_async_copy(source, target, sems.at[index])
        for index, (source, target) in enumerate(routes)
    ]
    return (copies[0:1], copies[1:2], copies[2:4], copies[4:6])


def load_pieces(step, order, chunks):
    @pl.when(step == 0)
    def start():
        for slot in order:
            for chunk in chunks:
                for copy in chunk[slot]:
                    copy.start()

    for index, slot in enumerate(order):

        @pl.when(step == index)
        def wait():
            for chunk in chunks:
                for copy in chunk[slot]:
                    copy.wait()


def attention_forward_kernel(
    info, x_ref, col_ref, w0, w1, w2, w3, w4, w5, a1_ref, p_ref, soft_ref, o_ref, h_ref, held, sems
):
    step = pl.program_id(0)
    copies = piece_copies(info, (w0, w1, w2, w3, w4, w5), held, sems)
    load_pieces(step, range(SHARDS), (copies,))

    @pl.when(step == 0)
    def first():
        col = col_ref[...].reshape(D, 8)
        values = x_ref[...].astype(F32)
        normed, _ = normalize(values)
        a1_ref[...] = (
            normed * col[:, GAIN1 : GAIN1 + 1] + col[:, SHIFT1 : SHIFT1 + 1]
        ).astype(BF16)
        h_ref[...] = values + col[:, BIAS_OUT : BIAS_OUT + 1]

    bias = col_ref[info[step]]
    projected = matmul(held[step, :QKV], a1_ref[...])
    queries = (projected[:FEATS] + bias[:, BIAS_Q : BIAS_Q + 1]).astype(BF16)
    keys = projected[FEATS : 2 * FEATS].astype(BF16)
    values = (projected[2 * FEATS :] + bias[:, BIAS_V : BIAS_V + 1]).astype(BF16)
    p_ref[0, :FEATS] = queries
    p_ref[0, FEATS : 2 * FEATS] = keys
    p_ref[0, 2 * FEATS :] = values
    scaled = queries * SCALE
    for head in range(HEADS_SHARD):
        rows = slice(head * HD, (head + 1) * HD)
        scores = matmul(keys[rows], scaled[rows], 0, 0)
        exps = jnp.exp(scores - jnp.max(scores, axis=0, keepdims=True))
        soft = exps * (1.0 / jnp.sum(exps, axis=0, keepdims=True))
        soft = soft.astype(BF16)
        soft_ref[0, head] = soft
        o_ref[0, rows] = matmul(values[rows], soft).astype(BF16)
    h_ref[...] += matmul(held[step, QKV:], o_ref[0], 0, 0)


def mlp_forward_kernel(
    info, h_ref, col_ref, b1_ref,
    w0, w1, w2, w3, w4, w5, v0, v1, v2, v3, v4, v5,
    a2_ref, u_ref, slope_ref, y_ref, held_one, held_two, a2_rows, total, sems_one, sems_two,
):
    step = pl.program_id(0)
    copies_one = piece_copies(info, (w0, w1, w2, w3, w4, w5), held_one, sems_one)
    copies_two = piece_copies(info, (v0, v1, v2, v3, v4, v5), held_two, sems_two)
    load_pieces(step, range(SHARDS), (copies_one, copies_two))

    @pl.when(step == 0)
    def first():
        col = col_ref[...].reshape(D, 8)
        normed, _ = normalize(h_ref[...])
        scaled = normed * col[:, GAIN2 : GAIN2 + 1] + col[:, SHIFT2 : SHIFT2 + 1]
        a2_ref[...] = scaled.astype(BF16)
        a2_rows[...] = scaled.T.astype(BF16)
        total[...] = jnp.zeros_like(total)

    inner = matmul(a2_rows[...], held_one[step]) + b1_ref[info[step]]
    phi = 0.5 + 0.5 * lax.erf(inner * 0.7071067811865476)
    density = 0.3989422804014327 * jnp.exp(-0.5 * inner * inner)
    active = (inner * phi).astype(BF16)
    u_ref[0] = active
    slope_ref[0] = (phi + inner * density).astype(BF16)
    total[...] += matmul(active, held_two[step])

    @pl.when(step == SHARDS - 1)
    def last():
        col = col_ref[...].reshape(D, 8)
        y_ref[...] = h_ref[...] + total[...].T + col[:, BIAS_FC2 : BIAS_FC2 + 1]


def mlp_backward_kernel(
    info, gy_ref, h_ref, a2_ref, col_ref, u_ref, slope_ref,
    w0, w1, w2, w3, w4, w5, v0, v1, v2, v3, v4, v5,
    gh_ref, send_one, keep_one, send_two, keep_two, db1_ref, dcol_ref,
    held_one, held_two, gy_rows, total, sems_one, sems_two,
):
    step = pl.program_id(0)
    copies_one = piece_copies(info, (w0, w1, w2, w3, w4, w5), held_one, sems_one)
    copies_two = piece_copies(info, (v0, v1, v2, v3, v4, v5), held_two, sems_two)
    load_pieces(step, BACK_ORDER, (copies_two, copies_one))

    @pl.when(step == 0)
    def first():
        gy_rows[...] = gy_ref[...].astype(F32).T.astype(BF16)
        total[...] = jnp.zeros_like(total)

    slot = info[5 + step]
    d_active = matmul(gy_rows[...], held_two[slot], 1, 1)
    d_inner = d_active * slope_ref[0].astype(F32)
    rounded = d_inner.astype(BF16)
    db1_ref[info[slot]] = jnp.sum(rounded.astype(F32), axis=0, keepdims=True)
    d_two = matmul(u_ref[0], gy_rows[...], 0, 0).astype(BF16)
    d_one = matmul(a2_ref[...], rounded).astype(BF16)

    @pl.when(step < 2)
    def sent():
        send_one[0] = d_one
        send_two[0] = d_two

    @pl.when(step >= 2)
    def kept():
        keep_one[0] = d_one
        keep_two[0] = d_two

    total[...] += matmul(rounded, held_one[slot], 1, 1)

    @pl.when(step == SHARDS - 1)
    def last():
        col = col_ref[...].reshape(D, 8)
        normed, inv_std = normalize(h_ref[...])
        d_mid = total[...].T
        upstream = gy_ref[...].astype(F32)
        d_hidden = upstream + norm_backward(d_mid, normed, inv_std, col[:, GAIN2 : GAIN2 + 1])
        gh_ref[...] = d_hidden
        dcol_ref[...] = columns(
            [row_sums(d_mid * normed), row_sums(d_mid), row_sums(d_hidden), row_sums(upstream)], 8
        )


def attention_backward_kernel(
    info, gh_ref, x_ref, a1_ref, col_ref, p_ref, soft_ref, o_ref,
    w0, w1, w2, w3, w4, w5,
    gx_ref, send_ref, keep_ref, dbqv_ref, dcol_ref,
    held, gh_rounded, g_p, total, sems,
):
    step = pl.program_id(0)
    copies = piece_copies(info, (w0, w1, w2, w3, w4, w5), held, sems)
    load_pieces(step, BACK_ORDER, (copies,))

    @pl.when(step == 0)
    def first():
        gh_rounded[...] = gh_ref[...].astype(BF16)
        total[...] = jnp.zeros_like(total)

    slot = info[5 + step]
    d_attended = matmul(held[slot, QKV:], gh_rounded[...]).astype(BF16)
    d_out = matmul(o_ref[0], gh_rounded[...], 1, 1).astype(BF16)
    for head in range(HEADS_SHARD):
        rows = slice(head * HD, (head + 1) * HD)
        queries = p_ref[0, rows]
        keys = p_ref[0, FEATS + head * HD : FEATS + (head + 1) * HD]
        values = p_ref[0, 2 * FEATS + head * HD : 2 * FEATS + (head + 1) * HD]
        soft = soft_ref[0, head]
        d_att = d_attended[rows]
        delta = jnp.sum(
            d_att.astype(F32) * o_ref[0, rows].astype(F32), axis=0, keepdims=True
        )
        d_soft = matmul(values, d_att, 0, 0)
        d_scores = (soft.astype(F32) * (d_soft - delta)).astype(BF16)
        g_p[rows] = (matmul(keys, d_scores) * SCALE).astype(BF16)
        g_p[FEATS + head * HD : FEATS + (head + 1) * HD] = (
            matmul(queries, d_scores, 1, 1) * SCALE
        ).astype(BF16)
        g_p[2 * FEATS + head * HD : 2 * FEATS + (head + 1) * HD] = matmul(
            d_att, soft, 1, 1
        ).astype(BF16)
    d_projected = g_p[...]
    d_qkv = matmul(d_projected, a1_ref[...], 1, 1).astype(BF16)
    total[...] += matmul(d_projected, held[slot, :QKV], 0, 0)
    dbqv_ref[info[slot]] = columns(
        [row_sums(d_projected[:FEATS].astype(F32)), row_sums(d_projected[2 * FEATS :].astype(F32))],
        8,
    )

    @pl.when(step < 2)
    def sent():
        send_ref[0, :QKV] = d_qkv
        send_ref[0, QKV:] = d_out

    @pl.when(step >= 2)
    def kept():
        keep_ref[0, :QKV] = d_qkv
        keep_ref[0, QKV:] = d_out

    @pl.when(step == SHARDS - 1)
    def last():
        col = col_ref[...].reshape(D, 8)
        normed, inv_std = normalize(x_ref[...].astype(F32))
        d_first = total[...].T
        gx_ref[...] = gh_ref[...] + norm_backward(
            d_first, normed, inv_std, col[:, GAIN1 : GAIN1 + 1]
        )
        dcol_ref[...] = columns([row_sums(d_first * normed), row_sums(d_first)], 8)


def whole(shape):
    return pl.BlockSpec(shape, lambda i, info: (0,) * len(shape))


def by_step(shape):
    return pl.BlockSpec((1,) + shape, lambda i, info: (i,) + (0,) * len(shape))


def by_slot(shape):
    return pl.BlockSpec((1,) + shape, lambda i, info: (info[5 + i],) + (0,) * len(shape))


SENT = pl.BlockSpec((1, D, D), lambda i, info: (jnp.minimum(i, 1), 0, 0))
KEPT = pl.BlockSpec((1, D, D), lambda i, info: (jnp.maximum(i - 2, 0), 0, 0))
PIECES = [pl.BlockSpec(memory_space=pl.ANY)] * 6
COPY_SEMS = pltpu.SemaphoreType.DMA((6,))
HELD = pltpu.VMEM((SHARDS, D, D), BF16)


def of(shape, dtype=BF16):
    return jax.ShapeDtypeStruct(shape, dtype)


def run(kernel, name, info, operands, in_specs, outs, out_specs, scratch, flops):
    moved = sum(a.size * a.dtype.itemsize for a in operands) + sum(
        a.size * a.dtype.itemsize for a in outs
    )
    return pl.pallas_call(
        kernel,
        name=name,
        out_shape=outs,
        grid_spec=pltpu.PrefetchScalarGridSpec(
            num_scalar_prefetch=1,
            grid=(SHARDS,),
            in_specs=in_specs,
            out_specs=out_specs,
            scratch_shapes=scratch,
        ),
        compiler_params=pltpu.CompilerParams(
            vmem_limit_bytes=VMEM_LIMIT, dimension_semantics=("arbitrary",)
        ),
        cost_estimate=pl.CostEstimate(flops=flops, bytes_accessed=moved, transcendentals=0),
    )(info, *operands)


STREAM = (D, FRAMES)
ATT_FLOPS = 2 * FRAMES * D * (4 * D + 2 * FRAMES)
MLP_FLOPS = 4 * FRAMES * D * SHARDS * FF_SHARD


def attention_forward(info, x, col, chunk):
    return run(
        attention_forward_kernel, "attention_forward", info, (x, col, *chunk),
        [whole(STREAM), whole((SHARDS, FEATS, 8))] + PIECES,
        [
            of(STREAM), of((SHARDS, QKV, FRAMES)), of((SHARDS, HEADS_SHARD, FRAMES, FRAMES)),
            of((SHARDS, FEATS, FRAMES)), of(STREAM, F32),
        ],
        [
            whole(STREAM), by_step((QKV, FRAMES)), by_step((HEADS_SHARD, FRAMES, FRAMES)),
            by_step((FEATS, FRAMES)), whole(STREAM),
        ],
        [HELD, COPY_SEMS],
        ATT_FLOPS,
    )


def mlp_forward(info, h, col, b1, chunk_one, chunk_two):
    return run(
        mlp_forward_kernel, "mlp_forward", info, (h, col, b1, *chunk_one, *chunk_two),
        [whole(STREAM), whole((SHARDS, FEATS, 8)), whole((SHARDS, 1, FF_SHARD))] + PIECES * 2,
        [of(STREAM), of((SHARDS, FRAMES, FF_SHARD)), of((SHARDS, FRAMES, FF_SHARD)), of(STREAM, F32)],
        [whole(STREAM), by_step((FRAMES, FF_SHARD)), by_step((FRAMES, FF_SHARD)), whole(STREAM)],
        [
            HELD, HELD, pltpu.VMEM((FRAMES, D), BF16), pltpu.VMEM((FRAMES, D), F32),
            COPY_SEMS, COPY_SEMS,
        ],
        MLP_FLOPS,
    )


def mlp_backward(info, gy, h, a2, col, u, slope, chunk_one, chunk_two):
    pair = of((2, D, D))
    return run(
        mlp_backward_kernel, "mlp_backward", info, (gy, h, a2, col, u, slope, *chunk_one, *chunk_two),
        [
            whole(STREAM), whole(STREAM), whole(STREAM), whole((SHARDS, FEATS, 8)),
            by_slot((FRAMES, FF_SHARD)), by_slot((FRAMES, FF_SHARD)),
        ]
        + PIECES * 2,
        [of(STREAM, F32), pair, pair, pair, pair, of((SHARDS, 1, FF_SHARD), F32), of((D, 8), F32)],
        [whole(STREAM), SENT, KEPT, SENT, KEPT, whole((SHARDS, 1, FF_SHARD)), whole((D, 8))],
        [
            HELD, HELD, pltpu.VMEM((FRAMES, D), BF16), pltpu.VMEM((FRAMES, D), F32),
            COPY_SEMS, COPY_SEMS,
        ],
        2 * MLP_FLOPS,
    )


def attention_backward(info, gh, x, a1, col, p, soft, o, chunk):
    pair = of((2, D, D))
    return run(
        attention_backward_kernel, "attention_backward", info, (gh, x, a1, col, p, soft, o, *chunk),
        [
            whole(STREAM), whole(STREAM), whole(STREAM), whole((SHARDS, FEATS, 8)),
            by_slot((QKV, FRAMES)), by_slot((HEADS_SHARD, FRAMES, FRAMES)), by_slot((FEATS, FRAMES)),
        ]
        + PIECES,
        [of(STREAM, F32), pair, pair, of((SHARDS, FEATS, 8), F32), of((D, 8), F32)],
        [whole(STREAM), SENT, KEPT, whole((SHARDS, FEATS, 8)), whole((D, 8))],
        [
            HELD, pltpu.VMEM(STREAM, BF16), pltpu.VMEM((QKV, FRAMES), BF16),
            pltpu.VMEM((FRAMES, D), F32), COPY_SEMS,
        ],
        2 * ATT_FLOPS,
    )


def flip(block, axis, bit):
    size = lax.axis_size(axis)
    return lax.ppermute(block, axis, [(i, i ^ bit) for i in range(size)])


def spread(own, zhalf):
    half = lax.dynamic_slice_in_dim(own, zhalf * HALF, HALF, axis=0)
    near = flip(half, "tensor", 2)
    far = flip(near, "dp", 1)
    other = flip(own, "tensor", 1)
    return (own, other, near, far, flip(near, "tensor", 1), flip(far, "tensor", 1))


def added(left, right):
    return (left.astype(F32) + right.astype(F32)).astype(BF16)


def reduce_chunk(send, keep, layer):
    other = flip(send, "tensor", 1)
    total = added(keep[1], other[1])
    away = added(keep[0], other[0])
    total = added(total, flip(away, "tensor", 2))
    total = added(total, lax.ppermute(total, "section", [(1 - layer, layer)]))
    n_dp = lax.axis_size("dp")
    if n_dp != 4:
        return lax.psum(total, "dp")
    axes = ("section", "dp")
    base = layer * n_dp
    total = added(total, lax.ppermute(total, axes, [(base, base + 1), (base + 3, base + 2)]))
    total = added(total, lax.ppermute(total, axes, [(base + 1, base + 2), (base + 2, base + 1)]))
    back = lax.ppermute(total, axes, [(base + 1, base), (base + 2, base + 3)])
    place = lax.axis_index("dp")
    return jnp.where((place == 0) | (place == 3), back, total)


def body(ends_in, ln_gain, ln_shift, w_qkv, b_qv, w_out, b_out, w_fc1, b_fc1, w_fc2, b_fc2):
    section = lax.axis_index("section")
    shard = lax.axis_index("tensor")
    zhalf = lax.axis_index("dp") % 2
    clips = ends_in.shape[1] // FRAMES
    info = jnp.stack(
        [shard, shard ^ 1, shard ^ 2, shard ^ 3, zhalf] + [jnp.int32(k) for k in BACK_ORDER]
    ).astype(jnp.int32)

    small = jnp.concatenate(
        [
            ln_gain[0], ln_shift[0], b_qv[0], b_out, b_fc2, b_fc1.reshape(SHARDS, FEATS),
        ],
        axis=0,
    )
    small = lax.all_gather(small, ("section", "tensor"), axis=0, tiled=False)
    small = small.reshape(2, SHARDS, 12, FEATS).astype(F32)
    cols = jnp.transpose(small[:, :, :8], (0, 1, 3, 2))
    b1s = small[:, :, 8:].reshape(2, SHARDS, 1, FF_SHARD)

    ends = ends_in[0].T.reshape(FEATS, clips, FRAMES).transpose(1, 0, 2)
    ends = lax.all_to_all(ends, ("section", "tensor"), split_axis=0, concat_axis=0, tiled=True)
    ends = ends.reshape(2, D, FRAMES)

    owned = [
        jnp.concatenate([w_qkv[0].transpose(1, 2, 0).reshape(QKV, D), w_out[0]], axis=0),
        w_fc1[0],
        w_fc2[0],
    ]
    chunks = [[], []]
    previous = None
    for own in owned:
        leaving = own
        if previous is not None:
            leaving, _ = lax.optimization_barrier((own, previous))
        previous = flip(leaving, "section", 1)
        chunks[0].append(jnp.where(section == 0, own, previous))
        chunks[1].append(jnp.where(section == 0, previous, own))
    chunks = [[spread(own, zhalf) for own in layer] for layer in chunks]

    stream = ends[0]
    stored = []
    for layer in range(2):
        chunk_a, chunk_one, chunk_two = chunks[layer]
        a1, p, soft, o, h = attention_forward(info, stream, cols[layer], chunk_a)
        a2, u, slope, y = mlp_forward(info, h, cols[layer], b1s[layer], chunk_one, chunk_two)
        stored.append((stream, a1, p, soft, o, h, a2, u, slope))
        stream = y

    upstream = ends[1]
    summed = [None, None]
    smalls = [None, None]
    for layer in (1, 0):
        chunk_a, chunk_one, chunk_two = chunks[layer]
        x, a1, p, soft, o, h, a2, u, slope = stored[layer]
        gh, send_one, keep_one, send_two, keep_two, db1, dcol_two = mlp_backward(
            info, upstream, h, a2, cols[layer], u, slope, chunk_one, chunk_two
        )
        grad_two = reduce_chunk(send_two, keep_two, layer)
        grad_one = reduce_chunk(send_one, keep_one, layer)
        upstream, send_a, keep_a, dbqv, dcol_one = attention_backward(
            info, gh, x, a1, cols[layer], p, soft, o, chunk_a
        )
        grad_a = reduce_chunk(send_a, keep_a, layer)
        summed[layer] = (grad_a, grad_one, grad_two)
        dcol = jnp.stack(
            [
                dcol_one[:, 0], dcol_two[:, 0], dcol_one[:, 1], dcol_two[:, 1],
                dbqv[:, :, 0].reshape(D), dbqv[:, :, 1].reshape(D), dcol_two[:, 2], dcol_two[:, 3],
            ]
        )
        smalls[layer] = jnp.concatenate(
            [
                dcol.reshape(8, SHARDS, FEATS).transpose(1, 0, 2),
                db1.reshape(SHARDS, SHARDS, FEATS),
            ],
            axis=1,
        )

    small_sum = lax.psum(jnp.stack(smalls), ("section", "tensor", "dp"))
    small_sum = lax.dynamic_slice(
        small_sum, (section, shard, 0, 0), (1, 1, 12, FEATS)
    ).reshape(12, FEATS)

    result = jnp.stack([upstream.astype(BF16), stream.astype(BF16)])
    result = result.reshape(2 * SHARDS, FEATS, FRAMES)
    result = lax.all_to_all(result, ("section", "tensor"), split_axis=0, concat_axis=0, tiled=True)
    result = result.transpose(1, 0, 2).reshape(FEATS, clips * FRAMES).T.astype(F32)

    grad_a, grad_one, grad_two = [
        jnp.where(section == 0, first, second).astype(F32)
        for first, second in zip(summed[0], summed[1])
    ]
    return (
        result[None],
        small_sum[None, 0:2],
        small_sum[None, 2:4],
        grad_a[:QKV].reshape(3, FEATS, D).transpose(2, 0, 1)[None],
        small_sum[None, 4:6],
        grad_a[QKV:][None],
        small_sum[6:7],
        grad_one[None],
        small_sum[8:12].reshape(1, FF_SHARD),
        grad_two[None],
        small_sum[7:8],
    )


def solution(mesh):
    placed = (
        P("section", "dp", "tensor"),
        P("section", None, "tensor"),
        P("section", None, "tensor"),
        P("section", None, None, "tensor"),
        P("section", None, "tensor"),
        P("section", "tensor", None),
        P("section", "tensor"),
        P("section", None, "tensor"),
        P("section", "tensor"),
        P("section", "tensor", None),
        P("section", "tensor"),
    )
    return jax.shard_map(
        body, mesh=mesh, in_specs=placed, out_specs=placed, check_vma=False
    )
```

time: 857 us -> 816 us (0.952)
  matrix products: 280 us -> 0 us
  waiting for transfers between devices: 282 us -> 437 us
  Pallas kernels: 0 us -> 146 us
  blocking collectives: 103 us -> 23.4 us
  starting transfers between devices: 21 us -> 90.4 us
  local copies, waits for them, and re-layouts: 86.1 us -> 43 us
    dot_general x54 -> x0, matrix products: 280 us -> none  [the longest x3 55.2 us: layer_forward(): jnp.dot(normed_mid, w_fc1, preferred_element_type=jnp.float32)]
    ppermute x4 -> x69, waiting for transfers between devices: 44.2 us -> 319 us  [the longest x45 205 us: flip(): return lax.ppermute(block, axis, [(i, i ^ bit) for i in range(size)])]
    pallas_call x0 -> x8, Pallas kernels: none -> 146 us  [run(): pl.pallas_call(kernel, name=name, out_shape=outs, grid_spec=pltpu.Prefetc...]
    reduce_scatter x4 -> x0, waiting for transfers between devices: 93.8 us -> none  [the longest x1 50.6 us: reduce_grads(): lax.psum_scatter(layer_grads[8].astype(jnp.bfloat16), 'tensor', scatter_d...]
    ppermute x4 -> x69, starting transfers between devices: 12.4 us -> 82.4 us  [the longest x45 45.5 us: flip(): return lax.ppermute(block, axis, [(i, i ^ bit) for i in range(size)])]
    unnamed x2 -> x0, blocking collectives: 63.6 us -> none
    unnamed x15 -> x1, waiting for transfers between devices: 29.2 us -> 0.02 us
    another operation x30 -> x15, local copies, waits for them, and re-layouts: 23.3 us -> 1.03 us  [the longest x14 0.94 us: body(): jnp.stack([dcol_one[:, 0], dcol_two[:, 0], dcol_one[:, 1], dcol_two[:, 1]...]
  transfers between devices with their start and end apart: 18 -> 72, of which waited for: 9 -> 26; matrix products, arithmetic and copies ran while one was open for 22% -> 10% of each run, Pallas kernels for 0% -> 5%
where the time goes in v1:
time: 816 us; the launch traced here: 809 us
  waiting for transfers between devices  437 us (54%)
  Pallas kernels  146 us (18%)
  starting transfers between devices  90.4 us (11%)
  other arithmetic  53 us (6%)
  local copies, waits for them, and re-layouts  43 us (5%)
  blocking collectives  23.4 us (3%)
  between operations  15.7 us (2%)
    ppermute x45, waiting for transfers between devices, flip(): return lax.ppermute(block, axis, [(i, i ^ bit) for i in range(size)])  205 us
    pallas_call x8, Pallas kernels, run(): pl.pallas_call(kernel, name=name, out_shape=outs, grid_spec=pltpu.Prefetc...  146 us
    psum x1, waiting for transfers between devices, body(): small_sum = lax.psum(jnp.stack(smalls), ('section', 'tensor', 'dp'))  119 us
    ppermute x6, waiting for transfers between devices, reduce_chunk(): back = lax.ppermute(total, axes, [(base + 1, base), (base + 2, base + 3)])  52.3 us
    ppermute x45, starting transfers between devices, flip(): return lax.ppermute(block, axis, [(i, i ^ bit) for i in range(size)])  45.5 us
    ppermute x6, waiting for transfers between devices, reduce_chunk(): lax.ppermute(total, axes, [(base, base + 1), (base + 3, base + 2)])  43 us
    convert_element_type x30, other arithmetic, added(): return (left.astype(F32) + right.astype(F32)).astype(BF16)  32.7 us
    all_gather x1, blocking collectives, body(): small = lax.all_gather(small, ('section', 'tensor'), axis=0, tiled=False)  23.4 us
  transfers between devices with their start and end apart: 72, of which 26 were waited for; matrix products, arithmetic and copies ran while one was open for 10% of the time, Pallas kernels for 5%

profile of v1, /device:TPU:0, one launch (start us, length us, event | category | flops | bytes accessed | tf_op | source)
XLA Modules:
  0.0 808.7 jit_solution(1442912295431127442)
XLA Ops:
  8.6 3.0 collective-permute-start
  11.6 26.0 %collective-permute-done = bf16[768,768]{1,0:T(8,128)(2,1)S(1)} collective-permute-done((bf16[768,768]{1,0:T(8,128)(2,1)S(1)}, bf16[768,768]{1,0:T(8,128)(2,1)S(1)}, u32[]{:S(2)}, u32[]{:S(2)}) %collective-permute-start) | collective-permute-done | bytes 1179680 | tf_op jit(solution)/shard_map/ppermute | solution.py:400
  43.7 13.7 %collective-permute-done.2.w2 = bf16[384,768]{1,0:T(8,128)(2,1)S(1)} collective-permute-done((bf16[384,768]{1,0:T(8,128)(2,1)S(1)}, bf16[384,768]{1,0:T(8,128)(2,1)S(1)}, u32[]{:S(2)}, u32[]{:S(2)}) %collective-permute-start.2) | collective-permute-done | bytes 589856 | tf_op jit(solution)/shard_map/ppermute | solution.py:400
  59.0 6.1 collective-permute-done.6
  65.1 4.6 collective-permute-done.19.w2
  72.8 3.2 broadcast_select_fusion.1
  77.4 7.9 collective-permute-done.20.w3
  88.6 8.7 %collective-permute-done.12 = bf16[768,768]{1,0:T(8,128)(2,1)S(1)} collective-permute-done((bf16[768,768]{1,0:T(8,128)(2,1)S(1)}, bf16[768,768]{1,0:T(8,128)(2,1)S(1)}, u32[]{:S(2)}, u32[]{:S(2)}) %collective-permute-start.12) | collective-permute-done | bytes 1179680 | tf_op jit(solution)/shard_map/ppermute | solution.py:400
  103.3 10.3 %collective-permute-done.24.w2 = bf16[384,768]{1,0:T(8,128)(2,1)} collective-permute-done((bf16[384,768]{1,0:T(8,128)(2,1)S(1)}, bf16[384,768]{1,0:T(8,128)(2,1)}, u32[]{:S(2)}, u32[]{:S(2)}) %collective-permute-start.24) | collective-permute-done | bytes 589856 | tf_op jit(solution)/shard_map/ppermute | solution.py:400
  113.6 4.2 reshape.167
  117.8 3.0 copy.134
  120.8 4.4 all-to-all-start
  126.2 23.4 %all-gather.1 = bf16[8,12,192]{2,1,0:T(8,128)(2,1)S(1)} all-gather(bf16[1,12,192]{2,1,0:T(8,128)(2,1)S(1)} %bitcast.141), channel_id=2, replica_groups=mesh['section'=2,'tensor'=4,'dp'=4] {'section','tensor'}, dimensions={0}, use_global_device_ids=true | all-gather | bytes 41472 | tf_op jit(solution)/shard_map/all_gather | solution.py:448
  158.0 10.0 %collective-permute-done.25.w3 = bf16[384,768]{1,0:T(8,128)(2,1)} collective-permute-done((bf16[384,768]{1,0:T(8,128)(2,1)}, bf16[384,768]{1,0:T(8,128)(2,1)}, u32[]{:S(2)}, u32[]{:S(2)}) %collective-permute-start.25) | collective-permute-done | bytes 589856 | tf_op jit(solution)/shard_map/ppermute | solution.py:400
  169.7 11.0 %collective-permute-done.15.v3 = bf16[384,768]{1,0:T(8,128)(2,1)} collective-permute-done((bf16[384,768]{1,0:T(8,128)(2,1)}, bf16[384,768]{1,0:T(8,128)(2,1)}, u32[]{:S(2)}, u32[]{:S(2)}) %collective-permute-start.15) | collective-permute-done | bytes 589856 | tf_op jit(solution)/shard_map/ppermute | solution.py:400
  182.0 2.4 fusion.23
  187.6 15.0 %attention_forward.2 = (bf16[768,448]{1,0:T(8,128)(2,1)S(1)}, bf16[4,576,448]{2,1,0:T(8,128)(2,1)}, bf16[4,3,448,448]{3,2,1,0:T(8,128)(2,1)}, bf16[4,192,448]{2,1,0:T(8,128)(2,1)S(1)}, f32[768,448]{1,0:T(8,128)}) custom-call(s32[9]{0:T(128)S(1)} %stack.79.info, bf16[768,448]{1,0:T(8,128)(2,1)S(1)} %bitcast.125, f32[4,192,8]{2,1,0:T(8,128)S(1)} %get-tuple-element.203.col_ref, ...), custom_call_target="tpu_custom_call" | custom-call | flops 2730491904 | bytes 15065088 | tf_op jit(solution)/shard_map/attention_forward/pallas_call | solution.py:306
  205.4 13.5 %mlp_forward.2 = (bf16[768,448]{1,0:T(8,128)(2,1)S(1)}, bf16[4,448,768]{2,1,0:T(8,128)(2,1)}, bf16[4,448,768]{2,1,0:T(8,128)(2,1)}, f32[768,448]{1,0:T(8,128)}) custom-call(s32[9]{0:T(128)S(1)} %stack.79.info, f32[768,448]{1,0:T(8,128)} %get-tuple-element.55.h_ref, f32[4,192,8]{2,1,0:T(8,128)S(1)} %get-tuple-element.203.col_ref, ...), custom_call_target="tpu_custom_call" | custom-call | flops 4227858432 | bytes 18419712 | tf_op jit(solution)/shard_map/mlp_forward/pallas_call | solution.py:306
  219.0 15.7 %attention_forward.3 = (bf16[768,448]{1,0:T(8,128)(2,1)S(1)}, bf16[4,576,448]{2,1,0:T(8,128)(2,1)}, bf16[4,3,448,448]{3,2,1,0:T(8,128)(2,1)}, bf16[4,192,448]{2,1,0:T(8,128)(2,1)S(1)}, f32[768,448]{1,0:T(8,128)}) custom-call(s32[9]{0:T(128)S(1)} %stack.79.info, f32[768,448]{1,0:T(8,128)} %get-tuple-element.58.x_ref, ...), custom_call_target="tpu_custom_call" | custom-call | flops 2730491904 | bytes 15753216 | tf_op jit(solution)/shard_map/attention_forward/pallas_call | solution.py:306
  234.7 13.7 %mlp_forward.3 = (bf16[768,448]{1,0:T(8,128)(2,1)S(1)}, bf16[4,448,768]{2,1,0:T(8,128)(2,1)}, bf16[4,448,768]{2,1,0:T(8,128)(2,1)}, f32[768,448]{1,0:T(8,128)}) custom-call(s32[9]{0:T(128)S(1)} %stack.79.info, f32[768,448]{1,0:T(8,128)} %get-tuple-element.59.h_ref, f32[4,192,8]{2,1,0:T(8,128)S(1)} %get-tuple-element.202.col_ref, ...), custom_call_target="tpu_custom_call" | custom-call | flops 4227858432 | bytes 18419712 | tf_op jit(solution)/shard_map/mlp_forward/pallas_call | solution.py:306
  249.3 21.8 %mlp_backward.2 = (f32[768,448]{1,0:T(8,128)}, bf16[2,768,768]{2,1,0:T(8,128)(2,1)}, bf16[2,768,768]{2,1,0:T(8,128)(2,1)}, bf16[2,768,768]{2,1,0:T(8,128)(2,1)},...) custom-call(s32[9]{0:T(128)S(1)} %stack.79.info, bf16[768,448]{1,0:T(8,128)(2,1)} %bitcast.138, ...), custom_call_target="tpu_custom_call" | custom-call | flops 8455716864 | bytes 28569600 | tf_op jit(solution)/shard_map/mlp_backward/pallas_call | solution.py:306
  271.1 21.7 %attention_backward.2 = (f32[768,448]{1,0:T(8,128)}, bf16[2,768,768]{2,1,0:T(8,128)(2,1)}, bf16[2,768,768]{2,1,0:T(8,128)(2,1)}, f32[4,192,8]{2,1,0:T(8,128)S(1)}, f32[768,8]{1,0:T(8,128)S(1)}) custom-call(s32[9]{0:T(128)S(1)} %stack.79.info, f32[768,448]{1,0:T(8,128)} %get-tuple-element.63.gh_ref, f32[768,448]{1,0:T(8,128)} %get-tuple-element.58.x_ref, ...), custom_call_target="tpu_custom_call" | custom-call | flops 5460983808 | bytes 21897216 | tf_op jit(solution)/shard_map/attention_backward/pallas_call | solution.py:306
  292.9 23.6 %mlp_backward.3 = (f32[768,448]{1,0:T(8,128)}, bf16[2,768,768]{2,1,0:T(8,128)(2,1)}, bf16[2,768,768]{2,1,0:T(8,128)(2,1)}, bf16[2,768,768]{2,1,0:T(8,128)(2,1)},...) custom-call(s32[9]{0:T(128)S(1)} %stack.79.info, ...), custom_call_target="tpu_custom_call" | custom-call | flops 8455716864 | bytes 29257728 | tf_op jit(solution)/shard_map/mlp_backward/pallas_call | solution.py:306
  316.5 21.0 %attention_backward.3 = (f32[768,448]{1,0:T(8,128)}, bf16[2,768,768]{2,1,0:T(8,128)(2,1)}, bf16[2,768,768]{2,1,0:T(8,128)(2,1)}, f32[4,192,8]{2,1,0:T(8,128)S(1)}, f32[768,8]{1,0:T(8,128)S(1)}) custom-call(s32[9]{0:T(128)S(1)} %stack.79.info, f32[768,448]{1,0:T(8,128)} %get-tuple-element.72.gh_ref, bf16[768,448]{1,0:T(8,128)(2,1)S(1)} %bitcast.126, ...), custom_call_target="tpu_custom_call" | custom-call | flops 5460983808 | bytes 21209088 | tf_op jit(solution)/shard_map/attention_backward/pallas_call | solution.py:306
  347.9 3.6 all-to-all-start.1
  351.5 118.6 %all-reduce.2.cloned.1.call-done = f32[2,4,12,192]{3,1,2,0:T(4,128)} async-done(((f32[2,4,12,192]{3,1,2,0:T(4,128)}), f32[2,4,12,192]{3,1,2,0:T(4,128)}) %all-reduce.2.cloned.1.call-update) | async-done | bytes 73744 | tf_op jit(solution)/shard_map/psum | solution.py:512
  483.1 5.3 collective-permute-start.52
  490.2 5.8 collective-permute-start.46
  497.7 6.0 collective-permute-start.64
  509.6 22.0 %collective-permute-done.34 = bf16[768,768]{1,0:T(8,128)(2,1)S(1)} collective-permute-done((bf16[768,768]{1,0:T(8,128)(2,1)S(1)}, bf16[768,768]{1,0:T(8,128)(2,1)S(1)}, u32[]{:S(2)}, u32[]{:S(2)}) %collective-permute-start.34) | collective-permute-done | bytes 1179680 | tf_op jit(solution)/shard_map/ppermute | solution.py:400
  531.6 3.4 collective-permute-start.41
  536.8 20.1 %collective-permute-done.52 = bf16[768,768]{1,0:T(8,128)(2,1)S(1)} collective-permute-done((bf16[768,768]{1,0:T(8,128)(2,1)S(1)}, bf16[768,768]{1,0:T(8,128)(2,1)S(1)}, u32[]{:S(2)}, u32[]{:S(2)}) %collective-permute-start.52) | collective-permute-done | bytes 1179680 | tf_op jit(solution)/shard_map/ppermute | solution.py:400
  560.0 22.2 %collective-permute-done.46 = bf16[768,768]{1,0:T(8,128)(2,1)S(1)} collective-permute-done((bf16[768,768]{1,0:T(8,128)(2,1)S(1)}, bf16[768,768]{1,0:T(8,128)(2,1)S(1)}, u32[]{:S(2)}, u32[]{:S(2)}) %collective-permute-start.46) | collective-permute-done | bytes 1179680 | tf_op jit(solution)/shard_map/ppermute | solution.py:400
  582.2 3.4 collective-permute-start.53
  587.4 20.1 %collective-permute-done.64 = bf16[768,768]{1,0:T(8,128)(2,1)S(1)} collective-permute-done((bf16[768,768]{1,0:T(8,128)(2,1)S(1)}, bf16[768,768]{1,0:T(8,128)(2,1)S(1)}, u32[]{:S(2)}, u32[]{:S(2)}) %collective-permute-start.64) | collective-permute-done | bytes 1179680 | tf_op jit(solution)/shard_map/ppermute | solution.py:400
  610.5 20.7 %collective-permute-done.58 = bf16[768,768]{1,0:T(8,128)(2,1)S(1)} collective-permute-done((bf16[768,768]{1,0:T(8,128)(2,1)S(1)}, bf16[768,768]{1,0:T(8,128)(2,1)S(1)}, u32[]{:S(2)}, u32[]{:S(2)}) %collective-permute-start.58) | collective-permute-done | bytes 1179680 | tf_op jit(solution)/shard_map/ppermute | solution.py:400
  631.2 3.4 collective-permute-start.65
  639.2 3.7 collective-permute-start.36
  644.2 14.4 %collective-permute-done.65 = bf16[768,768]{1,0:T(8,128)(2,1)S(1)} collective-permute-done((bf16[768,768]{1,0:T(8,128)(2,1)S(1)}, bf16[768,768]{1,0:T(8,128)(2,1)S(1)}, u32[]{:S(2)}, u32[]{:S(2)}) %collective-permute-start.65) | collective-permute-done | bytes 1179680 | tf_op jit(solution)/shard_map/ppermute | solution.py:420
  661.0 3.5 collective-permute-done.59
  671.4 23.1 %collective-permute-done.48 = bf16[768,768]{1,0:T(8,128)(2,1)S(1)} collective-permute-done((bf16[768,768]{1,0:T(8,128)(2,1)S(1)}, bf16[768,768]{1,0:T(8,128)(2,1)S(1)}, u32[]{:S(2)}, u32[]{:S(2)}) %collective-permute-start.48) | collective-permute-done | bytes 1179680 | tf_op jit(solution)/shard_map/ppermute | solution.py:426
  696.6 18.9 %collective-permute-done.60 = bf16[768,768]{1,0:T(8,128)(2,1)S(1)} collective-permute-done((bf16[768,768]{1,0:T(8,128)(2,1)S(1)}, bf16[768,768]{1,0:T(8,128)(2,1)S(1)}, u32[]{:S(2)}, u32[]{:S(2)}) %collective-permute-start.60) | collective-permute-done | bytes 1179680 | tf_op jit(solution)/shard_map/ppermute | solution.py:426
  736.1 2.4 reshape.185
  738.5 14.2 %collective-permute-done.38 = bf16[768,768]{1,0:T(8,128)(2,1)} collective-permute-done((bf16[768,768]{1,0:T(8,128)(2,1)}, bf16[768,768]{1,0:T(8,128)(2,1)}, u32[]{:S(2)}, u32[]{:S(2)}) %collective-permute-start.38) | collective-permute-done | bytes 1179680 | tf_op jit(solution)/shard_map/ppermute | solution.py:428
  756.7 21.2 %collective-permute-done.50 = bf16[768,768]{1,0:T(8,128)(2,1)} collective-permute-done((bf16[768,768]{1,0:T(8,128)(2,1)}, bf16[768,768]{1,0:T(8,128)(2,1)}, u32[]{:S(2)}, u32[]{:S(2)}) %collective-permute-start.50) | collective-permute-done | bytes 1179680 | tf_op jit(solution)/shard_map/ppermute | solution.py:428
  777.9 3.3 bitcast_convert_fusion.1
  781.2 16.9 %collective-permute-done.62 = bf16[768,768]{1,0:T(8,128)(2,1)} collective-permute-done((bf16[768,768]{1,0:T(8,128)(2,1)}, bf16[768,768]{1,0:T(8,128)(2,1)}, u32[]{:S(2)}, u32[]{:S(2)}) %collective-permute-start.62) | collective-permute-done | bytes 1179680 | tf_op jit(solution)/shard_map/ppermute | solution.py:428
  798.1 3.3 bitcast_convert_fusion
  (320 shorter events, 126.0 us)
Async XLA Ops:
  8.6 29.0 %collective-permute-start = (bf16[768,768]{1,0:T(8,128)(2,1)S(1)}, bf16[768,768]{1,0:T(8,128)(2,1)S(1)}, u32[]{:S(2)}, u32[]{:S(2)}) collective-permute-start(bf16[768,768]{1,0:T(8,128)(2,1)S(1)} %pad_maximum_fusion.1), channel_id=1, source_target_pairs={{0,16},{16,0},{1,17},{17,1},{2,18},{18,2},{3,19},{19,3},{4,20},{20... | collective-permute-start | bytes 3538952 | tf_op jit(solution)/shard_map/ppermute | solution.py:400
  41.1 29.6 %collective-permute-start.1 = (bf16[768,768]{1,0:T(8,128)(2,1)S(1)}, bf16[768,768]{1,0:T(8,128)(2,1)S(1)}, u32[]{:S(2)}, u32[]{:S(2)}) collective-permute-start(bf16[768,768]{1,0:T(8,128)(2,1)S(1)} %get-tuple-element.197.w0), channel_id=1, source_target_pairs={{0,4},{4,0},{8,12},{12,8},{1,5},{5,1},{9,13},{13,9},{2,6},{6,2},{1... | collective-permute-start | bytes 3538952 | tf_op jit(solution)/shard_map/ppermute | solution.py:400
  43.7 33.5 %collective-permute-start.18 = (bf16[768,768]{1,0:T(8,128)(2,1)S(1)}, bf16[768,768]{1,0:T(8,128)(2,1)S(1)}, u32[]{:S(2)}, u32[]{:S(2)}) collective-permute-start(bf16[768,768]{1,0:T(8,128)(2,1)S(1)} %get-tuple-element.196.w0), channel_id=1, source_target_pairs={{0,4},{4,0},{8,12},{12,8},{1,5},{5,1},{9,13},{13,9},{2,6},{6,2},{1... | collective-permute-start | bytes 3538952 | tf_op jit(solution)/shard_map/ppermute | solution.py:400
  69.7 27.6 %collective-permute-start.12 = (bf16[768,768]{1,0:T(8,128)(2,1)S(1)}, bf16[768,768]{1,0:T(8,128)(2,1)S(1)}, u32[]{:S(2)}, u32[]{:S(2)}) collective-permute-start(bf16[768,768]{1,0:T(8,128)(2,1)S(1)} %bitcast.137), channel_id=1, source_target_pairs={{0,16},{16,0},{1,17},{17,1},{2,18},{18,2},{3,19},{19,3},{4,20},{20... | collective-permute-start | bytes 3538952 | tf_op jit(solution)/shard_map/ppermute | solution.py:400
  77.2 74.4 %collective-permute-start.7 = (bf16[768,768]{1,0:T(8,128)(2,1)}, bf16[768,768]{1,0:T(8,128)(2,1)}, u32[]{:S(2)}, u32[]{:S(2)}) collective-permute-start(bf16[768,768]{1,0:T(8,128)(2,1)} %get-tuple-element.195.w0), channel_id=1, source_target_pairs={{0,4},{4,0},{8,12},{12,8},{1,5},{5,1},{9,13},{13,9},{2,6},{6,2},{1... | collective-permute-start | bytes 3538952 | tf_op jit(solution)/shard_map/ppermute | solution.py:400
  88.2 67.1 %collective-permute-start.23 = (bf16[768,768]{1,0:T(8,128)(2,1)}, bf16[768,768]{1,0:T(8,128)(2,1)}, u32[]{:S(2)}, u32[]{:S(2)}) collective-permute-start(bf16[768,768]{1,0:T(8,128)(2,1)} %get-tuple-element.194.w0), channel_id=1, source_target_pairs={{0,4},{4,0},{8,12},{12,8},{1,5},{5,1},{9,13},{13,9},{2,6},{6,2},{1... | collective-permute-start | bytes 3538952 | tf_op jit(solution)/shard_map/ppermute | solution.py:400
  100.0 53.1 %collective-permute-start.9 = (bf16[384,768]{1,0:T(8,128)(2,1)S(1)}, bf16[384,768]{1,0:T(8,128)(2,1)}, u32[]{:S(2)}, u32[]{:S(2)}) collective-permute-start(bf16[384,768]{1,0:T(8,128)(2,1)S(1)} %collective-permute-done.8.w2), channel_id=1, source_target_pairs={{0,1},{1,0},{2,3},{3,2},{4,5},{5,4},{6,7},{7,6},{8,9},{9,8},{10,11... | collective-permute-start | bytes 1769480 | tf_op jit(solution)/shard_map/ppermute | solution.py:400
  102.5 51.2 %collective-permute-start.14 = (bf16[384,768]{1,0:T(8,128)(2,1)S(1)}, bf16[384,768]{1,0:T(8,128)(2,1)}, u32[]{:S(2)}, u32[]{:S(2)}) collective-permute-start(bf16[384,768]{1,0:T(8,128)(2,1)S(1)} %constant_dynamic-slice_fusion.8), channel_id=1, source_target_pairs={{0,8},{4,12},{8,0},{12,4},{1,9},{5,13},{9,1},{13,5},{2,10},{6,14},... | collective-permute-start | bytes 1769480 | tf_op jit(solution)/shard_map/ppermute | solution.py:400
  113.6 41.7 %collective-permute-start.10 = (bf16[384,768]{1,0:T(8,128)(2,1)S(1)}, bf16[384,768]{1,0:T(8,128)(2,1)S(1)}, u32[]{:S(2)}, u32[]{:S(2)}) collective-permute-start(bf16[384,768]{1,0:T(8,128)(2,1)S(1)} %collective-permute-done.8.w2), channel_id=1, source_target_pairs={{0,4},{4,0},{8,12},{12,8},{1,5},{5,1},{9,13},{13,9},{2,6},{6,2},{1... | collective-permute-start | bytes 1769480 | tf_op jit(solution)/shard_map/ppermute | solution.py:400
  120.8 61.2 %all-to-all-start = ((bf16[8,192,448]{2,1,0:T(8,128)(2,1)}), bf16[8,192,448]{2,1,0:T(8,128)(2,1)}, u32[]{:S(2)}, u32[]{:S(2)}) async-start(bf16[8,192,448]{2,1,0:T(8,128)(2,1)} %bitcast.129), calls=%async_computation | async-start | bytes 3145728 | tf_op jit(solution)/shard_map/all_to_all | solution.py:454
  125.3 344.9 %all-reduce.2.cloned.1.call-start = ((), (), s32[]{:S(2)}) async-start(), calls=%async_computation.2 | async-start | bytes 196608 | tf_op jit(solution)/shard_map/psum | solution.py:512
  155.3 49.5 %collective-permute-start.13 = (bf16[768,768]{1,0:T(8,128)(2,1)}, bf16[768,768]{1,0:T(8,128)(2,1)}, u32[]{:S(2)}, u32[]{:S(2)}) collective-permute-start(bf16[768,768]{1,0:T(8,128)(2,1)} %copy-done.32), channel_id=1, source_target_pairs={{0,4},{4,0},{8,12},{12,8},{1,5},{5,1},{9,13},{13,9},{2,6},{6,2},{1... | collective-permute-start | bytes 3538952 | tf_op jit(solution)/shard_map/ppermute | solution.py:400
  168.0 36.3 %collective-permute-start.16 = (bf16[384,768]{1,0:T(8,128)(2,1)}, bf16[384,768]{1,0:T(8,128)(2,1)}, u32[]{:S(2)}, u32[]{:S(2)}) collective-permute-start(bf16[384,768]{1,0:T(8,128)(2,1)} %collective-permute-done.14.v2), channel_id=1, source_target_pairs={{0,4},{4,0},{8,12},{12,8},{1,5},{5,1},{9,13},{13,9},{2,6},{6,2},{1... | collective-permute-start | bytes 1769480 | tf_op jit(solution)/shard_map/ppermute | solution.py:400
  168.7 35.6 %collective-permute-start.30 = (bf16[384,768]{1,0:T(8,128)(2,1)}, bf16[384,768]{1,0:T(8,128)(2,1)}, u32[]{:S(2)}, u32[]{:S(2)}) collective-permute-start(bf16[384,768]{1,0:T(8,128)(2,1)} %collective-permute-done.29.v2), channel_id=1, source_target_pairs={{0,1},{1,0},{2,3},{3,2},{4,5},{5,4},{6,7},{7,6},{8,9},{9,8},{10,11... | collective-permute-start | bytes 1769480 | tf_op jit(solution)/shard_map/ppermute | solution.py:400
  181.4 53.3 %collective-permute-start.28 = (bf16[768,768]{1,0:T(8,128)(2,1)}, bf16[768,768]{1,0:T(8,128)(2,1)}, u32[]{:S(2)}, u32[]{:S(2)}) collective-permute-start(bf16[768,768]{1,0:T(8,128)(2,1)} %get-tuple-element.192.v0), channel_id=1, source_target_pairs={{0,4},{4,0},{8,12},{12,8},{1,5},{5,1},{9,13},{13,9},{2,6},{6,2},{1... | collective-permute-start | bytes 3538952 | tf_op jit(solution)/shard_map/ppermute | solution.py:400
  204.3 30.3 %collective-permute-start.26 = (bf16[384,768]{1,0:T(8,128)(2,1)}, bf16[384,768]{1,0:T(8,128)(2,1)S(1)}, u32[]{:S(2)}, u32[]{:S(2)}) collective-permute-start(bf16[384,768]{1,0:T(8,128)(2,1)} %collective-permute-done.24.w2), channel_id=1, source_target_pairs={{0,4},{4,0},{8,12},{12,8},{1,5},{5,1},{9,13},{13,9},{2,6},{6,2},{1... | collective-permute-start | bytes 1769480 | tf_op jit(solution)/shard_map/ppermute | solution.py:400
  204.3 30.3 %collective-permute-start.27 = (bf16[384,768]{1,0:T(8,128)(2,1)}, bf16[384,768]{1,0:T(8,128)(2,1)S(1)}, u32[]{:S(2)}, u32[]{:S(2)}) collective-permute-start(bf16[384,768]{1,0:T(8,128)(2,1)} %collective-permute-done.25.w3), channel_id=1, source_target_pairs={{0,4},{4,0},{8,12},{12,8},{1,5},{5,1},{9,13},{13,9},{2,6},{6,2},{1... | collective-permute-start | bytes 1769480 | tf_op jit(solution)/shard_map/ppermute | solution.py:400
  204.8 29.8 %collective-permute-start.31 = (bf16[384,768]{1,0:T(8,128)(2,1)}, bf16[384,768]{1,0:T(8,128)(2,1)S(1)}, u32[]{:S(2)}, u32[]{:S(2)}) collective-permute-start(bf16[384,768]{1,0:T(8,128)(2,1)} %collective-permute-done.29.v2), channel_id=1, source_target_pairs={{0,4},{4,0},{8,12},{12,8},{1,5},{5,1},{9,13},{13,9},{2,6},{6,2},{1... | collective-permute-start | bytes 1769480 | tf_op jit(solution)/shard_map/ppermute | solution.py:400
  204.9 29.8 %collective-permute-start.32 = (bf16[384,768]{1,0:T(8,128)(2,1)}, bf16[384,768]{1,0:T(8,128)(2,1)S(1)}, u32[]{:S(2)}, u32[]{:S(2)}) collective-permute-start(bf16[384,768]{1,0:T(8,128)(2,1)} %collective-permute-done.30.v3), channel_id=1, source_target_pairs={{0,4},{4,0},{8,12},{12,8},{1,5},{5,1},{9,13},{13,9},{2,6},{6,2},{1... | collective-permute-start | bytes 1769480 | tf_op jit(solution)/shard_map/ppermute | solution.py:400
  340.8 136.5 %collective-permute-start.33 = (bf16[2,768,768]{2,1,0:T(8,128)(2,1)}, bf16[2,768,768]{2,1,0:T(8,128)(2,1)}, u32[]{:S(2)}, u32[]{:S(2)}) collective-permute-start(bf16[2,768,768]{2,1,0:T(8,128)(2,1)} %get-tuple-element.88), channel_id=1, source_target_pairs={{0,4},{4,0},{8,12},{12,8},{1,5},{5,1},{9,13},{13,9},{2,6},{6,2},{1... | collective-permute-start | bytes 7077896 | tf_op jit(solution)/shard_map/ppermute | solution.py:400
  341.3 139.4 %collective-permute-start.51 = (bf16[2,768,768]{2,1,0:T(8,128)(2,1)}, bf16[2,768,768]{2,1,0:T(8,128)(2,1)}, u32[]{:S(2)}, u32[]{:S(2)}) collective-permute-start(bf16[2,768,768]{2,1,0:T(8,128)(2,1)} %get-tuple-element.94), channel_id=1, source_target_pairs={{0,4},{4,0},{8,12},{12,8},{1,5},{5,1},{9,13},{13,9},{2,6},{6,2},{1... | collective-permute-start | bytes 7077896 | tf_op jit(solution)/shard_map/ppermute | solution.py:400
  341.3 141.7 %collective-permute-start.45 = (bf16[2,768,768]{2,1,0:T(8,128)(2,1)}, bf16[2,768,768]{2,1,0:T(8,128)(2,1)}, u32[]{:S(2)}, u32[]{:S(2)}) collective-permute-start(bf16[2,768,768]{2,1,0:T(8,128)(2,1)} %get-tuple-element.92), channel_id=1, source_target_pairs={{0,4},{4,0},{8,12},{12,8},{1,5},{5,1},{9,13},{13,9},{2,6},{6,2},{1... | collective-permute-start | bytes 7077896 | tf_op jit(solution)/shard_map/ppermute | solution.py:400
  341.8 148.4 %collective-permute-start.63 = (bf16[2,768,768]{2,1,0:T(8,128)(2,1)}, bf16[2,768,768]{2,1,0:T(8,128)(2,1)}, u32[]{:S(2)}, u32[]{:S(2)}) collective-permute-start(bf16[2,768,768]{2,1,0:T(8,128)(2,1)} %get-tuple-element.98), channel_id=1, source_target_pairs={{0,4},{4,0},{8,12},{12,8},{1,5},{5,1},{9,13},{13,9},{2,6},{6,2},{1... | collective-permute-start | bytes 7077896 | tf_op jit(solution)/shard_map/ppermute | solution.py:400
  345.6 152.1 %collective-permute-start.57 = (bf16[2,768,768]{2,1,0:T(8,128)(2,1)}, bf16[2,768,768]{2,1,0:T(8,128)(2,1)}, u32[]{:S(2)}, u32[]{:S(2)}) collective-permute-start(bf16[2,768,768]{2,1,0:T(8,128)(2,1)} %get-tuple-element.96), channel_id=1, source_target_pairs={{0,4},{4,0},{8,12},{12,8},{1,5},{5,1},{9,13},{13,9},{2,6},{6,2},{1... | collective-permute-start | bytes 7077896 | tf_op jit(solution)/shard_map/ppermute | solution.py:400
  347.9 385.9 %all-to-all-start.1 = ((bf16[8,192,448]{2,1,0:T(8,128)(2,1)}), bf16[8,192,448]{2,1,0:T(8,128)(2,1)S(1)}, u32[]{:S(2)}, u32[]{:S(2)}) async-start(bf16[8,192,448]{2,1,0:T(8,128)(2,1)} %bitcast.26), calls=%async_computation.1 | async-start | bytes 3145728 | tf_op jit(solution)/shard_map/all_to_all | solution.py:519
  477.4 29.0 %collective-permute-start.40 = (bf16[768,768]{1,0:T(8,128)(2,1)S(1)}, bf16[768,768]{1,0:T(8,128)(2,1)S(1)}, u32[]{:S(2)}, u32[]{:S(2)}) collective-permute-start(bf16[768,768]{1,0:T(8,128)(2,1)S(1)} %fusion.9), channel_id=1, source_target_pairs={{0,8},{4,12},{8,0},{12,4},{1,9},{5,13},{9,1},{13,5},{2,10},{6,14},... | collective-permute-start | bytes 3538952 | tf_op jit(solution)/shard_map/ppermute | solution.py:400
  480.7 50.9 %collective-permute-start.34 = (bf16[768,768]{1,0:T(8,128)(2,1)S(1)}, bf16[768,768]{1,0:T(8,128)(2,1)S(1)}, u32[]{:S(2)}, u32[]{:S(2)}) collective-permute-start(bf16[768,768]{1,0:T(8,128)(2,1)S(1)} %fusion.7), channel_id=1, source_target_pairs={{0,8},{4,12},{8,0},{12,4},{1,9},{5,13},{9,1},{13,5},{2,10},{6,14},... | collective-permute-start | bytes 3538952 | tf_op jit(solution)/shard_map/ppermute | solution.py:400
  483.1 73.8 %collective-permute-start.52 = (bf16[768,768]{1,0:T(8,128)(2,1)S(1)}, bf16[768,768]{1,0:T(8,128)(2,1)S(1)}, u32[]{:S(2)}, u32[]{:S(2)}) collective-permute-start(bf16[768,768]{1,0:T(8,128)(2,1)S(1)} %fusion.13), channel_id=1, source_target_pairs={{0,8},{4,12},{8,0},{12,4},{1,9},{5,13},{9,1},{13,5},{2,10},{6,14},... | collective-permute-start | bytes 3538952 | tf_op jit(solution)/shard_map/ppermute | solution.py:400
  490.2 92.0 %collective-permute-start.46 = (bf16[768,768]{1,0:T(8,128)(2,1)S(1)}, bf16[768,768]{1,0:T(8,128)(2,1)S(1)}, u32[]{:S(2)}, u32[]{:S(2)}) collective-permute-start(bf16[768,768]{1,0:T(8,128)(2,1)S(1)} %fusion.11), channel_id=1, source_target_pairs={{0,8},{4,12},{8,0},{12,4},{1,9},{5,13},{9,1},{13,5},{2,10},{6,14},... | collective-permute-start | bytes 3538952 | tf_op jit(solution)/shard_map/ppermute | solution.py:400
  497.7 109.7 %collective-permute-start.64 = (bf16[768,768]{1,0:T(8,128)(2,1)S(1)}, bf16[768,768]{1,0:T(8,128)(2,1)S(1)}, u32[]{:S(2)}, u32[]{:S(2)}) collective-permute-start(bf16[768,768]{1,0:T(8,128)(2,1)S(1)} %fusion.17), channel_id=1, source_target_pairs={{0,8},{4,12},{8,0},{12,4},{1,9},{5,13},{9,1},{13,5},{2,10},{6,14},... | collective-permute-start | bytes 3538952 | tf_op jit(solution)/shard_map/ppermute | solution.py:400
  506.3 124.9 %collective-permute-start.58 = (bf16[768,768]{1,0:T(8,128)(2,1)S(1)}, bf16[768,768]{1,0:T(8,128)(2,1)S(1)}, u32[]{:S(2)}, u32[]{:S(2)}) collective-permute-start(bf16[768,768]{1,0:T(8,128)(2,1)S(1)} %fusion.15), channel_id=1, source_target_pairs={{0,8},{4,12},{8,0},{12,4},{1,9},{5,13},{9,1},{13,5},{2,10},{6,14},... | collective-permute-start | bytes 3538952 | tf_op jit(solution)/shard_map/ppermute | solution.py:400
  531.6 104.9 %collective-permute-start.41 = (bf16[768,768]{1,0:T(8,128)(2,1)S(1)}, bf16[768,768]{1,0:T(8,128)(2,1)S(1)}, u32[]{:S(2)}, u32[]{:S(2)}) collective-permute-start(bf16[768,768]{1,0:T(8,128)(2,1)S(1)} %fusion.4), channel_id=1, source_target_pairs={{0,16},{1,17},{2,18},{3,19},{4,20},{5,21},{6,22},{7,23},{8,24},{9,... | collective-permute-start | bytes 3538952 | tf_op jit(solution)/shard_map/ppermute | solution.py:420
  556.9 81.2 %collective-permute-start.35 = (bf16[768,768]{1,0:T(8,128)(2,1)S(1)}, bf16[768,768]{1,0:T(8,128)(2,1)S(1)}, u32[]{:S(2)}, u32[]{:S(2)}) collective-permute-start(bf16[768,768]{1,0:T(8,128)(2,1)S(1)} %fusion.5), channel_id=1, source_target_pairs={{16,0},{17,1},{18,2},{19,3},{20,4},{21,5},{22,6},{23,7},{24,8},{25... | collective-permute-start | bytes 3538952 | tf_op jit(solution)/shard_map/ppermute | solution.py:420
  582.2 57.0 %collective-permute-start.53 = (bf16[768,768]{1,0:T(8,128)(2,1)S(1)}, bf16[768,768]{1,0:T(8,128)(2,1)S(1)}, u32[]{:S(2)}, u32[]{:S(2)}) collective-permute-start(bf16[768,768]{1,0:T(8,128)(2,1)S(1)} %fusion.2), channel_id=1, source_target_pairs={{0,16},{1,17},{2,18},{3,19},{4,20},{5,21},{6,22},{7,23},{8,24},{9,... | collective-permute-start | bytes 3538952 | tf_op jit(solution)/shard_map/ppermute | solution.py:420
  607.5 35.7 %collective-permute-start.47 = (bf16[768,768]{1,0:T(8,128)(2,1)S(1)}, bf16[768,768]{1,0:T(8,128)(2,1)S(1)}, u32[]{:S(2)}, u32[]{:S(2)}) collective-permute-start(bf16[768,768]{1,0:T(8,128)(2,1)S(1)} %fusion.3), channel_id=1, source_target_pairs={{16,0},{17,1},{18,2},{19,3},{20,4},{21,5},{22,6},{23,7},{24,8},{25... | collective-permute-start | bytes 3538952 | tf_op jit(solution)/shard_map/ppermute | solution.py:420
  636.5 28.1 %collective-permute-start.59 = (bf16[768,768]{1,0:T(8,128)(2,1)S(1)}, bf16[768,768]{1,0:T(8,128)(2,1)S(1)}, u32[]{:S(2)}, u32[]{:S(2)}) collective-permute-start(bf16[768,768]{1,0:T(8,128)(2,1)S(1)} %fusion.1), channel_id=1, source_target_pairs={{16,0},{17,1},{18,2},{19,3},{20,4},{21,5},{22,6},{23,7},{24,8},{25... | collective-permute-start | bytes 3538952 | tf_op jit(solution)/shard_map/ppermute | solution.py:420
  638.1 27.5 %collective-permute-start.42 = (bf16[768,768]{1,0:T(8,128)(2,1)S(1)}, bf16[768,768]{1,0:T(8,128)(2,1)S(1)}, u32[]{:S(2)}, u32[]{:S(2)}) collective-permute-start(bf16[768,768]{1,0:T(8,128)(2,1)S(1)} %add_convert_fusion.22), channel_id=1, source_target_pairs={{16,17},{19,18},{20,21},{23,22},{24,25},{27,26},{28,29},{31,30}} | collective-permute-start | bytes 3538952 | tf_op jit(solution)/shard_map/ppermute | solution.py:426
  639.2 30.0 %collective-permute-start.36 = (bf16[768,768]{1,0:T(8,128)(2,1)S(1)}, bf16[768,768]{1,0:T(8,128)(2,1)S(1)}, u32[]{:S(2)}, u32[]{:S(2)}) collective-permute-start(bf16[768,768]{1,0:T(8,128)(2,1)S(1)} %add_convert_fusion.27), channel_id=1, source_target_pairs={{0,1},{3,2},{4,5},{7,6},{8,9},{11,10},{12,13},{15,14}} | collective-permute-start | bytes 3538952 | tf_op jit(solution)/shard_map/ppermute | solution.py:426
  658.6 35.9 %collective-permute-start.48 = (bf16[768,768]{1,0:T(8,128)(2,1)S(1)}, bf16[768,768]{1,0:T(8,128)(2,1)S(1)}, u32[]{:S(2)}, u32[]{:S(2)}) collective-permute-start(bf16[768,768]{1,0:T(8,128)(2,1)S(1)} %add_convert_fusion.17), channel_id=1, source_target_pairs={{0,1},{3,2},{4,5},{7,6},{8,9},{11,10},{12,13},{15,14}} | collective-permute-start | bytes 3538952 | tf_op jit(solution)/shard_map/ppermute | solution.py:426
  664.6 31.0 %collective-permute-start.66 = (bf16[768,768]{1,0:T(8,128)(2,1)S(1)}, bf16[768,768]{1,0:T(8,128)(2,1)S(1)}, u32[]{:S(2)}, u32[]{:S(2)}) collective-permute-start(bf16[768,768]{1,0:T(8,128)(2,1)S(1)} %add_convert_fusion.2), channel_id=1, source_target_pairs={{16,17},{19,18},{20,21},{23,22},{24,25},{27,26},{28,29},{31,30}} | collective-permute-start | bytes 3538952 | tf_op jit(solution)/shard_map/ppermute | solution.py:426
  665.6 49.9 %collective-permute-start.60 = (bf16[768,768]{1,0:T(8,128)(2,1)S(1)}, bf16[768,768]{1,0:T(8,128)(2,1)S(1)}, u32[]{:S(2)}, u32[]{:S(2)}) collective-permute-start(bf16[768,768]{1,0:T(8,128)(2,1)S(1)} %add_convert_fusion.7), channel_id=1, source_target_pairs={{0,1},{3,2},{4,5},{7,6},{8,9},{11,10},{12,13},{15,14}} | collective-permute-start | bytes 3538952 | tf_op jit(solution)/shard_map/ppermute | solution.py:426
  669.2 47.4 %collective-permute-start.43 = (bf16[768,768]{1,0:T(8,128)(2,1)S(1)}, bf16[768,768]{1,0:T(8,128)(2,1)S(1)}, u32[]{:S(2)}, u32[]{:S(2)}) collective-permute-start(bf16[768,768]{1,0:T(8,128)(2,1)S(1)} %add_convert_fusion.21), channel_id=1, source_target_pairs={{17,18},{18,17},{21,22},{22,21},{25,26},{26,25},{29,30},{30,29}} | collective-permute-start | bytes 3538952 | tf_op jit(solution)/shard_map/ppermute | solution.py:427
  670.3 47.4 %collective-permute-start.37 = (bf16[768,768]{1,0:T(8,128)(2,1)S(1)}, bf16[768,768]{1,0:T(8,128)(2,1)S(1)}, u32[]{:S(2)}, u32[]{:S(2)}) collective-permute-start(bf16[768,768]{1,0:T(8,128)(2,1)S(1)} %add_convert_fusion.26), channel_id=1, source_target_pairs={{1,2},{2,1},{5,6},{6,5},{9,10},{10,9},{13,14},{14,13}} | collective-permute-start | bytes 3538952 | tf_op jit(solution)/shard_map/ppermute | solution.py:427
  719.8 32.8 %collective-permute-start.38 = (bf16[768,768]{1,0:T(8,128)(2,1)}, bf16[768,768]{1,0:T(8,128)(2,1)}, u32[]{:S(2)}, u32[]{:S(2)}) collective-permute-start(bf16[768,768]{1,0:T(8,128)(2,1)} %add_convert_fusion.25), channel_id=1, source_target_pairs={{1,0},{2,3},{5,4},{6,7},{9,8},{10,11},{13,12},{14,15}} | collective-permute-start | bytes 3538952 | tf_op jit(solution)/shard_map/ppermute | solution.py:428
  722.4 34.3 %collective-permute-start.56 = (bf16[768,768]{1,0:T(8,128)(2,1)}, bf16[768,768]{1,0:T(8,128)(2,1)}, u32[]{:S(2)}, u32[]{:S(2)}) collective-permute-start(bf16[768,768]{1,0:T(8,128)(2,1)} %add_convert_fusion.10), channel_id=1, source_target_pairs={{17,16},{18,19},{21,20},{22,23},{25,24},{26,27},{29,28},{30,31}} | collective-permute-start | bytes 3538952 | tf_op jit(solution)/shard_map/ppermute | solution.py:428
  725.8 52.1 %collective-permute-start.50 = (bf16[768,768]{1,0:T(8,128)(2,1)}, bf16[768,768]{1,0:T(8,128)(2,1)}, u32[]{:S(2)}, u32[]{:S(2)}) collective-permute-start(bf16[768,768]{1,0:T(8,128)(2,1)} %add_convert_fusion.15), channel_id=1, source_target_pairs={{1,0},{2,3},{5,4},{6,7},{9,8},{10,11},{13,12},{14,15}} | collective-permute-start | bytes 3538952 | tf_op jit(solution)/shard_map/ppermute | solution.py:428
  728.5 52.7 %collective-permute-start.68 = (bf16[768,768]{1,0:T(8,128)(2,1)}, bf16[768,768]{1,0:T(8,128)(2,1)}, u32[]{:S(2)}, u32[]{:S(2)}) collective-permute-start(bf16[768,768]{1,0:T(8,128)(2,1)} %add_convert_fusion), channel_id=1, source_target_pairs={{17,16},{18,19},{21,20},{22,23},{25,24},{26,27},{29,28},{30,31}} | collective-permute-start | bytes 3538952 | tf_op jit(solution)/shard_map/ppermute | solution.py:428
  732.5 65.6 %collective-permute-start.62 = (bf16[768,768]{1,0:T(8,128)(2,1)}, bf16[768,768]{1,0:T(8,128)(2,1)}, u32[]{:S(2)}, u32[]{:S(2)}) collective-permute-start(bf16[768,768]{1,0:T(8,128)(2,1)} %add_convert_fusion.5), channel_id=1, source_target_pairs={{1,0},{2,3},{5,4},{6,7},{9,8},{10,11},{13,12},{14,15}} | collective-permute-start | bytes 3538952 | tf_op jit(solution)/shard_map/ppermute | solution.py:428
  (73 other events, 1097.2 us)
Sparse Core Ops, SparseCore 0:
  346.6 123.4 all-reduce.1

commit v2 on v1

v2 whole, which is shorter than its diff:
```python
import functools

import jax
import jax.numpy as jnp
from jax import lax
from jax.experimental import pallas as pl
from jax.experimental.pallas import tpu as pltpu
from jax.sharding import PartitionSpec as P

D = 768
HD = 64
FRAMES = 448
SHARDS = 4
HEADS_SHARD = 3
FEATS = HEADS_SHARD * HD
QKV = 3 * FEATS
FF_SHARD = 768
HALF = D // 2
EPSILON = 1e-05
SCALE = float(HD) ** (-0.5)
VMEM_LIMIT = 48 * 1024 * 1024
GAIN1, GAIN2, SHIFT1, SHIFT2, BIAS_Q, BIAS_V, BIAS_OUT, BIAS_FC2 = range(8)
BACK_ORDER = (3, 1, 2, 0)
F32 = jnp.float32
BF16 = jnp.bfloat16


def matmul(left, right, left_dim=1, right_dim=0):
    return lax.dot_general(
        left, right, (((left_dim,), (right_dim,)), ((), ())), preferred_element_type=F32
    )


def normalize(values):
    center = jnp.mean(values, axis=0, keepdims=True)
    moved = values - center
    inv_std = lax.rsqrt(jnp.mean(moved * moved, axis=0, keepdims=True) + EPSILON)
    return moved * inv_std, inv_std


def norm_backward(upstream, normed, inv_std, gain):
    scaled = upstream * gain
    mean_one = jnp.mean(scaled, axis=0, keepdims=True)
    mean_two = jnp.mean(scaled * normed, axis=0, keepdims=True)
    return inv_std * (scaled - mean_one - normed * mean_two)


def row_sums(values):
    return jnp.sum(values, axis=1, keepdims=True)


def columns(parts, lanes):
    lane = lax.broadcasted_iota(jnp.int32, (parts[0].shape[0], lanes), 1)
    total = jnp.zeros((parts[0].shape[0], lanes), F32)
    for index, part in enumerate(parts):
        total = jnp.where(lane == index, part, total)
    return total


def piece_copies(info, pieces, held, sems):
    own, other, near, far, other_near, other_far = pieces
    first = pl.multiple_of(info[4] * HALF, HALF)
    second = pl.multiple_of((1 - info[4]) * HALF, HALF)
    routes = (
        (own, held.at[0]),
        (other, held.at[1]),
        (near, held.at[2, pl.ds(first, HALF)]),
        (far, held.at[2, pl.ds(second, HALF)]),
        (other_near, held.at[3, pl.ds(first, HALF)]),
        (other_far, held.at[3, pl.ds(second, HALF)]),
    )
    copies = [
        pltpu.make_async_copy(source, target, sems.at[index])
        for index, (source, target) in enumerate(routes)
    ]
    return (copies[0:1], copies[1:2], copies[2:4], copies[4:6])


def load_pieces(step, order, chunks):
    @pl.when(step == 0)
    def start():
        for slot in order:
            for chunk in chunks:
                for copy in chunk[slot]:
                    copy.start()

    for index, slot in enumerate(order):

        @pl.when(step == index)
        def wait():
            for chunk in chunks:
                for copy in chunk[slot]:
                    copy.wait()


def attention_forward_kernel(
    info, x_ref, col_ref, bqv_ref, w0, w1, w2, w3, w4, w5, a1_ref, p_ref, soft_ref, o_ref, h_ref, held, sems
):
    step = pl.program_id(0)
    copies = piece_copies(info, (w0, w1, w2, w3, w4, w5), held, sems)
    load_pieces(step, range(SHARDS), (copies,))

    @pl.when(step == 0)
    def first():
        col = col_ref[...].reshape(D, 8)
        values = x_ref[...].astype(F32)
        normed, _ = normalize(values)
        a1_ref[...] = (
            normed * col[:, GAIN1 : GAIN1 + 1] + col[:, SHIFT1 : SHIFT1 + 1]
        ).astype(BF16)
        h_ref[...] = values + col[:, BIAS_OUT : BIAS_OUT + 1]

    bias = bqv_ref[step]
    projected = matmul(held[step, :QKV], a1_ref[...])
    queries = (projected[:FEATS] + bias[:, 0:1]).astype(BF16)
    keys = projected[FEATS : 2 * FEATS].astype(BF16)
    values = (projected[2 * FEATS :] + bias[:, 1:2]).astype(BF16)
    p_ref[0, :FEATS] = queries
    p_ref[0, FEATS : 2 * FEATS] = keys
    p_ref[0, 2 * FEATS :] = values
    scaled = queries * SCALE
    for head in range(HEADS_SHARD):
        rows = slice(head * HD, (head + 1) * HD)
        scores = matmul(keys[rows], scaled[rows], 0, 0)
        exps = jnp.exp(scores - jnp.max(scores, axis=0, keepdims=True))
        soft = exps * (1.0 / jnp.sum(exps, axis=0, keepdims=True))
        soft = soft.astype(BF16)
        soft_ref[0, head] = soft
        o_ref[0, rows] = matmul(values[rows], soft).astype(BF16)
    h_ref[...] += matmul(held[step, QKV:], o_ref[0], 0, 0)


def mlp_forward_kernel(
    info, h_ref, col_ref, b1_ref,
    w0, w1, w2, w3, w4, w5, v0, v1, v2, v3, v4, v5,
    a2_ref, u_ref, slope_ref, y_ref, held_one, held_two, a2_rows, total, sems_one, sems_two,
):
    step = pl.program_id(0)
    copies_one = piece_copies(info, (w0, w1, w2, w3, w4, w5), held_one, sems_one)
    copies_two = piece_copies(info, (v0, v1, v2, v3, v4, v5), held_two, sems_two)
    load_pieces(step, range(SHARDS), (copies_one, copies_two))

    @pl.when(step == 0)
    def first():
        col = col_ref[...].reshape(D, 8)
        normed, _ = normalize(h_ref[...])
        scaled = normed * col[:, GAIN2 : GAIN2 + 1] + col[:, SHIFT2 : SHIFT2 + 1]
        a2_ref[...] = scaled.astype(BF16)
        a2_rows[...] = scaled.T.astype(BF16)
        total[...] = jnp.zeros_like(total)

    inner = matmul(a2_rows[...], held_one[step]) + b1_ref[step]
    phi = 0.5 + 0.5 * lax.erf(inner * 0.7071067811865476)
    density = 0.3989422804014327 * jnp.exp(-0.5 * inner * inner)
    active = (inner * phi).astype(BF16)
    u_ref[0] = active
    slope_ref[0] = (phi + inner * density).astype(BF16)
    total[...] += matmul(active, held_two[step])

    @pl.when(step == SHARDS - 1)
    def last():
        col = col_ref[...].reshape(D, 8)
        y_ref[...] = h_ref[...] + total[...].T + col[:, BIAS_FC2 : BIAS_FC2 + 1]


def mlp_backward_kernel(
    last, info, gy_ref, h_ref, a2_ref, col_ref, u_ref, slope_ref, *refs
):
    step = pl.program_id(0)
    if last:
        before_ref, *refs = refs
    pieces_one, pieces_two, refs = refs[:6], refs[6:12], refs[12:]
    if last:
        gh_ref, dcol_ref, *refs = refs
    else:
        after_ref, *refs = refs
    grad_one, grad_two, db1_ref, held_one, held_two, gy_rows, total, sems_one, sems_two = refs
    copies_one = piece_copies(info, pieces_one, held_one, sems_one)
    copies_two = piece_copies(info, pieces_two, held_two, sems_two)
    load_pieces(step, BACK_ORDER[2:] if last else BACK_ORDER[:2], (copies_two, copies_one))

    @pl.when(step == 0)
    def first():
        gy_rows[...] = gy_ref[...].astype(F32).T.astype(BF16)
        total[...] = before_ref[...] if last else jnp.zeros_like(total)

    slot = info[(7 if last else 5) + step]
    d_active = matmul(gy_rows[...], held_two[slot], 1, 1)
    d_inner = d_active * slope_ref[0].astype(F32)
    rounded = d_inner.astype(BF16)
    db1_ref[step] = jnp.sum(rounded.astype(F32), axis=0, keepdims=True)
    grad_two[0] = matmul(u_ref[0], gy_rows[...], 0, 0).astype(BF16)
    grad_one[0] = matmul(a2_ref[...], rounded).astype(BF16)
    total[...] += matmul(rounded, held_one[slot], 1, 1)

    @pl.when(step == 1)
    def end():
        if not last:
            after_ref[...] = total[...]
            return
        col = col_ref[...].reshape(D, 8)
        normed, inv_std = normalize(h_ref[...])
        d_mid = total[...].T
        upstream = gy_ref[...].astype(F32)
        d_hidden = upstream + norm_backward(d_mid, normed, inv_std, col[:, GAIN2 : GAIN2 + 1])
        gh_ref[...] = d_hidden
        dcol_ref[...] = columns(
            [row_sums(d_mid * normed), row_sums(d_mid), row_sums(d_hidden), row_sums(upstream)], 8
        )


def attention_backward_kernel(
    last, info, gh_ref, x_ref, a1_ref, col_ref, p_ref, soft_ref, o_ref, *refs
):
    step = pl.program_id(0)
    if last:
        before_ref, *refs = refs
    pieces, refs = refs[:6], refs[6:]
    if last:
        gx_ref, dcol_ref, *refs = refs
    else:
        after_ref, *refs = refs
    grad_ref, dbqv_ref, held, gh_rounded, g_p, total, sems = refs
    copies = piece_copies(info, pieces, held, sems)
    load_pieces(step, BACK_ORDER[2:] if last else BACK_ORDER[:2], (copies,))

    @pl.when(step == 0)
    def first():
        gh_rounded[...] = gh_ref[...].astype(BF16)
        total[...] = before_ref[...] if last else jnp.zeros_like(total)

    slot = info[(7 if last else 5) + step]
    d_attended = matmul(held[slot, QKV:], gh_rounded[...]).astype(BF16)
    grad_ref[0, QKV:] = matmul(o_ref[0], gh_rounded[...], 1, 1).astype(BF16)
    for head in range(HEADS_SHARD):
        rows = slice(head * HD, (head + 1) * HD)
        queries = p_ref[0, rows]
        keys = p_ref[0, FEATS + head * HD : FEATS + (head + 1) * HD]
        values = p_ref[0, 2 * FEATS + head * HD : 2 * FEATS + (head + 1) * HD]
        soft = soft_ref[0, head]
        d_att = d_attended[rows]
        delta = jnp.sum(
            d_att.astype(F32) * o_ref[0, rows].astype(F32), axis=0, keepdims=True
        )
        d_soft = matmul(values, d_att, 0, 0)
        d_scores = (soft.astype(F32) * (d_soft - delta)).astype(BF16)
        g_p[rows] = (matmul(keys, d_scores) * SCALE).astype(BF16)
        g_p[FEATS + head * HD : FEATS + (head + 1) * HD] = (
            matmul(queries, d_scores, 1, 1) * SCALE
        ).astype(BF16)
        g_p[2 * FEATS + head * HD : 2 * FEATS + (head + 1) * HD] = matmul(
            d_att, soft, 1, 1
        ).astype(BF16)
    d_projected = g_p[...]
    grad_ref[0, :QKV] = matmul(d_projected, a1_ref[...], 1, 1).astype(BF16)
    total[...] += matmul(d_projected, held[slot, :QKV], 0, 0)
    dbqv_ref[step] = columns(
        [row_sums(d_projected[:FEATS].astype(F32)), row_sums(d_projected[2 * FEATS :].astype(F32))],
        8,
    )

    @pl.when(step == 1)
    def end():
        if not last:
            after_ref[...] = total[...]
            return
        col = col_ref[...].reshape(D, 8)
        normed, inv_std = normalize(x_ref[...].astype(F32))
        d_first = total[...].T
        gx_ref[...] = gh_ref[...] + norm_backward(
            d_first, normed, inv_std, col[:, GAIN1 : GAIN1 + 1]
        )
        dcol_ref[...] = columns([row_sums(d_first * normed), row_sums(d_first)], 8)


def whole(shape):
    return pl.BlockSpec(shape, lambda i, info: (0,) * len(shape))


def by_step(shape):
    return pl.BlockSpec((1,) + shape, lambda i, info: (i,) + (0,) * len(shape))


def by_slot(shape, last):
    first = 7 if last else 5
    return pl.BlockSpec((1,) + shape, lambda i, info: (info[first + i],) + (0,) * len(shape))


PIECES = [pl.BlockSpec(memory_space=pl.ANY)] * 6
COPY_SEMS = pltpu.SemaphoreType.DMA((6,))
HELD = pltpu.VMEM((SHARDS, D, D), BF16)


def of(shape, dtype=BF16):
    return jax.ShapeDtypeStruct(shape, dtype)


def run(kernel, name, steps, info, operands, in_specs, outs, out_specs, scratch, flops):
    moved = sum(a.size * a.dtype.itemsize for a in operands) + sum(
        a.size * a.dtype.itemsize for a in outs
    )
    return pl.pallas_call(
        kernel,
        name=name,
        out_shape=outs,
        grid_spec=pltpu.PrefetchScalarGridSpec(
            num_scalar_prefetch=1,
            grid=(steps,),
            in_specs=in_specs,
            out_specs=out_specs,
            scratch_shapes=scratch,
        ),
        compiler_params=pltpu.CompilerParams(
            vmem_limit_bytes=VMEM_LIMIT, dimension_semantics=("arbitrary",)
        ),
        cost_estimate=pl.CostEstimate(flops=flops, bytes_accessed=moved, transcendentals=0),
    )(info, *operands)


STREAM = (D, FRAMES)
ROWS = (FRAMES, D)
COLS = (SHARDS, FEATS, 8)
ATT_FLOPS = 2 * FRAMES * D * (4 * D + 2 * FRAMES)
MLP_FLOPS = 4 * FRAMES * D * SHARDS * FF_SHARD


def attention_forward(info, x, col, bqv, chunk):
    return run(
        attention_forward_kernel, "attention_forward", SHARDS, info, (x, col, bqv, *chunk),
        [whole(STREAM), whole(COLS), whole((SHARDS, FEATS, 2))] + PIECES,
        [
            of(STREAM), of((SHARDS, QKV, FRAMES)), of((SHARDS, HEADS_SHARD, FRAMES, FRAMES)),
            of((SHARDS, FEATS, FRAMES)), of(STREAM, F32),
        ],
        [
            whole(STREAM), by_step((QKV, FRAMES)), by_step((HEADS_SHARD, FRAMES, FRAMES)),
            by_step((FEATS, FRAMES)), whole(STREAM),
        ],
        [HELD, COPY_SEMS],
        ATT_FLOPS,
    )


def mlp_forward(info, h, col, b1, chunk_one, chunk_two):
    return run(
        mlp_forward_kernel, "mlp_forward", SHARDS, info, (h, col, b1, *chunk_one, *chunk_two),
        [whole(STREAM), whole(COLS), whole((SHARDS, 1, FF_SHARD))] + PIECES * 2,
        [of(STREAM), of((SHARDS, FRAMES, FF_SHARD)), of((SHARDS, FRAMES, FF_SHARD)), of(STREAM, F32)],
        [whole(STREAM), by_step((FRAMES, FF_SHARD)), by_step((FRAMES, FF_SHARD)), whole(STREAM)],
        [HELD, HELD, pltpu.VMEM(ROWS, BF16), pltpu.VMEM(ROWS, F32), COPY_SEMS, COPY_SEMS],
        MLP_FLOPS,
    )


def mlp_backward(info, gy, h, a2, col, u, slope, before, chunk_one, chunk_two):
    last = before is not None
    carried = (before,) if last else ()
    ends = [of(STREAM, F32), of((D, 8), F32)] if last else [of(ROWS, F32)]
    return run(
        functools.partial(mlp_backward_kernel, last), "mlp_backward", 2, info,
        (gy, h, a2, col, u, slope, *carried, *chunk_one, *chunk_two),
        [
            whole(STREAM), whole(STREAM), whole(STREAM), whole(COLS),
            by_slot((FRAMES, FF_SHARD), last), by_slot((FRAMES, FF_SHARD), last),
        ]
        + [whole(ROWS)] * len(carried)
        + PIECES * 2,
        ends + [of((2, D, D)), of((2, D, D)), of((2, 1, FF_SHARD), F32)],
        [whole(end.shape) for end in ends]
        + [by_step((D, D)), by_step((D, D)), whole((2, 1, FF_SHARD))],
        [HELD, HELD, pltpu.VMEM(ROWS, BF16), pltpu.VMEM(ROWS, F32), COPY_SEMS, COPY_SEMS],
        MLP_FLOPS,
    )


def attention_backward(info, gh, x, a1, col, p, soft, o, before, chunk):
    last = before is not None
    carried = (before,) if last else ()
    ends = [of(STREAM, F32), of((D, 8), F32)] if last else [of(ROWS, F32)]
    return run(
        functools.partial(attention_backward_kernel, last), "attention_backward", 2, info,
        (gh, x, a1, col, p, soft, o, *carried, *chunk),
        [
            whole(STREAM), whole(STREAM), whole(STREAM), whole(COLS),
            by_slot((QKV, FRAMES), last), by_slot((HEADS_SHARD, FRAMES, FRAMES), last),
            by_slot((FEATS, FRAMES), last),
        ]
        + [whole(ROWS)] * len(carried)
        + PIECES,
        ends + [of((2, D, D)), of((2, FEATS, 8), F32)],
        [whole(end.shape) for end in ends] + [by_step((D, D)), whole((2, FEATS, 8))],
        [HELD, pltpu.VMEM(STREAM, BF16), pltpu.VMEM((QKV, FRAMES), BF16), pltpu.VMEM(ROWS, F32), COPY_SEMS],
        ATT_FLOPS,
    )


def tie(groups):
    return lax.optimization_barrier(groups)


def flip(block, axis, bit):
    size = lax.axis_size(axis)
    return lax.ppermute(block, axis, [(i, i ^ bit) for i in range(size)])


def added(left, right):
    return (left.astype(F32) + right.astype(F32)).astype(BF16)


def by_bits(slots, shard):
    odd = shard % 2 == 1
    high = shard >= 2
    first, second, third, fourth = slots
    first, second = jnp.where(odd, second, first), jnp.where(odd, first, second)
    third, fourth = jnp.where(odd, fourth, third), jnp.where(odd, third, fourth)
    return jnp.stack(
        [
            jnp.where(high, third, first), jnp.where(high, fourth, second),
            jnp.where(high, first, third), jnp.where(high, second, fourth),
        ]
    )


class Chain:
    def __init__(self, layer):
        self.layer = layer
        self.total = None
        self.arrived = None

    def start(self, send):
        self.arrived = flip(send, "tensor", 1)

    def fold_cores(self, keep):
        self.away = added(keep[0], self.arrived[0])
        self.total = added(keep[1], self.arrived[1])

    def send_y(self):
        self.arrived = flip(self.away, "tensor", 2)

    def fold(self):
        if self.arrived is not None:
            self.total = added(self.total, self.arrived)

    def send_x(self):
        self.arrived = lax.ppermute(self.total, "section", [(1 - self.layer, self.layer)])

    def send_z(self, stage):
        if lax.axis_size("dp") != 4:
            self.total = lax.psum(self.total, "dp") if stage == 0 else self.total
            self.arrived = None
            return
        base = self.layer * 4
        pairs = (((0, 1), (3, 2)), ((1, 2), (2, 1)), ((1, 0), (2, 3)))[stage]
        pairs = [(base + source, base + target) for source, target in pairs]
        self.arrived = lax.ppermute(self.total, ("section", "dp"), pairs)

    def close(self):
        if self.arrived is None:
            return
        place = lax.axis_index("dp")
        self.total = jnp.where((place == 0) | (place == 3), self.arrived, self.total)


def sum_all(values):
    for axis in ("tensor", "section", "dp"):
        size, bit = lax.axis_size(axis), 1
        while bit < size:
            values = values + flip(values, axis, bit)
            bit *= 2
    return values


def body(ends_in, ln_gain, ln_shift, w_qkv, b_qv, w_out, b_out, w_fc1, b_fc1, w_fc2, b_fc2):
    section = lax.axis_index("section")
    shard = lax.axis_index("tensor")
    zhalf = lax.axis_index("dp") % 2
    clips = ends_in.shape[1] // FRAMES
    info = jnp.stack(
        [shard, shard ^ 1, shard ^ 2, shard ^ 3, zhalf] + [jnp.int32(k) for k in BACK_ORDER]
    ).astype(jnp.int32)

    ends = ends_in[0].T.reshape(FEATS, clips, FRAMES).transpose(1, 0, 2)
    ends = lax.all_to_all(ends, ("section", "tensor"), split_axis=0, concat_axis=0, tiled=True)
    ends = ends.reshape(2, D, FRAMES)

    small = jnp.concatenate(
        [ln_gain[0], ln_shift[0], b_qv[0], b_out, b_fc2, b_fc1.reshape(SHARDS, FEATS)], axis=0
    )
    beyond = flip(small, "section", 1)
    small = jnp.stack([jnp.where(section == 0, small, beyond), jnp.where(section == 0, beyond, small)])
    small_y = flip(small, "tensor", 2)
    pair = jnp.stack([small, small_y])
    pair_other = flip(pair, "tensor", 1)
    slots = jnp.stack([pair[0], pair_other[0], pair[1], pair_other[1]]).astype(F32)
    cols = jnp.transpose(by_bits(slots[:, :, :8], shard), (1, 0, 3, 2))
    bqvs = jnp.transpose(slots[:, :, 4:6], (1, 0, 3, 2))
    b1s = jnp.transpose(slots[:, :, 8:], (1, 0, 2, 3)).reshape(2, SHARDS, 1, FF_SHARD)

    owned = [
        jnp.concatenate([w_qkv[0].transpose(1, 2, 0).reshape(QKV, D), w_out[0]], axis=0),
        w_fc1[0],
        w_fc2[0],
    ]
    chunks = [[], []]
    beyond = flip(owned[0], "section", 1)
    for index, own in enumerate(owned):
        if index == 0:
            beyond, ends, cols, bqvs, b1s = tie((beyond, ends, cols, bqvs, b1s))
        arrived = beyond
        if index + 1 < len(owned):
            arrived, following = tie((arrived, owned[index + 1]))
            beyond = flip(following, "section", 1)
        both = [jnp.where(section == 0, own, arrived), jnp.where(section == 0, arrived, own)]
        halves = [lax.dynamic_slice_in_dim(w, zhalf * HALF, HALF, axis=0) for w in both]
        near = flip(halves[0], "tensor", 2)
        near, halves[1] = tie((near, halves[1]))
        near_late = flip(halves[1], "tensor", 2)
        far = flip(near, "dp", 1)
        far, near_late = tie((far, near_late))
        far_late = flip(near_late, "dp", 1)
        for layer, (w, n, f) in enumerate(((both[0], near, far), (both[1], near_late, far_late))):
            chunks[layer].append(
                (w, flip(w, "tensor", 1), n, f, flip(n, "tensor", 1), flip(f, "tensor", 1))
            )

    stream = ends[0]
    stored = []
    for layer in range(2):
        chunk_a, chunk_one, chunk_two = chunks[layer]
        a1, p, soft, o, h = attention_forward(info, stream, cols[layer], bqvs[layer], chunk_a)
        a2, u, slope, y = mlp_forward(info, h, cols[layer], b1s[layer], chunk_one, chunk_two)
        stored.append((stream, a1, p, soft, o, h, a2, u, slope))
        stream = y

    upstream = ends[1]
    chains = [[Chain(layer) for _ in range(3)] for layer in range(2)]
    smalls = [None, None]
    for layer in (1, 0):
        chunk_a, chunk_one, chunk_two = chunks[layer]
        x, a1, p, soft, o, h, a2, u, slope = stored[layer]
        chain_a, chain_one, chain_two = chains[layer]
        late_a, late_one, late_two = chains[1]
        after, send_one, send_two, db1_sent = mlp_backward(
            info, upstream, h, a2, cols[layer], u, slope, None, chunk_one, chunk_two
        )
        chain_two.start(send_two)
        chain_one.start(send_one)
        gh, dcol_two, keep_one, keep_two, db1_kept = mlp_backward(
            info, upstream, h, a2, cols[layer], u, slope, after, chunk_one, chunk_two
        )
        chain_two.fold_cores(keep_two)
        chain_one.fold_cores(keep_one)
        if layer == 1:
            gh, chain_two.away, chain_one.away = tie((gh, chain_two.away, chain_one.away))
            chain_two.send_y()
        else:
            late_one.fold()
            late_two.fold()
            gh, late_one.total, late_two.total, late_a.away, chain_two.away, chain_one.away = tie(
                (gh, late_one.total, late_two.total, late_a.away, chain_two.away, chain_one.away)
            )
            late_one.send_x()
            late_two.send_z(0)
            late_a.send_y()
        after, send_a, dbqv_sent = attention_backward(
            info, gh, x, a1, cols[layer], p, soft, o, None, chunk_a
        )
        chain_a.start(send_a)
        upstream, dcol_one, keep_a, dbqv_kept = attention_backward(
            info, gh, x, a1, cols[layer], p, soft, o, after, chunk_a
        )
        chain_a.fold_cores(keep_a)
        if layer == 1:
            late_two.fold()
            upstream, late_two.total, late_one.away = tie((upstream, late_two.total, late_one.away))
            late_two.send_x()
            late_one.send_y()
        db1 = by_bits([db1_kept[1], db1_sent[1], db1_kept[0], db1_sent[0]], shard)
        dbqv = by_bits([dbqv_kept[1], dbqv_sent[1], dbqv_kept[0], dbqv_sent[0]], shard)
        dcol = jnp.stack(
            [
                dcol_one[:, 0], dcol_two[:, 0], dcol_one[:, 1], dcol_two[:, 1],
                dbqv[:, :, 0].reshape(D), dbqv[:, :, 1].reshape(D), dcol_two[:, 2], dcol_two[:, 3],
            ]
        )
        smalls[layer] = jnp.concatenate(
            [
                dcol.reshape(8, SHARDS, FEATS).transpose(1, 0, 2),
                db1.reshape(SHARDS, SHARDS, FEATS),
            ],
            axis=1,
        )

    result = jnp.stack([upstream.astype(BF16), stream.astype(BF16)])
    result = result.reshape(2 * SHARDS, FEATS, FRAMES)
    result = lax.all_to_all(result, ("section", "tensor"), split_axis=0, concat_axis=0, tiled=True)
    result = result.transpose(1, 0, 2).reshape(FEATS, clips * FRAMES).T.astype(F32)

    small_sum = sum_all(jnp.stack(smalls))
    small_sum = lax.dynamic_slice(
        small_sum, (section, shard, 0, 0), (1, 1, 12, FEATS)
    ).reshape(12, FEATS)

    (late_a, late_one, late_two), (last_a, last_one, last_two) = chains[1], chains[0]
    late_a.fold()
    late_one.fold()
    late_two.fold()
    late_a.total, late_one.total, late_two.total, last_two.away = tie(
        (late_a.total, late_one.total, late_two.total, last_two.away)
    )
    late_a.send_x()
    late_one.send_z(0)
    late_two.send_z(1)
    last_two.send_y()
    late_a.fold()
    late_one.fold()
    late_two.fold()
    last_two.fold()
    late_a.total, late_one.total, late_two.total, last_two.total, last_one.away = tie(
        (late_a.total, late_one.total, late_two.total, last_two.total, last_one.away)
    )
    late_a.send_z(0)
    late_one.send_z(1)
    late_two.send_z(2)
    last_two.send_x()
    last_one.send_y()
    late_a.fold()
    late_one.fold()
    late_two.close()
    last_two.fold()
    last_one.fold()
    late_a.total, late_one.total, last_two.total, last_one.total, last_a.away = tie(
        (late_a.total, late_one.total, last_two.total, last_one.total, last_a.away)
    )
    late_a.send_z(1)
    late_one.send_z(2)
    last_two.send_z(0)
    last_one.send_x()
    last_a.send_y()
    late_a.fold()
    late_one.close()
    late_a.send_z(2)
    late_a.close()
    for chain in (last_two, last_one, last_a):
        chain.fold()
    last_two.send_z(1)
    last_one.send_z(0)
    last_a.send_x()
    for chain in (last_two, last_one, last_a):
        chain.fold()
    last_two.send_z(2)
    last_two.close()
    last_one.send_z(1)
    last_a.send_z(0)
    last_one.fold()
    last_a.fold()
    last_one.send_z(2)
    last_a.send_z(1)
    last_one.close()
    last_a.fold()
    last_a.send_z(2)
    last_a.close()

    grad_a, grad_one, grad_two = [
        jnp.where(section == 0, first.total, second.total).astype(F32)
        for first, second in zip(chains[0], chains[1])
    ]
    return (
        result[None],
        small_sum[None, 0:2],
        small_sum[None, 2:4],
        grad_a[:QKV].reshape(3, FEATS, D).transpose(2, 0, 1)[None],
        small_sum[None, 4:6],
        grad_a[QKV:][None],
        small_sum[6:7],
        grad_one[None],
        small_sum[8:12].reshape(1, FF_SHARD),
        grad_two[None],
        small_sum[7:8],
    )


def solution(mesh):
    placed = (
        P("section", "dp", "tensor"),
        P("section", None, "tensor"),
        P("section", None, "tensor"),
        P("section", None, None, "tensor"),
        P("section", None, "tensor"),
        P("section", "tensor", None),
        P("section", "tensor"),
        P("section", None, "tensor"),
        P("section", "tensor"),
        P("section", "tensor", None),
        P("section", "tensor"),
    )
    return jax.shard_map(
        body, mesh=mesh, in_specs=placed, out_specs=placed, check_vma=False
    )
```

time: 816 us -> 781 us (0.957)
  waiting for transfers between devices: 437 us -> 365 us
  other arithmetic: 53 us -> 85.8 us
  local copies, waits for them, and re-layouts: 43 us -> 70.6 us
  blocking collectives: 23.4 us -> 0 us
  Pallas kernels: 146 us -> 160 us
  between operations: 15.7 us -> 2.44 us
    psum x1 -> x0, waiting for transfers between devices: 119 us -> none  [body(): small_sum = lax.psum(jnp.stack(smalls), ('section', 'tensor', 'dp'))]
    ppermute x24, waiting for transfers between devices: 113 us -> 153 us  [the longest x18 93.7 us: send_z(): self.arrived = lax.ppermute(self.total, ('section', 'dp'), pairs)]
    convert_element_type x30, other arithmetic: 32.7 us -> 62.4 us  [added(): return (left.astype(F32) + right.astype(F32)).astype(BF16)]
    all_gather x1 -> x0, blocking collectives: 23.4 us -> none  [body(): small = lax.all_gather(small, ('section', 'tensor'), axis=0, tiled=False)]
    unnamed x115 -> x243, local copies, waits for them, and re-layouts: 9.72 us -> 31.8 us
    all_to_all x1, waiting for transfers between devices: 0.01 us -> 16.5 us  [body(): lax.all_to_all(ends, ('section', 'tensor'), split_axis=0, concat_axis=0,...]
    pallas_call x8 -> x12, Pallas kernels: 146 us -> 160 us  [run(): pl.pallas_call(kernel, name=name, out_shape=outs, grid_spec=pltpu.Prefetc...]
    ppermute x45 -> x53, waiting for transfers between devices: 205 us -> 195 us  [flip(): return lax.ppermute(block, axis, [(i, i ^ bit) for i in range(size)])]
  transfers between devices with their start and end apart: 72 -> 79, of which waited for: 26 -> 29; matrix products, arithmetic and copies ran while one was open for 10% -> 15% of each run, Pallas kernels for 5% -> 17%
where the time goes in v2:
time: 781 us; the launch traced here: 776 us
  waiting for transfers between devices  365 us (47%)
  Pallas kernels  160 us (20%)
  starting transfers between devices  92.1 us (12%)
  other arithmetic  85.8 us (11%)
  local copies, waits for them, and re-layouts  70.6 us (9%)
    ppermute x53, waiting for transfers between devices, flip(): return lax.ppermute(block, axis, [(i, i ^ bit) for i in range(size)])  195 us
    pallas_call x12, Pallas kernels, run(): pl.pallas_call(kernel, name=name, out_shape=outs, grid_spec=pltpu.Prefetc...  160 us
    ppermute x18, waiting for transfers between devices, send_z(): self.arrived = lax.ppermute(self.total, ('section', 'dp'), pairs)  93.7 us
    convert_element_type x30, other arithmetic, added(): return (left.astype(F32) + right.astype(F32)).astype(BF16)  62.4 us
    ppermute x6, waiting for transfers between devices, send_x(): lax.ppermute(self.total, 'section', [(1 - self.layer, self.layer)])  59.7 us
    ppermute x53, starting transfers between devices, flip(): return lax.ppermute(block, axis, [(i, i ^ bit) for i in range(size)])  40.5 us
    unnamed x243, local copies, waits for them, and re-layouts  31.8 us
    ppermute x18, starting transfers between devices, send_z(): self.arrived = lax.ppermute(self.total, ('section', 'dp'), pairs)  25.8 us
  transfers between devices with their start and end apart: 79, of which 29 were waited for; matrix products, arithmetic and copies ran while one was open for 15% of the time, Pallas kernels for 17%

profile of v2, /device:TPU:0, one launch (start us, length us, event | category | flops | bytes accessed | tf_op | source)
XLA Modules:
  0.0 775.9 jit_solution(637908093268284279)
XLA Ops:
  2.4 3.0 collective-permute-start.1
  17.0 3.2 reshape.229
  21.9 3.9 all-to-all-start
  32.4 11.8 %collective-permute-done = bf16[768,768]{1,0:T(8,128)(2,1)} collective-permute-done((bf16[768,768]{1,0:T(8,128)(2,1)}, bf16[768,768]{1,0:T(8,128)(2,1)}, u32[]{:S(2)}, u32[]{:S(2)}) %collective-permute-start) | collective-permute-done | bytes 1179680 | tf_op jit(solution)/shard_map/ppermute | solution.py:403
  44.2 16.5 %all-to-all-done = bf16[8,192,448]{2,1,0:T(8,128)(2,1)S(1)} async-done(((bf16[8,192,448]{2,1,0:T(8,128)(2,1)}), bf16[8,192,448]{2,1,0:T(8,128)(2,1)S(1)}, u32[]{:S(2)}, u32[]{:S(2)}) %all-to-all-start) | async-done | bytes 1376288 | tf_op jit(solution)/shard_map/all_to_all | solution.py:483
  65.9 13.1 %collective-permute-done.5.w2.refs_2_.refs_3_ = bf16[384,768]{1,0:T(8,128)(2,1)S(1)} collective-permute-done((bf16[384,768]{1,0:T(8,128)(2,1)S(1)}, bf16[384,768]{1,0:T(8,128)(2,1)S(1)}, u32[]{:S(2)}, u32[]{:S(2)}) %collective-permute-start.5) | collective-permute-done | bytes 589856 | tf_op jit(solution)/shard_map/ppermute | solution.py:403
  82.1 6.7 collective-permute-done.10
  100.2 15.5 %collective-permute-done.17 = bf16[768,768]{1,0:T(8,128)(2,1)S(1)} collective-permute-done((bf16[768,768]{1,0:T(8,128)(2,1)S(1)}, bf16[768,768]{1,0:T(8,128)(2,1)S(1)}, u32[]{:S(2)}, u32[]{:S(2)}) %collective-permute-start.17) | collective-permute-done | bytes 1179680 | tf_op jit(solution)/shard_map/ppermute | solution.py:403
  123.7 10.2 %collective-permute-done.19.v2.refs_8_.refs_9_ = bf16[384,768]{1,0:T(8,128)(2,1)} collective-permute-done((bf16[384,768]{1,0:T(8,128)(2,1)S(1)}, bf16[384,768]{1,0:T(8,128)(2,1)}, u32[]{:S(2)}, u32[]{:S(2)}) %collective-permute-start.19) | collective-permute-done | bytes 589856 | tf_op jit(solution)/shard_map/ppermute | solution.py:403
  135.8 10.1 %collective-permute-done.14.w2.refs_2_.refs_3_ = bf16[384,768]{1,0:T(8,128)(2,1)S(1)} collective-permute-done((bf16[384,768]{1,0:T(8,128)(2,1)S(1)}, bf16[384,768]{1,0:T(8,128)(2,1)S(1)}, u32[]{:S(2)}, u32[]{:S(2)}) %collective-permute-start.14) | collective-permute-done | bytes 589856 | tf_op jit(solution)/shard_map/ppermute | solution.py:403
  149.9 11.2 %collective-permute-done.21.v2.refs_8_.refs_9_ = bf16[384,768]{1,0:T(8,128)(2,1)} collective-permute-done((bf16[384,768]{1,0:T(8,128)(2,1)}, bf16[384,768]{1,0:T(8,128)(2,1)}, u32[]{:S(2)}, u32[]{:S(2)}) %collective-permute-start.21) | collective-permute-done | bytes 589856 | tf_op jit(solution)/shard_map/ppermute | solution.py:403
  167.1 11.6 %collective-permute-done.29.w3.refs_3_.refs_4_ = bf16[384,768]{1,0:T(8,128)(2,1)} collective-permute-done((bf16[384,768]{1,0:T(8,128)(2,1)S(1)}, bf16[384,768]{1,0:T(8,128)(2,1)}, u32[]{:S(2)}, u32[]{:S(2)}) %collective-permute-start.29) | collective-permute-done | bytes 589856 | tf_op jit(solution)/shard_map/ppermute | solution.py:403
  178.9 15.3 %attention_forward.2 = (bf16[768,448]{1,0:T(8,128)(2,1)S(1)}, bf16[4,576,448]{2,1,0:T(8,128)(2,1)}, bf16[4,3,448,448]{3,2,1,0:T(8,128)(2,1)}, bf16[4,192,448]{2,1,0:T(8,128)(2,1)S(1)}, f32[768,448]{1,0:T(8,128)}) custom-call(s32[9]{0:T(128)S(1)} %stack.151.info, bf16[768,448]{1,0:T(8,128)(2,1)S(1)} %get-tuple-element.320.x_ref, ...), custom_call_target="tpu_custom_call" | custom-call | flops 2730491904 | bytes 15071232 | tf_op jit(solution)/shard_map/attention_forward/pallas_call | solution.py:302
  196.3 13.5 %mlp_forward.2 = (bf16[768,448]{1,0:T(8,128)(2,1)S(1)}, bf16[4,448,768]{2,1,0:T(8,128)(2,1)}, bf16[4,448,768]{2,1,0:T(8,128)(2,1)}, f32[768,448]{1,0:T(8,128)}) custom-call(s32[9]{0:T(128)S(1)} %stack.151.info, f32[768,448]{1,0:T(8,128)} %get-tuple-element.116.h_ref, f32[4,192,8]{2,1,0:T(8,128)S(1)} %get-tuple-element.324.col_ref, ...), custom_call_target="tpu_custom_call" | custom-call | flops 4227858432 | bytes 18419712 | tf_op jit(solution)/shard_map/mlp_forward/pallas_call | solution.py:302
  210.0 16.4 %attention_forward.3 = (bf16[768,448]{1,0:T(8,128)(2,1)S(1)}, bf16[4,576,448]{2,1,0:T(8,128)(2,1)}, bf16[4,3,448,448]{3,2,1,0:T(8,128)(2,1)}, bf16[4,192,448]{2,1,0:T(8,128)(2,1)S(1)}, f32[768,448]{1,0:T(8,128)}) custom-call(s32[9]{0:T(128)S(1)} %stack.151.info, f32[768,448]{1,0:T(8,128)} %get-tuple-element.127.x_ref, ...), custom_call_target="tpu_custom_call" | custom-call | flops 2730491904 | bytes 15759360 | tf_op jit(solution)/shard_map/attention_forward/pallas_call | solution.py:302
  231.2 13.5 %mlp_forward.3 = (bf16[768,448]{1,0:T(8,128)(2,1)S(1)}, bf16[4,448,768]{2,1,0:T(8,128)(2,1)}, bf16[4,448,768]{2,1,0:T(8,128)(2,1)}, f32[768,448]{1,0:T(8,128)}) custom-call(s32[9]{0:T(128)S(1)} %stack.151.info, f32[768,448]{1,0:T(8,128)} %get-tuple-element.129.h_ref, f32[4,192,8]{2,1,0:T(8,128)S(1)} %get-tuple-element.323.col_ref, ...), custom_call_target="tpu_custom_call" | custom-call | flops 4227858432 | bytes 18419712 | tf_op jit(solution)/shard_map/mlp_forward/pallas_call | solution.py:302
  248.8 11.4 %mlp_backward.4 = (f32[448,768]{1,0:T(8,128)}, bf16[2,768,768]{2,1,0:T(8,128)(2,1)}, bf16[2,768,768]{2,1,0:T(8,128)(2,1)}, f32[2,1,768]{2,1,0:T(1,128)S(1)}) custom-call(s32[9]{0:T(128)S(1)} %stack.151.info, bf16[768,448]{1,0:T(8,128)(2,1)S(1)} %get-tuple-element.319.gy_ref, f32[768,448]{1,0:T(8,128)} %get-tuple-element.129.h_ref, ...), custom_call_target="tpu_custom_call" | custom-call | flops 4227858432 | bytes 23820288 | tf_op jit(solution)/shard_map/mlp_backward/pallas_call | solution.py:302
  260.8 14.2 %mlp_backward.5 = (f32[768,448]{1,0:T(8,128)}, f32[768,8]{1,0:T(8,128)S(1)}, bf16[2,768,768]{2,1,0:T(8,128)(2,1)}, bf16[2,768,768]{2,1,0:T(8,128)(2,1)}, f32[2,1,768]{2,1,0:T(1,128)S(1)}) custom-call(s32[9]{0:T(128)S(1)} %stack.151.info, bf16[768,448]{1,0:T(8,128)(2,1)} %copy-done, f32[768,448]{1,0:T(8,128)} %get-tuple-element.129.h_ref, ...), custom_call_target="tpu_custom_call" | custom-call | flops 4227858432 | bytes 25221120 | tf_op jit(solution)/shard_map/mlp_backward/pallas_call | solution.py:302
  280.6 11.7 %attention_backward.4 = (f32[448,768]{1,0:T(8,128)}, bf16[2,768,768]{2,1,0:T(8,128)(2,1)}, f32[2,192,8]{2,1,0:T(8,128)S(1)}) custom-call(s32[9]{0:T(128)S(1)} %stack.151.info, f32[768,448]{1,0:T(8,128)} %get-tuple-element.141.gh_ref, f32[768,448]{1,0:T(8,128)} %get-tuple-element.127.x_ref, bf16[768,448]{1,0:T(8,128)(2,1)S(1)} %get-tuple-element.142.a1_ref, ...), custom_call_target="tpu_custom_call" | custom-call | flops 2730491904 | bytes 19501056 | tf_op jit(solution)/shard_map/attention_backward/pallas_call | solution.py:302
  292.5 14.3 %attention_backward.5 = (f32[768,448]{1,0:T(8,128)}, f32[768,8]{1,0:T(8,128)S(1)}, bf16[2,768,768]{2,1,0:T(8,128)(2,1)}, f32[2,192,8]{2,1,0:T(8,128)S(1)}) custom-call(s32[9]{0:T(128)S(1)} %stack.151.info, f32[768,448]{1,0:T(8,128)} %get-tuple-element.141.gh_ref, f32[768,448]{1,0:T(8,128)} %get-tuple-element.127.x_ref, ...), custom_call_target="tpu_custom_call" | custom-call | flops 2730491904 | bytes 20901888 | tf_op jit(solution)/shard_map/attention_backward/pallas_call | solution.py:302
  310.2 10.9 %mlp_backward.6 = (f32[448,768]{1,0:T(8,128)}, bf16[2,768,768]{2,1,0:T(8,128)(2,1)}, bf16[2,768,768]{2,1,0:T(8,128)(2,1)}, f32[2,1,768]{2,1,0:T(1,128)S(1)}) custom-call(s32[9]{0:T(128)S(1)} %stack.151.info, f32[768,448]{1,0:T(8,128)} %get-tuple-element.150.gy_ref, f32[768,448]{1,0:T(8,128)} %get-tuple-element.116.h_ref, ...), custom_call_target="tpu_custom_call" | custom-call | flops 4227858432 | bytes 24508416 | tf_op jit(solution)/shard_map/mlp_backward/pallas_call | solution.py:302
  321.2 4.4 collective-permute-start.40
  326.7 14.1 %mlp_backward.7 = (f32[768,448]{1,0:T(8,128)}, f32[768,8]{1,0:T(8,128)S(1)}, bf16[2,768,768]{2,1,0:T(8,128)(2,1)}, bf16[2,768,768]{2,1,0:T(8,128)(2,1)}, f32[2,1,768]{2,1,0:T(1,128)S(1)}) custom-call(s32[9]{0:T(128)S(1)} %stack.151.info, f32[768,448]{1,0:T(8,128)} %get-tuple-element.150.gy_ref, f32[768,448]{1,0:T(8,128)} %get-tuple-element.116.h_ref, ...), custom_call_target="tpu_custom_call" | custom-call | flops 4227858432 | bytes 25909248 | tf_op jit(solution)/shard_map/mlp_backward/pallas_call | solution.py:302
  340.8 9.7 %collective-permute-done.40 = bf16[768,768]{1,0:T(8,128)(2,1)} collective-permute-done((bf16[768,768]{1,0:T(8,128)(2,1)S(1)}, bf16[768,768]{1,0:T(8,128)(2,1)}, u32[]{:S(2)}, u32[]{:S(2)}) %collective-permute-start.40) | collective-permute-done | bytes 1179680 | tf_op jit(solution)/shard_map/ppermute | solution.py:445
  354.4 3.2 fusion.4
  365.0 4.6 collective-permute-start.51
  379.3 14.6 %collective-permute-done.51 = bf16[768,768]{1,0:T(8,128)(2,1)} collective-permute-done((bf16[768,768]{1,0:T(8,128)(2,1)}, bf16[768,768]{1,0:T(8,128)(2,1)}, u32[]{:S(2)}, u32[]{:S(2)}) %collective-permute-start.51) | collective-permute-done | bytes 1179680 | tf_op jit(solution)/shard_map/ppermute | solution.py:445
  393.9 3.0 add_convert_fusion.19
  397.2 3.2 fusion.2
  403.1 5.2 collective-permute-start.53
  420.1 11.6 %attention_backward.6 = (f32[448,768]{1,0:T(8,128)}, bf16[2,768,768]{2,1,0:T(8,128)(2,1)}, f32[2,192,8]{2,1,0:T(8,128)S(1)}) custom-call(s32[9]{0:T(128)S(1)} %stack.151.info, f32[768,448]{1,0:T(8,128)} %get-tuple-element.164.gh_ref, bf16[768,448]{1,0:T(8,128)(2,1)S(1)} %get-tuple-element.320.x_ref, bf16[768,448]{1,0:T(8,128)(2,1)S(1)} %get-tuple-element.165.a1_ref, ...), custom_call_target="tpu_custom_call" | custom-call | flops 2730491904 | bytes 18812928 | tf_op jit(solution)/shard_map/attention_backward/pallas_call | solution.py:302
  433.9 3.0 add_convert_fusion.17
  439.6 20.5 %collective-permute-done.56 = bf16[768,768]{1,0:T(8,128)(2,1)S(1)} collective-permute-done((bf16[768,768]{1,0:T(8,128)(2,1)S(1)}, bf16[768,768]{1,0:T(8,128)(2,1)S(1)}, u32[]{:S(2)}, u32[]{:S(2)}) %collective-permute-start.56) | collective-permute-done | bytes 1179680 | tf_op jit(solution)/shard_map/ppermute | solution.py:403
  477.1 13.3 %attention_backward.7 = (f32[768,448]{1,0:T(8,128)}, f32[768,8]{1,0:T(8,128)S(1)}, bf16[2,768,768]{2,1,0:T(8,128)(2,1)}, f32[2,192,8]{2,1,0:T(8,128)S(1)}) custom-call(s32[9]{0:T(128)S(1)} %stack.151.info, f32[768,448]{1,0:T(8,128)} %get-tuple-element.164.gh_ref, bf16[768,448]{1,0:T(8,128)(2,1)S(1)} %get-tuple-element.320.x_ref, ...), custom_call_target="tpu_custom_call" | custom-call | flops 2730491904 | bytes 20213760 | tf_op jit(solution)/shard_map/attention_backward/pallas_call | solution.py:302
  492.5 2.9 fusion.17
  497.5 3.1 add_convert_fusion.12
  503.5 18.7 %collective-permute-done.59 = bf16[768,768]{1,0:T(8,128)(2,1)S(1)} collective-permute-done((bf16[768,768]{1,0:T(8,128)(2,1)}, bf16[768,768]{1,0:T(8,128)(2,1)S(1)}, u32[]{:S(2)}, u32[]{:S(2)}) %collective-permute-start.59) | collective-permute-done | bytes 1179680 | tf_op jit(solution)/shard_map/ppermute | solution.py:445
  526.7 23.5 %collective-permute-done.61 = bf16[768,768]{1,0:T(8,128)(2,1)} collective-permute-done((bf16[768,768]{1,0:T(8,128)(2,1)}, bf16[768,768]{1,0:T(8,128)(2,1)}, u32[]{:S(2)}, u32[]{:S(2)}) %collective-permute-start.61) | collective-permute-done | bytes 1179680 | tf_op jit(solution)/shard_map/ppermute | solution.py:403
  563.3 16.7 %collective-permute-done.62 = bf16[768,768]{1,0:T(8,128)(2,1)S(1)} collective-permute-done((bf16[768,768]{1,0:T(8,128)(2,1)S(1)}, bf16[768,768]{1,0:T(8,128)(2,1)S(1)}, u32[]{:S(2)}, u32[]{:S(2)}) %collective-permute-start.62) | collective-permute-done | bytes 1179680 | tf_op jit(solution)/shard_map/ppermute | solution.py:445
  584.2 4.5 collective-permute-done.46
  590.1 3.6 all-to-all-start.1
  593.7 42.9 %collective-permute-done.47 = f32[2,4,12,192]{3,1,2,0:T(4,128)S(1)} collective-permute-done((f32[2,4,12,192]{3,1,2,0:T(4,128)S(1)}, f32[2,4,12,192]{3,1,2,0:T(4,128)S(1)}, u32[]{:S(2)}, u32[]{:S(2)}) %collective-permute-start.47) | collective-permute-done | bytes 73760 | tf_op jit(solution)/shard_map/ppermute | solution.py:403
  636.6 3.6 collective-permute-start.48
  671.4 54.8 %collective-permute-done.75 = bf16[768,768]{1,0:T(8,128)(2,1)} collective-permute-done((bf16[768,768]{1,0:T(8,128)(2,1)}, bf16[768,768]{1,0:T(8,128)(2,1)}, u32[]{:S(2)}, u32[]{:S(2)}) %collective-permute-start.75) | collective-permute-done | bytes 1179680 | tf_op jit(solution)/shard_map/ppermute | solution.py:455
  726.2 3.3 bitcast_convert_fusion
  729.5 22.0 %collective-permute-done.71 = bf16[768,768]{1,0:T(8,128)(2,1)} collective-permute-done((bf16[768,768]{1,0:T(8,128)(2,1)}, bf16[768,768]{1,0:T(8,128)(2,1)}, u32[]{:S(2)}, u32[]{:S(2)}) %collective-permute-start.71) | collective-permute-done | bytes 1179680 | tf_op jit(solution)/shard_map/ppermute | solution.py:455
  751.5 3.3 bitcast_convert_fusion.1
  754.8 16.9 %collective-permute-done.65 = bf16[768,768]{1,0:T(8,128)(2,1)} collective-permute-done((bf16[768,768]{1,0:T(8,128)(2,1)}, bf16[768,768]{1,0:T(8,128)(2,1)}, u32[]{:S(2)}, u32[]{:S(2)}) %collective-permute-start.65) | collective-permute-done | bytes 1179680 | tf_op jit(solution)/shard_map/ppermute | solution.py:455
  (490 shorter events, 205.3 us)
Async XLA Ops:
  15.0 29.2 %collective-permute-start = (bf16[768,768]{1,0:T(8,128)(2,1)}, bf16[768,768]{1,0:T(8,128)(2,1)}, u32[]{:S(2)}, u32[]{:S(2)}) collective-permute-start(bf16[768,768]{1,0:T(8,128)(2,1)} %pad_maximum_fusion.1), channel_id=1, source_target_pairs={{0,16},{16,0},{1,17},{17,1},{2,18},{18,2},{3,19},{19,3},{4,20},{20... | collective-permute-start | bytes 3538952 | tf_op jit(solution)/shard_map/ppermute | solution.py:403
  21.9 38.8 %all-to-all-start = ((bf16[8,192,448]{2,1,0:T(8,128)(2,1)}), bf16[8,192,448]{2,1,0:T(8,128)(2,1)S(1)}, u32[]{:S(2)}, u32[]{:S(2)}) async-start(bf16[8,192,448]{2,1,0:T(8,128)(2,1)} %bitcast.148), calls=%async_computation | async-start | bytes 3145728 | tf_op jit(solution)/shard_map/all_to_all | solution.py:483
  60.7 28.1 %collective-permute-start.10 = (bf16[768,768]{1,0:T(8,128)(2,1)}, bf16[768,768]{1,0:T(8,128)(2,1)}, u32[]{:S(2)}, u32[]{:S(2)}) collective-permute-start(bf16[768,768]{1,0:T(8,128)(2,1)} %bitcast.156), channel_id=1, source_target_pairs={{0,16},{16,0},{1,17},{17,1},{2,18},{18,2},{3,19},{19,3},{4,20},{20... | collective-permute-start | bytes 3538952 | tf_op jit(solution)/shard_map/ppermute | solution.py:403
  88.8 26.9 %collective-permute-start.17 = (bf16[768,768]{1,0:T(8,128)(2,1)S(1)}, bf16[768,768]{1,0:T(8,128)(2,1)S(1)}, u32[]{:S(2)}, u32[]{:S(2)}) collective-permute-start(bf16[768,768]{1,0:T(8,128)(2,1)S(1)} %bitcast.157), channel_id=1, source_target_pairs={{0,16},{16,0},{1,17},{17,1},{2,18},{18,2},{3,19},{19,3},{4,20},{20... | collective-permute-start | bytes 3538952 | tf_op jit(solution)/shard_map/ppermute | solution.py:403
  90.4 26.6 %collective-permute-start.24 = (bf16[768,768]{1,0:T(8,128)(2,1)S(1)}, bf16[768,768]{1,0:T(8,128)(2,1)S(1)}, u32[]{:S(2)}, u32[]{:S(2)}) collective-permute-start(bf16[768,768]{1,0:T(8,128)(2,1)S(1)} %get-tuple-element.317.w0.refs_0_.refs_1_), channel_id=1, source_target_pairs={{0,4},{4,0},{8,12},{12,8},{1,5},{5,1},{9,13},{13,9},{2,6},{6,2},{1... | collective-permute-start | bytes 3538952 | tf_op jit(solution)/shard_map/ppermute | solution.py:403
  92.9 27.3 %collective-permute-start.4 = (bf16[768,768]{1,0:T(8,128)(2,1)S(1)}, bf16[768,768]{1,0:T(8,128)(2,1)S(1)}, u32[]{:S(2)}, u32[]{:S(2)}) collective-permute-start(bf16[768,768]{1,0:T(8,128)(2,1)S(1)} %get-tuple-element.318.w0.refs_0_.refs_1_), channel_id=1, source_target_pairs={{0,4},{4,0},{8,12},{12,8},{1,5},{5,1},{9,13},{13,9},{2,6},{6,2},{1... | collective-permute-start | bytes 3538952 | tf_op jit(solution)/shard_map/ppermute | solution.py:403
  120.2 25.8 %collective-permute-start.14 = (bf16[384,768]{1,0:T(8,128)(2,1)S(1)}, bf16[384,768]{1,0:T(8,128)(2,1)S(1)}, u32[]{:S(2)}, u32[]{:S(2)}) collective-permute-start(bf16[384,768]{1,0:T(8,128)(2,1)S(1)} %constant_dynamic-slice_fusion.2), channel_id=1, source_target_pairs={{0,8},{4,12},{8,0},{12,4},{1,9},{5,13},{9,1},{13,5},{2,10},{6,14},... | collective-permute-start | bytes 1769480 | tf_op jit(solution)/shard_map/ppermute | solution.py:403
  123.2 42.0 %collective-permute-start.28 = (bf16[768,768]{1,0:T(8,128)(2,1)}, bf16[768,768]{1,0:T(8,128)(2,1)}, u32[]{:S(2)}, u32[]{:S(2)}) collective-permute-start(bf16[768,768]{1,0:T(8,128)(2,1)} %get-tuple-element.315.w0.refs_0_.refs_1_), channel_id=1, source_target_pairs={{0,4},{4,0},{8,12},{12,8},{1,5},{5,1},{9,13},{13,9},{2,6},{6,2},{1... | collective-permute-start | bytes 3538952 | tf_op jit(solution)/shard_map/ppermute | solution.py:403
  123.2 42.1 %collective-permute-start.11 = (bf16[768,768]{1,0:T(8,128)(2,1)}, bf16[768,768]{1,0:T(8,128)(2,1)}, u32[]{:S(2)}, u32[]{:S(2)}) collective-permute-start(bf16[768,768]{1,0:T(8,128)(2,1)} %get-tuple-element.316.w0.refs_0_.refs_1_), channel_id=1, source_target_pairs={{0,4},{4,0},{8,12},{12,8},{1,5},{5,1},{9,13},{13,9},{2,6},{6,2},{1... | collective-permute-start | bytes 3538952 | tf_op jit(solution)/shard_map/ppermute | solution.py:403
  161.2 34.5 %collective-permute-start.18 = (bf16[768,768]{1,0:T(8,128)(2,1)}, bf16[768,768]{1,0:T(8,128)(2,1)}, u32[]{:S(2)}, u32[]{:S(2)}) collective-permute-start(bf16[768,768]{1,0:T(8,128)(2,1)} %copy-done.69), channel_id=1, source_target_pairs={{0,4},{4,0},{8,12},{12,8},{1,5},{5,1},{9,13},{13,9},{2,6},{6,2},{1... | collective-permute-start | bytes 3538952 | tf_op jit(solution)/shard_map/ppermute | solution.py:403
  165.2 29.9 %collective-permute-start.22 = (bf16[384,768]{1,0:T(8,128)(2,1)}, bf16[384,768]{1,0:T(8,128)(2,1)S(1)}, u32[]{:S(2)}, u32[]{:S(2)}) collective-permute-start(bf16[384,768]{1,0:T(8,128)(2,1)} %collective-permute-done.19.v2.refs_8_.refs_9_), channel_id=1, source_target_pairs={{0,4},{4,0},{8,12},{12,8},{1,5},{5,1},{9,13},{13,9},{2,6},{6,2},{1... | collective-permute-start | bytes 1769480 | tf_op jit(solution)/shard_map/ppermute | solution.py:403
  165.3 30.5 %collective-permute-start.23 = (bf16[384,768]{1,0:T(8,128)(2,1)}, bf16[384,768]{1,0:T(8,128)(2,1)S(1)}, u32[]{:S(2)}, u32[]{:S(2)}) collective-permute-start(bf16[384,768]{1,0:T(8,128)(2,1)} %collective-permute-done.20.v3.refs_9_.refs_10_), channel_id=1, source_target_pairs={{0,4},{4,0},{8,12},{12,8},{1,5},{5,1},{9,13},{13,9},{2,6},{6,2},{1... | collective-permute-start | bytes 1769480 | tf_op jit(solution)/shard_map/ppermute | solution.py:403
  166.6 29.6 %collective-permute-start.33 = (bf16[384,768]{1,0:T(8,128)(2,1)}, bf16[384,768]{1,0:T(8,128)(2,1)}, u32[]{:S(2)}, u32[]{:S(2)}) collective-permute-start(bf16[384,768]{1,0:T(8,128)(2,1)} %collective-permute-done.21.v2.refs_8_.refs_9_), channel_id=1, source_target_pairs={{0,1},{1,0},{2,3},{3,2},{4,5},{5,4},{6,7},{7,6},{8,9},{9,8},{10,11... | collective-permute-start | bytes 1769480 | tf_op jit(solution)/shard_map/ppermute | solution.py:403
  178.7 49.3 %collective-permute-start.32 = (bf16[768,768]{1,0:T(8,128)(2,1)}, bf16[768,768]{1,0:T(8,128)(2,1)}, u32[]{:S(2)}, u32[]{:S(2)}) collective-permute-start(bf16[768,768]{1,0:T(8,128)(2,1)} %get-tuple-element.313.v0.refs_6_.refs_7_), channel_id=1, source_target_pairs={{0,4},{4,0},{8,12},{12,8},{1,5},{5,1},{9,13},{13,9},{2,6},{6,2},{1... | collective-permute-start | bytes 3538952 | tf_op jit(solution)/shard_map/ppermute | solution.py:403
  195.1 31.2 %collective-permute-start.30 = (bf16[384,768]{1,0:T(8,128)(2,1)S(1)}, bf16[384,768]{1,0:T(8,128)(2,1)S(1)}, u32[]{:S(2)}, u32[]{:S(2)}) collective-permute-start(bf16[384,768]{1,0:T(8,128)(2,1)S(1)} %copy-done.27), channel_id=1, source_target_pairs={{0,4},{4,0},{8,12},{12,8},{1,5},{5,1},{9,13},{13,9},{2,6},{6,2},{1... | collective-permute-start | bytes 1769480 | tf_op jit(solution)/shard_map/ppermute | solution.py:403
  195.7 31.5 %collective-permute-start.31 = (bf16[384,768]{1,0:T(8,128)(2,1)}, bf16[384,768]{1,0:T(8,128)(2,1)S(1)}, u32[]{:S(2)}, u32[]{:S(2)}) collective-permute-start(bf16[384,768]{1,0:T(8,128)(2,1)} %collective-permute-done.29.w3.refs_3_.refs_4_), channel_id=1, source_target_pairs={{0,4},{4,0},{8,12},{12,8},{1,5},{5,1},{9,13},{13,9},{2,6},{6,2},{1... | collective-permute-start | bytes 1769480 | tf_op jit(solution)/shard_map/ppermute | solution.py:403
  195.8 32.2 %collective-permute-start.34 = (bf16[384,768]{1,0:T(8,128)(2,1)}, bf16[384,768]{1,0:T(8,128)(2,1)}, u32[]{:S(2)}, u32[]{:S(2)}) collective-permute-start(bf16[384,768]{1,0:T(8,128)(2,1)} %collective-permute-done.21.v2.refs_8_.refs_9_), channel_id=1, source_target_pairs={{0,4},{4,0},{8,12},{12,8},{1,5},{5,1},{9,13},{13,9},{2,6},{6,2},{1... | collective-permute-start | bytes 1769480 | tf_op jit(solution)/shard_map/ppermute | solution.py:403
  196.2 31.8 %collective-permute-start.35 = (bf16[384,768]{1,0:T(8,128)(2,1)}, bf16[384,768]{1,0:T(8,128)(2,1)}, u32[]{:S(2)}, u32[]{:S(2)}) collective-permute-start(bf16[384,768]{1,0:T(8,128)(2,1)} %collective-permute-done.33.v3.refs_9_.refs_10_), channel_id=1, source_target_pairs={{0,4},{4,0},{8,12},{12,8},{1,5},{5,1},{9,13},{13,9},{2,6},{6,2},{1... | collective-permute-start | bytes 1769480 | tf_op jit(solution)/shard_map/ppermute | solution.py:403
  280.1 28.3 %collective-permute-start.38 = (bf16[768,768]{1,0:T(8,128)(2,1)S(1)}, bf16[768,768]{1,0:T(8,128)(2,1)S(1)}, u32[]{:S(2)}, u32[]{:S(2)}) collective-permute-start(bf16[768,768]{1,0:T(8,128)(2,1)S(1)} %fusion.6), channel_id=1, source_target_pairs={{0,8},{4,12},{8,0},{12,4},{1,9},{5,13},{9,1},{13,5},{2,10},{6,14},... | collective-permute-start | bytes 3538952 | tf_op jit(solution)/shard_map/ppermute | solution.py:403
  292.3 65.2 %collective-permute-start.41 = (bf16[2,768,768]{2,1,0:T(8,128)(2,1)}, bf16[2,768,768]{2,1,0:T(8,128)(2,1)}, u32[]{:S(2)}, u32[]{:S(2)}) collective-permute-start(bf16[2,768,768]{2,1,0:T(8,128)(2,1)} %get-tuple-element.159), channel_id=1, source_target_pairs={{0,4},{4,0},{8,12},{12,8},{1,5},{5,1},{9,13},{13,9},{2,6},{6,2},{1... | collective-permute-start | bytes 7077896 | tf_op jit(solution)/shard_map/ppermute | solution.py:403
  321.2 39.1 %collective-permute-start.42 = (bf16[2,768,768]{2,1,0:T(8,128)(2,1)}, bf16[2,768,768]{2,1,0:T(8,128)(2,1)S(1)}, u32[]{:S(2)}, u32[]{:S(2)}) collective-permute-start(bf16[2,768,768]{2,1,0:T(8,128)(2,1)} %get-tuple-element.161), channel_id=1, source_target_pairs={{0,4},{4,0},{8,12},{12,8},{1,5},{5,1},{9,13},{13,9},{2,6},{6,2},{1... | collective-permute-start | bytes 7077896 | tf_op jit(solution)/shard_map/ppermute | solution.py:403
  321.2 29.3 %collective-permute-start.40 = (bf16[768,768]{1,0:T(8,128)(2,1)S(1)}, bf16[768,768]{1,0:T(8,128)(2,1)}, u32[]{:S(2)}, u32[]{:S(2)}) collective-permute-start(bf16[768,768]{1,0:T(8,128)(2,1)S(1)} %fusion.5), channel_id=1, source_target_pairs={{0,16},{1,17},{2,18},{3,19},{4,20},{5,21},{6,22},{7,23},{8,24},{9,... | collective-permute-start | bytes 3538952 | tf_op jit(solution)/shard_map/ppermute | solution.py:445
  325.7 36.4 %collective-permute-start.43 = (bf16[2,768,768]{2,1,0:T(8,128)(2,1)}, bf16[2,768,768]{2,1,0:T(8,128)(2,1)S(1)}, u32[]{:S(2)}, u32[]{:S(2)}) collective-permute-start(bf16[2,768,768]{2,1,0:T(8,128)(2,1)} %get-tuple-element.163), channel_id=1, source_target_pairs={{0,4},{4,0},{8,12},{12,8},{1,5},{5,1},{9,13},{13,9},{2,6},{6,2},{1... | collective-permute-start | bytes 7077896 | tf_op jit(solution)/shard_map/ppermute | solution.py:403
  325.9 28.5 %collective-permute-start.39 = (bf16[768,768]{1,0:T(8,128)(2,1)}, bf16[768,768]{1,0:T(8,128)(2,1)}, u32[]{:S(2)}, u32[]{:S(2)}) collective-permute-start(bf16[768,768]{1,0:T(8,128)(2,1)} %fusion.7), channel_id=1, source_target_pairs={{0,8},{4,12},{8,0},{12,4},{1,9},{5,13},{9,1},{13,5},{2,10},{6,14},... | collective-permute-start | bytes 3538952 | tf_op jit(solution)/shard_map/ppermute | solution.py:403
  365.0 29.0 %collective-permute-start.51 = (bf16[768,768]{1,0:T(8,128)(2,1)}, bf16[768,768]{1,0:T(8,128)(2,1)}, u32[]{:S(2)}, u32[]{:S(2)}) collective-permute-start(bf16[768,768]{1,0:T(8,128)(2,1)} %fusion.4), channel_id=1, source_target_pairs={{0,16},{1,17},{2,18},{3,19},{4,20},{5,21},{6,22},{7,23},{8,24},{9,... | collective-permute-start | bytes 3538952 | tf_op jit(solution)/shard_map/ppermute | solution.py:445
  369.6 27.6 %collective-permute-start.50 = (bf16[768,768]{1,0:T(8,128)(2,1)}, bf16[768,768]{1,0:T(8,128)(2,1)}, u32[]{:S(2)}, u32[]{:S(2)}) collective-permute-start(bf16[768,768]{1,0:T(8,128)(2,1)} %fusion.10), channel_id=1, source_target_pairs={{0,8},{4,12},{8,0},{12,4},{1,9},{5,13},{9,1},{13,5},{2,10},{6,14},... | collective-permute-start | bytes 3538952 | tf_op jit(solution)/shard_map/ppermute | solution.py:403
  370.4 30.0 %collective-permute-start.52 = (bf16[768,768]{1,0:T(8,128)(2,1)}, bf16[768,768]{1,0:T(8,128)(2,1)}, u32[]{:S(2)}, u32[]{:S(2)}) collective-permute-start(bf16[768,768]{1,0:T(8,128)(2,1)} %add_convert_fusion.25), channel_id=1, source_target_pairs={{16,17},{19,18},{20,21},{23,22},{24,25},{27,26},{28,29},{31,30}} | collective-permute-start | bytes 3538952 | tf_op jit(solution)/shard_map/ppermute | solution.py:455
  403.1 30.8 %collective-permute-start.53 = (bf16[768,768]{1,0:T(8,128)(2,1)}, bf16[768,768]{1,0:T(8,128)(2,1)}, u32[]{:S(2)}, u32[]{:S(2)}) collective-permute-start(bf16[768,768]{1,0:T(8,128)(2,1)} %fusion.2), channel_id=1, source_target_pairs={{0,16},{1,17},{2,18},{3,19},{4,20},{5,21},{6,22},{7,23},{8,24},{9,... | collective-permute-start | bytes 3538952 | tf_op jit(solution)/shard_map/ppermute | solution.py:445
  431.7 60.8 %collective-permute-start.49 = (bf16[2,768,768]{2,1,0:T(8,128)(2,1)}, bf16[2,768,768]{2,1,0:T(8,128)(2,1)}, u32[]{:S(2)}, u32[]{:S(2)}) collective-permute-start(bf16[2,768,768]{2,1,0:T(8,128)(2,1)} %get-tuple-element.185), channel_id=1, source_target_pairs={{0,4},{4,0},{8,12},{12,8},{1,5},{5,1},{9,13},{13,9},{2,6},{6,2},{1... | collective-permute-start | bytes 7077896 | tf_op jit(solution)/shard_map/ppermute | solution.py:403
  431.8 28.4 %collective-permute-start.56 = (bf16[768,768]{1,0:T(8,128)(2,1)S(1)}, bf16[768,768]{1,0:T(8,128)(2,1)S(1)}, u32[]{:S(2)}, u32[]{:S(2)}) collective-permute-start(bf16[768,768]{1,0:T(8,128)(2,1)S(1)} %copy-done.101), channel_id=1, source_target_pairs={{0,8},{4,12},{8,0},{12,4},{1,9},{5,13},{9,1},{13,5},{2,10},{6,14},... | collective-permute-start | bytes 3538952 | tf_op jit(solution)/shard_map/ppermute | solution.py:403
  461.7 33.7 %collective-permute-start.57 = (bf16[768,768]{1,0:T(8,128)(2,1)}, bf16[768,768]{1,0:T(8,128)(2,1)}, u32[]{:S(2)}, u32[]{:S(2)}) collective-permute-start(bf16[768,768]{1,0:T(8,128)(2,1)} %add_convert_fusion.17), channel_id=1, source_target_pairs={{16,17},{19,18},{20,21},{23,22},{24,25},{27,26},{28,29},{31,30}} | collective-permute-start | bytes 3538952 | tf_op jit(solution)/shard_map/ppermute | solution.py:455
  465.0 32.5 %collective-permute-start.58 = (bf16[768,768]{1,0:T(8,128)(2,1)}, bf16[768,768]{1,0:T(8,128)(2,1)}, u32[]{:S(2)}, u32[]{:S(2)}) collective-permute-start(bf16[768,768]{1,0:T(8,128)(2,1)} %add_convert_fusion.16), channel_id=1, source_target_pairs={{17,18},{18,17},{21,22},{22,21},{25,26},{26,25},{29,30},{30,29}} | collective-permute-start | bytes 3538952 | tf_op jit(solution)/shard_map/ppermute | solution.py:455
  472.1 28.6 %collective-permute-start.60 = (bf16[768,768]{1,0:T(8,128)(2,1)}, bf16[768,768]{1,0:T(8,128)(2,1)}, u32[]{:S(2)}, u32[]{:S(2)}) collective-permute-start(bf16[768,768]{1,0:T(8,128)(2,1)} %fusion.12), channel_id=1, source_target_pairs={{0,8},{4,12},{8,0},{12,4},{1,9},{5,13},{9,1},{13,5},{2,10},{6,14},... | collective-permute-start | bytes 3538952 | tf_op jit(solution)/shard_map/ppermute | solution.py:403
  491.0 31.2 %collective-permute-start.59 = (bf16[768,768]{1,0:T(8,128)(2,1)}, bf16[768,768]{1,0:T(8,128)(2,1)S(1)}, u32[]{:S(2)}, u32[]{:S(2)}) collective-permute-start(bf16[768,768]{1,0:T(8,128)(2,1)} %fusion.1), channel_id=1, source_target_pairs={{16,0},{17,1},{18,2},{19,3},{20,4},{21,5},{22,6},{23,7},{24,8},{25... | collective-permute-start | bytes 3538952 | tf_op jit(solution)/shard_map/ppermute | solution.py:445
  523.6 26.6 %collective-permute-start.61 = (bf16[768,768]{1,0:T(8,128)(2,1)}, bf16[768,768]{1,0:T(8,128)(2,1)}, u32[]{:S(2)}, u32[]{:S(2)}) collective-permute-start(bf16[768,768]{1,0:T(8,128)(2,1)} %fusion.17), channel_id=1, source_target_pairs={{0,8},{4,12},{8,0},{12,4},{1,9},{5,13},{9,1},{13,5},{2,10},{6,14},... | collective-permute-start | bytes 3538952 | tf_op jit(solution)/shard_map/ppermute | solution.py:403
  525.3 34.3 %collective-permute-start.68 = (bf16[768,768]{1,0:T(8,128)(2,1)S(1)}, bf16[768,768]{1,0:T(8,128)(2,1)S(1)}, u32[]{:S(2)}, u32[]{:S(2)}) collective-permute-start(bf16[768,768]{1,0:T(8,128)(2,1)S(1)} %copy-done.78), channel_id=1, source_target_pairs={{16,0},{17,1},{18,2},{19,3},{20,4},{21,5},{22,6},{23,7},{24,8},{25... | collective-permute-start | bytes 3538952 | tf_op jit(solution)/shard_map/ppermute | solution.py:445
  552.7 27.3 %collective-permute-start.62 = (bf16[768,768]{1,0:T(8,128)(2,1)S(1)}, bf16[768,768]{1,0:T(8,128)(2,1)S(1)}, u32[]{:S(2)}, u32[]{:S(2)}) collective-permute-start(bf16[768,768]{1,0:T(8,128)(2,1)S(1)} %fusion.3), channel_id=1, source_target_pairs={{16,0},{17,1},{18,2},{19,3},{20,4},{21,5},{22,6},{23,7},{24,8},{25... | collective-permute-start | bytes 3538952 | tf_op jit(solution)/shard_map/ppermute | solution.py:445
  555.6 28.4 %collective-permute-start.45 = (f32[2,4,12,192]{3,1,2,0:T(4,128)S(1)}, f32[2,4,12,192]{3,1,2,0:T(4,128)S(1)}, u32[]{:S(2)}, u32[]{:S(2)}) collective-permute-start(f32[2,4,12,192]{3,1,2,0:T(4,128)S(1)} %fusion.26), channel_id=1, source_target_pairs={{0,8},{4,12},{8,0},{12,4},{1,9},{5,13},{9,1},{13,5},{2,10},{6,14},... | collective-permute-start | bytes 221192 | tf_op jit(solution)/shard_map/ppermute | solution.py:403
  556.9 83.3 %collective-permute-start.73 = (bf16[768,768]{1,0:T(8,128)(2,1)}, bf16[768,768]{1,0:T(8,128)(2,1)}, u32[]{:S(2)}, u32[]{:S(2)}) collective-permute-start(bf16[768,768]{1,0:T(8,128)(2,1)} %add_convert_fusion.11), channel_id=1, source_target_pairs={{0,1},{3,2},{4,5},{7,6},{8,9},{11,10},{12,13},{15,14}} | collective-permute-start | bytes 3538952 | tf_op jit(solution)/shard_map/ppermute | solution.py:455
  560.9 82.0 %collective-permute-start.69 = (bf16[768,768]{1,0:T(8,128)(2,1)}, bf16[768,768]{1,0:T(8,128)(2,1)}, u32[]{:S(2)}, u32[]{:S(2)}) collective-permute-start(bf16[768,768]{1,0:T(8,128)(2,1)} %add_convert_fusion.4), channel_id=1, source_target_pairs={{0,1},{3,2},{4,5},{7,6},{8,9},{11,10},{12,13},{15,14}} | collective-permute-start | bytes 3538952 | tf_op jit(solution)/shard_map/ppermute | solution.py:455
  581.3 65.1 %collective-permute-start.63 = (bf16[768,768]{1,0:T(8,128)(2,1)}, bf16[768,768]{1,0:T(8,128)(2,1)}, u32[]{:S(2)}, u32[]{:S(2)}) collective-permute-start(bf16[768,768]{1,0:T(8,128)(2,1)} %add_convert_fusion.8), channel_id=1, source_target_pairs={{0,1},{3,2},{4,5},{7,6},{8,9},{11,10},{12,13},{15,14}} | collective-permute-start | bytes 3538952 | tf_op jit(solution)/shard_map/ppermute | solution.py:455
  588.7 47.9 %collective-permute-start.47 = (f32[2,4,12,192]{3,1,2,0:T(4,128)S(1)}, f32[2,4,12,192]{3,1,2,0:T(4,128)S(1)}, u32[]{:S(2)}, u32[]{:S(2)}) collective-permute-start(f32[2,4,12,192]{3,1,2,0:T(4,128)S(1)} %add.175), channel_id=1, source_target_pairs={{0,1},{1,0},{2,3},{3,2},{4,5},{5,4},{6,7},{7,6},{8,9},{9,8},{10,11... | collective-permute-start | bytes 221192 | tf_op jit(solution)/shard_map/ppermute | solution.py:403
  590.1 76.6 %all-to-all-start.1 = ((bf16[8,192,448]{2,1,0:T(8,128)(2,1)}), bf16[8,192,448]{2,1,0:T(8,128)(2,1)S(1)}, u32[]{:S(2)}, u32[]{:S(2)}) async-start(bf16[8,192,448]{2,1,0:T(8,128)(2,1)} %bitcast.44), calls=%async_computation.1 | async-start | bytes 3145728 | tf_op jit(solution)/shard_map/all_to_all | solution.py:596
  650.4 79.0 %collective-permute-start.72 = (bf16[768,768]{1,0:T(8,128)(2,1)}, bf16[768,768]{1,0:T(8,128)(2,1)}, u32[]{:S(2)}, u32[]{:S(2)}) collective-permute-start(bf16[768,768]{1,0:T(8,128)(2,1)} %add_convert_fusion.12), channel_id=1, source_target_pairs={{17,16},{18,19},{21,20},{22,23},{25,24},{26,27},{29,28},{30,31}} | collective-permute-start | bytes 3538952 | tf_op jit(solution)/shard_map/ppermute | solution.py:455
  653.5 72.7 %collective-permute-start.75 = (bf16[768,768]{1,0:T(8,128)(2,1)}, bf16[768,768]{1,0:T(8,128)(2,1)}, u32[]{:S(2)}, u32[]{:S(2)}) collective-permute-start(bf16[768,768]{1,0:T(8,128)(2,1)} %add_convert_fusion), channel_id=1, source_target_pairs={{1,0},{2,3},{5,4},{6,7},{9,8},{10,11},{13,12},{14,15}} | collective-permute-start | bytes 3538952 | tf_op jit(solution)/shard_map/ppermute | solution.py:455
  656.1 95.4 %collective-permute-start.71 = (bf16[768,768]{1,0:T(8,128)(2,1)}, bf16[768,768]{1,0:T(8,128)(2,1)}, u32[]{:S(2)}, u32[]{:S(2)}) collective-permute-start(bf16[768,768]{1,0:T(8,128)(2,1)} %add_convert_fusion.2), channel_id=1, source_target_pairs={{1,0},{2,3},{5,4},{6,7},{9,8},{10,11},{13,12},{14,15}} | collective-permute-start | bytes 3538952 | tf_op jit(solution)/shard_map/ppermute | solution.py:455
  658.8 96.0 %collective-permute-start.67 = (bf16[768,768]{1,0:T(8,128)(2,1)}, bf16[768,768]{1,0:T(8,128)(2,1)}, u32[]{:S(2)}, u32[]{:S(2)}) collective-permute-start(bf16[768,768]{1,0:T(8,128)(2,1)} %add_convert_fusion.5), channel_id=1, source_target_pairs={{17,16},{18,19},{21,20},{22,23},{25,24},{26,27},{29,28},{30,31}} | collective-permute-start | bytes 3538952 | tf_op jit(solution)/shard_map/ppermute | solution.py:455
  662.8 108.8 %collective-permute-start.65 = (bf16[768,768]{1,0:T(8,128)(2,1)}, bf16[768,768]{1,0:T(8,128)(2,1)}, u32[]{:S(2)}, u32[]{:S(2)}) collective-permute-start(bf16[768,768]{1,0:T(8,128)(2,1)} %add_convert_fusion.6), channel_id=1, source_target_pairs={{1,0},{2,3},{5,4},{6,7},{9,8},{10,11},{13,12},{14,15}} | collective-permute-start | bytes 3538952 | tf_op jit(solution)/shard_map/ppermute | solution.py:455
  (144 other events, 1829.3 us)

commit v3 on v2

--- a/solution.py
+++ b/solution.py
@@ -58,22 +58,17 @@
 
 
 def piece_copies(info, pieces, held, sems):
-    own, other, near, far, other_near, other_far = pieces
     first = pl.multiple_of(info[4] * HALF, HALF)
     second = pl.multiple_of((1 - info[4]) * HALF, HALF)
-    routes = (
-        (own, held.at[0]),
-        (other, held.at[1]),
-        (near, held.at[2, pl.ds(first, HALF)]),
-        (far, held.at[2, pl.ds(second, HALF)]),
-        (other_near, held.at[3, pl.ds(first, HALF)]),
-        (other_far, held.at[3, pl.ds(second, HALF)]),
-    )
-    copies = [
-        pltpu.make_async_copy(source, target, sems.at[index])
-        for index, (source, target) in enumerate(routes)
-    ]
-    return (copies[0:1], copies[1:2], copies[2:4], copies[4:6])
+    return tuple(
+        tuple(
+            pltpu.make_async_copy(
+                pieces[2 * slot + part], held.at[slot, pl.ds(start, HALF)], sems.at[2 * slot + part]
+            )
+            for part, start in enumerate((first, second))
+        )
+        for slot in range(SHARDS)
+    )
 
 
 def load_pieces(step, order, chunks):
@@ -94,10 +89,11 @@
 
 
 def attention_forward_kernel(
-    info, x_ref, col_ref, bqv_ref, w0, w1, w2, w3, w4, w5, a1_ref, p_ref, soft_ref, o_ref, h_ref, held, sems
+    info, x_ref, col_ref, bqv_ref, *refs
 ):
     step = pl.program_id(0)
-    copies = piece_copies(info, (w0, w1, w2, w3, w4, w5), held, sems)
+    pieces, (a1_ref, p_ref, soft_ref, o_ref, h_ref, held, sems) = refs[:8], refs[8:]
+    copies = piece_copies(info, pieces, held, sems)
     load_pieces(step, range(SHARDS), (copies,))
 
     @pl.when(step == 0)
@@ -131,13 +127,13 @@
 
 
 def mlp_forward_kernel(
-    info, h_ref, col_ref, b1_ref,
-    w0, w1, w2, w3, w4, w5, v0, v1, v2, v3, v4, v5,
-    a2_ref, u_ref, slope_ref, y_ref, held_one, held_two, a2_rows, total, sems_one, sems_two,
+    info, h_ref, col_ref, b1_ref, *refs
 ):
     step = pl.program_id(0)
-    copies_one = piece_copies(info, (w0, w1, w2, w3, w4, w5), held_one, sems_one)
-    copies_two = piece_copies(info, (v0, v1, v2, v3, v4, v5), held_two, sems_two)
+    pieces_one, pieces_two, refs = refs[:8], refs[8:16], refs[16:]
+    a2_ref, u_ref, slope_ref, y_ref, held_one, held_two, a2_rows, total, sems_one, sems_two = refs
+    copies_one = piece_copies(info, pieces_one, held_one, sems_one)
+    copies_two = piece_copies(info, pieces_two, held_two, sems_two)
     load_pieces(step, range(SHARDS), (copies_one, copies_two))
 
     @pl.when(step == 0)
@@ -169,7 +165,7 @@
     step = pl.program_id(0)
     if last:
         before_ref, *refs = refs
-    pieces_one, pieces_two, refs = refs[:6], refs[6:12], refs[12:]
+    pieces_one, pieces_two, refs = refs[:8], refs[8:16], refs[16:]
     if last:
         gh_ref, dcol_ref, *refs = refs
     else:
@@ -215,7 +211,7 @@
     step = pl.program_id(0)
     if last:
         before_ref, *refs = refs
-    pieces, refs = refs[:6], refs[6:]
+    pieces, refs = refs[:8], refs[8:]
     if last:
         gx_ref, dcol_ref, *refs = refs
     else:
@@ -286,8 +282,8 @@
     return pl.BlockSpec((1,) + shape, lambda i, info: (info[first + i],) + (0,) * len(shape))
 
 
-PIECES = [pl.BlockSpec(memory_space=pl.ANY)] * 6
-COPY_SEMS = pltpu.SemaphoreType.DMA((6,))
+PIECES = [pl.BlockSpec(memory_space=pltpu.HBM)] * 8
+COPY_SEMS = pltpu.SemaphoreType.DMA((8,))
 HELD = pltpu.VMEM((SHARDS, D, D), BF16)
 
 
@@ -421,53 +417,60 @@
     )
 
 
+def rows_of(value, place, parts):
+    size = value.shape[-2] // parts
+    return lax.dynamic_slice_in_dim(value, place * size, size, axis=value.ndim - 2)
+
+
+def joined(first, second, swap):
+    return jnp.where(
+        swap, jnp.concatenate([second, first], axis=0), jnp.concatenate([first, second], axis=0)
+    )
+
+
 class Chain:
-    def __init__(self, layer):
-        self.layer = layer
-        self.total = None
-        self.arrived = None
-
     def start(self, send):
         self.arrived = flip(send, "tensor", 1)
 
-    def fold_cores(self, keep):
-        self.away = added(keep[0], self.arrived[0])
-        self.total = added(keep[1], self.arrived[1])
+    def cores(self, keep):
+        self.value = added(keep, self.arrived)
 
     def send_y(self):
-        self.arrived = flip(self.away, "tensor", 2)
+        self.kept, self.arrived = self.value[1], flip(self.value[0], "tensor", 2)
+
+    def send_z(self, level):
+        mine = (lax.axis_index("dp") >> level) & 1
+        self.kept = rows_of(self.value, mine, 2)
+        self.arrived = flip(rows_of(self.value, 1 - mine, 2), "dp", 1 << level)
+
+    def send_x(self, first, second):
+        section = lax.axis_index("section")
+        self.kept = jnp.where(section == 0, first.value, second.value)
+        self.arrived = flip(jnp.where(section == 0, second.value, first.value), "section", 1)
 
     def fold(self):
-        if self.arrived is not None:
-            self.total = added(self.total, self.arrived)
-
-    def send_x(self):
-        self.arrived = lax.ppermute(self.total, "section", [(1 - self.layer, self.layer)])
-
-    def send_z(self, stage):
-        if lax.axis_size("dp") != 4:
-            self.total = lax.psum(self.total, "dp") if stage == 0 else self.total
-            self.arrived = None
-            return
-        base = self.layer * 4
-        pairs = (((0, 1), (3, 2)), ((1, 2), (2, 1)), ((1, 0), (2, 3)))[stage]
-        pairs = [(base + source, base + target) for source, target in pairs]
-        self.arrived = lax.ppermute(self.total, ("section", "dp"), pairs)
-
-    def close(self):
-        if self.arrived is None:
-            return
-        place = lax.axis_index("dp")
-        self.total = jnp.where((place == 0) | (place == 3), self.arrived, self.total)
-
-
-def sum_all(values):
-    for axis in ("tensor", "section", "dp"):
-        size, bit = lax.axis_size(axis), 1
-        while bit < size:
-            values = values + flip(values, axis, bit)
+        self.value = added(self.kept, self.arrived)
+
+    def finish_x(self):
+        self.fold()
+        bit = 4
+        while bit < lax.axis_size("dp"):
+            self.value = added(self.value, flip(self.value, "dp", bit))
             bit *= 2
-    return values
+
+    def gather_z(self, level):
+        self.level, self.arrived = level, flip(self.value, "dp", 1 << level)
+
+    def join(self):
+        mine = (lax.axis_index("dp") >> self.level) & 1
+        self.value = joined(self.value, self.arrived, mine == 1)
+
+
+def tied(chains, *others):
+    values = tie((tuple(chain.value for chain in chains), others))
+    for chain, value in zip(chains, values[0]):
+        chain.value = value
+    return values[1]
 
 
 def body(ends_in, ln_gain, ln_shift, w_qkv, b_qv, w_out, b_out, w_fc1, b_fc1, w_fc2, b_fc2):
@@ -479,15 +482,27 @@
         [shard, shard ^ 1, shard ^ 2, shard ^ 3, zhalf] + [jnp.int32(k) for k in BACK_ORDER]
     ).astype(jnp.int32)
 
-    ends = ends_in[0].T.reshape(FEATS, clips, FRAMES).transpose(1, 0, 2)
+    owned = [
+        jnp.concatenate([w_qkv[0].transpose(1, 2, 0).reshape(QKV, D), w_out[0]], axis=0),
+        w_fc1[0],
+        w_fc2[0],
+    ]
+    nears = [rows_of(own, zhalf, 2) for own in owned]
+    fars = [rows_of(own, 1 - zhalf, 2) for own in owned]
+    small = jnp.concatenate(
+        [ln_gain[0], ln_shift[0], b_qv[0], b_out, b_fc2, b_fc1.reshape(SHARDS, FEATS)], axis=0
+    )
+    nears[0], small, ends = tie((nears[0], small, ends_in[0]))
+    beyond = flip(nears[0], "section", 1)
+
+    ends = ends.T.reshape(FEATS, clips, FRAMES).transpose(1, 0, 2)
     ends = lax.all_to_all(ends, ("section", "tensor"), split_axis=0, concat_axis=0, tiled=True)
     ends = ends.reshape(2, D, FRAMES)
 
-    small = jnp.concatenate(
-        [ln_gain[0], ln_shift[0], b_qv[0], b_out, b_fc2, b_fc1.reshape(SHARDS, FEATS)], axis=0
-    )
-    beyond = flip(small, "section", 1)
-    small = jnp.stack([jnp.where(section == 0, small, beyond), jnp.where(section == 0, beyond, small)])
+    small_beyond = flip(small, "section", 1)
+    small = jnp.stack(
+        [jnp.where(section == 0, small, small_beyond), jnp.where(section == 0, small_beyond, small)]
+    )
     small_y = flip(small, "tensor", 2)
     pair = jnp.stack([small, small_y])
     pair_other = flip(pair, "tensor", 1)
@@ -496,50 +511,79 @@
     bqvs = jnp.transpose(slots[:, :, 4:6], (1, 0, 3, 2))
     b1s = jnp.transpose(slots[:, :, 8:], (1, 0, 2, 3)).reshape(2, SHARDS, 1, FF_SHARD)
 
-    owned = [
-        jnp.concatenate([w_qkv[0].transpose(1, 2, 0).reshape(QKV, D), w_out[0]], axis=0),
-        w_fc1[0],
-        w_fc2[0],
-    ]
-    chunks = [[], []]
-    beyond = flip(owned[0], "section", 1)
-    for index, own in enumerate(owned):
-        if index == 0:
-            beyond, ends, cols, bqvs, b1s = tie((beyond, ends, cols, bqvs, b1s))
-        arrived = beyond
-        if index + 1 < len(owned):
-            arrived, following = tie((arrived, owned[index + 1]))
-            beyond = flip(following, "section", 1)
-        both = [jnp.where(section == 0, own, arrived), jnp.where(section == 0, arrived, own)]
-        halves = [lax.dynamic_slice_in_dim(w, zhalf * HALF, HALF, axis=0) for w in both]
-        near = flip(halves[0], "tensor", 2)
-        near, halves[1] = tie((near, halves[1]))
-        near_late = flip(halves[1], "tensor", 2)
-        far = flip(near, "dp", 1)
-        far, near_late = tie((far, near_late))
-        far_late = flip(near_late, "dp", 1)
-        for layer, (w, n, f) in enumerate(((both[0], near, far), (both[1], near_late, far_late))):
-            chunks[layer].append(
-                (w, flip(w, "tensor", 1), n, f, flip(n, "tensor", 1), flip(f, "tensor", 1))
-            )
-
+    def layers(own, other):
+        return jnp.where(section == 0, own, other), jnp.where(section == 0, other, own)
+
+    near_own, far_own = [], []
+    for index in range(2):
+        near_other, following = tie((beyond, (nears[1], owned[2])[index]))
+        beyond = flip(following, "section", 1)
+        near_own.append(layers(nears[index], near_other))
+        far_own.append(layers(fars[index], flip(near_other, "dp", 1)))
+
+    def over_y(index, layer):
+        return flip(near_own[index][layer], "tensor", 2)
+
+    def chunk_of(index, layer, near_there, far_there):
+        here = [near_own[index][layer], far_own[index][layer]]
+        there = [near_there, far_there]
+        return (
+            here
+            + [flip(part, "tensor", 1) for part in here]
+            + there
+            + [flip(part, "tensor", 1) for part in there]
+        )
+
+    def attend(layer, stream, chunk):
+        return attention_forward(info, stream, cols[layer], bqvs[layer], chunk)
+
+    def feed(layer, h, chunk_one, chunk_two):
+        return mlp_forward(info, h, cols[layer], b1s[layer], chunk_one, chunk_two)
+
+    chunks = [[None] * 3, [None] * 3]
     stream = ends[0]
-    stored = []
-    for layer in range(2):
-        chunk_a, chunk_one, chunk_two = chunks[layer]
-        a1, p, soft, o, h = attention_forward(info, stream, cols[layer], bqvs[layer], chunk_a)
-        a2, u, slope, y = mlp_forward(info, h, cols[layer], b1s[layer], chunk_one, chunk_two)
-        stored.append((stream, a1, p, soft, o, h, a2, u, slope))
-        stream = y
+    there_a, there_one = over_y(0, 0), over_y(1, 0)
+    chunks[0][0] = chunk_of(0, 0, there_a, flip(there_a, "dp", 1))
+    away_one = flip(there_one, "dp", 1)
+    a1, p, soft, o, h = attend(0, stream, chunks[0][0])
+
+    h, away_one, beyond, far_one, late_a, late_one = tie(
+        (h, away_one, beyond, far_own[1], near_own[0][1], near_own[1][1])
+    )
+    far_own[1], near_own[0], near_own[1] = far_one, (None, late_a), (near_own[1][0], late_one)
+    chunks[0][1] = chunk_of(1, 0, there_one, away_one)
+    near_own.append(layers(nears[2], rows_of(beyond, zhalf, 2)))
+    far_own.append(layers(fars[2], rows_of(beyond, 1 - zhalf, 2)))
+    there_two = over_y(2, 0)
+    there_two, late_a = tie((there_two, late_a))
+    near_own[0] = (None, late_a)
+    chunks[0][2] = chunk_of(2, 0, there_two, flip(there_two, "dp", 1))
+    there_a = over_y(0, 1)
+    there_a, late_one, late_two = tie((there_a, near_own[1][1], near_own[2][1]))
+    near_own[1], near_own[2] = (None, late_one), (None, late_two)
+    away_a = flip(there_a, "dp", 1)
+    there_one, there_two = over_y(1, 1), over_y(2, 1)
+    a2, u, slope, y = feed(0, h, chunks[0][1], chunks[0][2])
+    stored = [(stream, a1, p, soft, o, h, a2, u, slope)]
+
+    stream, there_one, there_two, away_a = tie((y, there_one, there_two, away_a))
+    chunks[1][0] = chunk_of(0, 1, there_a, away_a)
+    chunks[1][1] = chunk_of(1, 1, there_one, flip(there_one, "dp", 1))
+    chunks[1][2] = chunk_of(2, 1, there_two, flip(there_two, "dp", 1))
+    a1, p, soft, o, h = attend(1, stream, chunks[1][0])
+    a2, u, slope, y = feed(1, h, chunks[1][1], chunks[1][2])
+    stored.append((stream, a1, p, soft, o, h, a2, u, slope))
+    stream = y
 
     upstream = ends[1]
-    chains = [[Chain(layer) for _ in range(3)] for layer in range(2)]
+    chains = [[Chain() for _ in range(3)] for _ in range(2)]
     smalls = [None, None]
+    late_a, late_one, late_two = chains[1]
+    last_a, last_one, last_two = chains[0]
     for layer in (1, 0):
         chunk_a, chunk_one, chunk_two = chunks[layer]
         x, a1, p, soft, o, h, a2, u, slope = stored[layer]
         chain_a, chain_one, chain_two = chains[layer]
-        late_a, late_one, late_two = chains[1]
         after, send_one, send_two, db1_sent = mlp_backward(
             info, upstream, h, a2, cols[layer], u, slope, None, chunk_one, chunk_two
         )
@@ -548,20 +592,19 @@
         gh, dcol_two, keep_one, keep_two, db1_kept = mlp_backward(
             info, upstream, h, a2, cols[layer], u, slope, after, chunk_one, chunk_two
         )
-        chain_two.fold_cores(keep_two)
-        chain_one.fold_cores(keep_one)
+        chain_two.cores(keep_two)
+        chain_one.cores(keep_one)
         if layer == 1:
-            gh, chain_two.away, chain_one.away = tie((gh, chain_two.away, chain_one.away))
-            chain_two.send_y()
+            (gh,) = tied((late_two, late_one), gh)
+            late_two.send_y()
+            late_one.send_z(0)
         else:
             late_one.fold()
-            late_two.fold()
-            gh, late_one.total, late_two.total, late_a.away, chain_two.away, chain_one.away = tie(
-                (gh, late_one.total, late_two.total, late_a.away, chain_two.away, chain_one.away)
-            )
-            late_one.send_x()
+            late_a.fold()
+            (gh,) = tied((late_one, late_a, last_two, last_one, late_two), gh)
+            last_two.send_y()
             late_two.send_z(0)
-            late_a.send_y()
+            late_one.send_z(1)
         after, send_a, dbqv_sent = attention_backward(
             info, gh, x, a1, cols[layer], p, soft, o, None, chunk_a
         )
@@ -569,23 +612,25 @@
         upstream, dcol_one, keep_a, dbqv_kept = attention_backward(
             info, gh, x, a1, cols[layer], p, soft, o, after, chunk_a
         )
-        chain_a.fold_cores(keep_a)
+        chain_a.cores(keep_a)
         if layer == 1:
             late_two.fold()
-            upstream, late_two.total, late_one.away = tie((upstream, late_two.total, late_one.away))
-            late_two.send_x()
+            late_one.fold()
+            (upstream,) = tied((late_two, late_one, late_a), upstream)
             late_one.send_y()
+            late_a.send_z(0)
         db1 = by_bits([db1_kept[1], db1_sent[1], db1_kept[0], db1_sent[0]], shard)
         dbqv = by_bits([dbqv_kept[1], dbqv_sent[1], dbqv_kept[0], dbqv_sent[0]], shard)
-        dcol = jnp.stack(
+        dcol = jnp.concatenate(
             [
-                dcol_one[:, 0], dcol_two[:, 0], dcol_one[:, 1], dcol_two[:, 1],
-                dbqv[:, :, 0].reshape(D), dbqv[:, :, 1].reshape(D), dcol_two[:, 2], dcol_two[:, 3],
-            ]
+                dcol_one[:, 0:1], dcol_two[:, 0:1], dcol_one[:, 1:2], dcol_two[:, 1:2],
+                dbqv[:, :, 0:2].reshape(D, 2), dcol_two[:, 2:4],
+            ],
+            axis=1,
         )
         smalls[layer] = jnp.concatenate(
             [
-                dcol.reshape(8, SHARDS, FEATS).transpose(1, 0, 2),
+                dcol.reshape(SHARDS, FEATS, 8).transpose(0, 2, 1),
                 db1.reshape(SHARDS, SHARDS, FEATS),
             ],
             axis=1,
@@ -593,78 +638,82 @@
 
     result = jnp.stack([upstream.astype(BF16), stream.astype(BF16)])
     result = result.reshape(2 * SHARDS, FEATS, FRAMES)
+    small_sum = jnp.stack(smalls)
+
+    late_two.fold()
+    late_one.fold()
+    last_two.fold()
+    tied((late_two, late_one, last_two, last_one))
+    last_one.send_y()
+    last_two.send_z(0)
+    late_two.send_z(1)
     result = lax.all_to_all(result, ("section", "tensor"), split_axis=0, concat_axis=0, tiled=True)
+    small_sum += flip(small_sum, "tensor", 1)
+
+    last_two.fold()
+    late_two.fold()
+    result, small_sum = tied((last_two, late_two), result, small_sum)
+    last_two.send_z(1)
+    small_sum += flip(small_sum, "tensor", 2)
     result = result.transpose(1, 0, 2).reshape(FEATS, clips * FRAMES).T.astype(F32)
 
-    small_sum = sum_all(jnp.stack(smalls))
+    last_one.fold()
+    last_two.fold()
+    result, small_sum = tied((last_one, last_two, last_a, late_a), result, small_sum)
+    last_a.send_y()
+    late_a.send_y()
+    last_one.send_z(0)
+    pair_two = Chain()
+    pair_two.send_x(last_two, late_two)
+    small_sum += flip(small_sum, "section", 1)
+
+    last_one.fold()
+    pair_two.finish_x()
+    (small_sum,) = tied((last_one, pair_two), small_sum)
+    last_one.send_z(1)
+    pair_two.gather_z(1)
+    small_sum += flip(small_sum, "dp", 1)
+
+    last_one.fold()
+    pair_two.join()
+    last_a.fold()
+    late_a.fold()
+    (small_sum,) = tied((last_one, pair_two, last_a, late_a), small_sum)
+    pair_one = Chain()
+    pair_one.send_x(last_one, late_one)
+    last_a.send_z(0)
+    late_a.send_z(1)
+    pair_two.gather_z(0)
+    bit = 2
+    while bit < lax.axis_size("dp"):
+        small_sum += flip(small_sum, "dp", bit)
+        bit *= 2
+
+    pair_one.finish_x()
+    last_a.fold()
+    late_a.fold()
+    (small_sum,) = tied((pair_one, last_a, late_a), small_sum)
+    pair_one.gather_z(1)
+    last_a.send_z(1)
     small_sum = lax.dynamic_slice(
         small_sum, (section, shard, 0, 0), (1, 1, 12, FEATS)
     ).reshape(12, FEATS)
 
-    (late_a, late_one, late_two), (last_a, last_one, last_two) = chains[1], chains[0]
-    late_a.fold()
-    late_one.fold()
-    late_two.fold()
-    late_a.total, late_one.total, late_two.total, last_two.away = tie(
-        (late_a.total, late_one.total, late_two.total, last_two.away)
-    )
-    late_a.send_x()
-    late_one.send_z(0)
-    late_two.send_z(1)
-    last_two.send_y()
-    late_a.fold()
-    late_one.fold()
-    late_two.fold()
-    last_two.fold()
-    late_a.total, late_one.total, late_two.total, last_two.total, last_one.away = tie(
-        (late_a.total, late_one.total, late_two.total, last_two.total, last_one.away)
-    )
-    late_a.send_z(0)
-    late_one.send_z(1)
-    late_two.send_z(2)
-    last_two.send_x()
-    last_one.send_y()
-    late_a.fold()
-    late_one.fold()
-    late_two.close()
-    last_two.fold()
-    last_one.fold()
-    late_a.total, late_one.total, last_two.total, last_one.total, last_a.away = tie(
-        (late_a.total, late_one.total, last_two.total, last_one.total, last_a.away)
-    )
-    late_a.send_z(1)
-    late_one.send_z(2)
-    last_two.send_z(0)
-    last_one.send_x()
-    last_a.send_y()
-    late_a.fold()
-    late_one.close()
-    late_a.send_z(2)
-    late_a.close()
-    for chain in (last_two, last_one, last_a):
-        chain.fold()
-    last_two.send_z(1)
-    last_one.send_z(0)
-    last_a.send_x()
-    for chain in (last_two, last_one, last_a):
-        chain.fold()
-    last_two.send_z(2)
-    last_two.close()
-    last_one.send_z(1)
-    last_a.send_z(0)
-    last_one.fold()
+    pair_one.join()
     last_a.fold()
-    last_one.send_z(2)
-    last_a.send_z(1)
-    last_one.close()
-    last_a.fold()
-    last_a.send_z(2)
-    last_a.close()
-
-    grad_a, grad_one, grad_two = [
-        jnp.where(section == 0, first.total, second.total).astype(F32)
-        for first, second in zip(chains[0], chains[1])
-    ]
+    pair_two.join()
+    tied((pair_one, last_a))
+    pair_a = Chain()
+    pair_a.send_x(last_a, late_a)
+    pair_one.gather_z(0)
+    pair_a.finish_x()
+    pair_a.gather_z(1)
+    pair_one.join()
+    pair_a.join()
+    pair_a.gather_z(0)
+    pair_a.join()
+
+    grad_a, grad_one, grad_two = [pair.value.astype(F32) for pair in (pair_a, pair_one, pair_two)]
     return (
         result[None],
         small_sum[None, 0:2],

time: 781 us -> 657 us (0.84)
  waiting for transfers between devices: 365 us -> 271 us
  other arithmetic: 85.8 us -> 64.3 us
  starting transfers between devices: 92.1 us -> 78.7 us
  Pallas kernels: 160 us -> 169 us
    ppermute x24 -> x0, waiting for transfers between devices: 153 us -> none  [the longest x18 93.7 us: send_z(): self.arrived = lax.ppermute(self.total, ('section', 'dp'), pairs)]
    ppermute x53 -> x82, waiting for transfers between devices: 195 us -> 271 us  [flip(): return lax.ppermute(block, axis, [(i, i ^ bit) for i in range(size)])]
    ppermute x24 -> x0, starting transfers between devices: 44.1 us -> none  [the longest x18 25.8 us: send_z(): self.arrived = lax.ppermute(self.total, ('section', 'dp'), pairs)]
    ppermute x53 -> x82, starting transfers between devices: 40.5 us -> 69.4 us  [flip(): return lax.ppermute(block, axis, [(i, i ^ bit) for i in range(size)])]
    convert_element_type x30 -> x27, other arithmetic: 62.4 us -> 37 us  [added(): return (left.astype(F32) + right.astype(F32)).astype(BF16)]
    unnamed x243 -> x173, local copies, waits for them, and re-layouts: 31.8 us -> 15.2 us
    all_to_all x1, waiting for transfers between devices: 16.5 us -> 0.01 us  [body(): lax.all_to_all(ends, ('section', 'tensor'), split_axis=0, concat_axis=0,...]
    pallas_call x12, Pallas kernels: 160 us -> 169 us  [run(): pl.pallas_call(kernel, name=name, out_shape=outs, grid_spec=pltpu.Prefetc...]
  transfers between devices with their start and end apart: 79 -> 84, of which waited for: 29 -> 33; matrix products, arithmetic and copies ran while one was open for 15% -> 15% of each run, Pallas kernels for 17% -> 18%
where the time goes in v3:
time: 657 us; the launch traced here: 652 us
  waiting for transfers between devices  271 us (41%)
  Pallas kernels  169 us (26%)
  starting transfers between devices  78.7 us (12%)
  local copies, waits for them, and re-layouts  66.6 us (10%)
  other arithmetic  64.3 us (10%)
    ppermute x82, waiting for transfers between devices, flip(): return lax.ppermute(block, axis, [(i, i ^ bit) for i in range(size)])  271 us
    pallas_call x12, Pallas kernels, run(): pl.pallas_call(kernel, name=name, out_shape=outs, grid_spec=pltpu.Prefetc...  169 us
    ppermute x82, starting transfers between devices, flip(): return lax.ppermute(block, axis, [(i, i ^ bit) for i in range(size)])  69.4 us
    convert_element_type x27, other arithmetic, added(): return (left.astype(F32) + right.astype(F32)).astype(BF16)  37 us
    unnamed x173, local copies, waits for them, and re-layouts  15.2 us
  transfers between devices with their start and end apart: 84, of which 33 were waited for; matrix products, arithmetic and copies ran while one was open for 15% of the time, Pallas kernels for 18%

profile of v3, /device:TPU:0, one launch (start us, length us, event | category | flops | bytes accessed | tf_op | source)
XLA Modules:
  0.0 652.3 jit_solution(4589983476951613117)
XLA Ops:
  3.1 3.0 collective-permute-start
  11.8 3.2 reshape.290
  16.7 4.6 all-to-all-start
  30.9 23.1 %collective-permute-done.11 = bf16[384,768]{1,0:T(8,128)(2,1)S(1)} collective-permute-done((bf16[384,768]{1,0:T(8,128)(2,1)S(1)}, bf16[384,768]{1,0:T(8,128)(2,1)S(1)}, u32[]{:S(2)}, u32[]{:S(2)}) %collective-permute-start.11) | collective-permute-done | bytes 589856 | tf_op jit(solution)/shard_map/ppermute | solution.py:399
  60.9 20.8 %collective-permute-done.8.refs_5_.refs_6_ = bf16[384,768]{1,0:T(8,128)(2,1)} collective-permute-done((bf16[384,768]{1,0:T(8,128)(2,1)}, bf16[384,768]{1,0:T(8,128)(2,1)}, u32[]{:S(2)}, u32[]{:S(2)}) %collective-permute-start.8) | collective-permute-done | bytes 589856 | tf_op jit(solution)/shard_map/ppermute | solution.py:399
  88.1 15.7 %attention_forward.2 = (bf16[768,448]{1,0:T(8,128)(2,1)}, bf16[4,576,448]{2,1,0:T(8,128)(2,1)}, bf16[4,3,448,448]{3,2,1,0:T(8,128)(2,1)}, bf16[4,192,448]{2,1,0:T(8,128)(2,1)}, f32[768,448]{1,0:T(8,128)}) custom-call(s32[9]{0:T(128)S(1)} %stack.113.info, bf16[768,448]{1,0:T(8,128)(2,1)} %bitcast.126, f32[4,192,8]{2,1,0:T(8,128)S(1)} %get-tuple-element.340.col_ref, ...), custom_call_target="tpu_custom_call" | custom-call | flops 2730491904 | bytes 15071232 | tf_op jit(solution)/shard_map/attention_forward/pallas_call | solution.py:298
  103.9 3.1 bitcast_select_fusion
  108.4 14.1 %collective-permute-done.22.refs_12_.refs_13_ = bf16[384,768]{1,0:T(8,128)(2,1)S(1)} collective-permute-done((bf16[384,768]{1,0:T(8,128)(2,1)S(1)}, bf16[384,768]{1,0:T(8,128)(2,1)S(1)}, u32[]{:S(2)}, u32[]{:S(2)}) %collective-permute-start.22) | collective-permute-done | bytes 589856 | tf_op jit(solution)/shard_map/ppermute | solution.py:399
  125.7 11.6 %collective-permute-done.26.refs_4_.refs_5_ = bf16[384,768]{1,0:T(8,128)(2,1)} collective-permute-done((bf16[384,768]{1,0:T(8,128)(2,1)S(1)}, bf16[384,768]{1,0:T(8,128)(2,1)}, u32[]{:S(2)}, u32[]{:S(2)}) %collective-permute-start.26) | collective-permute-done | bytes 589856 | tf_op jit(solution)/shard_map/ppermute | solution.py:399
  143.7 13.3 %collective-permute-done.27.refs_4_.refs_5_ = bf16[384,768]{1,0:T(8,128)(2,1)} collective-permute-done((bf16[384,768]{1,0:T(8,128)(2,1)S(1)}, bf16[384,768]{1,0:T(8,128)(2,1)}, u32[]{:S(2)}, u32[]{:S(2)}) %collective-permute-start.27) | collective-permute-done | bytes 589856 | tf_op jit(solution)/shard_map/ppermute | solution.py:399
  157.0 11.9 %collective-permute-done.28.refs_12_.refs_13_ = bf16[384,768]{1,0:T(8,128)(2,1)} collective-permute-done((bf16[384,768]{1,0:T(8,128)(2,1)}, bf16[384,768]{1,0:T(8,128)(2,1)}, u32[]{:S(2)}, u32[]{:S(2)}) %collective-permute-start.28) | collective-permute-done | bytes 589856 | tf_op jit(solution)/shard_map/ppermute | solution.py:399
  177.2 13.9 %mlp_forward.2 = (bf16[768,448]{1,0:T(8,128)(2,1)}, bf16[4,448,768]{2,1,0:T(8,128)(2,1)}, bf16[4,448,768]{2,1,0:T(8,128)(2,1)}, f32[768,448]{1,0:T(8,128)}) custom-call(s32[9]{0:T(128)S(1)} %stack.113.info, f32[768,448]{1,0:T(8,128)} %get-tuple-element.133.h_ref, f32[4,192,8]{2,1,0:T(8,128)S(1)} %get-tuple-element.340.col_ref, ...), custom_call_target="tpu_custom_call" | custom-call | flops 4227858432 | bytes 18419712 | tf_op jit(solution)/shard_map/mlp_forward/pallas_call | solution.py:298
  196.8 11.4 %collective-permute-done.36.refs_5_.refs_6_ = bf16[384,768]{1,0:T(8,128)(2,1)} collective-permute-done((bf16[384,768]{1,0:T(8,128)(2,1)}, bf16[384,768]{1,0:T(8,128)(2,1)}, u32[]{:S(2)}, u32[]{:S(2)}) %collective-permute-start.36) | collective-permute-done | bytes 589856 | tf_op jit(solution)/shard_map/ppermute | solution.py:399
  208.3 12.2 %collective-permute-done.41.refs_13_.refs_14_ = bf16[384,768]{1,0:T(8,128)(2,1)} collective-permute-done((bf16[384,768]{1,0:T(8,128)(2,1)}, bf16[384,768]{1,0:T(8,128)(2,1)}, u32[]{:S(2)}, u32[]{:S(2)}) %collective-permute-start.41) | collective-permute-done | bytes 589856 | tf_op jit(solution)/shard_map/ppermute | solution.py:399
  225.2 16.0 %attention_forward.3 = (bf16[768,448]{1,0:T(8,128)(2,1)}, bf16[4,576,448]{2,1,0:T(8,128)(2,1)}, bf16[4,3,448,448]{3,2,1,0:T(8,128)(2,1)}, bf16[4,192,448]{2,1,0:T(8,128)(2,1)}, f32[768,448]{1,0:T(8,128)}) custom-call(s32[9]{0:T(128)S(1)} %stack.113.info, f32[768,448]{1,0:T(8,128)} %get-tuple-element.145.x_ref, f32[4,192,8]{2,1,0:T(8,128)S(1)} %get-tuple-element.339.col_ref, ...), custom_call_target="tpu_custom_call" | custom-call | flops 2730491904 | bytes 15759360 | tf_op jit(solution)/shard_map/attention_forward/pallas_call | solution.py:298
  241.2 13.8 %mlp_forward.3 = (bf16[768,448]{1,0:T(8,128)(2,1)}, bf16[4,448,768]{2,1,0:T(8,128)(2,1)}, bf16[4,448,768]{2,1,0:T(8,128)(2,1)}, f32[768,448]{1,0:T(8,128)}) custom-call(s32[9]{0:T(128)S(1)} %stack.113.info, f32[768,448]{1,0:T(8,128)} %get-tuple-element.147.h_ref, f32[4,192,8]{2,1,0:T(8,128)S(1)} %get-tuple-element.339.col_ref, ...), custom_call_target="tpu_custom_call" | custom-call | flops 4227858432 | bytes 18419712 | tf_op jit(solution)/shard_map/mlp_forward/pallas_call | solution.py:298
  255.0 12.3 %mlp_backward.4 = (f32[448,768]{1,0:T(8,128)}, bf16[2,768,768]{2,1,0:T(8,128)(2,1)}, bf16[2,768,768]{2,1,0:T(8,128)(2,1)}, f32[2,1,768]{2,1,0:T(1,128)S(1)}) custom-call(s32[9]{0:T(128)S(1)} %stack.113.info, bf16[768,448]{1,0:T(8,128)(2,1)} %bitcast.129, f32[768,448]{1,0:T(8,128)} %get-tuple-element.147.h_ref, bf16[768,448]{1,0:T(8,128)(2,1)} %get-tuple-element.151.a2_ref, ...), custom_call_target="tpu_custom_call" | custom-call | flops 4227858432 | bytes 23820288 | tf_op jit(solution)/shard_map/mlp_backward/pallas_call | solution.py:298
  268.0 15.0 %mlp_backward.5 = (f32[768,448]{1,0:T(8,128)}, f32[768,8]{1,0:T(8,128)S(1)}, bf16[2,768,768]{2,1,0:T(8,128)(2,1)}, bf16[2,768,768]{2,1,0:T(8,128)(2,1)}, f32[2,1,768]{2,1,0:T(1,128)S(1)}) custom-call(s32[9]{0:T(128)S(1)} %stack.113.info, bf16[768,448]{1,0:T(8,128)(2,1)} %bitcast.130, f32[768,448]{1,0:T(8,128)} %get-tuple-element.147.h_ref, ...), custom_call_target="tpu_custom_call" | custom-call | flops 4227858432 | bytes 25221120 | tf_op jit(solution)/shard_map/mlp_backward/pallas_call | solution.py:298
  283.0 3.8 add_convert_fusion.5
  289.0 12.2 %attention_backward.4 = (f32[448,768]{1,0:T(8,128)}, bf16[2,768,768]{2,1,0:T(8,128)(2,1)}, f32[2,192,8]{2,1,0:T(8,128)S(1)}) custom-call(s32[9]{0:T(128)S(1)} %stack.113.info, f32[768,448]{1,0:T(8,128)} %get-tuple-element.162.gh_ref, f32[768,448]{1,0:T(8,128)} %get-tuple-element.145.x_ref, bf16[768,448]{1,0:T(8,128)(2,1)S(1)} %copy-done.6, ...), custom_call_target="tpu_custom_call" | custom-call | flops 2730491904 | bytes 19501056 | tf_op jit(solution)/shard_map/attention_backward/pallas_call | solution.py:298
  317.0 15.7 %attention_backward.5 = (f32[768,448]{1,0:T(8,128)}, f32[768,8]{1,0:T(8,128)S(1)}, bf16[2,768,768]{2,1,0:T(8,128)(2,1)}, f32[2,192,8]{2,1,0:T(8,128)S(1)}) custom-call(s32[9]{0:T(128)S(1)} %stack.113.info, f32[768,448]{1,0:T(8,128)} %get-tuple-element.162.gh_ref, f32[768,448]{1,0:T(8,128)} %get-tuple-element.145.x_ref, ...), custom_call_target="tpu_custom_call" | custom-call | flops 2730491904 | bytes 20901888 | tf_op jit(solution)/shard_map/attention_backward/pallas_call | solution.py:298
  338.8 3.9 add_convert_fusion.3
  342.7 11.9 %mlp_backward.6 = (f32[448,768]{1,0:T(8,128)}, bf16[2,768,768]{2,1,0:T(8,128)(2,1)}, bf16[2,768,768]{2,1,0:T(8,128)(2,1)}, f32[2,1,768]{2,1,0:T(1,128)S(1)}) custom-call(s32[9]{0:T(128)S(1)} %stack.113.info, f32[768,448]{1,0:T(8,128)} %get-tuple-element.173.gy_ref, f32[768,448]{1,0:T(8,128)} %get-tuple-element.133.h_ref, ...), custom_call_target="tpu_custom_call" | custom-call | flops 4227858432 | bytes 24508416 | tf_op jit(solution)/shard_map/mlp_backward/pallas_call | solution.py:298
  366.8 14.6 %mlp_backward.7 = (f32[768,448]{1,0:T(8,128)}, f32[768,8]{1,0:T(8,128)S(1)}, bf16[2,768,768]{2,1,0:T(8,128)(2,1)}, bf16[2,768,768]{2,1,0:T(8,128)(2,1)}, f32[2,1,768]{2,1,0:T(1,128)S(1)}) custom-call(s32[9]{0:T(128)S(1)} %stack.113.info, f32[768,448]{1,0:T(8,128)} %get-tuple-element.173.gy_ref, f32[768,448]{1,0:T(8,128)} %get-tuple-element.133.h_ref, ...), custom_call_target="tpu_custom_call" | custom-call | flops 4227858432 | bytes 25909248 | tf_op jit(solution)/shard_map/mlp_backward/pallas_call | solution.py:298
  385.2 8.0 %collective-permute-done.50 = bf16[2,384,768]{2,1,0:T(8,128)(2,1)} collective-permute-done((bf16[2,384,768]{2,1,0:T(8,128)(2,1)}, bf16[2,384,768]{2,1,0:T(8,128)(2,1)}, u32[]{:S(2)}, u32[]{:S(2)}) %collective-permute-start.50) | collective-permute-done | bytes 1179680 | tf_op jit(solution)/shard_map/ppermute | solution.py:399
  398.2 3.1 add_convert_fusion.1
  409.1 12.9 %attention_backward.6 = (f32[448,768]{1,0:T(8,128)}, bf16[2,768,768]{2,1,0:T(8,128)(2,1)}, f32[2,192,8]{2,1,0:T(8,128)S(1)}) custom-call(s32[9]{0:T(128)S(1)} %stack.113.info, f32[768,448]{1,0:T(8,128)} %get-tuple-element.191.gh_ref, bf16[768,448]{1,0:T(8,128)(2,1)S(1)} %bitcast.128, bf16[768,448]{1,0:T(8,128)(2,1)} %get-tuple-element.192.a1_ref, ...), custom_call_target="tpu_custom_call" | custom-call | flops 2730491904 | bytes 18812928 | tf_op jit(solution)/shard_map/attention_backward/pallas_call | solution.py:298
  422.0 15.3 %attention_backward.7 = (f32[768,448]{1,0:T(8,128)}, f32[768,8]{1,0:T(8,128)S(1)}, bf16[2,768,768]{2,1,0:T(8,128)(2,1)}, f32[2,192,8]{2,1,0:T(8,128)S(1)}) custom-call(s32[9]{0:T(128)S(1)} %stack.113.info, f32[768,448]{1,0:T(8,128)} %get-tuple-element.191.gh_ref, bf16[768,448]{1,0:T(8,128)(2,1)} %bitcast.127, bf16[768,448]{1,0:T(8,128)(2,1)} %get-tuple-element.192.a1_ref, ...), custom_call_target="tpu_custom_call" | custom-call | flops 2730491904 | bytes 20213760 | tf_op jit(solution)/shard_map/attention_backward/pallas_call | solution.py:298
  443.0 4.7 all-to-all-start.1
  457.8 11.9 %collective-permute-done.58 = bf16[192,768]{1,0:T(8,128)(2,1)S(1)} collective-permute-done((bf16[192,768]{1,0:T(8,128)(2,1)S(1)}, bf16[192,768]{1,0:T(8,128)(2,1)S(1)}, u32[]{:S(2)}, u32[]{:S(2)}) %collective-permute-start.58) | collective-permute-done | bytes 294944 | tf_op jit(solution)/shard_map/ppermute | solution.py:399
  470.4 4.7 collective-permute-done.57
  485.2 9.8 %collective-permute-done.62 = f32[2,4,12,192]{3,1,2,0:T(4,128)S(1)} collective-permute-done((f32[2,4,12,192]{3,1,2,0:T(4,128)}, f32[2,4,12,192]{3,1,2,0:T(4,128)S(1)}, u32[]{:S(2)}, u32[]{:S(2)}) %collective-permute-start.62) | collective-permute-done | bytes 73760 | tf_op jit(solution)/shard_map/ppermute | solution.py:399
  497.1 3.1 add_convert_fusion
  507.6 5.3 collective-permute-done.64
  513.0 5.5 collective-permute-done.63
  524.3 17.2 %collective-permute-done.67 = bf16[192,768]{1,0:T(8,128)(2,1)S(1)} collective-permute-done((bf16[192,768]{1,0:T(8,128)(2,1)S(1)}, bf16[192,768]{1,0:T(8,128)(2,1)S(1)}, u32[]{:S(2)}, u32[]{:S(2)}) %collective-permute-start.67) | collective-permute-done | bytes 294944 | tf_op jit(solution)/shard_map/ppermute | solution.py:399
  541.7 4.3 collective-permute-done.66
  551.3 8.3 %collective-permute-done.74 = f32[2,4,12,192]{3,1,2,0:T(4,128)S(1)} collective-permute-done((f32[2,4,12,192]{3,1,2,0:T(4,128)S(1)}, f32[2,4,12,192]{3,1,2,0:T(4,128)S(1)}, u32[]{:S(2)}, u32[]{:S(2)}) %collective-permute-start.74) | collective-permute-done | bytes 73760 | tf_op jit(solution)/shard_map/ppermute | solution.py:399
  560.2 4.1 collective-permute-done.73
  564.5 5.0 collective-permute-done.72
  572.7 17.8 %collective-permute-done.76 = bf16[192,768]{1,0:T(8,128)(2,1)S(1)} collective-permute-done((bf16[192,768]{1,0:T(8,128)(2,1)S(1)}, bf16[192,768]{1,0:T(8,128)(2,1)S(1)}, u32[]{:S(2)}, u32[]{:S(2)}) %collective-permute-start.76) | collective-permute-done | bytes 294944 | tf_op jit(solution)/shard_map/ppermute | solution.py:399
  590.7 4.9 collective-permute-done.75
  597.4 6.2 collective-permute-done.77
  603.7 3.7 collective-permute-start.81
  607.5 10.3 %collective-permute-done.78 = bf16[192,768]{1,0:T(8,128)(2,1)S(1)} collective-permute-done((bf16[192,768]{1,0:T(8,128)(2,1)S(1)}, bf16[192,768]{1,0:T(8,128)(2,1)S(1)}, u32[]{:S(2)}, u32[]{:S(2)}) %collective-permute-start.78) | collective-permute-done | bytes 294944 | tf_op jit(solution)/shard_map/ppermute | solution.py:399
  623.3 3.8 collective-permute-done.81
  628.6 11.0 %collective-permute-done.80 = bf16[384,768]{1,0:T(8,128)(2,1)S(1)} collective-permute-done((bf16[384,768]{1,0:T(8,128)(2,1)S(1)}, bf16[384,768]{1,0:T(8,128)(2,1)S(1)}, u32[]{:S(2)}, u32[]{:S(2)}) %collective-permute-start.80) | collective-permute-done | bytes 589856 | tf_op jit(solution)/shard_map/ppermute | solution.py:399
  641.3 8.2 %collective-permute-done.79 = bf16[384,768]{1,0:T(8,128)(2,1)S(1)} collective-permute-done((bf16[384,768]{1,0:T(8,128)(2,1)S(1)}, bf16[384,768]{1,0:T(8,128)(2,1)S(1)}, u32[]{:S(2)}, u32[]{:S(2)}) %collective-permute-start.79) | collective-permute-done | bytes 589856 | tf_op jit(solution)/shard_map/ppermute | solution.py:399
  (455 shorter events, 179.5 us)
Async XLA Ops:
  16.7 67.4 %all-to-all-start = ((bf16[8,192,448]{2,1,0:T(8,128)(2,1)}), bf16[8,192,448]{2,1,0:T(8,128)(2,1)}, u32[]{:S(2)}, u32[]{:S(2)}) async-start(bf16[8,192,448]{2,1,0:T(8,128)(2,1)} %bitcast.125), calls=%async_computation | async-start | bytes 3145728 | tf_op jit(solution)/shard_map/all_to_all | solution.py:499
  25.3 30.3 %collective-permute-start.7 = (bf16[384,768]{1,0:T(8,128)(2,1)S(1)}, bf16[384,768]{1,0:T(8,128)(2,1)}, u32[]{:S(2)}, u32[]{:S(2)}) collective-permute-start(bf16[384,768]{1,0:T(8,128)(2,1)S(1)} %get-tuple-element.334.refs_0_.refs_1_), channel_id=1, source_target_pairs={{0,8},{4,12},{8,0},{12,4},{1,9},{5,13},{9,1},{13,5},{2,10},{6,14},... | collective-permute-start | bytes 1769480 | tf_op jit(solution)/shard_map/ppermute | solution.py:399
  26.6 27.4 %collective-permute-start.11 = (bf16[384,768]{1,0:T(8,128)(2,1)S(1)}, bf16[384,768]{1,0:T(8,128)(2,1)S(1)}, u32[]{:S(2)}, u32[]{:S(2)}) collective-permute-start(bf16[384,768]{1,0:T(8,128)(2,1)S(1)} %copy-done.73), channel_id=1, source_target_pairs={{0,16},{16,0},{1,17},{17,1},{2,18},{18,2},{3,19},{19,3},{4,20},{20... | collective-permute-start | bytes 1769480 | tf_op jit(solution)/shard_map/ppermute | solution.py:399
  29.2 29.4 %collective-permute-start.4 = (bf16[384,768]{1,0:T(8,128)(2,1)}, bf16[384,768]{1,0:T(8,128)(2,1)S(1)}, u32[]{:S(2)}, u32[]{:S(2)}) collective-permute-start(bf16[384,768]{1,0:T(8,128)(2,1)} %collective-permute-done.3), channel_id=1, source_target_pairs={{0,1},{1,0},{2,3},{3,2},{4,5},{5,4},{6,7},{7,6},{8,9},{9,8},{10,11... | collective-permute-start | bytes 1769480 | tf_op jit(solution)/shard_map/ppermute | solution.py:399
  30.8 30.1 %collective-permute-start.5 = (bf16[384,768]{1,0:T(8,128)(2,1)S(1)}, bf16[384,768]{1,0:T(8,128)(2,1)S(1)}, u32[]{:S(2)}, u32[]{:S(2)}) collective-permute-start(bf16[384,768]{1,0:T(8,128)(2,1)S(1)} %get-tuple-element.334.refs_0_.refs_1_), channel_id=1, source_target_pairs={{0,4},{4,0},{8,12},{12,8},{1,5},{5,1},{9,13},{13,9},{2,6},{6,2},{1... | collective-permute-start | bytes 1769480 | tf_op jit(solution)/shard_map/ppermute | solution.py:399
  54.0 27.7 %collective-permute-start.15 = (bf16[384,768]{1,0:T(8,128)(2,1)S(1)}, bf16[384,768]{1,0:T(8,128)(2,1)S(1)}, u32[]{:S(2)}, u32[]{:S(2)}) collective-permute-start(bf16[384,768]{1,0:T(8,128)(2,1)S(1)} %collective-permute-done.11), channel_id=1, source_target_pairs={{0,1},{1,0},{2,3},{3,2},{4,5},{5,4},{6,7},{7,6},{8,9},{9,8},{10,11... | collective-permute-start | bytes 1769480 | tf_op jit(solution)/shard_map/ppermute | solution.py:399
  55.5 26.2 %collective-permute-start.8 = (bf16[384,768]{1,0:T(8,128)(2,1)}, bf16[384,768]{1,0:T(8,128)(2,1)}, u32[]{:S(2)}, u32[]{:S(2)}) collective-permute-start(bf16[384,768]{1,0:T(8,128)(2,1)} %collective-permute-done.7.refs_4_.refs_5_), channel_id=1, source_target_pairs={{0,1},{1,0},{2,3},{3,2},{4,5},{5,4},{6,7},{7,6},{8,9},{9,8},{10,11... | collective-permute-start | bytes 1769480 | tf_op jit(solution)/shard_map/ppermute | solution.py:399
  57.1 25.2 %collective-permute-start.12 = (bf16[384,768]{1,0:T(8,128)(2,1)S(1)}, bf16[384,768]{1,0:T(8,128)(2,1)}, u32[]{:S(2)}, u32[]{:S(2)}) collective-permute-start(bf16[384,768]{1,0:T(8,128)(2,1)S(1)} %get-tuple-element.332.refs_0_.refs_1_), channel_id=1, source_target_pairs={{0,8},{4,12},{8,0},{12,4},{1,9},{5,13},{9,1},{13,5},{2,10},{6,14},... | collective-permute-start | bytes 1769480 | tf_op jit(solution)/shard_map/ppermute | solution.py:399
  58.6 45.2 %collective-permute-start.14 = (bf16[768,768]{1,0:T(8,128)(2,1)}, bf16[768,768]{1,0:T(8,128)(2,1)}, u32[]{:S(2)}, u32[]{:S(2)}) collective-permute-start(bf16[768,768]{1,0:T(8,128)(2,1)} %bitcast.28), channel_id=1, source_target_pairs={{0,16},{16,0},{1,17},{17,1},{2,18},{18,2},{3,19},{19,3},{4,20},{20... | collective-permute-start | bytes 3538952 | tf_op jit(solution)/shard_map/ppermute | solution.py:399
  60.9 27.0 %collective-permute-start.6 = (bf16[384,768]{1,0:T(8,128)(2,1)}, bf16[384,768]{1,0:T(8,128)(2,1)}, u32[]{:S(2)}, u32[]{:S(2)}) collective-permute-start(bf16[384,768]{1,0:T(8,128)(2,1)} %get-tuple-element.326.refs_1_.refs_2_), channel_id=1, source_target_pairs={{0,4},{4,0},{8,12},{12,8},{1,5},{5,1},{9,13},{13,9},{2,6},{6,2},{1... | collective-permute-start | bytes 1769480 | tf_op jit(solution)/shard_map/ppermute | solution.py:399
  82.5 21.3 %collective-permute-start.13 = (bf16[384,768]{1,0:T(8,128)(2,1)}, bf16[384,768]{1,0:T(8,128)(2,1)}, u32[]{:S(2)}, u32[]{:S(2)}) collective-permute-start(bf16[384,768]{1,0:T(8,128)(2,1)} %collective-permute-done.12.refs_4_.refs_5_), channel_id=1, source_target_pairs={{0,1},{1,0},{2,3},{3,2},{4,5},{5,4},{6,7},{7,6},{8,9},{9,8},{10,11... | collective-permute-start | bytes 1769480 | tf_op jit(solution)/shard_map/ppermute | solution.py:399
  142.1 26.8 %collective-permute-start.28 = (bf16[384,768]{1,0:T(8,128)(2,1)}, bf16[384,768]{1,0:T(8,128)(2,1)}, u32[]{:S(2)}, u32[]{:S(2)}) collective-permute-start(bf16[384,768]{1,0:T(8,128)(2,1)} %get-tuple-element.143.refs_8_.refs_9_), channel_id=1, source_target_pairs={{0,8},{4,12},{8,0},{12,4},{1,9},{5,13},{9,1},{13,5},{2,10},{6,14},... | collective-permute-start | bytes 1769480 | tf_op jit(solution)/shard_map/ppermute | solution.py:399
  143.1 48.1 %collective-permute-start.31 = (bf16[384,768]{1,0:T(8,128)(2,1)}, bf16[384,768]{1,0:T(8,128)(2,1)}, u32[]{:S(2)}, u32[]{:S(2)}) collective-permute-start(bf16[384,768]{1,0:T(8,128)(2,1)} %get-tuple-element.325.refs_1_.refs_2_), channel_id=1, source_target_pairs={{0,4},{4,0},{8,12},{12,8},{1,5},{5,1},{9,13},{13,9},{2,6},{6,2},{1... | collective-permute-start | bytes 1769480 | tf_op jit(solution)/shard_map/ppermute | solution.py:399
  143.2 48.5 %collective-permute-start.35 = (bf16[384,768]{1,0:T(8,128)(2,1)}, bf16[384,768]{1,0:T(8,128)(2,1)}, u32[]{:S(2)}, u32[]{:S(2)}) collective-permute-start(bf16[384,768]{1,0:T(8,128)(2,1)} %get-tuple-element.148.refs_1_.refs_2_), channel_id=1, source_target_pairs={{0,4},{4,0},{8,12},{12,8},{1,5},{5,1},{9,13},{13,9},{2,6},{6,2},{1... | collective-permute-start | bytes 1769480 | tf_op jit(solution)/shard_map/ppermute | solution.py:399
  143.6 48.1 %collective-permute-start.40 = (bf16[384,768]{1,0:T(8,128)(2,1)}, bf16[384,768]{1,0:T(8,128)(2,1)}, u32[]{:S(2)}, u32[]{:S(2)}) collective-permute-start(bf16[384,768]{1,0:T(8,128)(2,1)} %get-tuple-element.321.refs_9_.refs_10_), channel_id=1, source_target_pairs={{0,4},{4,0},{8,12},{12,8},{1,5},{5,1},{9,13},{13,9},{2,6},{6,2},{1... | collective-permute-start | bytes 1769480 | tf_op jit(solution)/shard_map/ppermute | solution.py:399
  157.0 36.3 %collective-permute-start.30 = (bf16[384,768]{1,0:T(8,128)(2,1)S(1)}, bf16[384,768]{1,0:T(8,128)(2,1)}, u32[]{:S(2)}, u32[]{:S(2)}) collective-permute-start(bf16[384,768]{1,0:T(8,128)(2,1)S(1)} %get-tuple-element.140.refs_0_.refs_1_), channel_id=1, source_target_pairs={{0,4},{4,0},{8,12},{12,8},{1,5},{5,1},{9,13},{13,9},{2,6},{6,2},{1... | collective-permute-start | bytes 1769480 | tf_op jit(solution)/shard_map/ppermute | solution.py:399
  168.9 22.2 %collective-permute-start.29 = (bf16[384,768]{1,0:T(8,128)(2,1)}, bf16[384,768]{1,0:T(8,128)(2,1)}, u32[]{:S(2)}, u32[]{:S(2)}) collective-permute-start(bf16[384,768]{1,0:T(8,128)(2,1)} %collective-permute-done.26.refs_4_.refs_5_), channel_id=1, source_target_pairs={{0,1},{1,0},{2,3},{3,2},{4,5},{5,4},{6,7},{7,6},{8,9},{9,8},{10,11... | collective-permute-start | bytes 1769480 | tf_op jit(solution)/shard_map/ppermute | solution.py:399
  193.4 27.1 %collective-permute-start.41 = (bf16[384,768]{1,0:T(8,128)(2,1)}, bf16[384,768]{1,0:T(8,128)(2,1)}, u32[]{:S(2)}, u32[]{:S(2)}) collective-permute-start(bf16[384,768]{1,0:T(8,128)(2,1)} %collective-permute-done.28.refs_12_.refs_13_), channel_id=1, source_target_pairs={{0,1},{1,0},{2,3},{3,2},{4,5},{5,4},{6,7},{7,6},{8,9},{9,8},{10,11... | collective-permute-start | bytes 1769480 | tf_op jit(solution)/shard_map/ppermute | solution.py:399
  194.7 46.5 %collective-permute-start.39 = (bf16[384,768]{1,0:T(8,128)(2,1)}, bf16[384,768]{1,0:T(8,128)(2,1)}, u32[]{:S(2)}, u32[]{:S(2)}) collective-permute-start(bf16[384,768]{1,0:T(8,128)(2,1)} %get-tuple-element.143.refs_8_.refs_9_), channel_id=1, source_target_pairs={{0,4},{4,0},{8,12},{12,8},{1,5},{5,1},{9,13},{13,9},{2,6},{6,2},{1... | collective-permute-start | bytes 1769480 | tf_op jit(solution)/shard_map/ppermute | solution.py:399
  195.5 45.7 %collective-permute-start.37 = (bf16[384,768]{1,0:T(8,128)(2,1)}, bf16[384,768]{1,0:T(8,128)(2,1)}, u32[]{:S(2)}, u32[]{:S(2)}) collective-permute-start(bf16[384,768]{1,0:T(8,128)(2,1)} %collective-permute-done.27.refs_4_.refs_5_), channel_id=1, source_target_pairs={{0,4},{4,0},{8,12},{12,8},{1,5},{5,1},{9,13},{13,9},{2,6},{6,2},{1... | collective-permute-start | bytes 1769480 | tf_op jit(solution)/shard_map/ppermute | solution.py:399
  196.8 44.4 %collective-permute-start.42 = (bf16[384,768]{1,0:T(8,128)(2,1)}, bf16[384,768]{1,0:T(8,128)(2,1)}, u32[]{:S(2)}, u32[]{:S(2)}) collective-permute-start(bf16[384,768]{1,0:T(8,128)(2,1)} %collective-permute-done.28.refs_12_.refs_13_), channel_id=1, source_target_pairs={{0,4},{4,0},{8,12},{12,8},{1,5},{5,1},{9,13},{13,9},{2,6},{6,2},{1... | collective-permute-start | bytes 1769480 | tf_op jit(solution)/shard_map/ppermute | solution.py:399
  208.2 32.9 %collective-permute-start.38 = (bf16[384,768]{1,0:T(8,128)(2,1)}, bf16[384,768]{1,0:T(8,128)(2,1)}, u32[]{:S(2)}, u32[]{:S(2)}) collective-permute-start(bf16[384,768]{1,0:T(8,128)(2,1)} %collective-permute-done.36.refs_5_.refs_6_), channel_id=1, source_target_pairs={{0,4},{4,0},{8,12},{12,8},{1,5},{5,1},{9,13},{13,9},{2,6},{6,2},{1... | collective-permute-start | bytes 1769480 | tf_op jit(solution)/shard_map/ppermute | solution.py:399
  220.4 20.8 %collective-permute-start.43 = (bf16[384,768]{1,0:T(8,128)(2,1)}, bf16[384,768]{1,0:T(8,128)(2,1)}, u32[]{:S(2)}, u32[]{:S(2)}) collective-permute-start(bf16[384,768]{1,0:T(8,128)(2,1)} %collective-permute-done.41.refs_13_.refs_14_), channel_id=1, source_target_pairs={{0,4},{4,0},{8,12},{12,8},{1,5},{5,1},{9,13},{13,9},{2,6},{6,2},{1... | collective-permute-start | bytes 1769480 | tf_op jit(solution)/shard_map/ppermute | solution.py:399
  267.9 18.9 %collective-permute-start.45 = (bf16[2,768,768]{2,1,0:T(8,128)(2,1)}, bf16[2,768,768]{2,1,0:T(8,128)(2,1)S(1)}, u32[]{:S(2)}, u32[]{:S(2)}) collective-permute-start(bf16[2,768,768]{2,1,0:T(8,128)(2,1)} %get-tuple-element.158), channel_id=1, source_target_pairs={{0,4},{4,0},{8,12},{12,8},{1,5},{5,1},{9,13},{13,9},{2,6},{6,2},{1... | collective-permute-start | bytes 7077896 | tf_op jit(solution)/shard_map/ppermute | solution.py:399
  302.0 36.8 %collective-permute-start.48 = (bf16[2,768,768]{2,1,0:T(8,128)(2,1)}, bf16[2,768,768]{2,1,0:T(8,128)(2,1)}, u32[]{:S(2)}, u32[]{:S(2)}) collective-permute-start(bf16[2,768,768]{2,1,0:T(8,128)(2,1)} %get-tuple-element.169), channel_id=1, source_target_pairs={{0,4},{4,0},{8,12},{12,8},{1,5},{5,1},{9,13},{13,9},{2,6},{6,2},{1... | collective-permute-start | bytes 7077896 | tf_op jit(solution)/shard_map/ppermute | solution.py:399
  304.9 28.3 %collective-permute-start.47 = (bf16[2,384,768]{2,1,0:T(8,128)(2,1)}, bf16[2,384,768]{2,1,0:T(8,128)(2,1)}, u32[]{:S(2)}, u32[]{:S(2)}) collective-permute-start(bf16[2,384,768]{2,1,0:T(8,128)(2,1)} %constant_dynamic-slice_fusion.16), channel_id=1, source_target_pairs={{0,1},{1,0},{2,3},{3,2},{4,5},{5,4},{6,7},{7,6},{8,9},{9,8},{10,11... | collective-permute-start | bytes 3538952 | tf_op jit(solution)/shard_map/ppermute | solution.py:399
  307.6 28.4 %collective-permute-start.46 = (bf16[768,768]{1,0:T(8,128)(2,1)}, bf16[768,768]{1,0:T(8,128)(2,1)}, u32[]{:S(2)}, u32[]{:S(2)}) collective-permute-start(bf16[768,768]{1,0:T(8,128)(2,1)} %slice_bitcast_fusion.3), channel_id=1, source_target_pairs={{0,8},{4,12},{8,0},{12,4},{1,9},{5,13},{9,1},{13,5},{2,10},{6,14},... | collective-permute-start | bytes 3538952 | tf_op jit(solution)/shard_map/ppermute | solution.py:399
  354.7 41.1 %collective-permute-start.51 = (bf16[2,768,768]{2,1,0:T(8,128)(2,1)}, bf16[2,768,768]{2,1,0:T(8,128)(2,1)}, u32[]{:S(2)}, u32[]{:S(2)}) collective-permute-start(bf16[2,768,768]{2,1,0:T(8,128)(2,1)} %get-tuple-element.179), channel_id=1, source_target_pairs={{0,4},{4,0},{8,12},{12,8},{1,5},{5,1},{9,13},{13,9},{2,6},{6,2},{1... | collective-permute-start | bytes 7077896 | tf_op jit(solution)/shard_map/ppermute | solution.py:399
  358.9 39.4 %collective-permute-start.52 = (bf16[2,768,768]{2,1,0:T(8,128)(2,1)}, bf16[2,768,768]{2,1,0:T(8,128)(2,1)}, u32[]{:S(2)}, u32[]{:S(2)}) collective-permute-start(bf16[2,768,768]{2,1,0:T(8,128)(2,1)} %get-tuple-element.181), channel_id=1, source_target_pairs={{0,4},{4,0},{8,12},{12,8},{1,5},{5,1},{9,13},{13,9},{2,6},{6,2},{1... | collective-permute-start | bytes 7077896 | tf_op jit(solution)/shard_map/ppermute | solution.py:399
  361.7 22.0 %collective-permute-start.49 = (bf16[384,768]{1,0:T(8,128)(2,1)}, bf16[384,768]{1,0:T(8,128)(2,1)}, u32[]{:S(2)}, u32[]{:S(2)}) collective-permute-start(bf16[384,768]{1,0:T(8,128)(2,1)} %slice_bitcast_fusion.8), channel_id=1, source_target_pairs={{0,8},{4,12},{8,0},{12,4},{1,9},{5,13},{9,1},{13,5},{2,10},{6,14},... | collective-permute-start | bytes 1769480 | tf_op jit(solution)/shard_map/ppermute | solution.py:399
  365.3 28.0 %collective-permute-start.50 = (bf16[2,384,768]{2,1,0:T(8,128)(2,1)}, bf16[2,384,768]{2,1,0:T(8,128)(2,1)}, u32[]{:S(2)}, u32[]{:S(2)}) collective-permute-start(bf16[2,384,768]{2,1,0:T(8,128)(2,1)} %constant_dynamic-slice_fusion.15), channel_id=1, source_target_pairs={{0,1},{1,0},{2,3},{3,2},{4,5},{5,4},{6,7},{7,6},{8,9},{9,8},{10,11... | collective-permute-start | bytes 3538952 | tf_op jit(solution)/shard_map/ppermute | solution.py:399
  402.2 46.5 %collective-permute-start.54 = (bf16[192,768]{1,0:T(8,128)(2,1)}, bf16[192,768]{1,0:T(8,128)(2,1)}, u32[]{:S(2)}, u32[]{:S(2)}) collective-permute-start(bf16[192,768]{1,0:T(8,128)(2,1)} %constant_dynamic-slice_fusion.13), channel_id=1, source_target_pairs={{0,2},{1,3},{2,0},{3,1},{4,6},{5,7},{6,4},{7,5},{8,10},{9,11},{10,... | collective-permute-start | bytes 884744 | tf_op jit(solution)/shard_map/ppermute | solution.py:399
  405.7 44.2 %collective-permute-start.53 = (bf16[384,768]{1,0:T(8,128)(2,1)}, bf16[384,768]{1,0:T(8,128)(2,1)}, u32[]{:S(2)}, u32[]{:S(2)}) collective-permute-start(bf16[384,768]{1,0:T(8,128)(2,1)} %constant_dynamic-slice_fusion.14), channel_id=1, source_target_pairs={{0,1},{1,0},{2,3},{3,2},{4,5},{5,4},{6,7},{7,6},{8,9},{9,8},{10,11... | collective-permute-start | bytes 1769480 | tf_op jit(solution)/shard_map/ppermute | solution.py:399
  408.4 42.9 %collective-permute-start.55 = (bf16[768,768]{1,0:T(8,128)(2,1)}, bf16[768,768]{1,0:T(8,128)(2,1)}, u32[]{:S(2)}, u32[]{:S(2)}) collective-permute-start(bf16[768,768]{1,0:T(8,128)(2,1)} %slice_bitcast_fusion.2), channel_id=1, source_target_pairs={{0,8},{4,12},{8,0},{12,4},{1,9},{5,13},{9,1},{13,5},{2,10},{6,14},... | collective-permute-start | bytes 3538952 | tf_op jit(solution)/shard_map/ppermute | solution.py:399
  443.0 32.3 %all-to-all-start.1 = ((bf16[8,192,448]{2,1,0:T(8,128)(2,1)}), bf16[8,192,448]{2,1,0:T(8,128)(2,1)}, u32[]{:S(2)}, u32[]{:S(2)}) async-start(bf16[8,192,448]{2,1,0:T(8,128)(2,1)} %bitcast.131), calls=%async_computation.1 | async-start | bytes 3145728 | tf_op jit(solution)/shard_map/all_to_all | solution.py:650
  448.6 48.4 %collective-permute-start.61 = (bf16[2,768,768]{2,1,0:T(8,128)(2,1)}, bf16[2,768,768]{2,1,0:T(8,128)(2,1)}, u32[]{:S(2)}, u32[]{:S(2)}) collective-permute-start(bf16[2,768,768]{2,1,0:T(8,128)(2,1)} %get-tuple-element.213), channel_id=1, source_target_pairs={{0,4},{4,0},{8,12},{12,8},{1,5},{5,1},{9,13},{13,9},{2,6},{6,2},{1... | collective-permute-start | bytes 7077896 | tf_op jit(solution)/shard_map/ppermute | solution.py:399
  453.4 21.8 %collective-permute-start.57 = (bf16[384,768]{1,0:T(8,128)(2,1)S(1)}, bf16[384,768]{1,0:T(8,128)(2,1)S(1)}, u32[]{:S(2)}, u32[]{:S(2)}) collective-permute-start(bf16[384,768]{1,0:T(8,128)(2,1)S(1)} %constant_dynamic-slice_fusion.12), channel_id=1, source_target_pairs={{0,1},{1,0},{2,3},{3,2},{4,5},{5,4},{6,7},{7,6},{8,9},{9,8},{10,11... | collective-permute-start | bytes 1769480 | tf_op jit(solution)/shard_map/ppermute | solution.py:399
  455.8 44.4 %collective-permute-start.56 = (bf16[768,768]{1,0:T(8,128)(2,1)}, bf16[768,768]{1,0:T(8,128)(2,1)}, u32[]{:S(2)}, u32[]{:S(2)}) collective-permute-start(bf16[768,768]{1,0:T(8,128)(2,1)} %slice_bitcast_fusion.1), channel_id=1, source_target_pairs={{0,8},{4,12},{8,0},{12,4},{1,9},{5,13},{9,1},{13,5},{2,10},{6,14},... | collective-permute-start | bytes 3538952 | tf_op jit(solution)/shard_map/ppermute | solution.py:399
  475.3 19.7 %collective-permute-start.62 = (f32[2,4,12,192]{3,1,2,0:T(4,128)}, f32[2,4,12,192]{3,1,2,0:T(4,128)S(1)}, u32[]{:S(2)}, u32[]{:S(2)}) collective-permute-start(f32[2,4,12,192]{3,1,2,0:T(4,128)} %fusion.25), channel_id=1, source_target_pairs={{0,8},{4,12},{8,0},{12,4},{1,9},{5,13},{9,1},{13,5},{2,10},{6,14},... | collective-permute-start | bytes 221192 | tf_op jit(solution)/shard_map/ppermute | solution.py:399
  505.4 40.8 %collective-permute-start.68 = (bf16[768,768]{1,0:T(8,128)(2,1)S(1)}, bf16[768,768]{1,0:T(8,128)(2,1)S(1)}, u32[]{:S(2)}, u32[]{:S(2)}) collective-permute-start(bf16[768,768]{1,0:T(8,128)(2,1)S(1)} %slice_bitcast_fusion), channel_id=1, source_target_pairs={{0,8},{4,12},{8,0},{12,4},{1,9},{5,13},{9,1},{13,5},{2,10},{6,14},... | collective-permute-start | bytes 3538952 | tf_op jit(solution)/shard_map/ppermute | solution.py:399
  519.4 22.2 %collective-permute-start.67 = (bf16[192,768]{1,0:T(8,128)(2,1)S(1)}, bf16[192,768]{1,0:T(8,128)(2,1)S(1)}, u32[]{:S(2)}, u32[]{:S(2)}) collective-permute-start(bf16[192,768]{1,0:T(8,128)(2,1)S(1)} %add_convert_fusion.17), channel_id=1, source_target_pairs={{0,2},{1,3},{2,0},{3,1},{4,6},{5,7},{6,4},{7,5},{8,10},{9,11},{10,... | collective-permute-start | bytes 884744 | tf_op jit(solution)/shard_map/ppermute | solution.py:399
  519.7 26.3 %collective-permute-start.66 = (bf16[192,768]{1,0:T(8,128)(2,1)S(1)}, bf16[192,768]{1,0:T(8,128)(2,1)S(1)}, u32[]{:S(2)}, u32[]{:S(2)}) collective-permute-start(bf16[192,768]{1,0:T(8,128)(2,1)S(1)} %constant_dynamic-slice_fusion.8), channel_id=1, source_target_pairs={{0,2},{1,3},{2,0},{3,1},{4,6},{5,7},{6,4},{7,5},{8,10},{9,11},{10,... | collective-permute-start | bytes 884744 | tf_op jit(solution)/shard_map/ppermute | solution.py:399
  549.6 20.0 %collective-permute-start.72 = (bf16[384,768]{1,0:T(8,128)(2,1)S(1)}, bf16[384,768]{1,0:T(8,128)(2,1)S(1)}, u32[]{:S(2)}, u32[]{:S(2)}) collective-permute-start(bf16[384,768]{1,0:T(8,128)(2,1)S(1)} %constant_dynamic-slice_fusion.7), channel_id=1, source_target_pairs={{0,1},{1,0},{2,3},{3,2},{4,5},{5,4},{6,7},{7,6},{8,9},{9,8},{10,11... | collective-permute-start | bytes 1769480 | tf_op jit(solution)/shard_map/ppermute | solution.py:399
  569.8 20.8 %collective-permute-start.76 = (bf16[192,768]{1,0:T(8,128)(2,1)S(1)}, bf16[192,768]{1,0:T(8,128)(2,1)S(1)}, u32[]{:S(2)}, u32[]{:S(2)}) collective-permute-start(bf16[192,768]{1,0:T(8,128)(2,1)S(1)} %constant_dynamic-slice_fusion.4), channel_id=1, source_target_pairs={{0,2},{1,3},{2,0},{3,1},{4,6},{5,7},{6,4},{7,5},{8,10},{9,11},{10,... | collective-permute-start | bytes 884744 | tf_op jit(solution)/shard_map/ppermute | solution.py:399
  570.7 24.9 %collective-permute-start.75 = (bf16[192,768]{1,0:T(8,128)(2,1)S(1)}, bf16[192,768]{1,0:T(8,128)(2,1)S(1)}, u32[]{:S(2)}, u32[]{:S(2)}) collective-permute-start(bf16[192,768]{1,0:T(8,128)(2,1)S(1)} %add_convert_fusion.15), channel_id=1, source_target_pairs={{0,2},{1,3},{2,0},{3,1},{4,6},{5,7},{6,4},{7,5},{8,10},{9,11},{10,... | collective-permute-start | bytes 884744 | tf_op jit(solution)/shard_map/ppermute | solution.py:399
  603.7 23.3 %collective-permute-start.81 = (bf16[384,768]{1,0:T(8,128)(2,1)S(1)}, bf16[384,768]{1,0:T(8,128)(2,1)S(1)}, u32[]{:S(2)}, u32[]{:S(2)}) collective-permute-start(bf16[384,768]{1,0:T(8,128)(2,1)S(1)} %maximum_select_fusion.3), channel_id=1, source_target_pairs={{0,1},{1,0},{2,3},{3,2},{4,5},{5,4},{6,7},{7,6},{8,9},{9,8},{10,11... | collective-permute-start | bytes 1769480 | tf_op jit(solution)/shard_map/ppermute | solution.py:399
  607.5 32.2 %collective-permute-start.80 = (bf16[384,768]{1,0:T(8,128)(2,1)S(1)}, bf16[384,768]{1,0:T(8,128)(2,1)S(1)}, u32[]{:S(2)}, u32[]{:S(2)}) collective-permute-start(bf16[384,768]{1,0:T(8,128)(2,1)S(1)} %maximum_select_fusion.4), channel_id=1, source_target_pairs={{0,1},{1,0},{2,3},{3,2},{4,5},{5,4},{6,7},{7,6},{8,9},{9,8},{10,11... | collective-permute-start | bytes 1769480 | tf_op jit(solution)/shard_map/ppermute | solution.py:399
  618.0 31.5 %collective-permute-start.79 = (bf16[384,768]{1,0:T(8,128)(2,1)S(1)}, bf16[384,768]{1,0:T(8,128)(2,1)S(1)}, u32[]{:S(2)}, u32[]{:S(2)}) collective-permute-start(bf16[384,768]{1,0:T(8,128)(2,1)S(1)} %maximum_select_fusion.5), channel_id=1, source_target_pairs={{0,1},{1,0},{2,3},{3,2},{4,5},{5,4},{6,7},{7,6},{8,9},{9,8},{10,11... | collective-permute-start | bytes 1769480 | tf_op jit(solution)/shard_map/ppermute | solution.py:399
  (121 other events, 1191.3 us)

commit v4 on v3

--- a/solution.py
+++ b/solution.py
@@ -422,12 +422,6 @@
     return lax.dynamic_slice_in_dim(value, place * size, size, axis=value.ndim - 2)
 
 
-def joined(first, second, swap):
-    return jnp.where(
-        swap, jnp.concatenate([second, first], axis=0), jnp.concatenate([first, second], axis=0)
-    )
-
-
 class Chain:
     def start(self, send):
         self.arrived = flip(send, "tensor", 1)
@@ -435,13 +429,16 @@
     def cores(self, keep):
         self.value = added(keep, self.arrived)
 
+    def scatter(self):
+        parts = lax.axis_size("dp")
+        rows = self.value.shape[-2] // parts
+        split = self.value.reshape(-1, parts, rows, D)
+        split = jnp.swapaxes(split, 0, 1)
+        total = lax.psum_scatter(split, "dp", scatter_dimension=0, tiled=False)
+        self.value = total if self.value.ndim == 3 else total[0]
+
     def send_y(self):
         self.kept, self.arrived = self.value[1], flip(self.value[0], "tensor", 2)
-
-    def send_z(self, level):
-        mine = (lax.axis_index("dp") >> level) & 1
-        self.kept = rows_of(self.value, mine, 2)
-        self.arrived = flip(rows_of(self.value, 1 - mine, 2), "dp", 1 << level)
 
     def send_x(self, first, second):
         section = lax.axis_index("section")
@@ -451,19 +448,17 @@
     def fold(self):
         self.value = added(self.kept, self.arrived)
 
-    def finish_x(self):
-        self.fold()
-        bit = 4
+    def gather(self):
+        bit = 1
         while bit < lax.axis_size("dp"):
-            self.value = added(self.value, flip(self.value, "dp", bit))
+            arrived = flip(self.value, "dp", bit)
+            upper = (lax.axis_index("dp") & bit) != 0
+            self.value = jnp.where(
+                upper,
+                jnp.concatenate([arrived, self.value], axis=0),
+                jnp.concatenate([self.value, arrived], axis=0),
+            )
             bit *= 2
-
-    def gather_z(self, level):
-        self.level, self.arrived = level, flip(self.value, "dp", 1 << level)
-
-    def join(self):
-        mine = (lax.axis_index("dp") >> self.level) & 1
-        self.value = joined(self.value, self.arrived, mine == 1)
 
 
 def tied(chains, *others):
@@ -492,10 +487,9 @@
     small = jnp.concatenate(
         [ln_gain[0], ln_shift[0], b_qv[0], b_out, b_fc2, b_fc1.reshape(SHARDS, FEATS)], axis=0
     )
-    nears[0], small, ends = tie((nears[0], small, ends_in[0]))
-    beyond = flip(nears[0], "section", 1)
-
-    ends = ends.T.reshape(FEATS, clips, FRAMES).transpose(1, 0, 2)
+    ends = ends_in[0].T.reshape(FEATS, clips, FRAMES).transpose(1, 0, 2)
+    beyond, small, ends, nears[1] = tie((flip(nears[0], "section", 1), small, ends, nears[1]))
+
     ends = lax.all_to_all(ends, ("section", "tensor"), split_axis=0, concat_axis=0, tiled=True)
     ends = ends.reshape(2, D, FRAMES)
 
@@ -515,9 +509,13 @@
         return jnp.where(section == 0, own, other), jnp.where(section == 0, other, own)
 
     near_own, far_own = [], []
-    for index in range(2):
-        near_other, following = tie((beyond, (nears[1], owned[2])[index]))
-        beyond = flip(following, "section", 1)
+    for index in range(3):
+        near_other = beyond
+        if index < 2:
+            following = nears[index + 1]
+            if index:
+                near_other, following = tie((beyond, following))
+            beyond = flip(following, "section", 1)
         near_own.append(layers(nears[index], near_other))
         far_own.append(layers(fars[index], flip(near_other, "dp", 1)))
 
@@ -547,30 +545,38 @@
     away_one = flip(there_one, "dp", 1)
     a1, p, soft, o, h = attend(0, stream, chunks[0][0])
 
-    h, away_one, beyond, far_one, late_a, late_one = tie(
-        (h, away_one, beyond, far_own[1], near_own[0][1], near_own[1][1])
-    )
-    far_own[1], near_own[0], near_own[1] = far_one, (None, late_a), (near_own[1][0], late_one)
+    there_two = over_y(2, 0)
+    late = [near_own[index][1] for index in range(3)]
+    h, away_one, there_two, late, far_two = tie((h, away_one, there_two, late, far_own[2]))
+    far_own[2] = far_two
+    for index in range(3):
+        near_own[index] = (near_own[index][0], late[index])
     chunks[0][1] = chunk_of(1, 0, there_one, away_one)
-    near_own.append(layers(nears[2], rows_of(beyond, zhalf, 2)))
-    far_own.append(layers(fars[2], rows_of(beyond, 1 - zhalf, 2)))
-    there_two = over_y(2, 0)
-    there_two, late_a = tie((there_two, late_a))
-    near_own[0] = (None, late_a)
     chunks[0][2] = chunk_of(2, 0, there_two, flip(there_two, "dp", 1))
     there_a = over_y(0, 1)
-    there_a, late_one, late_two = tie((there_a, near_own[1][1], near_own[2][1]))
+    there_a, late_one, late_two = tie((there_a, late[1], late[2]))
     near_own[1], near_own[2] = (None, late_one), (None, late_two)
     away_a = flip(there_a, "dp", 1)
     there_one, there_two = over_y(1, 1), over_y(2, 1)
     a2, u, slope, y = feed(0, h, chunks[0][1], chunks[0][2])
     stored = [(stream, a1, p, soft, o, h, a2, u, slope)]
 
-    stream, there_one, there_two, away_a = tie((y, there_one, there_two, away_a))
+    stream, there_a, there_one, there_two, away_a, near_a, far_a = tie(
+        (y, there_a, there_one, there_two, away_a, near_own[0][1], far_own[0][1])
+    )
+    near_own[0], far_own[0] = (None, near_a), (None, far_a)
     chunks[1][0] = chunk_of(0, 1, there_a, away_a)
-    chunks[1][1] = chunk_of(1, 1, there_one, flip(there_one, "dp", 1))
-    chunks[1][2] = chunk_of(2, 1, there_two, flip(there_two, "dp", 1))
+    away_one, away_two = flip(there_one, "dp", 1), flip(there_two, "dp", 1)
     a1, p, soft, o, h = attend(1, stream, chunks[1][0])
+    parts = [[near_own[k][1], far_own[k][1]] for k in (1, 2)]
+    h, there_one, there_two, away_one, away_two, parts = tie(
+        (h, there_one, there_two, away_one, away_two, parts)
+    )
+    for index in (1, 2):
+        near_own[index] = (None, parts[index - 1][0])
+        far_own[index] = (None, parts[index - 1][1])
+    chunks[1][1] = chunk_of(1, 1, there_one, away_one)
+    chunks[1][2] = chunk_of(2, 1, there_two, away_two)
     a2, u, slope, y = feed(1, h, chunks[1][1], chunks[1][2])
     stored.append((stream, a1, p, soft, o, h, a2, u, slope))
     stream = y
@@ -594,17 +600,13 @@
         )
         chain_two.cores(keep_two)
         chain_one.cores(keep_one)
+        (gh,) = tied((chain_two, chain_one), gh)
         if layer == 1:
-            (gh,) = tied((late_two, late_one), gh)
-            late_two.send_y()
-            late_one.send_z(0)
+            late_two.scatter()
+            late_one.scatter()
         else:
-            late_one.fold()
-            late_a.fold()
-            (gh,) = tied((late_one, late_a, last_two, last_one, late_two), gh)
             last_two.send_y()
-            late_two.send_z(0)
-            late_one.send_z(1)
+            last_one.scatter()
         after, send_a, dbqv_sent = attention_backward(
             info, gh, x, a1, cols[layer], p, soft, o, None, chunk_a
         )
@@ -613,12 +615,9 @@
             info, gh, x, a1, cols[layer], p, soft, o, after, chunk_a
         )
         chain_a.cores(keep_a)
+        (upstream,) = tied((chain_a,), upstream)
         if layer == 1:
-            late_two.fold()
-            late_one.fold()
-            (upstream,) = tied((late_two, late_one, late_a), upstream)
-            late_one.send_y()
-            late_a.send_z(0)
+            late_a.scatter()
         db1 = by_bits([db1_kept[1], db1_sent[1], db1_kept[0], db1_sent[0]], shard)
         dbqv = by_bits([dbqv_kept[1], dbqv_sent[1], dbqv_kept[0], dbqv_sent[0]], shard)
         dcol = jnp.concatenate(
@@ -640,78 +639,49 @@
     result = result.reshape(2 * SHARDS, FEATS, FRAMES)
     small_sum = jnp.stack(smalls)
 
+    last_two.fold()
+    result, small_sum = tied((last_a, last_two), result, small_sum)
+    last_a.send_y()
+    last_two.scatter()
+    late_two.send_y()
+    late_one.send_y()
+    small_sum += flip(small_sum, "tensor", 1)
     late_two.fold()
     late_one.fold()
-    last_two.fold()
-    tied((late_two, late_one, last_two, last_one))
+    small_sum += flip(small_sum, "tensor", 2)
+
+    result, small_sum = tied((late_two, late_one, late_a, last_one), result, small_sum)
     last_one.send_y()
-    last_two.send_z(0)
-    late_two.send_z(1)
+    late_a.send_y()
     result = lax.all_to_all(result, ("section", "tensor"), split_axis=0, concat_axis=0, tiled=True)
-    small_sum += flip(small_sum, "tensor", 1)
-
-    last_two.fold()
-    late_two.fold()
-    result, small_sum = tied((last_two, late_two), result, small_sum)
-    last_two.send_z(1)
-    small_sum += flip(small_sum, "tensor", 2)
-    result = result.transpose(1, 0, 2).reshape(FEATS, clips * FRAMES).T.astype(F32)
-
+    small_sum += flip(small_sum, "section", 1)
     last_one.fold()
-    last_two.fold()
-    result, small_sum = tied((last_one, last_two, last_a, late_a), result, small_sum)
-    last_a.send_y()
-    late_a.send_y()
-    last_one.send_z(0)
+    late_a.fold()
+    last_a.fold()
+    result, small_sum = tied((late_a, last_one, last_a), result, small_sum)
+    last_a.scatter()
+    pair_one = Chain()
+    pair_one.send_x(last_one, late_one)
+    pair_one.fold()
+    small_sum += flip(small_sum, "dp", 1)
+    result, small_sum = tied((pair_one, last_two), result, small_sum)
     pair_two = Chain()
     pair_two.send_x(last_two, late_two)
-    small_sum += flip(small_sum, "section", 1)
-
-    last_one.fold()
-    pair_two.finish_x()
-    (small_sum,) = tied((last_one, pair_two), small_sum)
-    last_one.send_z(1)
-    pair_two.gather_z(1)
-    small_sum += flip(small_sum, "dp", 1)
-
-    last_one.fold()
-    pair_two.join()
-    last_a.fold()
-    late_a.fold()
-    (small_sum,) = tied((last_one, pair_two, last_a, late_a), small_sum)
-    pair_one = Chain()
-    pair_one.send_x(last_one, late_one)
-    last_a.send_z(0)
-    late_a.send_z(1)
-    pair_two.gather_z(0)
+    pair_two.fold()
+    pair_one.gather()
+    pair_two.gather()
     bit = 2
     while bit < lax.axis_size("dp"):
         small_sum += flip(small_sum, "dp", bit)
         bit *= 2
-
-    pair_one.finish_x()
-    last_a.fold()
-    late_a.fold()
-    (small_sum,) = tied((pair_one, last_a, late_a), small_sum)
-    pair_one.gather_z(1)
-    last_a.send_z(1)
+    result = result.transpose(1, 0, 2).reshape(FEATS, clips * FRAMES).T.astype(F32)
     small_sum = lax.dynamic_slice(
         small_sum, (section, shard, 0, 0), (1, 1, 12, FEATS)
     ).reshape(12, FEATS)
-
-    pair_one.join()
-    last_a.fold()
-    pair_two.join()
-    tied((pair_one, last_a))
     pair_a = Chain()
     pair_a.send_x(last_a, late_a)
-    pair_one.gather_z(0)
-    pair_a.finish_x()
-    pair_a.gather_z(1)
-    pair_one.join()
-    pair_a.join()
-    pair_a.gather_z(0)
-    pair_a.join()
+    pair_a.fold()
+    pair_a.gather()
 
     grad_a, grad_one, grad_two = [pair.value.astype(F32) for pair in (pair_a, pair_one, pair_two)]
     return (

time: 657 us -> 657 us (level)
  starting transfers between devices: 78.7 us -> 61.3 us
  between operations: 2.5 us -> 15.7 us
  local copies, waits for them, and re-layouts: 66.6 us -> 78.2 us
  other arithmetic: 64.3 us -> 53.9 us
    reduce_scatter x0 -> x6, waiting for transfers between devices: none -> 31.5 us  [scatter(): total = lax.psum_scatter(split, 'dp', scatter_dimension=0, tiled=False)]
    ppermute x82 -> x71, waiting for transfers between devices: 271 us -> 240 us  [flip(): return lax.ppermute(block, axis, [(i, i ^ bit) for i in range(size)])]
    unnamed x173 -> x175, local copies, waits for them, and re-layouts: 15.2 us -> 33.5 us
    ppermute x82 -> x71, starting transfers between devices: 69.4 us -> 51.7 us  [flip(): return lax.ppermute(block, axis, [(i, i ^ bit) for i in range(size)])]
    convert_element_type x27 -> x15, other arithmetic: 37 us -> 26.8 us  [added(): return (left.astype(F32) + right.astype(F32)).astype(BF16)]
    reshape x2 -> x6, local copies, waits for them, and re-layouts: 4.87 us -> 12.8 us  [the longest x4 7.94 us: scatter(): split = self.value.reshape(-1, parts, rows, D)]
  transfers between devices with their start and end apart: 84 -> 79, of which waited for: 33 -> 33; matrix products, arithmetic and copies ran while one was open for 15% -> 15% of each run, Pallas kernels for 18% -> 22%
where the time goes in v4:
time: 657 us; the launch traced here: 650 us
  waiting for transfers between devices  272 us (41%)
  Pallas kernels  169 us (26%)
  local copies, waits for them, and re-layouts  78.2 us (12%)
  starting transfers between devices  61.3 us (9%)
  other arithmetic  53.9 us (8%)
  between operations  15.7 us (2%)
    ppermute x71, waiting for transfers between devices, flip(): return lax.ppermute(block, axis, [(i, i ^ bit) for i in range(size)])  240 us
    pallas_call x12, Pallas kernels, run(): pl.pallas_call(kernel, name=name, out_shape=outs, grid_spec=pltpu.Prefetc...  169 us
    ppermute x71, starting transfers between devices, flip(): return lax.ppermute(block, axis, [(i, i ^ bit) for i in range(size)])  51.7 us
    unnamed x175, local copies, waits for them, and re-layouts  33.5 us
    reduce_scatter x6, waiting for transfers between devices, scatter(): total = lax.psum_scatter(split, 'dp', scatter_dimension=0, tiled=False)  31.5 us
    convert_element_type x15, other arithmetic, added(): return (left.astype(F32) + right.astype(F32)).astype(BF16)  26.8 us
  transfers between devices with their start and end apart: 79, of which 33 were waited for; matrix products, arithmetic and copies ran while one was open for 15% of the time, Pallas kernels for 22%

profile of v4, /device:TPU:0, one launch (start us, length us, event | category | flops | bytes accessed | tf_op | source)
XLA Modules:
  0.0 649.6 jit_solution(2223233025695637636)
XLA Ops:
  8.6 3.0 collective-permute-start
  12.4 3.3 reshape.406
  18.5 6.5 %collective-permute-done = bf16[384,768]{1,0:T(8,128)(2,1)} collective-permute-done((bf16[384,768]{1,0:T(8,128)(2,1)S(1)}, bf16[384,768]{1,0:T(8,128)(2,1)}, u32[]{:S(2)}, u32[]{:S(2)}) %collective-permute-start) | collective-permute-done | bytes 589856 | tf_op jit(solution)/shard_map/ppermute | solution.py:399
  39.1 4.3 all-to-all-start
  46.6 29.5 %collective-permute-done.11 = bf16[384,768]{1,0:T(8,128)(2,1)} collective-permute-done((bf16[384,768]{1,0:T(8,128)(2,1)S(1)}, bf16[384,768]{1,0:T(8,128)(2,1)}, u32[]{:S(2)}, u32[]{:S(2)}) %collective-permute-start.11) | collective-permute-done | bytes 589856 | tf_op jit(solution)/shard_map/ppermute | solution.py:399
  80.2 10.8 %collective-permute-done.14 = bf16[384,768]{1,0:T(8,128)(2,1)S(1)} collective-permute-done((bf16[384,768]{1,0:T(8,128)(2,1)S(1)}, bf16[384,768]{1,0:T(8,128)(2,1)S(1)}, u32[]{:S(2)}, u32[]{:S(2)}) %collective-permute-start.14) | collective-permute-done | bytes 589856 | tf_op jit(solution)/shard_map/ppermute | solution.py:399
  91.5 2.8 broadcast_select_fusion
  99.7 8.6 %collective-permute-done.16 = bf16[384,768]{1,0:T(8,128)(2,1)S(1)} collective-permute-done((bf16[384,768]{1,0:T(8,128)(2,1)S(1)}, bf16[384,768]{1,0:T(8,128)(2,1)S(1)}, u32[]{:S(2)}, u32[]{:S(2)}) %collective-permute-start.16) | collective-permute-done | bytes 589856 | tf_op jit(solution)/shard_map/ppermute | solution.py:399
  109.6 2.8 fusion.20
  115.0 6.0 collective-permute-done.13.refs_5_.refs_6_
  121.1 15.9 %attention_forward.2 = (bf16[768,448]{1,0:T(8,128)(2,1)}, bf16[4,576,448]{2,1,0:T(8,128)(2,1)}, bf16[4,3,448,448]{3,2,1,0:T(8,128)(2,1)}, bf16[4,192,448]{2,1,0:T(8,128)(2,1)}, f32[768,448]{1,0:T(8,128)}) custom-call(s32[9]{0:T(128)S(1)} %stack.113.info, bf16[768,448]{1,0:T(8,128)(2,1)} %bitcast.160, f32[4,192,8]{2,1,0:T(8,128)S(1)} %get-tuple-element.336.col_ref, ...), custom_call_target="tpu_custom_call" | custom-call | flops 2730491904 | bytes 15071232 | tf_op jit(solution)/shard_map/attention_forward/pallas_call | solution.py:298
  141.7 11.2 %collective-permute-done.27.refs_4_.refs_5_ = bf16[384,768]{1,0:T(8,128)(2,1)} collective-permute-done((bf16[384,768]{1,0:T(8,128)(2,1)S(1)}, bf16[384,768]{1,0:T(8,128)(2,1)}, u32[]{:S(2)}, u32[]{:S(2)}) %collective-permute-start.27) | collective-permute-done | bytes 589856 | tf_op jit(solution)/shard_map/ppermute | solution.py:399
  166.8 13.6 %mlp_forward.2 = (bf16[768,448]{1,0:T(8,128)(2,1)}, bf16[4,448,768]{2,1,0:T(8,128)(2,1)}, bf16[4,448,768]{2,1,0:T(8,128)(2,1)}, f32[768,448]{1,0:T(8,128)}) custom-call(s32[9]{0:T(128)S(1)} %stack.113.info, f32[768,448]{1,0:T(8,128)} %get-tuple-element.130.h_ref, f32[4,192,8]{2,1,0:T(8,128)S(1)} %get-tuple-element.336.col_ref, ...), custom_call_target="tpu_custom_call" | custom-call | flops 4227858432 | bytes 18419712 | tf_op jit(solution)/shard_map/mlp_forward/pallas_call | solution.py:298
  180.4 3.5 collective-permute-done.29.refs_12_.refs_13_
  188.7 15.7 %attention_forward.3 = (bf16[768,448]{1,0:T(8,128)(2,1)}, bf16[4,576,448]{2,1,0:T(8,128)(2,1)}, bf16[4,3,448,448]{3,2,1,0:T(8,128)(2,1)}, bf16[4,192,448]{2,1,0:T(8,128)(2,1)}, f32[768,448]{1,0:T(8,128)}) custom-call(s32[9]{0:T(128)S(1)} %stack.113.info, f32[768,448]{1,0:T(8,128)} %get-tuple-element.141.x_ref, f32[4,192,8]{2,1,0:T(8,128)S(1)} %get-tuple-element.335.col_ref, ...), custom_call_target="tpu_custom_call" | custom-call | flops 2730491904 | bytes 15759360 | tf_op jit(solution)/shard_map/attention_forward/pallas_call | solution.py:298
  204.4 8.7 %collective-permute-done.36.refs_13_.refs_14_ = bf16[384,768]{1,0:T(8,128)(2,1)} collective-permute-done((bf16[384,768]{1,0:T(8,128)(2,1)}, bf16[384,768]{1,0:T(8,128)(2,1)}, u32[]{:S(2)}, u32[]{:S(2)}) %collective-permute-start.36) | collective-permute-done | bytes 589856 | tf_op jit(solution)/shard_map/ppermute | solution.py:399
  226.1 13.6 %mlp_forward.3 = (bf16[768,448]{1,0:T(8,128)(2,1)}, bf16[4,448,768]{2,1,0:T(8,128)(2,1)}, bf16[4,448,768]{2,1,0:T(8,128)(2,1)}, f32[768,448]{1,0:T(8,128)}) custom-call(s32[9]{0:T(128)S(1)} %stack.113.info, f32[768,448]{1,0:T(8,128)} %get-tuple-element.150.h_ref, f32[4,192,8]{2,1,0:T(8,128)S(1)} %get-tuple-element.335.col_ref, ...), custom_call_target="tpu_custom_call" | custom-call | flops 4227858432 | bytes 18419712 | tf_op jit(solution)/shard_map/mlp_forward/pallas_call | solution.py:298
  239.8 12.0 %mlp_backward.4 = (f32[448,768]{1,0:T(8,128)}, bf16[2,768,768]{2,1,0:T(8,128)(2,1)}, bf16[2,768,768]{2,1,0:T(8,128)(2,1)}, f32[2,1,768]{2,1,0:T(1,128)S(1)}) custom-call(s32[9]{0:T(128)S(1)} %stack.113.info, bf16[768,448]{1,0:T(8,128)(2,1)} %bitcast.171, f32[768,448]{1,0:T(8,128)} %get-tuple-element.150.h_ref, bf16[768,448]{1,0:T(8,128)(2,1)} %get-tuple-element.159.a2_ref, ...), custom_call_target="tpu_custom_call" | custom-call | flops 4227858432 | bytes 23820288 | tf_op jit(solution)/shard_map/mlp_backward/pallas_call | solution.py:298
  252.4 14.6 %mlp_backward.5 = (f32[768,448]{1,0:T(8,128)}, f32[768,8]{1,0:T(8,128)S(1)}, bf16[2,768,768]{2,1,0:T(8,128)(2,1)}, bf16[2,768,768]{2,1,0:T(8,128)(2,1)}, f32[2,1,768]{2,1,0:T(1,128)S(1)}) custom-call(s32[9]{0:T(128)S(1)} %stack.113.info, bf16[768,448]{1,0:T(8,128)(2,1)} %bitcast.172, f32[768,448]{1,0:T(8,128)} %get-tuple-element.150.h_ref, ...), custom_call_target="tpu_custom_call" | custom-call | flops 4227858432 | bytes 25221120 | tf_op jit(solution)/shard_map/mlp_backward/pallas_call | solution.py:298
  268.4 4.6 add_convert_fusion.5
  275.7 3.2 copy.264
  285.5 12.5 %attention_backward.4 = (f32[448,768]{1,0:T(8,128)}, bf16[2,768,768]{2,1,0:T(8,128)(2,1)}, f32[2,192,8]{2,1,0:T(8,128)S(1)}) custom-call(s32[9]{0:T(128)S(1)} %stack.113.info, f32[768,448]{1,0:T(8,128)} %get-tuple-element.170.gh_ref, f32[768,448]{1,0:T(8,128)} %get-tuple-element.141.x_ref, bf16[768,448]{1,0:T(8,128)(2,1)S(1)} %copy-done.13, ...), custom_call_target="tpu_custom_call" | custom-call | flops 2730491904 | bytes 19501056 | tf_op jit(solution)/shard_map/attention_backward/pallas_call | solution.py:298
  298.4 15.6 %attention_backward.5 = (f32[768,448]{1,0:T(8,128)}, f32[768,8]{1,0:T(8,128)S(1)}, bf16[2,768,768]{2,1,0:T(8,128)(2,1)}, f32[2,192,8]{2,1,0:T(8,128)S(1)}) custom-call(s32[9]{0:T(128)S(1)} %stack.113.info, f32[768,448]{1,0:T(8,128)} %get-tuple-element.170.gh_ref, f32[768,448]{1,0:T(8,128)} %get-tuple-element.141.x_ref, ...), custom_call_target="tpu_custom_call" | custom-call | flops 2730491904 | bytes 20901888 | tf_op jit(solution)/shard_map/attention_backward/pallas_call | solution.py:298
  314.1 2.5 add_convert_fusion.3
  322.7 11.9 %mlp_backward.6 = (f32[448,768]{1,0:T(8,128)}, bf16[2,768,768]{2,1,0:T(8,128)(2,1)}, bf16[2,768,768]{2,1,0:T(8,128)(2,1)}, f32[2,1,768]{2,1,0:T(1,128)S(1)}) custom-call(s32[9]{0:T(128)S(1)} %stack.113.info, f32[768,448]{1,0:T(8,128)} %get-tuple-element.180.gy_ref, f32[768,448]{1,0:T(8,128)} %get-tuple-element.130.h_ref, ...), custom_call_target="tpu_custom_call" | custom-call | flops 4227858432 | bytes 24508416 | tf_op jit(solution)/shard_map/mlp_backward/pallas_call | solution.py:298
  335.2 14.4 %mlp_backward.7 = (f32[768,448]{1,0:T(8,128)}, f32[768,8]{1,0:T(8,128)S(1)}, bf16[2,768,768]{2,1,0:T(8,128)(2,1)}, bf16[2,768,768]{2,1,0:T(8,128)(2,1)}, f32[2,1,768]{2,1,0:T(1,128)S(1)}) custom-call(s32[9]{0:T(128)S(1)} %stack.113.info, f32[768,448]{1,0:T(8,128)} %get-tuple-element.180.gy_ref, f32[768,448]{1,0:T(8,128)} %get-tuple-element.130.h_ref, ...), custom_call_target="tpu_custom_call" | custom-call | flops 4227858432 | bytes 25909248 | tf_op jit(solution)/shard_map/mlp_backward/pallas_call | solution.py:298
  349.7 3.9 add_convert_fusion.2
  359.9 13.0 %attention_backward.6 = (f32[448,768]{1,0:T(8,128)}, bf16[2,768,768]{2,1,0:T(8,128)(2,1)}, f32[2,192,8]{2,1,0:T(8,128)S(1)}) custom-call(s32[9]{0:T(128)S(1)} %stack.113.info, f32[768,448]{1,0:T(8,128)} %get-tuple-element.191.gh_ref, bf16[768,448]{1,0:T(8,128)(2,1)S(1)} %bitcast.162, bf16[768,448]{1,0:T(8,128)(2,1)} %get-tuple-element.192.a1_ref, ...), custom_call_target="tpu_custom_call" | custom-call | flops 2730491904 | bytes 18812928 | tf_op jit(solution)/shard_map/attention_backward/pallas_call | solution.py:298
  379.7 15.7 %attention_backward.7 = (f32[768,448]{1,0:T(8,128)}, f32[768,8]{1,0:T(8,128)S(1)}, bf16[2,768,768]{2,1,0:T(8,128)(2,1)}, f32[2,192,8]{2,1,0:T(8,128)S(1)}) custom-call(s32[9]{0:T(128)S(1)} %stack.113.info, f32[768,448]{1,0:T(8,128)} %get-tuple-element.191.gh_ref, bf16[768,448]{1,0:T(8,128)(2,1)} %bitcast.161, bf16[768,448]{1,0:T(8,128)(2,1)} %get-tuple-element.192.a1_ref, ...), custom_call_target="tpu_custom_call" | custom-call | flops 2730491904 | bytes 20213760 | tf_op jit(solution)/shard_map/attention_backward/pallas_call | solution.py:298
  396.4 10.3 %collective-permute-done.53 = bf16[768,768]{1,0:T(8,128)(2,1)} collective-permute-done((bf16[768,768]{1,0:T(8,128)(2,1)}, bf16[768,768]{1,0:T(8,128)(2,1)}, u32[]{:S(2)}, u32[]{:S(2)}) %collective-permute-start.53) | collective-permute-done | bytes 1179680 | tf_op jit(solution)/shard_map/ppermute | solution.py:399
  406.8 2.9 fusion.1
  409.7 3.0 add_convert_fusion
  422.1 4.3 collective-permute-done.48
  429.1 28.4 %collective-permute-done.47 = bf16[192,768]{1,0:T(8,128)(2,1)S(1)} collective-permute-done((bf16[192,768]{1,0:T(8,128)(2,1)S(1)}, bf16[192,768]{1,0:T(8,128)(2,1)S(1)}, u32[]{:S(2)}, u32[]{:S(2)}) %collective-permute-start.47) | collective-permute-done | bytes 294944 | tf_op jit(solution)/shard_map/ppermute | solution.py:399
  458.6 15.9 %reduce-scatter.13.cloned.1.call-done = bf16[1,2,192,768]{3,2,1,0:T(8,128)(2,1)} async-done(((bf16[4,2,192,768]{3,2,1,0:T(8,128)(2,1)}), bf16[1,2,192,768]{3,2,1,0:T(8,128)(2,1)}) %reduce-scatter.13.cloned.1.call-update) | async-done | bytes 589840 | tf_op jit(solution)/shard_map/reduce_scatter | solution.py:437
  474.6 4.5 all-to-all-start.1
  485.4 2.6 fusion
  487.9 13.3 %collective-permute-done.59 = f32[2,4,12,192]{3,1,2,0:T(4,128)S(1)} collective-permute-done((f32[2,4,12,192]{3,1,2,0:T(4,128)S(1)}, f32[2,4,12,192]{3,1,2,0:T(4,128)S(1)}, u32[]{:S(2)}, u32[]{:S(2)}) %collective-permute-start.59) | collective-permute-done | bytes 73760 | tf_op jit(solution)/shard_map/ppermute | solution.py:399
  501.2 4.6 collective-permute-done.57
  505.9 5.8 collective-permute-done.56
  514.5 4.3 collective-permute-done.61
  524.7 2.5 collective-permute-start.68
  533.4 15.5 %reduce-scatter.17.cloned.1.call-done = bf16[1,1,192,768]{3,2,1,0:T(8,128)(2,1)} async-done(((bf16[4,1,192,768]{3,2,1,0:T(8,128)(2,1)}), bf16[1,1,192,768]{3,2,1,0:T(8,128)(2,1)}) %reduce-scatter.17.cloned.1.call-update) | async-done | bytes 294928 | tf_op jit(solution)/shard_map/reduce_scatter | solution.py:437
  553.5 5.1 collective-permute-done.63
  565.1 7.8 %collective-permute-done.64 = bf16[192,768]{1,0:T(8,128)(2,1)S(1)} collective-permute-done((bf16[192,768]{1,0:T(8,128)(2,1)S(1)}, bf16[192,768]{1,0:T(8,128)(2,1)S(1)}, u32[]{:S(2)}, u32[]{:S(2)}) %collective-permute-start.64) | collective-permute-done | bytes 294944 | tf_op jit(solution)/shard_map/ppermute | solution.py:399
  578.2 38.8 %collective-permute-done.67 = bf16[384,768]{1,0:T(8,128)(2,1)S(1)} collective-permute-done((bf16[384,768]{1,0:T(8,128)(2,1)S(1)}, bf16[384,768]{1,0:T(8,128)(2,1)S(1)}, u32[]{:S(2)}, u32[]{:S(2)}) %collective-permute-start.67) | collective-permute-done | bytes 589856 | tf_op jit(solution)/shard_map/ppermute | solution.py:399
  618.6 11.0 %collective-permute-done.70 = bf16[384,768]{1,0:T(8,128)(2,1)S(1)} collective-permute-done((bf16[384,768]{1,0:T(8,128)(2,1)S(1)}, bf16[384,768]{1,0:T(8,128)(2,1)S(1)}, u32[]{:S(2)}, u32[]{:S(2)}) %collective-permute-start.70) | collective-permute-done | bytes 589856 | tf_op jit(solution)/shard_map/ppermute | solution.py:399
  631.3 8.8 %collective-permute-done.65 = bf16[384,768]{1,0:T(8,128)(2,1)S(1)} collective-permute-done((bf16[384,768]{1,0:T(8,128)(2,1)S(1)}, bf16[384,768]{1,0:T(8,128)(2,1)S(1)}, u32[]{:S(2)}, u32[]{:S(2)}) %collective-permute-start.65) | collective-permute-done | bytes 589856 | tf_op jit(solution)/shard_map/ppermute | solution.py:399
  (435 shorter events, 160.5 us)
Async XLA Ops:
  8.6 16.4 %collective-permute-start = (bf16[384,768]{1,0:T(8,128)(2,1)S(1)}, bf16[384,768]{1,0:T(8,128)(2,1)}, u32[]{:S(2)}, u32[]{:S(2)}) collective-permute-start(bf16[384,768]{1,0:T(8,128)(2,1)S(1)} %fusion.6), channel_id=1, source_target_pairs={{0,16},{16,0},{1,17},{17,1},{2,18},{18,2},{3,19},{19,3},{4,20},{20... | collective-permute-start | bytes 1769480 | tf_op jit(solution)/shard_map/ppermute | solution.py:399
  35.5 44.1 %collective-permute-start.7 = (bf16[384,768]{1,0:T(8,128)(2,1)S(1)}, bf16[384,768]{1,0:T(8,128)(2,1)}, u32[]{:S(2)}, u32[]{:S(2)}) collective-permute-start(bf16[384,768]{1,0:T(8,128)(2,1)S(1)} %get-tuple-element.330.refs_0_.refs_1_), channel_id=1, source_target_pairs={{0,8},{4,12},{8,0},{12,4},{1,9},{5,13},{9,1},{13,5},{2,10},{6,14},... | collective-permute-start | bytes 1769480 | tf_op jit(solution)/shard_map/ppermute | solution.py:399
  37.3 57.1 %collective-permute-start.5 = (bf16[384,768]{1,0:T(8,128)(2,1)S(1)}, bf16[384,768]{1,0:T(8,128)(2,1)}, u32[]{:S(2)}, u32[]{:S(2)}) collective-permute-start(bf16[384,768]{1,0:T(8,128)(2,1)S(1)} %get-tuple-element.330.refs_0_.refs_1_), channel_id=1, source_target_pairs={{0,4},{4,0},{8,12},{12,8},{1,5},{5,1},{9,13},{13,9},{2,6},{6,2},{1... | collective-permute-start | bytes 1769480 | tf_op jit(solution)/shard_map/ppermute | solution.py:399
  37.6 42.5 %collective-permute-start.4 = (bf16[384,768]{1,0:T(8,128)(2,1)}, bf16[384,768]{1,0:T(8,128)(2,1)}, u32[]{:S(2)}, u32[]{:S(2)}) collective-permute-start(bf16[384,768]{1,0:T(8,128)(2,1)} %collective-permute-done), channel_id=1, source_target_pairs={{0,1},{1,0},{2,3},{3,2},{4,5},{5,4},{6,7},{7,6},{8,9},{9,8},{10,11... | collective-permute-start | bytes 1769480 | tf_op jit(solution)/shard_map/ppermute | solution.py:399
  39.1 70.5 %all-to-all-start = ((bf16[8,192,448]{2,1,0:T(8,128)(2,1)}), bf16[8,192,448]{2,1,0:T(8,128)(2,1)}, u32[]{:S(2)}, u32[]{:S(2)}) async-start(bf16[8,192,448]{2,1,0:T(8,128)(2,1)} %bitcast.173), calls=%async_computation | async-start | bytes 3145728 | tf_op jit(solution)/shard_map/all_to_all | solution.py:493
  43.4 371.9 %reduce-scatter.9.cloned.1.call-start = ((), (), s32[]{:S(2)}) async-start(), calls=%async_computation.9 | async-start | bytes 2949120 | tf_op jit(solution)/shard_map/reduce_scatter | solution.py:437
  43.5 32.7 %collective-permute-start.11 = (bf16[384,768]{1,0:T(8,128)(2,1)S(1)}, bf16[384,768]{1,0:T(8,128)(2,1)}, u32[]{:S(2)}, u32[]{:S(2)}) collective-permute-start(bf16[384,768]{1,0:T(8,128)(2,1)S(1)} %dynamic-slice_bitcast_fusion.1), channel_id=1, source_target_pairs={{0,16},{16,0},{1,17},{17,1},{2,18},{18,2},{3,19},{19,3},{4,20},{20... | collective-permute-start | bytes 1769480 | tf_op jit(solution)/shard_map/ppermute | solution.py:399
  77.9 17.9 %collective-permute-start.12 = (bf16[384,768]{1,0:T(8,128)(2,1)S(1)}, bf16[384,768]{1,0:T(8,128)(2,1)}, u32[]{:S(2)}, u32[]{:S(2)}) collective-permute-start(bf16[384,768]{1,0:T(8,128)(2,1)S(1)} %get-tuple-element.328.refs_0_.refs_1_), channel_id=1, source_target_pairs={{0,8},{4,12},{8,0},{12,4},{1,9},{5,13},{9,1},{13,5},{2,10},{6,14},... | collective-permute-start | bytes 1769480 | tf_op jit(solution)/shard_map/ppermute | solution.py:399
  79.6 16.2 %collective-permute-start.8 = (bf16[384,768]{1,0:T(8,128)(2,1)}, bf16[384,768]{1,0:T(8,128)(2,1)}, u32[]{:S(2)}, u32[]{:S(2)}) collective-permute-start(bf16[384,768]{1,0:T(8,128)(2,1)} %collective-permute-done.7.refs_4_.refs_5_), channel_id=1, source_target_pairs={{0,1},{1,0},{2,3},{3,2},{4,5},{5,4},{6,7},{7,6},{8,9},{9,8},{10,11... | collective-permute-start | bytes 1769480 | tf_op jit(solution)/shard_map/ppermute | solution.py:399
  80.1 17.4 %collective-permute-start.9 = (bf16[384,768]{1,0:T(8,128)(2,1)}, bf16[384,768]{1,0:T(8,128)(2,1)S(1)}, u32[]{:S(2)}, u32[]{:S(2)}) collective-permute-start(bf16[384,768]{1,0:T(8,128)(2,1)} %collective-permute-done.7.refs_4_.refs_5_), channel_id=1, source_target_pairs={{0,4},{4,0},{8,12},{12,8},{1,5},{5,1},{9,13},{13,9},{2,6},{6,2},{1... | collective-permute-start | bytes 1769480 | tf_op jit(solution)/shard_map/ppermute | solution.py:399
  91.0 17.3 %collective-permute-start.16 = (bf16[384,768]{1,0:T(8,128)(2,1)S(1)}, bf16[384,768]{1,0:T(8,128)(2,1)S(1)}, u32[]{:S(2)}, u32[]{:S(2)}) collective-permute-start(bf16[384,768]{1,0:T(8,128)(2,1)S(1)} %collective-permute-done.14), channel_id=1, source_target_pairs={{0,1},{1,0},{2,3},{3,2},{4,5},{5,4},{6,7},{7,6},{8,9},{9,8},{10,11... | collective-permute-start | bytes 1769480 | tf_op jit(solution)/shard_map/ppermute | solution.py:399
  94.4 20.1 %collective-permute-start.6 = (bf16[384,768]{1,0:T(8,128)(2,1)}, bf16[384,768]{1,0:T(8,128)(2,1)}, u32[]{:S(2)}, u32[]{:S(2)}) collective-permute-start(bf16[384,768]{1,0:T(8,128)(2,1)} %get-tuple-element.320.refs_1_.refs_2_), channel_id=1, source_target_pairs={{0,4},{4,0},{8,12},{12,8},{1,5},{5,1},{9,13},{13,9},{2,6},{6,2},{1... | collective-permute-start | bytes 1769480 | tf_op jit(solution)/shard_map/ppermute | solution.py:399
  95.8 18.8 %collective-permute-start.10 = (bf16[384,768]{1,0:T(8,128)(2,1)}, bf16[384,768]{1,0:T(8,128)(2,1)}, u32[]{:S(2)}, u32[]{:S(2)}) collective-permute-start(bf16[384,768]{1,0:T(8,128)(2,1)} %collective-permute-done.8.refs_5_.refs_6_), channel_id=1, source_target_pairs={{0,4},{4,0},{8,12},{12,8},{1,5},{5,1},{9,13},{13,9},{2,6},{6,2},{1... | collective-permute-start | bytes 1769480 | tf_op jit(solution)/shard_map/ppermute | solution.py:399
  95.8 25.3 %collective-permute-start.13 = (bf16[384,768]{1,0:T(8,128)(2,1)}, bf16[384,768]{1,0:T(8,128)(2,1)}, u32[]{:S(2)}, u32[]{:S(2)}) collective-permute-start(bf16[384,768]{1,0:T(8,128)(2,1)} %collective-permute-done.12.refs_4_.refs_5_), channel_id=1, source_target_pairs={{0,1},{1,0},{2,3},{3,2},{4,5},{5,4},{6,7},{7,6},{8,9},{9,8},{10,11... | collective-permute-start | bytes 1769480 | tf_op jit(solution)/shard_map/ppermute | solution.py:399
  98.3 39.2 %collective-permute-start.17 = (bf16[384,768]{1,0:T(8,128)(2,1)}, bf16[384,768]{1,0:T(8,128)(2,1)}, u32[]{:S(2)}, u32[]{:S(2)}) collective-permute-start(bf16[384,768]{1,0:T(8,128)(2,1)} %collective-permute-done.11), channel_id=1, source_target_pairs={{0,1},{1,0},{2,3},{3,2},{4,5},{5,4},{6,7},{7,6},{8,9},{9,8},{10,11... | collective-permute-start | bytes 1769480 | tf_op jit(solution)/shard_map/ppermute | solution.py:399
  109.1 27.9 %collective-permute-start.15 = (bf16[384,768]{1,0:T(8,128)(2,1)S(1)}, bf16[384,768]{1,0:T(8,128)(2,1)}, u32[]{:S(2)}, u32[]{:S(2)}) collective-permute-start(bf16[384,768]{1,0:T(8,128)(2,1)S(1)} %get-tuple-element.326.refs_8_.refs_9_), channel_id=1, source_target_pairs={{0,8},{4,12},{8,0},{12,4},{1,9},{5,13},{9,1},{13,5},{2,10},{6,14},... | collective-permute-start | bytes 1769480 | tf_op jit(solution)/shard_map/ppermute | solution.py:399
  114.5 25.6 %collective-permute-start.18 = (bf16[384,768]{1,0:T(8,128)(2,1)S(1)}, bf16[384,768]{1,0:T(8,128)(2,1)S(1)}, u32[]{:S(2)}, u32[]{:S(2)}) collective-permute-start(bf16[384,768]{1,0:T(8,128)(2,1)S(1)} %get-tuple-element.328.refs_0_.refs_1_), channel_id=1, source_target_pairs={{0,4},{4,0},{8,12},{12,8},{1,5},{5,1},{9,13},{13,9},{2,6},{6,2},{1... | collective-permute-start | bytes 1769480 | tf_op jit(solution)/shard_map/ppermute | solution.py:399
  114.6 26.9 %collective-permute-start.22 = (bf16[384,768]{1,0:T(8,128)(2,1)S(1)}, bf16[384,768]{1,0:T(8,128)(2,1)S(1)}, u32[]{:S(2)}, u32[]{:S(2)}) collective-permute-start(bf16[384,768]{1,0:T(8,128)(2,1)S(1)} %get-tuple-element.326.refs_8_.refs_9_), channel_id=1, source_target_pairs={{0,4},{4,0},{8,12},{12,8},{1,5},{5,1},{9,13},{13,9},{2,6},{6,2},{1... | collective-permute-start | bytes 1769480 | tf_op jit(solution)/shard_map/ppermute | solution.py:399
  121.0 19.2 %collective-permute-start.20 = (bf16[384,768]{1,0:T(8,128)(2,1)}, bf16[384,768]{1,0:T(8,128)(2,1)S(1)}, u32[]{:S(2)}, u32[]{:S(2)}) collective-permute-start(bf16[384,768]{1,0:T(8,128)(2,1)} %collective-permute-done.12.refs_4_.refs_5_), channel_id=1, source_target_pairs={{0,4},{4,0},{8,12},{12,8},{1,5},{5,1},{9,13},{13,9},{2,6},{6,2},{1... | collective-permute-start | bytes 1769480 | tf_op jit(solution)/shard_map/ppermute | solution.py:399
  137.0 15.9 %collective-permute-start.27 = (bf16[384,768]{1,0:T(8,128)(2,1)S(1)}, bf16[384,768]{1,0:T(8,128)(2,1)}, u32[]{:S(2)}, u32[]{:S(2)}) collective-permute-start(bf16[384,768]{1,0:T(8,128)(2,1)S(1)} %get-tuple-element.142.refs_0_.refs_1_), channel_id=1, source_target_pairs={{0,8},{4,12},{8,0},{12,4},{1,9},{5,13},{9,1},{13,5},{2,10},{6,14},... | collective-permute-start | bytes 1769480 | tf_op jit(solution)/shard_map/ppermute | solution.py:399
  154.5 25.9 %collective-permute-start.30 = (bf16[384,768]{1,0:T(8,128)(2,1)}, bf16[384,768]{1,0:T(8,128)(2,1)}, u32[]{:S(2)}, u32[]{:S(2)}) collective-permute-start(bf16[384,768]{1,0:T(8,128)(2,1)} %collective-permute-done.27.refs_4_.refs_5_), channel_id=1, source_target_pairs={{0,1},{1,0},{2,3},{3,2},{4,5},{5,4},{6,7},{7,6},{8,9},{9,8},{10,11... | collective-permute-start | bytes 1769480 | tf_op jit(solution)/shard_map/ppermute | solution.py:399
  155.8 24.6 %collective-permute-start.28 = (bf16[384,768]{1,0:T(8,128)(2,1)S(1)}, bf16[384,768]{1,0:T(8,128)(2,1)}, u32[]{:S(2)}, u32[]{:S(2)}) collective-permute-start(bf16[384,768]{1,0:T(8,128)(2,1)S(1)} %get-tuple-element.151.refs_0_.refs_1_), channel_id=1, source_target_pairs={{0,8},{4,12},{8,0},{12,4},{1,9},{5,13},{9,1},{13,5},{2,10},{6,14},... | collective-permute-start | bytes 1769480 | tf_op jit(solution)/shard_map/ppermute | solution.py:399
  157.3 26.7 %collective-permute-start.29 = (bf16[384,768]{1,0:T(8,128)(2,1)}, bf16[384,768]{1,0:T(8,128)(2,1)}, u32[]{:S(2)}, u32[]{:S(2)}) collective-permute-start(bf16[384,768]{1,0:T(8,128)(2,1)} %get-tuple-element.155.refs_8_.refs_9_), channel_id=1, source_target_pairs={{0,8},{4,12},{8,0},{12,4},{1,9},{5,13},{9,1},{13,5},{2,10},{6,14},... | collective-permute-start | bytes 1769480 | tf_op jit(solution)/shard_map/ppermute | solution.py:399
  185.0 19.5 %collective-permute-start.35 = (bf16[384,768]{1,0:T(8,128)(2,1)}, bf16[384,768]{1,0:T(8,128)(2,1)}, u32[]{:S(2)}, u32[]{:S(2)}) collective-permute-start(bf16[384,768]{1,0:T(8,128)(2,1)} %collective-permute-done.28.refs_4_.refs_5_), channel_id=1, source_target_pairs={{0,1},{1,0},{2,3},{3,2},{4,5},{5,4},{6,7},{7,6},{8,9},{9,8},{10,11... | collective-permute-start | bytes 1769480 | tf_op jit(solution)/shard_map/ppermute | solution.py:399
  186.5 26.6 %collective-permute-start.36 = (bf16[384,768]{1,0:T(8,128)(2,1)}, bf16[384,768]{1,0:T(8,128)(2,1)}, u32[]{:S(2)}, u32[]{:S(2)}) collective-permute-start(bf16[384,768]{1,0:T(8,128)(2,1)} %collective-permute-done.29.refs_12_.refs_13_), channel_id=1, source_target_pairs={{0,1},{1,0},{2,3},{3,2},{4,5},{5,4},{6,7},{7,6},{8,9},{9,8},{10,11... | collective-permute-start | bytes 1769480 | tf_op jit(solution)/shard_map/ppermute | solution.py:399
  252.2 20.8 %collective-permute-start.46 = (bf16[2,768,768]{2,1,0:T(8,128)(2,1)}, bf16[2,768,768]{2,1,0:T(8,128)(2,1)S(1)}, u32[]{:S(2)}, u32[]{:S(2)}) collective-permute-start(bf16[2,768,768]{2,1,0:T(8,128)(2,1)} %get-tuple-element.166), channel_id=1, source_target_pairs={{0,4},{4,0},{8,12},{12,8},{1,5},{5,1},{9,13},{13,9},{2,6},{6,2},{1... | collective-permute-start | bytes 7077896 | tf_op jit(solution)/shard_map/ppermute | solution.py:399
  275.2 144.3 %reduce-scatter.7.cloned.1.call-start = ((), (), s32[]{:S(2)}) async-start(), calls=%async_computation.8 | async-start | bytes 2949120 | tf_op jit(solution)/shard_map/reduce_scatter | solution.py:437
  278.9 179.7 %reduce-scatter.11.cloned.1.call-start = ((), (), s32[]{:S(2)}) async-start(), calls=%async_computation.10 | async-start | bytes 2949120 | tf_op jit(solution)/shard_map/reduce_scatter | solution.py:437
  298.0 16.1 %collective-permute-start.49 = (bf16[2,768,768]{2,1,0:T(8,128)(2,1)}, bf16[2,768,768]{2,1,0:T(8,128)(2,1)S(1)}, u32[]{:S(2)}, u32[]{:S(2)}) collective-permute-start(bf16[2,768,768]{2,1,0:T(8,128)(2,1)} %get-tuple-element.177), channel_id=1, source_target_pairs={{0,4},{4,0},{8,12},{12,8},{1,5},{5,1},{9,13},{13,9},{2,6},{6,2},{1... | collective-permute-start | bytes 7077896 | tf_op jit(solution)/shard_map/ppermute | solution.py:399
  318.3 156.3 %reduce-scatter.13.cloned.1.call-start = ((), (), s32[]{:S(2)}) async-start(), calls=%async_computation.11 | async-start | bytes 2949120 | tf_op jit(solution)/shard_map/reduce_scatter | solution.py:437
  334.9 18.7 %collective-permute-start.51 = (bf16[2,768,768]{2,1,0:T(8,128)(2,1)}, bf16[2,768,768]{2,1,0:T(8,128)(2,1)S(1)}, u32[]{:S(2)}, u32[]{:S(2)}) collective-permute-start(bf16[2,768,768]{2,1,0:T(8,128)(2,1)} %get-tuple-element.188), channel_id=1, source_target_pairs={{0,4},{4,0},{8,12},{12,8},{1,5},{5,1},{9,13},{13,9},{2,6},{6,2},{1... | collective-permute-start | bytes 7077896 | tf_op jit(solution)/shard_map/ppermute | solution.py:399
  355.8 166.2 %reduce-scatter.15.cloned.1.call-start = ((), (), s32[]{:S(2)}) async-start(), calls=%async_computation.12 | async-start | bytes 1474560 | tf_op jit(solution)/shard_map/reduce_scatter | solution.py:437
  373.0 36.7 %collective-permute-start.52 = (bf16[2,768,768]{2,1,0:T(8,128)(2,1)}, bf16[2,768,768]{2,1,0:T(8,128)(2,1)}, u32[]{:S(2)}, u32[]{:S(2)}) collective-permute-start(bf16[2,768,768]{2,1,0:T(8,128)(2,1)} %get-tuple-element.198), channel_id=1, source_target_pairs={{0,4},{4,0},{8,12},{12,8},{1,5},{5,1},{9,13},{13,9},{2,6},{6,2},{1... | collective-permute-start | bytes 7077896 | tf_op jit(solution)/shard_map/ppermute | solution.py:399
  378.2 28.6 %collective-permute-start.53 = (bf16[768,768]{1,0:T(8,128)(2,1)}, bf16[768,768]{1,0:T(8,128)(2,1)}, u32[]{:S(2)}, u32[]{:S(2)}) collective-permute-start(bf16[768,768]{1,0:T(8,128)(2,1)} %slice_bitcast_fusion.1), channel_id=1, source_target_pairs={{0,8},{4,12},{8,0},{12,4},{1,9},{5,13},{9,1},{13,5},{2,10},{6,14},... | collective-permute-start | bytes 3538952 | tf_op jit(solution)/shard_map/ppermute | solution.py:399
  419.0 66.4 %collective-permute-start.58 = (bf16[768,768]{1,0:T(8,128)(2,1)}, bf16[768,768]{1,0:T(8,128)(2,1)}, u32[]{:S(2)}, u32[]{:S(2)}) collective-permute-start(bf16[768,768]{1,0:T(8,128)(2,1)} %slice_bitcast_fusion), channel_id=1, source_target_pairs={{0,8},{4,12},{8,0},{12,4},{1,9},{5,13},{9,1},{13,5},{2,10},{6,14},... | collective-permute-start | bytes 3538952 | tf_op jit(solution)/shard_map/ppermute | solution.py:399
  420.5 37.0 %collective-permute-start.47 = (bf16[192,768]{1,0:T(8,128)(2,1)S(1)}, bf16[192,768]{1,0:T(8,128)(2,1)S(1)}, u32[]{:S(2)}, u32[]{:S(2)}) collective-permute-start(bf16[192,768]{1,0:T(8,128)(2,1)S(1)} %slice_bitcast_fusion.11), channel_id=1, source_target_pairs={{0,8},{4,12},{8,0},{12,4},{1,9},{5,13},{9,1},{13,5},{2,10},{6,14},... | collective-permute-start | bytes 884744 | tf_op jit(solution)/shard_map/ppermute | solution.py:399
  427.5 31.0 %collective-permute-start.55 = (f32[2,4,12,192]{3,1,2,0:T(4,128)S(1)}, f32[2,4,12,192]{3,1,2,0:T(4,128)S(1)}, u32[]{:S(2)}, u32[]{:S(2)}) collective-permute-start(f32[2,4,12,192]{3,1,2,0:T(4,128)S(1)} %add.112), channel_id=1, source_target_pairs={{0,8},{4,12},{8,0},{12,4},{1,9},{5,13},{9,1},{13,5},{2,10},{6,14},... | collective-permute-start | bytes 221192 | tf_op jit(solution)/shard_map/ppermute | solution.py:399
  474.6 38.0 %all-to-all-start.1 = ((bf16[8,192,448]{2,1,0:T(8,128)(2,1)}), bf16[8,192,448]{2,1,0:T(8,128)(2,1)}, u32[]{:S(2)}, u32[]{:S(2)}) async-start(bf16[8,192,448]{2,1,0:T(8,128)(2,1)} %bitcast.174), calls=%async_computation.5 | async-start | bytes 3145728 | tf_op jit(solution)/shard_map/all_to_all | solution.py:656
  479.1 69.8 %reduce-scatter.17.cloned.1.call-start = ((), (), s32[]{:S(2)}) async-start(), calls=%async_computation.13 | async-start | bytes 1474560 | tf_op jit(solution)/shard_map/reduce_scatter | solution.py:437
  479.2 22.0 %collective-permute-start.59 = (f32[2,4,12,192]{3,1,2,0:T(4,128)S(1)}, f32[2,4,12,192]{3,1,2,0:T(4,128)S(1)}, u32[]{:S(2)}, u32[]{:S(2)}) collective-permute-start(f32[2,4,12,192]{3,1,2,0:T(4,128)S(1)} %add.113), channel_id=1, source_target_pairs={{0,16},{16,0},{1,17},{17,1},{2,18},{18,2},{3,19},{19,3},{4,20},{20... | collective-permute-start | bytes 221192 | tf_op jit(solution)/shard_map/ppermute | solution.py:399
  482.2 23.6 %collective-permute-start.57 = (bf16[192,768]{1,0:T(8,128)(2,1)S(1)}, bf16[192,768]{1,0:T(8,128)(2,1)S(1)}, u32[]{:S(2)}, u32[]{:S(2)}) collective-permute-start(bf16[192,768]{1,0:T(8,128)(2,1)S(1)} %slice_bitcast_fusion.13), channel_id=1, source_target_pairs={{0,8},{4,12},{8,0},{12,4},{1,9},{5,13},{9,1},{13,5},{2,10},{6,14},... | collective-permute-start | bytes 884744 | tf_op jit(solution)/shard_map/ppermute | solution.py:399
  484.7 27.0 %collective-permute-start.56 = (bf16[192,768]{1,0:T(8,128)(2,1)S(1)}, bf16[192,768]{1,0:T(8,128)(2,1)S(1)}, u32[]{:S(2)}, u32[]{:S(2)}) collective-permute-start(bf16[192,768]{1,0:T(8,128)(2,1)S(1)} %slice_bitcast_fusion.14), channel_id=1, source_target_pairs={{0,8},{4,12},{8,0},{12,4},{1,9},{5,13},{9,1},{13,5},{2,10},{6,14},... | collective-permute-start | bytes 884744 | tf_op jit(solution)/shard_map/ppermute | solution.py:399
  522.0 29.4 %collective-permute-start.62 = (f32[2,4,12,192]{3,1,2,0:T(4,128)S(1)}, f32[2,4,12,192]{3,1,2,0:T(4,128)}, u32[]{:S(2)}, u32[]{:S(2)}) collective-permute-start(f32[2,4,12,192]{3,1,2,0:T(4,128)S(1)} %add.119), channel_id=1, source_target_pairs={{0,2},{1,3},{2,0},{3,1},{4,6},{5,7},{6,4},{7,5},{8,10},{9,11},{10,... | collective-permute-start | bytes 221192 | tf_op jit(solution)/shard_map/ppermute | solution.py:399
  524.7 27.6 %collective-permute-start.68 = (bf16[192,768]{1,0:T(8,128)(2,1)}, bf16[192,768]{1,0:T(8,128)(2,1)}, u32[]{:S(2)}, u32[]{:S(2)}) collective-permute-start(bf16[192,768]{1,0:T(8,128)(2,1)} %broadcast_select_fusion.8), channel_id=1, source_target_pairs={{0,16},{16,0},{1,17},{17,1},{2,18},{18,2},{3,19},{19,3},{4,20},{20... | collective-permute-start | bytes 884744 | tf_op jit(solution)/shard_map/ppermute | solution.py:399
  527.2 33.2 %collective-permute-start.66 = (bf16[192,768]{1,0:T(8,128)(2,1)}, bf16[192,768]{1,0:T(8,128)(2,1)}, u32[]{:S(2)}, u32[]{:S(2)}) collective-permute-start(bf16[192,768]{1,0:T(8,128)(2,1)} %add_convert_fusion.8), channel_id=1, source_target_pairs={{0,1},{1,0},{2,3},{3,2},{4,5},{5,4},{6,7},{7,6},{8,9},{9,8},{10,11... | collective-permute-start | bytes 884744 | tf_op jit(solution)/shard_map/ppermute | solution.py:399
  561.8 55.1 %collective-permute-start.67 = (bf16[384,768]{1,0:T(8,128)(2,1)S(1)}, bf16[384,768]{1,0:T(8,128)(2,1)S(1)}, u32[]{:S(2)}, u32[]{:S(2)}) collective-permute-start(bf16[384,768]{1,0:T(8,128)(2,1)S(1)} %maximum_select_fusion.4), channel_id=1, source_target_pairs={{0,2},{1,3},{2,0},{3,1},{4,6},{5,7},{6,4},{7,5},{8,10},{9,11},{10,... | collective-permute-start | bytes 1769480 | tf_op jit(solution)/shard_map/ppermute | solution.py:399
  563.8 65.8 %collective-permute-start.70 = (bf16[384,768]{1,0:T(8,128)(2,1)S(1)}, bf16[384,768]{1,0:T(8,128)(2,1)S(1)}, u32[]{:S(2)}, u32[]{:S(2)}) collective-permute-start(bf16[384,768]{1,0:T(8,128)(2,1)S(1)} %maximum_select_fusion.5), channel_id=1, source_target_pairs={{0,2},{1,3},{2,0},{3,1},{4,6},{5,7},{6,4},{7,5},{8,10},{9,11},{10,... | collective-permute-start | bytes 1769480 | tf_op jit(solution)/shard_map/ppermute | solution.py:399
  573.1 67.0 %collective-permute-start.65 = (bf16[384,768]{1,0:T(8,128)(2,1)S(1)}, bf16[384,768]{1,0:T(8,128)(2,1)S(1)}, u32[]{:S(2)}, u32[]{:S(2)}) collective-permute-start(bf16[384,768]{1,0:T(8,128)(2,1)S(1)} %maximum_select_fusion.3), channel_id=1, source_target_pairs={{0,2},{1,3},{2,0},{3,1},{4,6},{5,7},{6,4},{7,5},{8,10},{9,11},{10,... | collective-permute-start | bytes 1769480 | tf_op jit(solution)/shard_map/ppermute | solution.py:399
  (117 other events, 929.1 us)
Sparse Core Ops, SparseCore 0:
  275.3 49.7 reduce-scatter.8
  327.4 47.5 reduce-scatter.6
  377.3 47.4 reduce-scatter.10
  427.0 47.5 reduce-scatter.12
  476.7 28.6 reduce-scatter.14
  512.7 36.1 reduce-scatter.16

commit v5 on v4

--- a/solution.py
+++ b/solution.py
@@ -60,15 +60,19 @@
 def piece_copies(info, pieces, held, sems):
     first = pl.multiple_of(info[4] * HALF, HALF)
     second = pl.multiple_of((1 - info[4]) * HALF, HALF)
-    return tuple(
-        tuple(
-            pltpu.make_async_copy(
-                pieces[2 * slot + part], held.at[slot, pl.ds(start, HALF)], sems.at[2 * slot + part]
+    copies, taken = [], 0
+    for slot in range(SHARDS):
+        targets = [held.at[slot]]
+        if pieces[taken].shape[0] == HALF:
+            targets = [held.at[slot, pl.ds(first, HALF)], held.at[slot, pl.ds(second, HALF)]]
+        copies.append(
+            tuple(
+                pltpu.make_async_copy(pieces[taken + k], target, sems.at[2 * slot + k])
+                for k, target in enumerate(targets)
             )
-            for part, start in enumerate((first, second))
-        )
-        for slot in range(SHARDS)
-    )
+        )
+        taken += len(targets)
+    return tuple(copies)
 
 
 def load_pieces(step, order, chunks):
@@ -89,10 +93,10 @@
 
 
 def attention_forward_kernel(
-    info, x_ref, col_ref, bqv_ref, *refs
+    count, info, x_ref, col_ref, bqv_ref, *refs
 ):
     step = pl.program_id(0)
-    pieces, (a1_ref, p_ref, soft_ref, o_ref, h_ref, held, sems) = refs[:8], refs[8:]
+    pieces, (a1_ref, p_ref, soft_ref, o_ref, h_ref, held, sems) = refs[:count], refs[count:]
     copies = piece_copies(info, pieces, held, sems)
     load_pieces(step, range(SHARDS), (copies,))
 
@@ -127,10 +131,10 @@
 
 
 def mlp_forward_kernel(
-    info, h_ref, col_ref, b1_ref, *refs
+    counts, info, h_ref, col_ref, b1_ref, *refs
 ):
     step = pl.program_id(0)
-    pieces_one, pieces_two, refs = refs[:8], refs[8:16], refs[16:]
+    pieces_one, pieces_two, refs = refs[:counts[0]], refs[counts[0]:sum(counts)], refs[sum(counts):]
     a2_ref, u_ref, slope_ref, y_ref, held_one, held_two, a2_rows, total, sems_one, sems_two = refs
     copies_one = piece_copies(info, pieces_one, held_one, sems_one)
     copies_two = piece_copies(info, pieces_two, held_two, sems_two)
@@ -160,12 +164,12 @@
 
 
 def mlp_backward_kernel(
-    last, info, gy_ref, h_ref, a2_ref, col_ref, u_ref, slope_ref, *refs
+    last, counts, info, gy_ref, h_ref, a2_ref, col_ref, u_ref, slope_ref, *refs
 ):
     step = pl.program_id(0)
     if last:
         before_ref, *refs = refs
-    pieces_one, pieces_two, refs = refs[:8], refs[8:16], refs[16:]
+    pieces_one, pieces_two, refs = refs[:counts[0]], refs[counts[0]:sum(counts)], refs[sum(counts):]
     if last:
         gh_ref, dcol_ref, *refs = refs
     else:
@@ -206,12 +210,12 @@
 
 
 def attention_backward_kernel(
-    last, info, gh_ref, x_ref, a1_ref, col_ref, p_ref, soft_ref, o_ref, *refs
+    last, count, info, gh_ref, x_ref, a1_ref, col_ref, p_ref, soft_ref, o_ref, *refs
 ):
     step = pl.program_id(0)
     if last:
         before_ref, *refs = refs
-    pieces, refs = refs[:8], refs[8:]
+    pieces, refs = refs[:count], refs[count:]
     if last:
         gx_ref, dcol_ref, *refs = refs
     else:
@@ -282,8 +286,8 @@
     return pl.BlockSpec((1,) + shape, lambda i, info: (info[first + i],) + (0,) * len(shape))
 
 
-PIECES = [pl.BlockSpec(memory_space=pltpu.HBM)] * 8
-COPY_SEMS = pltpu.SemaphoreType.DMA((8,))
+PIECE = [pl.BlockSpec(memory_space=pltpu.HBM)]
+COPY_SEMS = pltpu.SemaphoreType.DMA((2 * SHARDS,))
 HELD = pltpu.VMEM((SHARDS, D, D), BF16)
 
 
@@ -292,9 +296,6 @@
 
 
 def run(kernel, name, steps, info, operands, in_specs, outs, out_specs, scratch, flops):
-    moved = sum(a.size * a.dtype.itemsize for a in operands) + sum(
-        a.size * a.dtype.itemsize for a in outs
-    )
     return pl.pallas_call(
         kernel,
         name=name,
@@ -309,7 +310,7 @@
         compiler_params=pltpu.CompilerParams(
             vmem_limit_bytes=VMEM_LIMIT, dimension_semantics=("arbitrary",)
         ),
-        cost_estimate=pl.CostEstimate(flops=flops, bytes_accessed=moved, transcendentals=0),
+        cost_estimate=pl.CostEstimate(flops=flops // 16, bytes_accessed=2**20, transcendentals=0),
     )(info, *operands)
 
 
@@ -322,8 +323,8 @@
 
 def attention_forward(info, x, col, bqv, chunk):
     return run(
-        attention_forward_kernel, "attention_forward", SHARDS, info, (x, col, bqv, *chunk),
-        [whole(STREAM), whole(COLS), whole((SHARDS, FEATS, 2))] + PIECES,
+        functools.partial(attention_forward_kernel, len(chunk)), "attention_forward", SHARDS, info, (x, col, bqv, *chunk),
+        [whole(STREAM), whole(COLS), whole((SHARDS, FEATS, 2))] + PIECE * len(chunk),
         [
             of(STREAM), of((SHARDS, QKV, FRAMES)), of((SHARDS, HEADS_SHARD, FRAMES, FRAMES)),
             of((SHARDS, FEATS, FRAMES)), of(STREAM, F32),
@@ -339,8 +340,8 @@
 
 def mlp_forward(info, h, col, b1, chunk_one, chunk_two):
     return run(
-        mlp_forward_kernel, "mlp_forward", SHARDS, info, (h, col, b1, *chunk_one, *chunk_two),
-        [whole(STREAM), whole(COLS), whole((SHARDS, 1, FF_SHARD))] + PIECES * 2,
+        functools.partial(mlp_forward_kernel, (len(chunk_one), len(chunk_two))), "mlp_forward", SHARDS, info, (h, col, b1, *chunk_one, *chunk_two),
+        [whole(STREAM), whole(COLS), whole((SHARDS, 1, FF_SHARD))] + PIECE * len(chunk_one + chunk_two),
         [of(STREAM), of((SHARDS, FRAMES, FF_SHARD)), of((SHARDS, FRAMES, FF_SHARD)), of(STREAM, F32)],
         [whole(STREAM), by_step((FRAMES, FF_SHARD)), by_step((FRAMES, FF_SHARD)), whole(STREAM)],
         [HELD, HELD, pltpu.VMEM(ROWS, BF16), pltpu.VMEM(ROWS, F32), COPY_SEMS, COPY_SEMS],
@@ -353,14 +354,14 @@
     carried = (before,) if last else ()
     ends = [of(STREAM, F32), of((D, 8), F32)] if last else [of(ROWS, F32)]
     return run(
-        functools.partial(mlp_backward_kernel, last), "mlp_backward", 2, info,
+        functools.partial(mlp_backward_kernel, last, (len(chunk_one), len(chunk_two))), "mlp_backward", 2, info,
         (gy, h, a2, col, u, slope, *carried, *chunk_one, *chunk_two),
         [
             whole(STREAM), whole(STREAM), whole(STREAM), whole(COLS),
             by_slot((FRAMES, FF_SHARD), last), by_slot((FRAMES, FF_SHARD), last),
         ]
         + [whole(ROWS)] * len(carried)
-        + PIECES * 2,
+        + PIECE * len(chunk_one + chunk_two),
         ends + [of((2, D, D)), of((2, D, D)), of((2, 1, FF_SHARD), F32)],
         [whole(end.shape) for end in ends]
         + [by_step((D, D)), by_step((D, D)), whole((2, 1, FF_SHARD))],
@@ -374,7 +375,7 @@
     carried = (before,) if last else ()
     ends = [of(STREAM, F32), of((D, 8), F32)] if last else [of(ROWS, F32)]
     return run(
-        functools.partial(attention_backward_kernel, last), "attention_backward", 2, info,
+        functools.partial(attention_backward_kernel, last, len(chunk)), "attention_backward", 2, info,
         (gh, x, a1, col, p, soft, o, *carried, *chunk),
         [
             whole(STREAM), whole(STREAM), whole(STREAM), whole(COLS),
@@ -382,7 +383,7 @@
             by_slot((FEATS, FRAMES), last),
         ]
         + [whole(ROWS)] * len(carried)
-        + PIECES,
+        + PIECE * len(chunk),
         ends + [of((2, D, D)), of((2, FEATS, 8), F32)],
         [whole(end.shape) for end in ends] + [by_step((D, D)), whole((2, FEATS, 8))],
         [HELD, pltpu.VMEM(STREAM, BF16), pltpu.VMEM((QKV, FRAMES), BF16), pltpu.VMEM(ROWS, F32), COPY_SEMS],
@@ -448,17 +449,28 @@
     def fold(self):
         self.value = added(self.kept, self.arrived)
 
-    def gather(self):
-        bit = 1
-        while bit < lax.axis_size("dp"):
-            arrived = flip(self.value, "dp", bit)
-            upper = (lax.axis_index("dp") & bit) != 0
-            self.value = jnp.where(
-                upper,
-                jnp.concatenate([arrived, self.value], axis=0),
-                jnp.concatenate([self.value, arrived], axis=0),
-            )
-            bit *= 2
+    def split(self):
+        self.value = self.value.reshape(lax.axis_size("dp"), -1, D)
+
+    def send_half(self, bit):
+        mine = ((lax.axis_index("dp") & bit) != 0).astype(jnp.int32)
+        blocks = self.value.reshape(-1, 2, *self.value.shape[1:])
+        self.kept = lax.dynamic_index_in_dim(blocks, mine, 1, keepdims=False)
+        self.arrived = flip(
+            lax.dynamic_index_in_dim(blocks, 1 - mine, 1, keepdims=False), "dp", bit
+        )
+
+    def send_back(self, bit):
+        self.arrived = flip(self.value, "dp", bit)
+
+    def join(self, bit):
+        upper = (lax.axis_index("dp") & bit) != 0
+        value = jnp.where(
+            upper,
+            jnp.stack([self.arrived, self.value], axis=1),
+            jnp.stack([self.value, self.arrived], axis=1),
+        )
+        self.value = value.reshape(-1, *value.shape[2:])
 
 
 def tied(chains, *others):
@@ -482,13 +494,16 @@
         w_fc1[0],
         w_fc2[0],
     ]
-    nears = [rows_of(own, zhalf, 2) for own in owned]
-    fars = [rows_of(own, 1 - zhalf, 2) for own in owned]
     small = jnp.concatenate(
         [ln_gain[0], ln_shift[0], b_qv[0], b_out, b_fc2, b_fc1.reshape(SHARDS, FEATS)], axis=0
     )
     ends = ends_in[0].T.reshape(FEATS, clips, FRAMES).transpose(1, 0, 2)
-    beyond, small, ends, nears[1] = tie((flip(nears[0], "section", 1), small, ends, nears[1]))
+    beyond_a, small, owned[1], owned[2] = tie(
+        (flip(owned[0], "section", 1), small, owned[1], owned[2])
+    )
+    own_there_a = flip(owned[0], "tensor", 2)
+    beyond_one = flip(owned[1], "section", 1)
+    beyond_two = flip(owned[2], "section", 1)
 
     ends = lax.all_to_all(ends, ("section", "tensor"), split_axis=0, concat_axis=0, tiled=True)
     ends = ends.reshape(2, D, FRAMES)
@@ -508,29 +523,21 @@
     def layers(own, other):
         return jnp.where(section == 0, own, other), jnp.where(section == 0, other, own)
 
-    near_own, far_own = [], []
-    for index in range(3):
-        near_other = beyond
-        if index < 2:
-            following = nears[index + 1]
-            if index:
-                near_other, following = tie((beyond, following))
-            beyond = flip(following, "section", 1)
-        near_own.append(layers(nears[index], near_other))
-        far_own.append(layers(fars[index], flip(near_other, "dp", 1)))
-
-    def over_y(index, layer):
-        return flip(near_own[index][layer], "tensor", 2)
-
-    def chunk_of(index, layer, near_there, far_there):
-        here = [near_own[index][layer], far_own[index][layer]]
-        there = [near_there, far_there]
-        return (
-            here
-            + [flip(part, "tensor", 1) for part in here]
-            + there
-            + [flip(part, "tensor", 1) for part in there]
-        )
+    def over_y(block):
+        return flip(block, "tensor", 2)
+
+    def whole_chunk(own, there):
+        return (own, flip(own, "tensor", 1), there, flip(there, "tensor", 1))
+
+    def shared_chunk(own, near, far):
+        return (own, flip(own, "tensor", 1), near, far, flip(near, "tensor", 1), flip(far, "tensor", 1))
+
+    n_dp = lax.axis_size("dp")
+    a_own = layers(owned[0], beyond_a)
+    there_a, beyond_one = tie((over_y(beyond_a), beyond_one))
+    a_there = layers(own_there_a, there_a)
+    one_own = layers(owned[1], beyond_one)
+    one_there = over_y(one_own[0])
 
     def attend(layer, stream, chunk):
         return attention_forward(info, stream, cols[layer], bqvs[layer], chunk)
@@ -538,52 +545,37 @@
     def feed(layer, h, chunk_one, chunk_two):
         return mlp_forward(info, h, cols[layer], b1s[layer], chunk_one, chunk_two)
 
-    chunks = [[None] * 3, [None] * 3]
+    chunks = [[whole_chunk(a_own[0], a_there[0])], []]
     stream = ends[0]
-    there_a, there_one = over_y(0, 0), over_y(1, 0)
-    chunks[0][0] = chunk_of(0, 0, there_a, flip(there_a, "dp", 1))
-    away_one = flip(there_one, "dp", 1)
     a1, p, soft, o, h = attend(0, stream, chunks[0][0])
-
-    there_two = over_y(2, 0)
-    late = [near_own[index][1] for index in range(3)]
-    h, away_one, there_two, late, far_two = tie((h, away_one, there_two, late, far_own[2]))
-    far_own[2] = far_two
-    for index in range(3):
-        near_own[index] = (near_own[index][0], late[index])
-    chunks[0][1] = chunk_of(1, 0, there_one, away_one)
-    chunks[0][2] = chunk_of(2, 0, there_two, flip(there_two, "dp", 1))
-    there_a = over_y(0, 1)
-    there_a, late_one, late_two = tie((there_a, late[1], late[2]))
-    near_own[1], near_own[2] = (None, late_one), (None, late_two)
-    away_a = flip(there_a, "dp", 1)
-    there_one, there_two = over_y(1, 1), over_y(2, 1)
-    a2, u, slope, y = feed(0, h, chunks[0][1], chunks[0][2])
+    h, beyond_two, one_there, late_a, late_one = tie(
+        (h, beyond_two, one_there, (a_own[1], a_there[1]), one_own[1])
+    )
+    two_own = layers(owned[2], beyond_two)
+    two_there = over_y(two_own[0])
+    chunks[0].append(whole_chunk(one_own[0], one_there))
+    two_there, halves = tie(
+        (two_there, [rows_of(late_one, zhalf, 2), rows_of(two_own[1], zhalf, 2)])
+    )
+    nears = [over_y(half) for half in halves]
+    chunks[0].append(whole_chunk(two_own[0], two_there))
+    a2, u, slope, y = feed(0, h, *chunks[0][1:])
     stored = [(stream, a1, p, soft, o, h, a2, u, slope)]
-
-    stream, there_a, there_one, there_two, away_a, near_a, far_a = tie(
-        (y, there_a, there_one, there_two, away_a, near_own[0][1], far_own[0][1])
-    )
-    near_own[0], far_own[0] = (None, near_a), (None, far_a)
-    chunks[1][0] = chunk_of(0, 1, there_a, away_a)
-    away_one, away_two = flip(there_one, "dp", 1), flip(there_two, "dp", 1)
+    stream, nears, late_a, late_one, late_two = tie((y, nears, late_a, late_one, two_own[1]))
+    chunks[1].append(whole_chunk(*late_a))
+    fars = [flip(near, "dp", 1) for near in nears]
     a1, p, soft, o, h = attend(1, stream, chunks[1][0])
-    parts = [[near_own[k][1], far_own[k][1]] for k in (1, 2)]
-    h, there_one, there_two, away_one, away_two, parts = tie(
-        (h, there_one, there_two, away_one, away_two, parts)
-    )
-    for index in (1, 2):
-        near_own[index] = (None, parts[index - 1][0])
-        far_own[index] = (None, parts[index - 1][1])
-    chunks[1][1] = chunk_of(1, 1, there_one, away_one)
-    chunks[1][2] = chunk_of(2, 1, there_two, away_two)
-    a2, u, slope, y = feed(1, h, chunks[1][1], chunks[1][2])
+    h, nears, fars, late_one, late_two = tie((h, nears, fars, late_one, late_two))
+    chunks[1].append(shared_chunk(late_one, nears[0], fars[0]))
+    chunks[1].append(shared_chunk(late_two, nears[1], fars[1]))
+    a2, u, slope, y = feed(1, h, *chunks[1][1:])
     stored.append((stream, a1, p, soft, o, h, a2, u, slope))
     stream = y
 
     upstream = ends[1]
     chains = [[Chain() for _ in range(3)] for _ in range(2)]
     smalls = [None, None]
+    ends_of = [None, None]
     late_a, late_one, late_two = chains[1]
     last_a, last_one, last_two = chains[0]
     for layer in (1, 0):
@@ -600,13 +592,16 @@
         )
         chain_two.cores(keep_two)
         chain_one.cores(keep_one)
-        (gh,) = tied((chain_two, chain_one), gh)
-        if layer == 1:
-            late_two.scatter()
+        if layer == 0:
+            late_a.fold()
+            (gh,) = tied((late_a, last_two, last_one, late_one), gh)
+            late_a.scatter()
+            last_two.send_y()
+            last_one.send_y()
+        else:
+            (gh,) = tied((late_two, late_one), gh)
             late_one.scatter()
-        else:
-            last_two.send_y()
-            last_one.scatter()
+            late_two.send_y()
         after, send_a, dbqv_sent = attention_backward(
             info, gh, x, a1, cols[layer], p, soft, o, None, chunk_a
         )
@@ -615,9 +610,21 @@
             info, gh, x, a1, cols[layer], p, soft, o, after, chunk_a
         )
         chain_a.cores(keep_a)
-        (upstream,) = tied((chain_a,), upstream)
         if layer == 1:
-            late_a.scatter()
+            late_two.fold()
+            (upstream,) = tied((late_two, late_a), upstream)
+            late_two.scatter()
+            late_a.send_y()
+        else:
+            last_two.fold()
+            (upstream,) = tied((last_two, last_a, late_two), upstream)
+            last_two.scatter()
+            last_a.send_y()
+        ends_of[layer] = (db1_kept, db1_sent, dbqv_kept, dbqv_sent, dcol_one, dcol_two)
+
+    upstream, ends_of = tie((upstream, ends_of))
+    for layer in range(2):
+        db1_kept, db1_sent, dbqv_kept, dbqv_sent, dcol_one, dcol_two = ends_of[layer]
         db1 = by_bits([db1_kept[1], db1_sent[1], db1_kept[0], db1_sent[0]], shard)
         dbqv = by_bits([dbqv_kept[1], dbqv_sent[1], dbqv_kept[0], dbqv_sent[0]], shard)
         dcol = jnp.concatenate(
@@ -639,49 +646,70 @@
     result = result.reshape(2 * SHARDS, FEATS, FRAMES)
     small_sum = jnp.stack(smalls)
 
-    last_two.fold()
-    result, small_sum = tied((last_a, last_two), result, small_sum)
-    last_a.send_y()
-    last_two.scatter()
-    late_two.send_y()
+    small_sum += flip(small_sum, "tensor", 1)
+    small_y = flip(small_sum, "tensor", 2)
     late_one.send_y()
-    small_sum += flip(small_sum, "tensor", 1)
-    late_two.fold()
+
+    last_one.fold()
+    small_y, result, last_a.arrived = tied((last_one,), small_y, result, last_a.arrived)
+    last_one.scatter()
+    result = lax.all_to_all(result, ("section", "tensor"), split_axis=0, concat_axis=0, tiled=True)
+    small_sum += small_y
+    small_sum += flip(small_sum, "section", 1)
+    bits = [1 << k for k in range(n_dp.bit_length() - 1)]
+    for bit in bits:
+        small_sum += flip(small_sum, "dp", bit)
+
+    last_a.fold()
     late_one.fold()
-    small_sum += flip(small_sum, "tensor", 2)
-
-    result, small_sum = tied((late_two, late_one, late_a, last_one), result, small_sum)
-    last_one.send_y()
-    late_a.send_y()
-    result = lax.all_to_all(result, ("section", "tensor"), split_axis=0, concat_axis=0, tiled=True)
-    small_sum += flip(small_sum, "section", 1)
-    last_one.fold()
-    late_a.fold()
-    last_a.fold()
-    result, small_sum = tied((late_a, last_one, last_a), result, small_sum)
-    last_a.scatter()
-    pair_one = Chain()
-    pair_one.send_x(last_one, late_one)
-    pair_one.fold()
-    small_sum += flip(small_sum, "dp", 1)
-    result, small_sum = tied((pair_one, last_two), result, small_sum)
-    pair_two = Chain()
+    (small_sum,) = tied((last_a, late_one, last_two), small_sum)
+    last_a.split()
+    last_a.send_half(bits[0])
+    pair_two, pair_one, pair_a = Chain(), Chain(), Chain()
     pair_two.send_x(last_two, late_two)
-    pair_two.fold()
-    pair_one.gather()
-    pair_two.gather()
-    bit = 2
-    while bit < lax.axis_size("dp"):
-        small_sum += flip(small_sum, "dp", bit)
-        bit *= 2
-    result = result.transpose(1, 0, 2).reshape(FEATS, clips * FRAMES).T.astype(F32)
     small_sum = lax.dynamic_slice(
         small_sum, (section, shard, 0, 0), (1, 1, 12, FEATS)
     ).reshape(12, FEATS)
-    pair_a = Chain()
+
+    last_a.fold()
+    pair_two.fold()
+    (small_sum,) = tied((last_a, pair_two), small_sum)
+    pair_two.value = pair_two.value[None]
+    for bit in bits[1:]:
+        last_a.send_half(bit)
+        if bit != bits[-1]:
+            last_a.fold()
+    pair_two.send_back(bits[-1])
+
+    last_a.fold()
+    last_a.value = last_a.value[0]
+    pair_two.join(bits[-1])
+    for bit in bits[-2:0:-1]:
+        pair_two.send_back(bit)
+        pair_two.join(bit)
+    result, small_sum = tied((last_a, pair_two, last_one), result, small_sum)
+    pair_one.send_x(last_one, late_one)
     pair_a.send_x(last_a, late_a)
-    pair_a.fold()
-    pair_a.gather()
+    pair_two.send_back(bits[0])
+
+    for pair in (pair_one, pair_a):
+        pair.fold()
+        pair.value = pair.value[None]
+    pair_two.join(bits[0])
+    result, small_sum = tied((pair_one, pair_a, pair_two), result, small_sum)
+    for bit in bits[:0:-1]:
+        for pair in (pair_one, pair_a):
+            pair.send_back(bit)
+        for pair in (pair_one, pair_a):
+            pair.join(bit)
+    result, small_sum = tied((pair_one, pair_a), result, small_sum)
+    for pair in (pair_one, pair_a):
+        pair.send_back(bits[0])
+    result = result.transpose(1, 0, 2).reshape(FEATS, clips * FRAMES).T.astype(F32)
+    for pair in (pair_one, pair_a):
+        pair.join(bits[0])
+    for pair in (pair_two, pair_one, pair_a):
+        pair.value = pair.value.reshape(D, D)
 
     grad_a, grad_one, grad_two = [pair.value.astype(F32) for pair in (pair_a, pair_one, pair_two)]
     return (

time: 657 us -> 671 us (1.021)
  waiting for transfers between devices: 272 us -> 315 us
  local copies, waits for them, and re-layouts: 78.2 us -> 62.1 us
  starting transfers between devices: 61.3 us -> 50.5 us
    ppermute x71 -> x56, waiting for transfers between devices: 240 us -> 314 us  [flip(): return lax.ppermute(block, axis, [(i, i ^ bit) for i in range(size)])]
    reduce_scatter x6 -> x5, waiting for transfers between devices: 31.5 us -> 0.07 us  [scatter(): total = lax.psum_scatter(split, 'dp', scatter_dimension=0, tiled=False)]
    unnamed x175 -> x176, local copies, waits for them, and re-layouts: 33.5 us -> 20.5 us
    ppermute x71 -> x56, starting transfers between devices: 51.7 us -> 42.6 us  [flip(): return lax.ppermute(block, axis, [(i, i ^ bit) for i in range(size)])]
    convert_element_type x15 -> x14, other arithmetic: 26.8 us -> 25.9 us  [added(): return (left.astype(F32) + right.astype(F32)).astype(BF16)]
  transfers between devices with their start and end apart: 79 -> 63, of which waited for: 33 -> 35; matrix products, arithmetic and copies ran while one was open for 15% -> 13% of each run, Pallas kernels for 22% -> 17%
where the time goes in v5:
time: 671 us; the launch traced here: 665 us
  waiting for transfers between devices  315 us (47%)
  Pallas kernels  165 us (25%)
  local copies, waits for them, and re-layouts  62.1 us (9%)
  other arithmetic  58.1 us (9%)
  starting transfers between devices  50.5 us (8%)
  between operations  15.2 us (2%)
    ppermute x56, waiting for transfers between devices, flip(): return lax.ppermute(block, axis, [(i, i ^ bit) for i in range(size)])  314 us
    pallas_call x12, Pallas kernels, run(): pl.pallas_call(kernel, name=name, out_shape=outs, grid_spec=pltpu.Prefetc...  165 us
    ppermute x56, starting transfers between devices, flip(): return lax.ppermute(block, axis, [(i, i ^ bit) for i in range(size)])  42.6 us
    convert_element_type x14, other arithmetic, added(): return (left.astype(F32) + right.astype(F32)).astype(BF16)  25.9 us
    unnamed x176, local copies, waits for them, and re-layouts  20.5 us
  transfers between devices with their start and end apart: 63, of which 35 were waited for; matrix products, arithmetic and copies ran while one was open for 13% of the time, Pallas kernels for 17%

profile of v5, /device:TPU:0, one launch (start us, length us, event | category | flops | bytes accessed | tf_op | source)
XLA Modules:
  0.0 665.2 jit_solution(13496673847924023803)
XLA Ops:
  7.2 2.5 pad_maximum_fusion.1
  9.6 2.9 collective-permute-start
  16.2 3.7 all-to-all-start
  20.1 19.5 %collective-permute-done = bf16[768,768]{1,0:T(8,128)(2,1)} collective-permute-done((bf16[768,768]{1,0:T(8,128)(2,1)}, bf16[768,768]{1,0:T(8,128)(2,1)}, u32[]{:S(2)}, u32[]{:S(2)}) %collective-permute-start) | collective-permute-done | bytes 1179680 | tf_op jit(solution)/shard_map/ppermute | solution.py:400
  44.2 13.4 %collective-permute-done.1 = bf16[12,192]{0,1:T(8,128)(2,1)S(1)} collective-permute-done((bf16[12,192]{0,1:T(8,128)(2,1)S(1)}, bf16[12,192]{0,1:T(8,128)(2,1)S(1)}, u32[]{:S(2)}, u32[]{:S(2)}) %collective-permute-start.1) | collective-permute-done | bytes 4640 | tf_op jit(solution)/shard_map/ppermute | solution.py:400
  59.7 3.0 broadcast_select_fusion.4
  64.2 38.6 %collective-permute-done.2 = bf16[2,12,192]{1,2,0:T(8,128)(2,1)S(1)} collective-permute-done((bf16[2,12,192]{1,2,0:T(8,128)(2,1)S(1)}, bf16[2,12,192]{1,2,0:T(8,128)(2,1)S(1)}, u32[]{:S(2)}, u32[]{:S(2)}) %collective-permute-start.2) | collective-permute-done | bytes 9248 | tf_op jit(solution)/shard_map/ppermute | solution.py:400
  104.6 2.8 broadcast_select_fusion.3
  107.7 3.0 broadcast_select_fusion.2
  113.9 15.0 %attention_forward.2 = (bf16[768,448]{1,0:T(8,128)(2,1)S(1)}, bf16[4,576,448]{2,1,0:T(8,128)(2,1)}, bf16[4,3,448,448]{3,2,1,0:T(8,128)(2,1)}, bf16[4,192,448]{2,1,0:T(8,128)(2,1)S(1)}, f32[768,448]{1,0:T(8,128)}) custom-call(s32[9]{0:T(128)S(1)} %stack.183.info, bf16[768,448]{1,0:T(8,128)(2,1)S(1)} %bitcast.163, ...), custom_call_target="tpu_custom_call" | custom-call | flops 170655744 | bytes 1048576 | tf_op jit(solution)/shard_map/attention_forward/pallas_call | solution.py:299
  129.0 9.9 %collective-permute-done.10.refs_2_.refs_3_ = bf16[768,768]{1,0:T(8,128)(2,1)S(1)} collective-permute-done((bf16[768,768]{1,0:T(8,128)(2,1)S(1)}, bf16[768,768]{1,0:T(8,128)(2,1)S(1)}, u32[]{:S(2)}, u32[]{:S(2)}) %collective-permute-start.10) | collective-permute-done | bytes 1179680 | tf_op jit(solution)/shard_map/ppermute | solution.py:400
  138.9 3.6 broadcast_select_fusion
  147.5 22.7 %collective-permute-done.14.refs_6_.refs_7_ = bf16[768,768]{1,0:T(8,128)(2,1)} collective-permute-done((bf16[768,768]{1,0:T(8,128)(2,1)}, bf16[768,768]{1,0:T(8,128)(2,1)}, u32[]{:S(2)}, u32[]{:S(2)}) %collective-permute-start.14) | collective-permute-done | bytes 1179680 | tf_op jit(solution)/shard_map/ppermute | solution.py:400
  177.4 13.4 %mlp_forward.2 = (bf16[768,448]{1,0:T(8,128)(2,1)S(1)}, bf16[4,448,768]{2,1,0:T(8,128)(2,1)}, bf16[4,448,768]{2,1,0:T(8,128)(2,1)}, f32[768,448]{1,0:T(8,128)}) custom-call(s32[9]{0:T(128)S(1)} %stack.183.info, f32[768,448]{1,0:T(8,128)} %get-tuple-element.150.h_ref, f32[4,192,8]{2,1,0:T(8,128)S(1)} %get-tuple-element.306.col_ref, ...), custom_call_target="tpu_custom_call" | custom-call | flops 264241152 | bytes 1048576 | tf_op jit(solution)/shard_map/mlp_forward/pallas_call | solution.py:299
  191.7 7.2 %collective-permute-done.17.refs_8_.refs_9_ = bf16[384,768]{1,0:T(8,128)(2,1)} collective-permute-done((bf16[384,768]{1,0:T(8,128)(2,1)}, bf16[384,768]{1,0:T(8,128)(2,1)}, u32[]{:S(2)}, u32[]{:S(2)}) %collective-permute-start.17) | collective-permute-done | bytes 589856 | tf_op jit(solution)/shard_map/ppermute | solution.py:400
  204.4 15.6 %attention_forward.3 = (bf16[768,448]{1,0:T(8,128)(2,1)S(1)}, bf16[4,576,448]{2,1,0:T(8,128)(2,1)}, bf16[4,3,448,448]{3,2,1,0:T(8,128)(2,1)}, bf16[4,192,448]{2,1,0:T(8,128)(2,1)S(1)}, f32[768,448]{1,0:T(8,128)}) custom-call(s32[9]{0:T(128)S(1)} %stack.183.info, f32[768,448]{1,0:T(8,128)} %get-tuple-element.160.x_ref, ...), custom_call_target="tpu_custom_call" | custom-call | flops 170655744 | bytes 1048576 | tf_op jit(solution)/shard_map/attention_forward/pallas_call | solution.py:299
  221.9 5.7 collective-permute-done.21.refs_9_.refs_10_
  236.9 14.0 %mlp_forward.3 = (bf16[768,448]{1,0:T(8,128)(2,1)S(1)}, bf16[4,448,768]{2,1,0:T(8,128)(2,1)}, bf16[4,448,768]{2,1,0:T(8,128)(2,1)}, f32[768,448]{1,0:T(8,128)}) custom-call(s32[9]{0:T(128)S(1)} %stack.183.info, f32[768,448]{1,0:T(8,128)} %get-tuple-element.168.h_ref, f32[4,192,8]{2,1,0:T(8,128)S(1)} %get-tuple-element.305.col_ref, ...), custom_call_target="tpu_custom_call" | custom-call | flops 264241152 | bytes 1048576 | tf_op jit(solution)/shard_map/mlp_forward/pallas_call | solution.py:299
  251.8 11.6 %mlp_backward.4 = (f32[448,768]{1,0:T(8,128)}, bf16[2,768,768]{2,1,0:T(8,128)(2,1)}, bf16[2,768,768]{2,1,0:T(8,128)(2,1)}, f32[2,1,768]{2,1,0:T(1,128)S(1)}) custom-call(s32[9]{0:T(128)S(1)} %stack.183.info, bf16[768,448]{1,0:T(8,128)(2,1)S(1)} %bitcast.167, f32[768,448]{1,0:T(8,128)} %get-tuple-element.168.h_ref, bf16[768,448]{1,0:T(8,128)(2,1)} %copy-done.31, ...), custom_call_target="tpu_custom_call" | custom-call | flops 264241152 | bytes 1048576 | tf_op jit(solution)/shard_map/mlp_backward/pallas_call | solution.py:299
  263.9 14.2 %mlp_backward.5 = (f32[768,448]{1,0:T(8,128)}, f32[768,8]{1,0:T(8,128)S(1)}, bf16[2,768,768]{2,1,0:T(8,128)(2,1)}, bf16[2,768,768]{2,1,0:T(8,128)(2,1)}, f32[2,1,768]{2,1,0:T(1,128)S(1)}) custom-call(s32[9]{0:T(128)S(1)} %stack.183.info, bf16[768,448]{1,0:T(8,128)(2,1)} %bitcast.166, f32[768,448]{1,0:T(8,128)} %get-tuple-element.168.h_ref, ...), custom_call_target="tpu_custom_call" | custom-call | flops 264241152 | bytes 1048576 | tf_op jit(solution)/shard_map/mlp_backward/pallas_call | solution.py:299
  278.1 3.1 add_convert_fusion.5
  284.2 13.0 %attention_backward.4 = (f32[448,768]{1,0:T(8,128)}, bf16[2,768,768]{2,1,0:T(8,128)(2,1)}, f32[2,192,8]{2,1,0:T(8,128)S(1)}) custom-call(s32[9]{0:T(128)S(1)} %stack.183.info, f32[768,448]{1,0:T(8,128)} %get-tuple-element.185.gh_ref, f32[768,448]{1,0:T(8,128)} %get-tuple-element.160.x_ref, bf16[768,448]{1,0:T(8,128)(2,1)S(1)} %copy-done.20, ...), custom_call_target="tpu_custom_call" | custom-call | flops 170655744 | bytes 1048576 | tf_op jit(solution)/shard_map/attention_backward/pallas_call | solution.py:299
  305.7 14.6 %attention_backward.5 = (f32[768,448]{1,0:T(8,128)}, f32[768,8]{1,0:T(8,128)S(1)}, bf16[2,768,768]{2,1,0:T(8,128)(2,1)}, f32[2,192,8]{2,1,0:T(8,128)S(1)}) custom-call(s32[9]{0:T(128)S(1)} %stack.183.info, f32[768,448]{1,0:T(8,128)} %get-tuple-element.185.gh_ref, f32[768,448]{1,0:T(8,128)} %get-tuple-element.160.x_ref, bf16[768,448]{1,0:T(8,128)(2,1)S(1)} %copy-done.21, ...), custom_call_target="tpu_custom_call" | custom-call | flops 170655744 | bytes 1048576 | tf_op jit(solution)/shard_map/attention_backward/pallas_call | solution.py:299
  320.3 6.8 %collective-permute-done.30 = bf16[768,768]{1,0:T(8,128)(2,1)} collective-permute-done((bf16[768,768]{1,0:T(8,128)(2,1)}, bf16[768,768]{1,0:T(8,128)(2,1)}, u32[]{:S(2)}, u32[]{:S(2)}) %collective-permute-start.30) | collective-permute-done | bytes 1179680 | tf_op jit(solution)/shard_map/ppermute | solution.py:400
  327.1 2.6 fusion.4
  329.7 2.5 add_convert_fusion.3
  332.2 12.2 %mlp_backward.6 = (f32[448,768]{1,0:T(8,128)}, bf16[2,768,768]{2,1,0:T(8,128)(2,1)}, bf16[2,768,768]{2,1,0:T(8,128)(2,1)}, f32[2,1,768]{2,1,0:T(1,128)S(1)}) custom-call(s32[9]{0:T(128)S(1)} %stack.183.info, f32[768,448]{1,0:T(8,128)} %get-tuple-element.195.gy_ref, f32[768,448]{1,0:T(8,128)} %get-tuple-element.150.h_ref, bf16[768,448]{1,0:T(8,128)(2,1)S(1)} %copy-done.18, ...), custom_call_target="tpu_custom_call" | custom-call | flops 264241152 | bytes 1048576 | tf_op jit(solution)/shard_map/mlp_backward/pallas_call | solution.py:299
  345.8 14.0 %mlp_backward.7 = (f32[768,448]{1,0:T(8,128)}, f32[768,8]{1,0:T(8,128)S(1)}, bf16[2,768,768]{2,1,0:T(8,128)(2,1)}, bf16[2,768,768]{2,1,0:T(8,128)(2,1)}, f32[2,1,768]{2,1,0:T(1,128)S(1)}) custom-call(s32[9]{0:T(128)S(1)} %stack.183.info, f32[768,448]{1,0:T(8,128)} %get-tuple-element.195.gy_ref, f32[768,448]{1,0:T(8,128)} %get-tuple-element.150.h_ref, ...), custom_call_target="tpu_custom_call" | custom-call | flops 264241152 | bytes 1048576 | tf_op jit(solution)/shard_map/mlp_backward/pallas_call | solution.py:299
  359.7 13.4 %collective-permute-done.32 = bf16[768,768]{1,0:T(8,128)(2,1)S(1)} collective-permute-done((bf16[768,768]{1,0:T(8,128)(2,1)S(1)}, bf16[768,768]{1,0:T(8,128)(2,1)S(1)}, u32[]{:S(2)}, u32[]{:S(2)}) %collective-permute-start.32) | collective-permute-done | bytes 1179680 | tf_op jit(solution)/shard_map/ppermute | solution.py:400
  380.9 12.3 %attention_backward.6 = (f32[448,768]{1,0:T(8,128)}, bf16[2,768,768]{2,1,0:T(8,128)(2,1)}, f32[2,192,8]{2,1,0:T(8,128)S(1)}) custom-call(s32[9]{0:T(128)S(1)} %stack.183.info, f32[768,448]{1,0:T(8,128)} %get-tuple-element.207.gh_ref, bf16[768,448]{1,0:T(8,128)(2,1)S(1)} %bitcast.164, bf16[768,448]{1,0:T(8,128)(2,1)S(1)} %copy-done.26, ...), custom_call_target="tpu_custom_call" | custom-call | flops 170655744 | bytes 1048576 | tf_op jit(solution)/shard_map/attention_backward/pallas_call | solution.py:299
  398.8 15.0 %attention_backward.7 = (f32[768,448]{1,0:T(8,128)}, f32[768,8]{1,0:T(8,128)S(1)}, bf16[2,768,768]{2,1,0:T(8,128)(2,1)}, f32[2,192,8]{2,1,0:T(8,128)S(1)}) custom-call(s32[9]{0:T(128)S(1)} %stack.183.info, f32[768,448]{1,0:T(8,128)} %get-tuple-element.207.gh_ref, bf16[768,448]{1,0:T(8,128)(2,1)S(1)} %bitcast.165, bf16[768,448]{1,0:T(8,128)(2,1)S(1)} %copy-done.27, ...), custom_call_target="tpu_custom_call" | custom-call | flops 170655744 | bytes 1048576 | tf_op jit(solution)/shard_map/attention_backward/pallas_call | solution.py:299
  413.8 10.5 %collective-permute-done.37 = bf16[768,768]{1,0:T(8,128)(2,1)S(1)} collective-permute-done((bf16[768,768]{1,0:T(8,128)(2,1)S(1)}, bf16[768,768]{1,0:T(8,128)(2,1)S(1)}, u32[]{:S(2)}, u32[]{:S(2)}) %collective-permute-start.37) | collective-permute-done | bytes 1179680 | tf_op jit(solution)/shard_map/ppermute | solution.py:400
  425.7 23.5 %collective-permute-done.35 = bf16[768,768]{1,0:T(8,128)(2,1)S(1)} collective-permute-done((bf16[768,768]{1,0:T(8,128)(2,1)S(1)}, bf16[768,768]{1,0:T(8,128)(2,1)S(1)}, u32[]{:S(2)}, u32[]{:S(2)}) %collective-permute-start.35) | collective-permute-done | bytes 1179680 | tf_op jit(solution)/shard_map/ppermute | solution.py:400
  450.6 3.7 add_convert_fusion
  472.6 15.6 %collective-permute-done.39 = f32[2,4,12,192]{3,1,2,0:T(4,128)S(1)} collective-permute-done((f32[2,4,12,192]{3,1,2,0:T(4,128)S(1)}, f32[2,4,12,192]{3,1,2,0:T(4,128)S(1)}, u32[]{:S(2)}, u32[]{:S(2)}) %collective-permute-start.39) | collective-permute-done | bytes 73760 | tf_op jit(solution)/shard_map/ppermute | solution.py:400
  498.8 4.7 collective-permute-done.43
  505.8 9.8 %collective-permute-done.44 = f32[2,4,12,192]{3,1,2,0:T(4,128)S(1)} collective-permute-done((f32[2,4,12,192]{3,1,2,0:T(4,128)S(1)}, f32[2,4,12,192]{3,1,2,0:T(4,128)S(1)}, u32[]{:S(2)}, u32[]{:S(2)}) %collective-permute-start.44) | collective-permute-done | bytes 73760 | tf_op jit(solution)/shard_map/ppermute | solution.py:400
  518.3 3.9 all-to-all-start.1
  526.2 5.3 collective-permute-done.45
  532.7 2.5 collective-permute-start.48
  536.0 33.5 %collective-permute-done.48 = bf16[1,192,768]{2,1,0:T(8,128)(2,1)} collective-permute-done((bf16[1,192,768]{2,1,0:T(8,128)(2,1)}, bf16[1,192,768]{2,1,0:T(8,128)(2,1)}, u32[]{:S(2)}, u32[]{:S(2)}) %collective-permute-start.48) | collective-permute-done | bytes 294944 | tf_op jit(solution)/shard_map/ppermute | solution.py:400
  570.8 8.2 %collective-permute-done.47 = bf16[1,192,768]{2,1,0:T(8,128)(2,1)S(1)} collective-permute-done((bf16[1,192,768]{2,1,0:T(8,128)(2,1)S(1)}, bf16[1,192,768]{2,1,0:T(8,128)(2,1)S(1)}, u32[]{:S(2)}, u32[]{:S(2)}) %collective-permute-start.47) | collective-permute-done | bytes 294944 | tf_op jit(solution)/shard_map/ppermute | solution.py:400
  584.4 6.8 %collective-permute-done.50 = bf16[192,768]{1,0:T(8,128)(2,1)S(1)} collective-permute-done((bf16[192,768]{1,0:T(8,128)(2,1)S(1)}, bf16[192,768]{1,0:T(8,128)(2,1)S(1)}, u32[]{:S(2)}, u32[]{:S(2)}) %collective-permute-start.50) | collective-permute-done | bytes 294944 | tf_op jit(solution)/shard_map/ppermute | solution.py:400
  591.3 5.1 collective-permute-done.49
  602.2 16.9 %collective-permute-done.52 = bf16[1,192,768]{2,1,0:T(8,128)(2,1)S(1)} collective-permute-done((bf16[1,192,768]{2,1,0:T(8,128)(2,1)S(1)}, bf16[1,192,768]{2,1,0:T(8,128)(2,1)S(1)}, u32[]{:S(2)}, u32[]{:S(2)}) %collective-permute-start.52) | collective-permute-done | bytes 294944 | tf_op jit(solution)/shard_map/ppermute | solution.py:400
  620.1 5.3 collective-permute-done.53
  634.7 8.7 %collective-permute-done.54 = bf16[2,192,768]{2,1,0:T(8,128)(2,1)} collective-permute-done((bf16[2,192,768]{2,1,0:T(8,128)(2,1)}, bf16[2,192,768]{2,1,0:T(8,128)(2,1)}, u32[]{:S(2)}, u32[]{:S(2)}) %collective-permute-start.54) | collective-permute-done | bytes 589856 | tf_op jit(solution)/shard_map/ppermute | solution.py:400
  647.6 7.5 %collective-permute-done.55 = bf16[2,192,768]{2,1,0:T(8,128)(2,1)} collective-permute-done((bf16[2,192,768]{2,1,0:T(8,128)(2,1)}, bf16[2,192,768]{2,1,0:T(8,128)(2,1)}, u32[]{:S(2)}, u32[]{:S(2)}) %collective-permute-start.55) | collective-permute-done | bytes 589856 | tf_op jit(solution)/shard_map/ppermute | solution.py:400
  (408 shorter events, 147.0 us)
Async XLA Ops:
  9.6 30.0 %collective-permute-start = (bf16[768,768]{1,0:T(8,128)(2,1)}, bf16[768,768]{1,0:T(8,128)(2,1)}, u32[]{:S(2)}, u32[]{:S(2)}) collective-permute-start(bf16[768,768]{1,0:T(8,128)(2,1)} %pad_maximum_fusion.1), channel_id=1, source_target_pairs={{0,16},{16,0},{1,17},{17,1},{2,18},{18,2},{3,19},{19,3},{4,20},{20... | collective-permute-start | bytes 3538952 | tf_op jit(solution)/shard_map/ppermute | solution.py:400
  16.2 86.7 %all-to-all-start = ((bf16[8,192,448]{2,1,0:T(8,128)(2,1)}), bf16[8,192,448]{2,1,0:T(8,128)(2,1)S(1)}, u32[]{:S(2)}, u32[]{:S(2)}) async-start(bf16[8,192,448]{2,1,0:T(8,128)(2,1)} %bitcast.161), calls=%async_computation | async-start | bytes 3145728 | tf_op jit(solution)/shard_map/all_to_all | solution.py:508
  19.9 358.8 %reduce-scatter.6.cloned.1.call-start = ((), (), s32[]{:S(2)}) async-start(), calls=%async_computation.7 | async-start | bytes 2949120 | tf_op jit(solution)/shard_map/reduce_scatter | solution.py:438
  39.8 17.7 %collective-permute-start.1 = (bf16[12,192]{0,1:T(8,128)(2,1)S(1)}, bf16[12,192]{0,1:T(8,128)(2,1)S(1)}, u32[]{:S(2)}, u32[]{:S(2)}) collective-permute-start(bf16[12,192]{0,1:T(8,128)(2,1)S(1)} %copy.274), channel_id=1, source_target_pairs={{0,16},{16,0},{1,17},{17,1},{2,18},{18,2},{3,19},{19,3},{4,20},{20... | collective-permute-start | bytes 13832 | tf_op jit(solution)/shard_map/ppermute | solution.py:400
  41.9 62.7 %collective-permute-start.5 = (bf16[768,768]{1,0:T(8,128)(2,1)}, bf16[768,768]{1,0:T(8,128)(2,1)}, u32[]{:S(2)}, u32[]{:S(2)}) collective-permute-start(bf16[768,768]{1,0:T(8,128)(2,1)} %pad_maximum_fusion.1), channel_id=1, source_target_pairs={{0,8},{4,12},{8,0},{12,4},{1,9},{5,13},{9,1},{13,5},{2,10},{6,14},... | collective-permute-start | bytes 3538952 | tf_op jit(solution)/shard_map/ppermute | solution.py:400
  43.5 61.1 %collective-permute-start.6 = (bf16[768,768]{1,0:T(8,128)(2,1)}, bf16[768,768]{1,0:T(8,128)(2,1)}, u32[]{:S(2)}, u32[]{:S(2)}) collective-permute-start(bf16[768,768]{1,0:T(8,128)(2,1)} %collective-permute-done), channel_id=1, source_target_pairs={{0,8},{4,12},{8,0},{12,4},{1,9},{5,13},{9,1},{13,5},{2,10},{6,14},... | collective-permute-start | bytes 3538952 | tf_op jit(solution)/shard_map/ppermute | solution.py:400
  44.0 60.6 %collective-permute-start.7 = (bf16[768,768]{1,0:T(8,128)(2,1)}, bf16[768,768]{1,0:T(8,128)(2,1)}, u32[]{:S(2)}, u32[]{:S(2)}) collective-permute-start(bf16[768,768]{1,0:T(8,128)(2,1)} %bitcast.17), channel_id=1, source_target_pairs={{0,16},{16,0},{1,17},{17,1},{2,18},{18,2},{3,19},{19,3},{4,20},{20... | collective-permute-start | bytes 3538952 | tf_op jit(solution)/shard_map/ppermute | solution.py:400
  57.6 45.2 %collective-permute-start.2 = (bf16[2,12,192]{1,2,0:T(8,128)(2,1)S(1)}, bf16[2,12,192]{1,2,0:T(8,128)(2,1)S(1)}, u32[]{:S(2)}, u32[]{:S(2)}) collective-permute-start(bf16[2,12,192]{1,2,0:T(8,128)(2,1)S(1)} %get-tuple-element.322), channel_id=1, source_target_pairs={{0,8},{4,12},{8,0},{12,4},{1,9},{5,13},{9,1},{13,5},{2,10},{6,14},... | collective-permute-start | bytes 27656 | tf_op jit(solution)/shard_map/ppermute | solution.py:400
  62.7 66.2 %collective-permute-start.9 = (bf16[768,768]{1,0:T(8,128)(2,1)}, bf16[768,768]{1,0:T(8,128)(2,1)}, u32[]{:S(2)}, u32[]{:S(2)}) collective-permute-start(bf16[768,768]{1,0:T(8,128)(2,1)} %bitcast.18), channel_id=1, source_target_pairs={{0,16},{16,0},{1,17},{17,1},{2,18},{18,2},{3,19},{19,3},{4,20},{20... | collective-permute-start | bytes 3538952 | tf_op jit(solution)/shard_map/ppermute | solution.py:400
  104.3 8.4 %collective-permute-start.4 = (bf16[768,768]{1,0:T(8,128)(2,1)}, bf16[768,768]{1,0:T(8,128)(2,1)S(1)}, u32[]{:S(2)}, u32[]{:S(2)}) collective-permute-start(bf16[768,768]{1,0:T(8,128)(2,1)} %get-tuple-element.298.refs_0_.refs_1_), channel_id=1, source_target_pairs={{0,4},{4,0},{8,12},{12,8},{1,5},{5,1},{9,13},{13,9},{2,6},{6,2},{1... | collective-permute-start | bytes 3538952 | tf_op jit(solution)/shard_map/ppermute | solution.py:400
  110.7 28.1 %collective-permute-start.10 = (bf16[768,768]{1,0:T(8,128)(2,1)S(1)}, bf16[768,768]{1,0:T(8,128)(2,1)S(1)}, u32[]{:S(2)}, u32[]{:S(2)}) collective-permute-start(bf16[768,768]{1,0:T(8,128)(2,1)S(1)} %get-tuple-element.294.refs_0_.refs_1_), channel_id=1, source_target_pairs={{0,8},{4,12},{8,0},{12,4},{1,9},{5,13},{9,1},{13,5},{2,10},{6,14},... | collective-permute-start | bytes 3538952 | tf_op jit(solution)/shard_map/ppermute | solution.py:400
  142.5 27.7 %collective-permute-start.14 = (bf16[768,768]{1,0:T(8,128)(2,1)}, bf16[768,768]{1,0:T(8,128)(2,1)}, u32[]{:S(2)}, u32[]{:S(2)}) collective-permute-start(bf16[768,768]{1,0:T(8,128)(2,1)} %get-tuple-element.292.refs_4_.refs_5_), channel_id=1, source_target_pairs={{0,8},{4,12},{8,0},{12,4},{1,9},{5,13},{9,1},{13,5},{2,10},{6,14},... | collective-permute-start | bytes 3538952 | tf_op jit(solution)/shard_map/ppermute | solution.py:400
  143.2 27.7 %collective-permute-start.11 = (bf16[768,768]{1,0:T(8,128)(2,1)S(1)}, bf16[768,768]{1,0:T(8,128)(2,1)}, u32[]{:S(2)}, u32[]{:S(2)}) collective-permute-start(bf16[768,768]{1,0:T(8,128)(2,1)S(1)} %get-tuple-element.294.refs_0_.refs_1_), channel_id=1, source_target_pairs={{0,4},{4,0},{8,12},{12,8},{1,5},{5,1},{9,13},{13,9},{2,6},{6,2},{1... | collective-permute-start | bytes 3538952 | tf_op jit(solution)/shard_map/ppermute | solution.py:400
  143.2 32.9 %collective-permute-start.13 = (bf16[768,768]{1,0:T(8,128)(2,1)}, bf16[768,768]{1,0:T(8,128)(2,1)}, u32[]{:S(2)}, u32[]{:S(2)}) collective-permute-start(bf16[768,768]{1,0:T(8,128)(2,1)} %get-tuple-element.292.refs_4_.refs_5_), channel_id=1, source_target_pairs={{0,4},{4,0},{8,12},{12,8},{1,5},{5,1},{9,13},{13,9},{2,6},{6,2},{1... | collective-permute-start | bytes 3538952 | tf_op jit(solution)/shard_map/ppermute | solution.py:400
  143.7 32.4 %collective-permute-start.12 = (bf16[768,768]{1,0:T(8,128)(2,1)}, bf16[768,768]{1,0:T(8,128)(2,1)}, u32[]{:S(2)}, u32[]{:S(2)}) collective-permute-start(bf16[768,768]{1,0:T(8,128)(2,1)} %copy-done.5), channel_id=1, source_target_pairs={{0,4},{4,0},{8,12},{12,8},{1,5},{5,1},{9,13},{13,9},{2,6},{6,2},{1... | collective-permute-start | bytes 3538952 | tf_op jit(solution)/shard_map/ppermute | solution.py:400
  170.2 21.5 %collective-permute-start.16 = (bf16[384,768]{1,0:T(8,128)(2,1)}, bf16[384,768]{1,0:T(8,128)(2,1)}, u32[]{:S(2)}, u32[]{:S(2)}) collective-permute-start(bf16[384,768]{1,0:T(8,128)(2,1)} %constant_dynamic-slice_fusion.2), channel_id=1, source_target_pairs={{0,8},{4,12},{8,0},{12,4},{1,9},{5,13},{9,1},{13,5},{2,10},{6,14},... | collective-permute-start | bytes 1769480 | tf_op jit(solution)/shard_map/ppermute | solution.py:400
  170.8 28.1 %collective-permute-start.17 = (bf16[384,768]{1,0:T(8,128)(2,1)}, bf16[384,768]{1,0:T(8,128)(2,1)}, u32[]{:S(2)}, u32[]{:S(2)}) collective-permute-start(bf16[384,768]{1,0:T(8,128)(2,1)} %constant_dynamic-slice_fusion.1), channel_id=1, source_target_pairs={{0,8},{4,12},{8,0},{12,4},{1,9},{5,13},{9,1},{13,5},{2,10},{6,14},... | collective-permute-start | bytes 1769480 | tf_op jit(solution)/shard_map/ppermute | solution.py:400
  199.4 22.5 %collective-permute-start.20 = (bf16[384,768]{1,0:T(8,128)(2,1)}, bf16[384,768]{1,0:T(8,128)(2,1)}, u32[]{:S(2)}, u32[]{:S(2)}) collective-permute-start(bf16[384,768]{1,0:T(8,128)(2,1)} %collective-permute-done.16.refs_2_.refs_3_), channel_id=1, source_target_pairs={{0,1},{1,0},{2,3},{3,2},{4,5},{5,4},{6,7},{7,6},{8,9},{9,8},{10,11... | collective-permute-start | bytes 1769480 | tf_op jit(solution)/shard_map/ppermute | solution.py:400
  201.0 26.6 %collective-permute-start.21 = (bf16[384,768]{1,0:T(8,128)(2,1)}, bf16[384,768]{1,0:T(8,128)(2,1)}, u32[]{:S(2)}, u32[]{:S(2)}) collective-permute-start(bf16[384,768]{1,0:T(8,128)(2,1)} %collective-permute-done.17.refs_8_.refs_9_), channel_id=1, source_target_pairs={{0,1},{1,0},{2,3},{3,2},{4,5},{5,4},{6,7},{7,6},{8,9},{9,8},{10,11... | collective-permute-start | bytes 1769480 | tf_op jit(solution)/shard_map/ppermute | solution.py:400
  263.4 14.8 %collective-permute-start.28 = (bf16[2,768,768]{2,1,0:T(8,128)(2,1)}, bf16[2,768,768]{2,1,0:T(8,128)(2,1)}, u32[]{:S(2)}, u32[]{:S(2)}) collective-permute-start(bf16[2,768,768]{2,1,0:T(8,128)(2,1)} %get-tuple-element.180), channel_id=1, source_target_pairs={{0,4},{4,0},{8,12},{12,8},{1,5},{5,1},{9,13},{13,9},{2,6},{6,2},{1... | collective-permute-start | bytes 7077896 | tf_op jit(solution)/shard_map/ppermute | solution.py:400
  263.6 17.7 %collective-permute-start.29 = (bf16[2,768,768]{2,1,0:T(8,128)(2,1)}, bf16[2,768,768]{2,1,0:T(8,128)(2,1)S(1)}, u32[]{:S(2)}, u32[]{:S(2)}) collective-permute-start(bf16[2,768,768]{2,1,0:T(8,128)(2,1)} %get-tuple-element.182), channel_id=1, source_target_pairs={{0,4},{4,0},{8,12},{12,8},{1,5},{5,1},{9,13},{13,9},{2,6},{6,2},{1... | collective-permute-start | bytes 7077896 | tf_op jit(solution)/shard_map/ppermute | solution.py:400
  297.2 32.5 %collective-permute-start.31 = (bf16[2,768,768]{2,1,0:T(8,128)(2,1)}, bf16[2,768,768]{2,1,0:T(8,128)(2,1)}, u32[]{:S(2)}, u32[]{:S(2)}) collective-permute-start(bf16[2,768,768]{2,1,0:T(8,128)(2,1)} %get-tuple-element.192), channel_id=1, source_target_pairs={{0,4},{4,0},{8,12},{12,8},{1,5},{5,1},{9,13},{13,9},{2,6},{6,2},{1... | collective-permute-start | bytes 7077896 | tf_op jit(solution)/shard_map/ppermute | solution.py:400
  298.5 28.6 %collective-permute-start.30 = (bf16[768,768]{1,0:T(8,128)(2,1)}, bf16[768,768]{1,0:T(8,128)(2,1)}, u32[]{:S(2)}, u32[]{:S(2)}) collective-permute-start(bf16[768,768]{1,0:T(8,128)(2,1)} %slice_bitcast_fusion.4), channel_id=1, source_target_pairs={{0,8},{4,12},{8,0},{12,4},{1,9},{5,13},{9,1},{13,5},{2,10},{6,14},... | collective-permute-start | bytes 3538952 | tf_op jit(solution)/shard_map/ppermute | solution.py:400
  300.8 153.5 %reduce-scatter.8.cloned.1.call-start = ((), (), s32[]{:S(2)}) async-start(), calls=%async_computation.8 | async-start | bytes 1474560 | tf_op jit(solution)/shard_map/reduce_scatter | solution.py:438
  344.4 30.0 %collective-permute-start.33 = (bf16[2,768,768]{2,1,0:T(8,128)(2,1)}, bf16[2,768,768]{2,1,0:T(8,128)(2,1)S(1)}, u32[]{:S(2)}, u32[]{:S(2)}) collective-permute-start(bf16[2,768,768]{2,1,0:T(8,128)(2,1)} %get-tuple-element.201), channel_id=1, source_target_pairs={{0,4},{4,0},{8,12},{12,8},{1,5},{5,1},{9,13},{13,9},{2,6},{6,2},{1... | collective-permute-start | bytes 7077896 | tf_op jit(solution)/shard_map/ppermute | solution.py:400
  344.5 32.0 %collective-permute-start.34 = (bf16[2,768,768]{2,1,0:T(8,128)(2,1)}, bf16[2,768,768]{2,1,0:T(8,128)(2,1)S(1)}, u32[]{:S(2)}, u32[]{:S(2)}) collective-permute-start(bf16[2,768,768]{2,1,0:T(8,128)(2,1)} %get-tuple-element.203), channel_id=1, source_target_pairs={{0,4},{4,0},{8,12},{12,8},{1,5},{5,1},{9,13},{13,9},{2,6},{6,2},{1... | collective-permute-start | bytes 7077896 | tf_op jit(solution)/shard_map/ppermute | solution.py:400
  345.1 28.0 %collective-permute-start.32 = (bf16[768,768]{1,0:T(8,128)(2,1)S(1)}, bf16[768,768]{1,0:T(8,128)(2,1)S(1)}, u32[]{:S(2)}, u32[]{:S(2)}) collective-permute-start(bf16[768,768]{1,0:T(8,128)(2,1)S(1)} %slice_bitcast_fusion.3), channel_id=1, source_target_pairs={{0,8},{4,12},{8,0},{12,4},{1,9},{5,13},{9,1},{13,5},{2,10},{6,14},... | collective-permute-start | bytes 3538952 | tf_op jit(solution)/shard_map/ppermute | solution.py:400
  393.9 56.6 %collective-permute-start.36 = (bf16[2,768,768]{2,1,0:T(8,128)(2,1)}, bf16[2,768,768]{2,1,0:T(8,128)(2,1)}, u32[]{:S(2)}, u32[]{:S(2)}) collective-permute-start(bf16[2,768,768]{2,1,0:T(8,128)(2,1)} %get-tuple-element.214), channel_id=1, source_target_pairs={{0,4},{4,0},{8,12},{12,8},{1,5},{5,1},{9,13},{13,9},{2,6},{6,2},{1... | collective-permute-start | bytes 7077896 | tf_op jit(solution)/shard_map/ppermute | solution.py:400
  394.0 121.8 %reduce-scatter.10.cloned.1.call-start = ((), (), s32[]{:S(2)}) async-start(), calls=%async_computation.9 | async-start | bytes 1474560 | tf_op jit(solution)/shard_map/reduce_scatter | solution.py:438
  395.5 28.8 %collective-permute-start.37 = (bf16[768,768]{1,0:T(8,128)(2,1)S(1)}, bf16[768,768]{1,0:T(8,128)(2,1)S(1)}, u32[]{:S(2)}, u32[]{:S(2)}) collective-permute-start(bf16[768,768]{1,0:T(8,128)(2,1)S(1)} %slice_bitcast_fusion.1), channel_id=1, source_target_pairs={{0,8},{4,12},{8,0},{12,4},{1,9},{5,13},{9,1},{13,5},{2,10},{6,14},... | collective-permute-start | bytes 3538952 | tf_op jit(solution)/shard_map/ppermute | solution.py:400
  396.3 53.0 %collective-permute-start.35 = (bf16[768,768]{1,0:T(8,128)(2,1)S(1)}, bf16[768,768]{1,0:T(8,128)(2,1)S(1)}, u32[]{:S(2)}, u32[]{:S(2)}) collective-permute-start(bf16[768,768]{1,0:T(8,128)(2,1)S(1)} %slice_bitcast_fusion.2), channel_id=1, source_target_pairs={{0,8},{4,12},{8,0},{12,4},{1,9},{5,13},{9,1},{13,5},{2,10},{6,14},... | collective-permute-start | bytes 3538952 | tf_op jit(solution)/shard_map/ppermute | solution.py:400
  454.3 125.8 %reduce-scatter.12.cloned.1.call-start = ((), (), s32[]{:S(2)}) async-start(), calls=%async_computation.10 | async-start | bytes 1474560 | tf_op jit(solution)/shard_map/reduce_scatter | solution.py:438
  458.4 29.9 %collective-permute-start.40 = (bf16[768,768]{1,0:T(8,128)(2,1)}, bf16[768,768]{1,0:T(8,128)(2,1)}, u32[]{:S(2)}, u32[]{:S(2)}) collective-permute-start(bf16[768,768]{1,0:T(8,128)(2,1)} %slice_bitcast_fusion), channel_id=1, source_target_pairs={{0,8},{4,12},{8,0},{12,4},{1,9},{5,13},{9,1},{13,5},{2,10},{6,14},... | collective-permute-start | bytes 3538952 | tf_op jit(solution)/shard_map/ppermute | solution.py:400
  469.8 18.5 %collective-permute-start.39 = (f32[2,4,12,192]{3,1,2,0:T(4,128)S(1)}, f32[2,4,12,192]{3,1,2,0:T(4,128)S(1)}, u32[]{:S(2)}, u32[]{:S(2)}) collective-permute-start(f32[2,4,12,192]{3,1,2,0:T(4,128)S(1)} %copy.308), channel_id=1, source_target_pairs={{0,8},{4,12},{8,0},{12,4},{1,9},{5,13},{9,1},{13,5},{2,10},{6,14},... | collective-permute-start | bytes 221192 | tf_op jit(solution)/shard_map/ppermute | solution.py:400
  488.3 91.8 %reduce-scatter.14.cloned.1.call-start = ((), (), s32[]{:S(2)}) async-start(), calls=%async_computation.11 | async-start | bytes 1474560 | tf_op jit(solution)/shard_map/reduce_scatter | solution.py:438
  494.3 9.2 %collective-permute-start.43 = (f32[2,4,12,192]{3,1,2,0:T(4,128)S(1)}, f32[2,4,12,192]{3,1,2,0:T(4,128)S(1)}, u32[]{:S(2)}, u32[]{:S(2)}) collective-permute-start(f32[2,4,12,192]{3,1,2,0:T(4,128)S(1)} %copy.313), channel_id=1, source_target_pairs={{0,1},{1,0},{2,3},{3,2},{4,5},{5,4},{6,7},{7,6},{8,9},{9,8},{10,11... | collective-permute-start | bytes 221192 | tf_op jit(solution)/shard_map/ppermute | solution.py:400
  503.6 12.1 %collective-permute-start.44 = (f32[2,4,12,192]{3,1,2,0:T(4,128)S(1)}, f32[2,4,12,192]{3,1,2,0:T(4,128)S(1)}, u32[]{:S(2)}, u32[]{:S(2)}) collective-permute-start(f32[2,4,12,192]{3,1,2,0:T(4,128)S(1)} %copy.315), channel_id=1, source_target_pairs={{0,2},{1,3},{2,0},{3,1},{4,6},{5,7},{6,4},{7,5},{8,10},{9,11},{10,... | collective-permute-start | bytes 221192 | tf_op jit(solution)/shard_map/ppermute | solution.py:400
  516.6 14.9 %collective-permute-start.45 = (bf16[2,192,768]{2,1,0:T(8,128)(2,1)}, bf16[2,192,768]{2,1,0:T(8,128)(2,1)}, u32[]{:S(2)}, u32[]{:S(2)}) collective-permute-start(bf16[2,192,768]{2,1,0:T(8,128)(2,1)} %dynamic-slice_bitcast_fusion), channel_id=1, source_target_pairs={{0,1},{1,0},{2,3},{3,2},{4,5},{5,4},{6,7},{7,6},{8,9},{9,8},{10,11... | collective-permute-start | bytes 1769480 | tf_op jit(solution)/shard_map/ppermute | solution.py:400
  518.3 61.7 %all-to-all-start.1 = ((bf16[8,192,448]{2,1,0:T(8,128)(2,1)}), bf16[8,192,448]{2,1,0:T(8,128)(2,1)S(1)}, u32[]{:S(2)}, u32[]{:S(2)}) async-start(bf16[8,192,448]{2,1,0:T(8,128)(2,1)} %bitcast.55), calls=%async_computation.5 | async-start | bytes 3145728 | tf_op jit(solution)/shard_map/all_to_all | solution.py:656
  532.7 36.8 %collective-permute-start.48 = (bf16[1,192,768]{2,1,0:T(8,128)(2,1)}, bf16[1,192,768]{2,1,0:T(8,128)(2,1)}, u32[]{:S(2)}, u32[]{:S(2)}) collective-permute-start(bf16[1,192,768]{2,1,0:T(8,128)(2,1)} %bitcast.67), channel_id=1, source_target_pairs={{0,2},{1,3},{2,0},{3,1},{4,6},{5,7},{6,4},{7,5},{8,10},{9,11},{10,... | collective-permute-start | bytes 884744 | tf_op jit(solution)/shard_map/ppermute | solution.py:400
  535.2 43.8 %collective-permute-start.47 = (bf16[1,192,768]{2,1,0:T(8,128)(2,1)S(1)}, bf16[1,192,768]{2,1,0:T(8,128)(2,1)S(1)}, u32[]{:S(2)}, u32[]{:S(2)}) collective-permute-start(bf16[1,192,768]{2,1,0:T(8,128)(2,1)S(1)} %constant_dynamic-slice_fusion), channel_id=1, source_target_pairs={{0,2},{1,3},{2,0},{3,1},{4,6},{5,7},{6,4},{7,5},{8,10},{9,11},{10,... | collective-permute-start | bytes 884744 | tf_op jit(solution)/shard_map/ppermute | solution.py:400
  581.2 9.9 %collective-permute-start.50 = (bf16[192,768]{1,0:T(8,128)(2,1)S(1)}, bf16[192,768]{1,0:T(8,128)(2,1)S(1)}, u32[]{:S(2)}, u32[]{:S(2)}) collective-permute-start(bf16[192,768]{1,0:T(8,128)(2,1)S(1)} %bitcast_select_fusion), channel_id=1, source_target_pairs={{0,16},{16,0},{1,17},{17,1},{2,18},{18,2},{3,19},{19,3},{4,20},{20... | collective-permute-start | bytes 884744 | tf_op jit(solution)/shard_map/ppermute | solution.py:400
  582.5 15.0 %collective-permute-start.51 = (bf16[2,192,768]{2,1,0:T(8,128)(2,1)S(1)}, bf16[2,192,768]{2,1,0:T(8,128)(2,1)S(1)}, u32[]{:S(2)}, u32[]{:S(2)}) collective-permute-start(bf16[2,192,768]{2,1,0:T(8,128)(2,1)S(1)} %maximum_select_fusion.3), channel_id=1, source_target_pairs={{0,1},{1,0},{2,3},{3,2},{4,5},{5,4},{6,7},{7,6},{8,9},{9,8},{10,11... | collective-permute-start | bytes 1769480 | tf_op jit(solution)/shard_map/ppermute | solution.py:400
  582.5 13.8 %collective-permute-start.49 = (bf16[192,768]{1,0:T(8,128)(2,1)S(1)}, bf16[192,768]{1,0:T(8,128)(2,1)S(1)}, u32[]{:S(2)}, u32[]{:S(2)}) collective-permute-start(bf16[192,768]{1,0:T(8,128)(2,1)S(1)} %broadcast_select_fusion.8), channel_id=1, source_target_pairs={{0,16},{16,0},{1,17},{17,1},{2,18},{18,2},{3,19},{19,3},{4,20},{20... | collective-permute-start | bytes 884744 | tf_op jit(solution)/shard_map/ppermute | solution.py:400
  597.7 21.5 %collective-permute-start.52 = (bf16[1,192,768]{2,1,0:T(8,128)(2,1)S(1)}, bf16[1,192,768]{2,1,0:T(8,128)(2,1)S(1)}, u32[]{:S(2)}, u32[]{:S(2)}) collective-permute-start(bf16[1,192,768]{2,1,0:T(8,128)(2,1)S(1)} %fusion.10), channel_id=1, source_target_pairs={{0,2},{1,3},{2,0},{3,1},{4,6},{5,7},{6,4},{7,5},{8,10},{9,11},{10,... | collective-permute-start | bytes 884744 | tf_op jit(solution)/shard_map/ppermute | solution.py:400
  598.3 27.0 %collective-permute-start.53 = (bf16[1,192,768]{2,1,0:T(8,128)(2,1)S(1)}, bf16[1,192,768]{2,1,0:T(8,128)(2,1)S(1)}, u32[]{:S(2)}, u32[]{:S(2)}) collective-permute-start(bf16[1,192,768]{2,1,0:T(8,128)(2,1)S(1)} %fusion.11), channel_id=1, source_target_pairs={{0,2},{1,3},{2,0},{3,1},{4,6},{5,7},{6,4},{7,5},{8,10},{9,11},{10,... | collective-permute-start | bytes 884744 | tf_op jit(solution)/shard_map/ppermute | solution.py:400
  626.9 16.5 %collective-permute-start.54 = (bf16[2,192,768]{2,1,0:T(8,128)(2,1)}, bf16[2,192,768]{2,1,0:T(8,128)(2,1)}, u32[]{:S(2)}, u32[]{:S(2)}) collective-permute-start(bf16[2,192,768]{2,1,0:T(8,128)(2,1)} %maximum_select_fusion.5), channel_id=1, source_target_pairs={{0,1},{1,0},{2,3},{3,2},{4,5},{5,4},{6,7},{7,6},{8,9},{9,8},{10,11... | collective-permute-start | bytes 1769480 | tf_op jit(solution)/shard_map/ppermute | solution.py:400
  626.9 28.2 %collective-permute-start.55 = (bf16[2,192,768]{2,1,0:T(8,128)(2,1)}, bf16[2,192,768]{2,1,0:T(8,128)(2,1)}, u32[]{:S(2)}, u32[]{:S(2)}) collective-permute-start(bf16[2,192,768]{2,1,0:T(8,128)(2,1)} %maximum_select_fusion.4), channel_id=1, source_target_pairs={{0,1},{1,0},{2,3},{3,2},{4,5},{5,4},{6,7},{7,6},{8,9},{9,8},{10,11... | collective-permute-start | bytes 1769480 | tf_op jit(solution)/shard_map/ppermute | solution.py:400
  (103 other events, 704.3 us)
Sparse Core Ops, SparseCore 0:
  300.9 48.5 reduce-scatter.5
  394.1 29.4 reduce-scatter.7
  454.4 29.3 reduce-scatter.9
  488.4 34.9 reduce-scatter.11
  525.6 48.4 reduce-scatter.13

commit v6 on v5

--- a/solution.py
+++ b/solution.py
@@ -310,7 +310,7 @@
         compiler_params=pltpu.CompilerParams(
             vmem_limit_bytes=VMEM_LIMIT, dimension_semantics=("arbitrary",)
         ),
-        cost_estimate=pl.CostEstimate(flops=flops // 16, bytes_accessed=2**20, transcendentals=0),
+        cost_estimate=pl.CostEstimate(flops=flops * 16, bytes_accessed=2**28, transcendentals=0),
     )(info, *operands)
 
 
@@ -404,6 +404,11 @@
     return (left.astype(F32) + right.astype(F32)).astype(BF16)
 
 
+def with_rows(blocks, small):
+    pad = ((0, 0), (0, 16 - small.shape[1]), (0, blocks.shape[2] - small.shape[2]))
+    return jnp.concatenate([blocks, jnp.pad(small.astype(BF16), pad)], axis=1)
+
+
 def by_bits(slots, shard):
     odd = shard % 2 == 1
     high = shard >= 2
@@ -494,29 +499,20 @@
         w_fc1[0],
         w_fc2[0],
     ]
+    nears = [rows_of(own, zhalf, 2) for own in owned]
+    fars = [rows_of(own, 1 - zhalf, 2) for own in owned]
+    beyond_a = flip(nears[0], "section", 1)
+
     small = jnp.concatenate(
         [ln_gain[0], ln_shift[0], b_qv[0], b_out, b_fc2, b_fc1.reshape(SHARDS, FEATS)], axis=0
     )
     ends = ends_in[0].T.reshape(FEATS, clips, FRAMES).transpose(1, 0, 2)
-    beyond_a, small, owned[1], owned[2] = tie(
-        (flip(owned[0], "section", 1), small, owned[1], owned[2])
-    )
-    own_there_a = flip(owned[0], "tensor", 2)
-    beyond_one = flip(owned[1], "section", 1)
-    beyond_two = flip(owned[2], "section", 1)
-
+    ends = with_rows(ends, jnp.broadcast_to(small, (clips,) + small.shape))
     ends = lax.all_to_all(ends, ("section", "tensor"), split_axis=0, concat_axis=0, tiled=True)
-    ends = ends.reshape(2, D, FRAMES)
-
-    small_beyond = flip(small, "section", 1)
-    small = jnp.stack(
-        [jnp.where(section == 0, small, small_beyond), jnp.where(section == 0, small_beyond, small)]
-    )
-    small_y = flip(small, "tensor", 2)
-    pair = jnp.stack([small, small_y])
-    pair_other = flip(pair, "tensor", 1)
-    slots = jnp.stack([pair[0], pair_other[0], pair[1], pair_other[1]]).astype(F32)
-    cols = jnp.transpose(by_bits(slots[:, :, :8], shard), (1, 0, 3, 2))
+    small = ends[:, FEATS : FEATS + 12, :FEATS].reshape(2, SHARDS, 12, FEATS).astype(F32)
+    ends = ends[:, :FEATS].reshape(2, D, FRAMES)
+    cols = jnp.transpose(small[:, :, :8], (0, 1, 3, 2))
+    slots = by_bits([small[:, index] for index in range(SHARDS)], shard)
     bqvs = jnp.transpose(slots[:, :, 4:6], (1, 0, 3, 2))
     b1s = jnp.transpose(slots[:, :, 8:], (1, 0, 2, 3)).reshape(2, SHARDS, 1, FF_SHARD)
 
@@ -526,18 +522,24 @@
     def over_y(block):
         return flip(block, "tensor", 2)
 
-    def whole_chunk(own, there):
-        return (own, flip(own, "tensor", 1), there, flip(there, "tensor", 1))
-
-    def shared_chunk(own, near, far):
-        return (own, flip(own, "tensor", 1), near, far, flip(near, "tensor", 1), flip(far, "tensor", 1))
+    def chunk_of(own, there):
+        return tuple(
+            part for pair in (own, there) for parts in (pair, [flip(x, "tensor", 1) for x in pair])
+            for part in parts
+        )
 
     n_dp = lax.axis_size("dp")
-    a_own = layers(owned[0], beyond_a)
-    there_a, beyond_one = tie((over_y(beyond_a), beyond_one))
-    a_there = layers(own_there_a, there_a)
-    one_own = layers(owned[1], beyond_one)
-    one_there = over_y(one_own[0])
+    beyond_a, near_one, own_two = tie((beyond_a, nears[1], owned[2]))
+    beyond_one = flip(near_one, "section", 1)
+    beyond_two = flip(own_two, "section", 1)
+    near_a = layers(nears[0], beyond_a)
+    far_a = layers(fars[0], flip(beyond_a, "dp", 1))
+    there_a = over_y(near_a[0])
+    there_a, beyond_one = tie((there_a, beyond_one))
+    away_a = flip(there_a, "dp", 1)
+    near_one = layers(nears[1], beyond_one)
+    beyond_far_one = flip(beyond_one, "dp", 1)
+    there_one = over_y(near_one[0])
 
     def attend(layer, stream, chunk):
         return attention_forward(info, stream, cols[layer], bqvs[layer], chunk)
@@ -545,29 +547,38 @@
     def feed(layer, h, chunk_one, chunk_two):
         return mlp_forward(info, h, cols[layer], b1s[layer], chunk_one, chunk_two)
 
-    chunks = [[whole_chunk(a_own[0], a_there[0])], []]
+    chunks = [[chunk_of((near_a[0], far_a[0]), (there_a, away_a))], []]
     stream = ends[0]
     a1, p, soft, o, h = attend(0, stream, chunks[0][0])
-    h, beyond_two, one_there, late_a, late_one = tie(
-        (h, beyond_two, one_there, (a_own[1], a_there[1]), one_own[1])
-    )
-    two_own = layers(owned[2], beyond_two)
-    two_there = over_y(two_own[0])
-    chunks[0].append(whole_chunk(one_own[0], one_there))
-    two_there, halves = tie(
-        (two_there, [rows_of(late_one, zhalf, 2), rows_of(two_own[1], zhalf, 2)])
-    )
-    nears = [over_y(half) for half in halves]
-    chunks[0].append(whole_chunk(two_own[0], two_there))
+    h, beyond_two, there_one, beyond_far_one, late_a, late_far_a, late_one = tie(
+        (h, beyond_two, there_one, beyond_far_one, near_a[1], far_a[1], near_one[1])
+    )
+    near_two = layers(nears[2], rows_of(beyond_two, zhalf, 2))
+    far_two = layers(fars[2], rows_of(beyond_two, 1 - zhalf, 2))
+    there_two = over_y(near_two[0])
+    far_one = layers(fars[1], beyond_far_one)
+    away_one = flip(there_one, "dp", 1)
+    chunks[0].append(chunk_of((near_one[0], far_one[0]), (there_one, away_one)))
+    there_two, late_a, late_one, late_two = tie((there_two, late_a, late_one, near_two[1]))
+    chunks[0].append(chunk_of((near_two[0], far_two[0]), (there_two, flip(there_two, "dp", 1))))
+    there_a, there_one, there_two = over_y(late_a), over_y(late_one), over_y(late_two)
+    away_a = flip(there_a, "dp", 1)
     a2, u, slope, y = feed(0, h, *chunks[0][1:])
     stored = [(stream, a1, p, soft, o, h, a2, u, slope)]
-    stream, nears, late_a, late_one, late_two = tie((y, nears, late_a, late_one, two_own[1]))
-    chunks[1].append(whole_chunk(*late_a))
-    fars = [flip(near, "dp", 1) for near in nears]
+    stream, there_a, away_a, there_one, there_two, late_a, late_far_a = tie(
+        (y, there_a, away_a, there_one, there_two, late_a, late_far_a)
+    )
+    chunks[1].append(chunk_of((late_a, late_far_a), (there_a, away_a)))
+    away_one, away_two = flip(there_one, "dp", 1), flip(there_two, "dp", 1)
     a1, p, soft, o, h = attend(1, stream, chunks[1][0])
-    h, nears, fars, late_one, late_two = tie((h, nears, fars, late_one, late_two))
-    chunks[1].append(shared_chunk(late_one, nears[0], fars[0]))
-    chunks[1].append(shared_chunk(late_two, nears[1], fars[1]))
+    h, late = tie(
+        (
+            h,
+            (late_one, far_one[1], there_one, away_one, late_two, far_two[1], there_two, away_two),
+        )
+    )
+    chunks[1].append(chunk_of(late[0:2], late[2:4]))
+    chunks[1].append(chunk_of(late[4:6], late[6:8]))
     a2, u, slope, y = feed(1, h, *chunks[1][1:])
     stored.append((stream, a1, p, soft, o, h, a2, u, slope))
     stream = y
@@ -643,37 +654,29 @@
         )
 
     result = jnp.stack([upstream.astype(BF16), stream.astype(BF16)])
-    result = result.reshape(2 * SHARDS, FEATS, FRAMES)
-    small_sum = jnp.stack(smalls)
-
-    small_sum += flip(small_sum, "tensor", 1)
-    small_y = flip(small_sum, "tensor", 2)
+    result = with_rows(
+        result.reshape(2 * SHARDS, FEATS, FRAMES), jnp.stack(smalls).reshape(-1, 12, FEATS)
+    )
+
     late_one.send_y()
+    bits = [1 << k for k in range(n_dp.bit_length() - 1)]
 
     last_one.fold()
-    small_y, result, last_a.arrived = tied((last_one,), small_y, result, last_a.arrived)
+    result, last_a.arrived = tied((last_one, late_a), result, last_a.arrived)
     last_one.scatter()
     result = lax.all_to_all(result, ("section", "tensor"), split_axis=0, concat_axis=0, tiled=True)
-    small_sum += small_y
-    small_sum += flip(small_sum, "section", 1)
-    bits = [1 << k for k in range(n_dp.bit_length() - 1)]
-    for bit in bits:
-        small_sum += flip(small_sum, "dp", bit)
 
     last_a.fold()
     late_one.fold()
-    (small_sum,) = tied((last_a, late_one, last_two), small_sum)
+    tied((last_a, late_one, last_two))
     last_a.split()
     last_a.send_half(bits[0])
     pair_two, pair_one, pair_a = Chain(), Chain(), Chain()
     pair_two.send_x(last_two, late_two)
-    small_sum = lax.dynamic_slice(
-        small_sum, (section, shard, 0, 0), (1, 1, 12, FEATS)
-    ).reshape(12, FEATS)
 
     last_a.fold()
     pair_two.fold()
-    (small_sum,) = tied((last_a, pair_two), small_sum)
+    (result,) = tied((last_a, pair_two), result)
     pair_two.value = pair_two.value[None]
     for bit in bits[1:]:
         last_a.send_half(bit)
@@ -687,25 +690,29 @@
     for bit in bits[-2:0:-1]:
         pair_two.send_back(bit)
         pair_two.join(bit)
-    result, small_sum = tied((last_a, pair_two, last_one), result, small_sum)
+    (result,) = tied((last_a, pair_two, last_one), result)
     pair_one.send_x(last_one, late_one)
     pair_a.send_x(last_a, late_a)
     pair_two.send_back(bits[0])
+    small_sum = result[:, FEATS : FEATS + 12, :FEATS].astype(F32).sum(axis=0)
 
     for pair in (pair_one, pair_a):
         pair.fold()
         pair.value = pair.value[None]
     pair_two.join(bits[0])
     result, small_sum = tied((pair_one, pair_a, pair_two), result, small_sum)
+    small_sum += flip(small_sum, "dp", bits[0])
     for bit in bits[:0:-1]:
         for pair in (pair_one, pair_a):
             pair.send_back(bit)
         for pair in (pair_one, pair_a):
             pair.join(bit)
     result, small_sum = tied((pair_one, pair_a), result, small_sum)
+    for bit in bits[1:]:
+        small_sum += flip(small_sum, "dp", bit)
     for pair in (pair_one, pair_a):
         pair.send_back(bits[0])
-    result = result.transpose(1, 0, 2).reshape(FEATS, clips * FRAMES).T.astype(F32)
+    result = result[:, :FEATS].transpose(1, 0, 2).reshape(FEATS, clips * FRAMES).T.astype(F32)
     for pair in (pair_one, pair_a):
         pair.join(bits[0])
     for pair in (pair_two, pair_one, pair_a):

time: 671 us -> 612 us (0.912)
  waiting for transfers between devices: 315 us -> 214 us
  local copies, waits for them, and re-layouts: 62.1 us -> 84.1 us
  starting transfers between devices: 50.5 us -> 61.2 us
    ppermute x56 -> x66, waiting for transfers between devices: 314 us -> 214 us  [flip(): return lax.ppermute(block, axis, [(i, i ^ bit) for i in range(size)])]
    ppermute x56 -> x66, starting transfers between devices: 42.6 us -> 51.9 us  [flip(): return lax.ppermute(block, axis, [(i, i ^ bit) for i in range(size)])]
    unnamed x176 -> x237, local copies, waits for them, and re-layouts: 20.5 us -> 27.6 us
  transfers between devices with their start and end apart: 63 -> 73, of which waited for: 35 -> 27; matrix products, arithmetic and copies ran while one was open for 13% -> 18% of each run, Pallas kernels for 17% -> 24%
where the time goes in v6:
time: 612 us; the launch traced here: 605 us
  waiting for transfers between devices  214 us (35%)
  Pallas kernels  168 us (27%)
  local copies, waits for them, and re-layouts  84.1 us (14%)
  other arithmetic  61.5 us (10%)
  starting transfers between devices  61.2 us (10%)
  between operations  15.6 us (3%)
    ppermute x66, waiting for transfers between devices, flip(): return lax.ppermute(block, axis, [(i, i ^ bit) for i in range(size)])  214 us
    pallas_call x12, Pallas kernels, run(): pl.pallas_call(kernel, name=name, out_shape=outs, grid_spec=pltpu.Prefetc...  168 us
    ppermute x66, starting transfers between devices, flip(): return lax.ppermute(block, axis, [(i, i ^ bit) for i in range(size)])  51.9 us
    convert_element_type x14, other arithmetic, added(): return (left.astype(F32) + right.astype(F32)).astype(BF16)  31.5 us
    unnamed x237, local copies, waits for them, and re-layouts  27.6 us
  transfers between devices with their start and end apart: 73, of which 27 were waited for; matrix products, arithmetic and copies ran while one was open for 18% of the time, Pallas kernels for 24%

profile of v6, /device:TPU:0, one launch (start us, length us, event | category | flops | bytes accessed | tf_op | source)
XLA Modules:
  0.0 605.3 jit_solution(14982117309040167266)
XLA Ops:
  8.7 3.0 collective-permute-start
  16.5 4.4 all-to-all-start
  21.1 4.9 collective-permute-done
  33.1 21.9 %collective-permute-done.4.refs_4_.refs_5_ = bf16[384,768]{1,0:T(8,128)(2,1)} collective-permute-done((bf16[384,768]{1,0:T(8,128)(2,1)S(1)}, bf16[384,768]{1,0:T(8,128)(2,1)}, u32[]{:S(2)}, u32[]{:S(2)}) %collective-permute-start.4) | collective-permute-done | bytes 589856 | tf_op jit(solution)/shard_map/ppermute | solution.py:400
  81.8 2.7 fusion.33
  87.1 15.4 %attention_forward.2 = (bf16[768,448]{1,0:T(8,128)(2,1)}, bf16[4,576,448]{2,1,0:T(8,128)(2,1)}, bf16[4,3,448,448]{3,2,1,0:T(8,128)(2,1)}, bf16[4,192,448]{2,1,0:T(8,128)(2,1)}, f32[768,448]{1,0:T(8,128)}) custom-call(s32[9]{0:T(128)S(1)} %stack.167.info, bf16[768,448]{1,0:T(8,128)(2,1)} %bitcast.167, f32[4,192,8]{2,1,0:T(8,128)S(1)} %copy-done.9, ...), custom_call_target="tpu_custom_call" | custom-call | flops 43687870464 | bytes 268435456 | tf_op jit(solution)/shard_map/attention_forward/pallas_call | solution.py:299
  102.5 3.2 bitcast_select_fusion
  108.9 11.8 %collective-permute-done.19.refs_12_.refs_13_ = bf16[384,768]{1,0:T(8,128)(2,1)} collective-permute-done((bf16[384,768]{1,0:T(8,128)(2,1)S(1)}, bf16[384,768]{1,0:T(8,128)(2,1)}, u32[]{:S(2)}, u32[]{:S(2)}) %collective-permute-start.19) | collective-permute-done | bytes 589856 | tf_op jit(solution)/shard_map/ppermute | solution.py:400
  125.4 12.2 %collective-permute-done.20.refs_13_.refs_14_ = bf16[384,768]{1,0:T(8,128)(2,1)} collective-permute-done((bf16[384,768]{1,0:T(8,128)(2,1)}, bf16[384,768]{1,0:T(8,128)(2,1)}, u32[]{:S(2)}, u32[]{:S(2)}) %collective-permute-start.20) | collective-permute-done | bytes 589856 | tf_op jit(solution)/shard_map/ppermute | solution.py:400
  148.2 13.6 %mlp_forward.2 = (bf16[768,448]{1,0:T(8,128)(2,1)}, bf16[4,448,768]{2,1,0:T(8,128)(2,1)}, bf16[4,448,768]{2,1,0:T(8,128)(2,1)}, f32[768,448]{1,0:T(8,128)}) custom-call(s32[9]{0:T(128)S(1)} %stack.167.info, f32[768,448]{1,0:T(8,128)} %get-tuple-element.150.h_ref, f32[4,192,8]{2,1,0:T(8,128)S(1)} %copy-done.10, f32[4,1,768]{2,1,0:T(1,128)S(1)} %squeeze.137.b1_ref, ...), custom_call_target="tpu_custom_call" | custom-call | flops 67645734912 | bytes 268435456 | tf_op jit(solution)/shard_map/mlp_forward/pallas_call | solution.py:299
  161.9 6.4 %collective-permute-done.26.refs_12_.refs_13_ = bf16[384,768]{1,0:T(8,128)(2,1)} collective-permute-done((bf16[384,768]{1,0:T(8,128)(2,1)}, bf16[384,768]{1,0:T(8,128)(2,1)}, u32[]{:S(2)}, u32[]{:S(2)}) %collective-permute-start.26) | collective-permute-done | bytes 589856 | tf_op jit(solution)/shard_map/ppermute | solution.py:400
  172.8 15.8 %attention_forward.3 = (bf16[768,448]{1,0:T(8,128)(2,1)}, bf16[4,576,448]{2,1,0:T(8,128)(2,1)}, bf16[4,3,448,448]{3,2,1,0:T(8,128)(2,1)}, bf16[4,192,448]{2,1,0:T(8,128)(2,1)}, f32[768,448]{1,0:T(8,128)}) custom-call(s32[9]{0:T(128)S(1)} %stack.167.info, f32[768,448]{1,0:T(8,128)} %get-tuple-element.162.x_ref, f32[4,192,8]{2,1,0:T(8,128)S(1)} %copy-done.13, ...), custom_call_target="tpu_custom_call" | custom-call | flops 43687870464 | bytes 268435456 | tf_op jit(solution)/shard_map/attention_forward/pallas_call | solution.py:299
  188.7 8.6 %collective-permute-done.32.refs_13_.refs_14_ = bf16[384,768]{1,0:T(8,128)(2,1)} collective-permute-done((bf16[384,768]{1,0:T(8,128)(2,1)}, bf16[384,768]{1,0:T(8,128)(2,1)}, u32[]{:S(2)}, u32[]{:S(2)}) %collective-permute-start.32) | collective-permute-done | bytes 589856 | tf_op jit(solution)/shard_map/ppermute | solution.py:400
  212.2 13.7 %mlp_forward.3 = (bf16[768,448]{1,0:T(8,128)(2,1)}, bf16[4,448,768]{2,1,0:T(8,128)(2,1)}, bf16[4,448,768]{2,1,0:T(8,128)(2,1)}, f32[768,448]{1,0:T(8,128)}) custom-call(s32[9]{0:T(128)S(1)} %stack.167.info, f32[768,448]{1,0:T(8,128)} %get-tuple-element.170.h_ref, f32[4,192,8]{2,1,0:T(8,128)S(1)} %copy-done.14, f32[4,1,768]{2,1,0:T(1,128)S(1)} %squeeze.138.b1_ref, ...), custom_call_target="tpu_custom_call" | custom-call | flops 67645734912 | bytes 268435456 | tf_op jit(solution)/shard_map/mlp_forward/pallas_call | solution.py:299
  226.0 12.1 %mlp_backward.4 = (f32[448,768]{1,0:T(8,128)}, bf16[2,768,768]{2,1,0:T(8,128)(2,1)}, bf16[2,768,768]{2,1,0:T(8,128)(2,1)}, f32[2,1,768]{2,1,0:T(1,128)S(1)}) custom-call(s32[9]{0:T(128)S(1)} %stack.167.info, bf16[768,448]{1,0:T(8,128)(2,1)} %bitcast.207, f32[768,448]{1,0:T(8,128)} %get-tuple-element.170.h_ref, bf16[768,448]{1,0:T(8,128)(2,1)} %get-tuple-element.179.a2_ref, ...), custom_call_target="tpu_custom_call" | custom-call | flops 67645734912 | bytes 268435456 | tf_op jit(solution)/shard_map/mlp_backward/pallas_call | solution.py:299
  239.3 14.1 %mlp_backward.5 = (f32[768,448]{1,0:T(8,128)}, f32[768,8]{1,0:T(8,128)S(1)}, bf16[2,768,768]{2,1,0:T(8,128)(2,1)}, bf16[2,768,768]{2,1,0:T(8,128)(2,1)}, f32[2,1,768]{2,1,0:T(1,128)S(1)}) custom-call(s32[9]{0:T(128)S(1)} %copy-done.27, bf16[768,448]{1,0:T(8,128)(2,1)} %bitcast.208, f32[768,448]{1,0:T(8,128)} %get-tuple-element.170.h_ref, ...), custom_call_target="tpu_custom_call" | custom-call | flops 67645734912 | bytes 268435456 | tf_op jit(solution)/shard_map/mlp_backward/pallas_call | solution.py:299
  253.5 2.6 convert_bitcast_fusion.1
  257.5 3.8 add_convert_fusion.5
  263.6 2.5 slice_bitcast_fusion.4
  270.1 12.7 %attention_backward.4 = (f32[448,768]{1,0:T(8,128)}, bf16[2,768,768]{2,1,0:T(8,128)(2,1)}, f32[2,192,8]{2,1,0:T(8,128)S(1)}) custom-call(s32[9]{0:T(128)S(1)} %copy-done.28, f32[768,448]{1,0:T(8,128)} %get-tuple-element.189.gh_ref, f32[768,448]{1,0:T(8,128)} %get-tuple-element.162.x_ref, bf16[768,448]{1,0:T(8,128)(2,1)S(1)} %copy-done.69, ...), custom_call_target="tpu_custom_call" | custom-call | flops 43687870464 | bytes 268435456 | tf_op jit(solution)/shard_map/attention_backward/pallas_call | solution.py:299
  282.9 15.6 %attention_backward.5 = (f32[768,448]{1,0:T(8,128)}, f32[768,8]{1,0:T(8,128)S(1)}, bf16[2,768,768]{2,1,0:T(8,128)(2,1)}, f32[2,192,8]{2,1,0:T(8,128)S(1)}) custom-call(s32[9]{0:T(128)S(1)} %copy-done.28, f32[768,448]{1,0:T(8,128)} %get-tuple-element.189.gh_ref, f32[768,448]{1,0:T(8,128)} %get-tuple-element.162.x_ref, ...), custom_call_target="tpu_custom_call" | custom-call | flops 43687870464 | bytes 268435456 | tf_op jit(solution)/shard_map/attention_backward/pallas_call | solution.py:299
  298.5 2.8 fusion.5
  304.8 12.3 %mlp_backward.6 = (f32[448,768]{1,0:T(8,128)}, bf16[2,768,768]{2,1,0:T(8,128)(2,1)}, bf16[2,768,768]{2,1,0:T(8,128)(2,1)}, f32[2,1,768]{2,1,0:T(1,128)S(1)}) custom-call(s32[9]{0:T(128)S(1)} %copy-done.28, f32[768,448]{1,0:T(8,128)} %get-tuple-element.199.gy_ref, f32[768,448]{1,0:T(8,128)} %get-tuple-element.150.h_ref, ...), custom_call_target="tpu_custom_call" | custom-call | flops 67645734912 | bytes 268435456 | tf_op jit(solution)/shard_map/mlp_backward/pallas_call | solution.py:299
  322.1 14.7 %mlp_backward.7 = (f32[768,448]{1,0:T(8,128)}, f32[768,8]{1,0:T(8,128)S(1)}, bf16[2,768,768]{2,1,0:T(8,128)(2,1)}, bf16[2,768,768]{2,1,0:T(8,128)(2,1)}, f32[2,1,768]{2,1,0:T(1,128)S(1)}) custom-call(s32[9]{0:T(128)S(1)} %copy-done.29, f32[768,448]{1,0:T(8,128)} %get-tuple-element.199.gy_ref, f32[768,448]{1,0:T(8,128)} %get-tuple-element.150.h_ref, ...), custom_call_target="tpu_custom_call" | custom-call | flops 67645734912 | bytes 268435456 | tf_op jit(solution)/shard_map/mlp_backward/pallas_call | solution.py:299
  336.9 2.8 fusion.4
  339.7 2.5 add_convert_fusion.2
  342.2 4.5 add_convert_fusion.1
  354.2 12.9 %attention_backward.6 = (f32[448,768]{1,0:T(8,128)}, bf16[2,768,768]{2,1,0:T(8,128)(2,1)}, f32[2,192,8]{2,1,0:T(8,128)S(1)}) custom-call(s32[9]{0:T(128)S(1)} %copy-done.30, f32[768,448]{1,0:T(8,128)} %get-tuple-element.211.gh_ref, bf16[768,448]{1,0:T(8,128)(2,1)S(1)} %bitcast.169, bf16[768,448]{1,0:T(8,128)(2,1)} %get-tuple-element.212.a1_ref, ...), custom_call_target="tpu_custom_call" | custom-call | flops 43687870464 | bytes 268435456 | tf_op jit(solution)/shard_map/attention_backward/pallas_call | solution.py:299
  368.0 15.5 %attention_backward.7 = (f32[768,448]{1,0:T(8,128)}, f32[768,8]{1,0:T(8,128)S(1)}, bf16[2,768,768]{2,1,0:T(8,128)(2,1)}, f32[2,192,8]{2,1,0:T(8,128)S(1)}) custom-call(s32[9]{0:T(128)S(1)} %copy-done.31, f32[768,448]{1,0:T(8,128)} %get-tuple-element.211.gh_ref, bf16[768,448]{1,0:T(8,128)(2,1)} %bitcast.168, bf16[768,448]{1,0:T(8,128)(2,1)} %get-tuple-element.212.a1_ref, ...), custom_call_target="tpu_custom_call" | custom-call | flops 43687870464 | bytes 268435456 | tf_op jit(solution)/shard_map/attention_backward/pallas_call | solution.py:299
  383.9 2.9 fusion.1
  386.9 21.9 %collective-permute-done.48 = bf16[768,768]{1,0:T(8,128)(2,1)} collective-permute-done((bf16[768,768]{1,0:T(8,128)(2,1)}, bf16[768,768]{1,0:T(8,128)(2,1)}, u32[]{:S(2)}, u32[]{:S(2)}) %collective-permute-start.48) | collective-permute-done | bytes 1179680 | tf_op jit(solution)/shard_map/ppermute | solution.py:400
  408.8 2.7 fusion.3
  411.5 3.8 add_convert_fusion
  429.6 19.1 %collective-permute-done.51 = bf16[768,768]{1,0:T(8,128)(2,1)} collective-permute-done((bf16[768,768]{1,0:T(8,128)(2,1)}, bf16[768,768]{1,0:T(8,128)(2,1)}, u32[]{:S(2)}, u32[]{:S(2)}) %collective-permute-start.51) | collective-permute-done | bytes 1179680 | tf_op jit(solution)/shard_map/ppermute | solution.py:400
  450.5 4.7 all-to-all-start.1
  460.9 21.9 %collective-permute-done.54 = bf16[192,768]{1,0:T(8,128)(2,1)S(1)} collective-permute-done((bf16[192,768]{1,0:T(8,128)(2,1)S(1)}, bf16[192,768]{1,0:T(8,128)(2,1)S(1)}, u32[]{:S(2)}, u32[]{:S(2)}) %collective-permute-start.54) | collective-permute-done | bytes 294944 | tf_op jit(solution)/shard_map/ppermute | solution.py:400
  482.9 7.1 %collective-permute-done.53 = bf16[2,192,768]{2,1,0:T(8,128)(2,1)} collective-permute-done((bf16[2,192,768]{2,1,0:T(8,128)(2,1)S(1)}, bf16[2,192,768]{2,1,0:T(8,128)(2,1)}, u32[]{:S(2)}, u32[]{:S(2)}) %collective-permute-start.53) | collective-permute-done | bytes 589856 | tf_op jit(solution)/shard_map/ppermute | solution.py:400
  494.3 20.5 %collective-permute-done.56 = bf16[1,192,768]{2,1,0:T(8,128)(2,1)S(1)} collective-permute-done((bf16[1,192,768]{2,1,0:T(8,128)(2,1)S(1)}, bf16[1,192,768]{2,1,0:T(8,128)(2,1)S(1)}, u32[]{:S(2)}, u32[]{:S(2)}) %collective-permute-start.56) | collective-permute-done | bytes 294944 | tf_op jit(solution)/shard_map/ppermute | solution.py:400
  514.9 4.2 collective-permute-done.55
  523.5 5.8 collective-permute-done.58
  529.4 4.1 collective-permute-done.57
  533.5 2.4 collective-permute-done.59
  537.5 3.4 collective-permute-start.60
  542.5 16.9 %collective-permute-done.60 = bf16[1,192,768]{2,1,0:T(8,128)(2,1)S(1)} collective-permute-done((bf16[1,192,768]{2,1,0:T(8,128)(2,1)S(1)}, bf16[1,192,768]{2,1,0:T(8,128)(2,1)S(1)}, u32[]{:S(2)}, u32[]{:S(2)}) %collective-permute-start.60) | collective-permute-done | bytes 294944 | tf_op jit(solution)/shard_map/ppermute | solution.py:400
  560.3 5.0 collective-permute-done.61
  566.2 3.2 collective-permute-start.64
  577.4 6.6 %collective-permute-done.64 = bf16[2,192,768]{2,1,0:T(8,128)(2,1)} collective-permute-done((bf16[2,192,768]{2,1,0:T(8,128)(2,1)}, bf16[2,192,768]{2,1,0:T(8,128)(2,1)}, u32[]{:S(2)}, u32[]{:S(2)}) %collective-permute-start.64) | collective-permute-done | bytes 589856 | tf_op jit(solution)/shard_map/ppermute | solution.py:400
  588.2 6.8 %collective-permute-done.65 = bf16[2,192,768]{2,1,0:T(8,128)(2,1)} collective-permute-done((bf16[2,192,768]{2,1,0:T(8,128)(2,1)}, bf16[2,192,768]{2,1,0:T(8,128)(2,1)}, u32[]{:S(2)}, u32[]{:S(2)}) %collective-permute-start.65) | collective-permute-done | bytes 589856 | tf_op jit(solution)/shard_map/ppermute | solution.py:400
  (494 shorter events, 157.8 us)
Async XLA Ops:
  8.7 17.3 %collective-permute-start = (bf16[384,768]{1,0:T(8,128)(2,1)S(1)}, bf16[384,768]{1,0:T(8,128)(2,1)}, u32[]{:S(2)}, u32[]{:S(2)}) collective-permute-start(bf16[384,768]{1,0:T(8,128)(2,1)S(1)} %fusion.11), channel_id=1, source_target_pairs={{0,16},{16,0},{1,17},{17,1},{2,18},{18,2},{3,19},{19,3},{4,20},{20... | collective-permute-start | bytes 1769480 | tf_op jit(solution)/shard_map/ppermute | solution.py:400
  16.5 46.1 %all-to-all-start = ((bf16[8,208,448]{2,1,0:T(8,128)(2,1)}), bf16[8,208,448]{2,1,0:T(8,128)(2,1)}, u32[]{:S(2)}, u32[]{:S(2)}) async-start(bf16[8,208,448]{2,1,0:T(8,128)(2,1)} %copy.201), calls=%async_computation | async-start | bytes 3407872 | tf_op jit(solution)/shard_map/all_to_all | solution.py:511
  20.9 325.8 %reduce-scatter.6.cloned.1.call-start = ((), (), s32[]{:S(2)}) async-start(), calls=%async_computation.7 | async-start | bytes 2949120 | tf_op jit(solution)/shard_map/reduce_scatter | solution.py:443
  27.2 27.9 %collective-permute-start.4 = (bf16[384,768]{1,0:T(8,128)(2,1)S(1)}, bf16[384,768]{1,0:T(8,128)(2,1)}, u32[]{:S(2)}, u32[]{:S(2)}) collective-permute-start(bf16[384,768]{1,0:T(8,128)(2,1)S(1)} %get-tuple-element.306.refs_0_.refs_1_), channel_id=1, source_target_pairs={{0,8},{4,12},{8,0},{12,4},{1,9},{5,13},{9,1},{13,5},{2,10},{6,14},... | collective-permute-start | bytes 1769480 | tf_op jit(solution)/shard_map/ppermute | solution.py:400
  29.3 27.5 %collective-permute-start.5 = (bf16[384,768]{1,0:T(8,128)(2,1)S(1)}, bf16[384,768]{1,0:T(8,128)(2,1)S(1)}, u32[]{:S(2)}, u32[]{:S(2)}) collective-permute-start(bf16[384,768]{1,0:T(8,128)(2,1)S(1)} %dynamic-slice_bitcast_fusion.1), channel_id=1, source_target_pairs={{0,16},{16,0},{1,17},{17,1},{2,18},{18,2},{3,19},{19,3},{4,20},{20... | collective-permute-start | bytes 1769480 | tf_op jit(solution)/shard_map/ppermute | solution.py:400
  30.8 28.2 %collective-permute-start.1 = (bf16[384,768]{1,0:T(8,128)(2,1)}, bf16[384,768]{1,0:T(8,128)(2,1)}, u32[]{:S(2)}, u32[]{:S(2)}) collective-permute-start(bf16[384,768]{1,0:T(8,128)(2,1)} %collective-permute-done), channel_id=1, source_target_pairs={{0,1},{1,0},{2,3},{3,2},{4,5},{5,4},{6,7},{7,6},{8,9},{9,8},{10,11... | collective-permute-start | bytes 1769480 | tf_op jit(solution)/shard_map/ppermute | solution.py:400
  32.5 52.1 %collective-permute-start.2 = (bf16[384,768]{1,0:T(8,128)(2,1)S(1)}, bf16[384,768]{1,0:T(8,128)(2,1)}, u32[]{:S(2)}, u32[]{:S(2)}) collective-permute-start(bf16[384,768]{1,0:T(8,128)(2,1)S(1)} %get-tuple-element.306.refs_0_.refs_1_), channel_id=1, source_target_pairs={{0,4},{4,0},{8,12},{12,8},{1,5},{5,1},{9,13},{13,9},{2,6},{6,2},{1... | collective-permute-start | bytes 1769480 | tf_op jit(solution)/shard_map/ppermute | solution.py:400
  32.5 69.9 %collective-permute-start.9 = (bf16[768,768]{1,0:T(8,128)(2,1)}, bf16[768,768]{1,0:T(8,128)(2,1)}, u32[]{:S(2)}, u32[]{:S(2)}) collective-permute-start(bf16[768,768]{1,0:T(8,128)(2,1)} %bitcast.27), channel_id=1, source_target_pairs={{0,16},{16,0},{1,17},{17,1},{2,18},{18,2},{3,19},{19,3},{4,20},{20... | collective-permute-start | bytes 3538952 | tf_op jit(solution)/shard_map/ppermute | solution.py:400
  56.9 28.7 %collective-permute-start.7 = (bf16[384,768]{1,0:T(8,128)(2,1)}, bf16[384,768]{1,0:T(8,128)(2,1)}, u32[]{:S(2)}, u32[]{:S(2)}) collective-permute-start(bf16[384,768]{1,0:T(8,128)(2,1)} %collective-permute-done.4.refs_4_.refs_5_), channel_id=1, source_target_pairs={{0,4},{4,0},{8,12},{12,8},{1,5},{5,1},{9,13},{13,9},{2,6},{6,2},{1... | collective-permute-start | bytes 1769480 | tf_op jit(solution)/shard_map/ppermute | solution.py:400
  56.9 20.2 %collective-permute-start.6 = (bf16[384,768]{1,0:T(8,128)(2,1)}, bf16[384,768]{1,0:T(8,128)(2,1)}, u32[]{:S(2)}, u32[]{:S(2)}) collective-permute-start(bf16[384,768]{1,0:T(8,128)(2,1)} %collective-permute-done.4.refs_4_.refs_5_), channel_id=1, source_target_pairs={{0,1},{1,0},{2,3},{3,2},{4,5},{5,4},{6,7},{7,6},{8,9},{9,8},{10,11... | collective-permute-start | bytes 1769480 | tf_op jit(solution)/shard_map/ppermute | solution.py:400
  61.0 26.1 %collective-permute-start.3 = (bf16[384,768]{1,0:T(8,128)(2,1)S(1)}, bf16[384,768]{1,0:T(8,128)(2,1)}, u32[]{:S(2)}, u32[]{:S(2)}) collective-permute-start(bf16[384,768]{1,0:T(8,128)(2,1)S(1)} %get-tuple-element.300.refs_1_.refs_2_), channel_id=1, source_target_pairs={{0,4},{4,0},{8,12},{12,8},{1,5},{5,1},{9,13},{13,9},{2,6},{6,2},{1... | collective-permute-start | bytes 1769480 | tf_op jit(solution)/shard_map/ppermute | solution.py:400
  84.5 17.9 %collective-permute-start.11 = (bf16[384,768]{1,0:T(8,128)(2,1)S(1)}, bf16[384,768]{1,0:T(8,128)(2,1)S(1)}, u32[]{:S(2)}, u32[]{:S(2)}) collective-permute-start(bf16[384,768]{1,0:T(8,128)(2,1)S(1)} %copy-done.100), channel_id=1, source_target_pairs={{0,1},{1,0},{2,3},{3,2},{4,5},{5,4},{6,7},{7,6},{8,9},{9,8},{10,11... | collective-permute-start | bytes 1769480 | tf_op jit(solution)/shard_map/ppermute | solution.py:400
  85.5 16.9 %collective-permute-start.10 = (bf16[384,768]{1,0:T(8,128)(2,1)S(1)}, bf16[384,768]{1,0:T(8,128)(2,1)S(1)}, u32[]{:S(2)}, u32[]{:S(2)}) collective-permute-start(bf16[384,768]{1,0:T(8,128)(2,1)S(1)} %get-tuple-element.304.refs_0_.refs_1_), channel_id=1, source_target_pairs={{0,8},{4,12},{8,0},{12,4},{1,9},{5,13},{9,1},{13,5},{2,10},{6,14},... | collective-permute-start | bytes 1769480 | tf_op jit(solution)/shard_map/ppermute | solution.py:400
  106.3 17.7 %collective-permute-start.15 = (bf16[384,768]{1,0:T(8,128)(2,1)S(1)}, bf16[384,768]{1,0:T(8,128)(2,1)S(1)}, u32[]{:S(2)}, u32[]{:S(2)}) collective-permute-start(bf16[384,768]{1,0:T(8,128)(2,1)S(1)} %collective-permute-done.10.refs_4_.refs_5_), channel_id=1, source_target_pairs={{0,4},{4,0},{8,12},{12,8},{1,5},{5,1},{9,13},{13,9},{2,6},{6,2},{1... | collective-permute-start | bytes 1769480 | tf_op jit(solution)/shard_map/ppermute | solution.py:400
  106.8 16.9 %collective-permute-start.14 = (bf16[384,768]{1,0:T(8,128)(2,1)S(1)}, bf16[384,768]{1,0:T(8,128)(2,1)}, u32[]{:S(2)}, u32[]{:S(2)}) collective-permute-start(bf16[384,768]{1,0:T(8,128)(2,1)S(1)} %collective-permute-done.10.refs_4_.refs_5_), channel_id=1, source_target_pairs={{0,1},{1,0},{2,3},{3,2},{4,5},{5,4},{6,7},{7,6},{8,9},{9,8},{10,11... | collective-permute-start | bytes 1769480 | tf_op jit(solution)/shard_map/ppermute | solution.py:400
  123.8 16.5 %collective-permute-start.16 = (bf16[384,768]{1,0:T(8,128)(2,1)}, bf16[384,768]{1,0:T(8,128)(2,1)}, u32[]{:S(2)}, u32[]{:S(2)}) collective-permute-start(bf16[384,768]{1,0:T(8,128)(2,1)} %collective-permute-done.14.refs_5_.refs_6_), channel_id=1, source_target_pairs={{0,4},{4,0},{8,12},{12,8},{1,5},{5,1},{9,13},{13,9},{2,6},{6,2},{1... | collective-permute-start | bytes 1769480 | tf_op jit(solution)/shard_map/ppermute | solution.py:400
  124.9 17.0 %collective-permute-start.23 = (bf16[384,768]{1,0:T(8,128)(2,1)S(1)}, bf16[384,768]{1,0:T(8,128)(2,1)}, u32[]{:S(2)}, u32[]{:S(2)}) collective-permute-start(bf16[384,768]{1,0:T(8,128)(2,1)S(1)} %get-tuple-element.163.refs_0_.refs_1_), channel_id=1, source_target_pairs={{0,8},{4,12},{8,0},{12,4},{1,9},{5,13},{9,1},{13,5},{2,10},{6,14},... | collective-permute-start | bytes 1769480 | tf_op jit(solution)/shard_map/ppermute | solution.py:400
  125.4 17.6 %collective-permute-start.21 = (bf16[384,768]{1,0:T(8,128)(2,1)}, bf16[384,768]{1,0:T(8,128)(2,1)}, u32[]{:S(2)}, u32[]{:S(2)}) collective-permute-start(bf16[384,768]{1,0:T(8,128)(2,1)} %collective-permute-done.19.refs_12_.refs_13_), channel_id=1, source_target_pairs={{0,4},{4,0},{8,12},{12,8},{1,5},{5,1},{9,13},{13,9},{2,6},{6,2},{1... | collective-permute-start | bytes 1769480 | tf_op jit(solution)/shard_map/ppermute | solution.py:400
  139.7 22.1 %collective-permute-start.25 = (bf16[384,768]{1,0:T(8,128)(2,1)S(1)}, bf16[384,768]{1,0:T(8,128)(2,1)S(1)}, u32[]{:S(2)}, u32[]{:S(2)}) collective-permute-start(bf16[384,768]{1,0:T(8,128)(2,1)S(1)} %get-tuple-element.171.refs_0_.refs_1_), channel_id=1, source_target_pairs={{0,8},{4,12},{8,0},{12,4},{1,9},{5,13},{9,1},{13,5},{2,10},{6,14},... | collective-permute-start | bytes 1769480 | tf_op jit(solution)/shard_map/ppermute | solution.py:400
  140.3 28.0 %collective-permute-start.26 = (bf16[384,768]{1,0:T(8,128)(2,1)}, bf16[384,768]{1,0:T(8,128)(2,1)}, u32[]{:S(2)}, u32[]{:S(2)}) collective-permute-start(bf16[384,768]{1,0:T(8,128)(2,1)} %get-tuple-element.175.refs_8_.refs_9_), channel_id=1, source_target_pairs={{0,8},{4,12},{8,0},{12,4},{1,9},{5,13},{9,1},{13,5},{2,10},{6,14},... | collective-permute-start | bytes 1769480 | tf_op jit(solution)/shard_map/ppermute | solution.py:400
  141.8 26.4 %collective-permute-start.24 = (bf16[384,768]{1,0:T(8,128)(2,1)}, bf16[384,768]{1,0:T(8,128)(2,1)S(1)}, u32[]{:S(2)}, u32[]{:S(2)}) collective-permute-start(bf16[384,768]{1,0:T(8,128)(2,1)} %collective-permute-done.23.refs_4_.refs_5_), channel_id=1, source_target_pairs={{0,1},{1,0},{2,3},{3,2},{4,5},{5,4},{6,7},{7,6},{8,9},{9,8},{10,11... | collective-permute-start | bytes 1769480 | tf_op jit(solution)/shard_map/ppermute | solution.py:400
  169.3 19.4 %collective-permute-start.31 = (bf16[384,768]{1,0:T(8,128)(2,1)S(1)}, bf16[384,768]{1,0:T(8,128)(2,1)}, u32[]{:S(2)}, u32[]{:S(2)}) collective-permute-start(bf16[384,768]{1,0:T(8,128)(2,1)S(1)} %collective-permute-done.25.refs_4_.refs_5_), channel_id=1, source_target_pairs={{0,1},{1,0},{2,3},{3,2},{4,5},{5,4},{6,7},{7,6},{8,9},{9,8},{10,11... | collective-permute-start | bytes 1769480 | tf_op jit(solution)/shard_map/ppermute | solution.py:400
  170.4 26.9 %collective-permute-start.32 = (bf16[384,768]{1,0:T(8,128)(2,1)}, bf16[384,768]{1,0:T(8,128)(2,1)}, u32[]{:S(2)}, u32[]{:S(2)}) collective-permute-start(bf16[384,768]{1,0:T(8,128)(2,1)} %collective-permute-done.26.refs_12_.refs_13_), channel_id=1, source_target_pairs={{0,1},{1,0},{2,3},{3,2},{4,5},{5,4},{6,7},{7,6},{8,9},{9,8},{10,11... | collective-permute-start | bytes 1769480 | tf_op jit(solution)/shard_map/ppermute | solution.py:400
  238.1 17.9 %collective-permute-start.41 = (bf16[2,768,768]{2,1,0:T(8,128)(2,1)}, bf16[2,768,768]{2,1,0:T(8,128)(2,1)S(1)}, u32[]{:S(2)}, u32[]{:S(2)}) collective-permute-start(bf16[2,768,768]{2,1,0:T(8,128)(2,1)} %get-tuple-element.184), channel_id=1, source_target_pairs={{0,4},{4,0},{8,12},{12,8},{1,5},{5,1},{9,13},{13,9},{2,6},{6,2},{1... | collective-permute-start | bytes 7077896 | tf_op jit(solution)/shard_map/ppermute | solution.py:400
  238.5 22.7 %collective-permute-start.42 = (bf16[2,768,768]{2,1,0:T(8,128)(2,1)}, bf16[2,768,768]{2,1,0:T(8,128)(2,1)S(1)}, u32[]{:S(2)}, u32[]{:S(2)}) collective-permute-start(bf16[2,768,768]{2,1,0:T(8,128)(2,1)} %get-tuple-element.186), channel_id=1, source_target_pairs={{0,4},{4,0},{8,12},{12,8},{1,5},{5,1},{9,13},{13,9},{2,6},{6,2},{1... | collective-permute-start | bytes 7077896 | tf_op jit(solution)/shard_map/ppermute | solution.py:400
  263.5 151.7 %reduce-scatter.8.cloned.1.call-start = ((), (), s32[]{:S(2)}) async-start(), calls=%async_computation.8 | async-start | bytes 1474560 | tf_op jit(solution)/shard_map/reduce_scatter | solution.py:443
  266.1 32.4 %collective-permute-start.43 = (bf16[768,768]{1,0:T(8,128)(2,1)}, bf16[768,768]{1,0:T(8,128)(2,1)}, u32[]{:S(2)}, u32[]{:S(2)}) collective-permute-start(bf16[768,768]{1,0:T(8,128)(2,1)} %slice_bitcast_fusion.4), channel_id=1, source_target_pairs={{0,8},{4,12},{8,0},{12,4},{1,9},{5,13},{9,1},{13,5},{2,10},{6,14},... | collective-permute-start | bytes 3538952 | tf_op jit(solution)/shard_map/ppermute | solution.py:400
  282.8 18.5 %collective-permute-start.44 = (bf16[2,768,768]{2,1,0:T(8,128)(2,1)}, bf16[2,768,768]{2,1,0:T(8,128)(2,1)S(1)}, u32[]{:S(2)}, u32[]{:S(2)}) collective-permute-start(bf16[2,768,768]{2,1,0:T(8,128)(2,1)} %get-tuple-element.196), channel_id=1, source_target_pairs={{0,4},{4,0},{8,12},{12,8},{1,5},{5,1},{9,13},{13,9},{2,6},{6,2},{1... | collective-permute-start | bytes 7077896 | tf_op jit(solution)/shard_map/ppermute | solution.py:400
  303.1 33.8 %collective-permute-start.45 = (bf16[768,768]{1,0:T(8,128)(2,1)}, bf16[768,768]{1,0:T(8,128)(2,1)}, u32[]{:S(2)}, u32[]{:S(2)}) collective-permute-start(bf16[768,768]{1,0:T(8,128)(2,1)} %slice_bitcast_fusion.3), channel_id=1, source_target_pairs={{0,8},{4,12},{8,0},{12,4},{1,9},{5,13},{9,1},{13,5},{2,10},{6,14},... | collective-permute-start | bytes 3538952 | tf_op jit(solution)/shard_map/ppermute | solution.py:400
  317.1 22.6 %collective-permute-start.46 = (bf16[2,768,768]{2,1,0:T(8,128)(2,1)}, bf16[2,768,768]{2,1,0:T(8,128)(2,1)}, u32[]{:S(2)}, u32[]{:S(2)}) collective-permute-start(bf16[2,768,768]{2,1,0:T(8,128)(2,1)} %get-tuple-element.205), channel_id=1, source_target_pairs={{0,4},{4,0},{8,12},{12,8},{1,5},{5,1},{9,13},{13,9},{2,6},{6,2},{1... | collective-permute-start | bytes 7077896 | tf_op jit(solution)/shard_map/ppermute | solution.py:400
  317.7 24.5 %collective-permute-start.47 = (bf16[2,768,768]{2,1,0:T(8,128)(2,1)}, bf16[2,768,768]{2,1,0:T(8,128)(2,1)}, u32[]{:S(2)}, u32[]{:S(2)}) collective-permute-start(bf16[2,768,768]{2,1,0:T(8,128)(2,1)} %get-tuple-element.207), channel_id=1, source_target_pairs={{0,4},{4,0},{8,12},{12,8},{1,5},{5,1},{9,13},{13,9},{2,6},{6,2},{1... | collective-permute-start | bytes 7077896 | tf_op jit(solution)/shard_map/ppermute | solution.py:400
  317.8 111.8 %reduce-scatter.10.cloned.1.call-start = ((), (), s32[]{:S(2)}) async-start(), calls=%async_computation.9 | async-start | bytes 1474560 | tf_op jit(solution)/shard_map/reduce_scatter | solution.py:443
  348.5 100.2 %collective-permute-start.52 = (bf16[192,768]{1,0:T(8,128)(2,1)}, bf16[192,768]{1,0:T(8,128)(2,1)}, u32[]{:S(2)}, u32[]{:S(2)}) collective-permute-start(bf16[192,768]{1,0:T(8,128)(2,1)} %slice_bitcast_fusion.11), channel_id=1, source_target_pairs={{0,8},{4,12},{8,0},{12,4},{1,9},{5,13},{9,1},{13,5},{2,10},{6,14},... | collective-permute-start | bytes 884744 | tf_op jit(solution)/shard_map/ppermute | solution.py:400
  352.2 31.7 %collective-permute-start.50 = (bf16[768,768]{1,0:T(8,128)(2,1)}, bf16[768,768]{1,0:T(8,128)(2,1)}, u32[]{:S(2)}, u32[]{:S(2)}) collective-permute-start(bf16[768,768]{1,0:T(8,128)(2,1)} %slice_bitcast_fusion.1), channel_id=1, source_target_pairs={{0,8},{4,12},{8,0},{12,4},{1,9},{5,13},{9,1},{13,5},{2,10},{6,14},... | collective-permute-start | bytes 3538952 | tf_op jit(solution)/shard_map/ppermute | solution.py:400
  352.8 56.0 %collective-permute-start.48 = (bf16[768,768]{1,0:T(8,128)(2,1)}, bf16[768,768]{1,0:T(8,128)(2,1)}, u32[]{:S(2)}, u32[]{:S(2)}) collective-permute-start(bf16[768,768]{1,0:T(8,128)(2,1)} %slice_bitcast_fusion.2), channel_id=1, source_target_pairs={{0,8},{4,12},{8,0},{12,4},{1,9},{5,13},{9,1},{13,5},{2,10},{6,14},... | collective-permute-start | bytes 3538952 | tf_op jit(solution)/shard_map/ppermute | solution.py:400
  367.1 44.3 %collective-permute-start.49 = (bf16[2,768,768]{2,1,0:T(8,128)(2,1)}, bf16[2,768,768]{2,1,0:T(8,128)(2,1)}, u32[]{:S(2)}, u32[]{:S(2)}) collective-permute-start(bf16[2,768,768]{2,1,0:T(8,128)(2,1)} %get-tuple-element.218), channel_id=1, source_target_pairs={{0,4},{4,0},{8,12},{12,8},{1,5},{5,1},{9,13},{13,9},{2,6},{6,2},{1... | collective-permute-start | bytes 7077896 | tf_op jit(solution)/shard_map/ppermute | solution.py:400
  367.3 89.5 %reduce-scatter.12.cloned.1.call-start = ((), (), s32[]{:S(2)}) async-start(), calls=%async_computation.10 | async-start | bytes 1474560 | tf_op jit(solution)/shard_map/reduce_scatter | solution.py:443
  420.8 27.9 %collective-permute-start.51 = (bf16[768,768]{1,0:T(8,128)(2,1)}, bf16[768,768]{1,0:T(8,128)(2,1)}, u32[]{:S(2)}, u32[]{:S(2)}) collective-permute-start(bf16[768,768]{1,0:T(8,128)(2,1)} %slice_bitcast_fusion), channel_id=1, source_target_pairs={{0,8},{4,12},{8,0},{12,4},{1,9},{5,13},{9,1},{13,5},{2,10},{6,14},... | collective-permute-start | bytes 3538952 | tf_op jit(solution)/shard_map/ppermute | solution.py:400
  422.3 96.9 %reduce-scatter.14.cloned.1.call-start = ((), (), s32[]{:S(2)}) async-start(), calls=%async_computation.11 | async-start | bytes 1474560 | tf_op jit(solution)/shard_map/reduce_scatter | solution.py:443
  450.5 40.8 %all-to-all-start.1 = ((bf16[8,208,448]{2,1,0:T(8,128)(2,1)}), bf16[8,208,448]{2,1,0:T(8,128)(2,1)}, u32[]{:S(2)}, u32[]{:S(2)}) async-start(bf16[8,208,448]{2,1,0:T(8,128)(2,1)} %fusion.6), calls=%async_computation.5 | async-start | bytes 3407872 | tf_op jit(solution)/shard_map/all_to_all | solution.py:667
  456.8 33.2 %collective-permute-start.53 = (bf16[2,192,768]{2,1,0:T(8,128)(2,1)S(1)}, bf16[2,192,768]{2,1,0:T(8,128)(2,1)}, u32[]{:S(2)}, u32[]{:S(2)}) collective-permute-start(bf16[2,192,768]{2,1,0:T(8,128)(2,1)S(1)} %dynamic-slice_bitcast_fusion), channel_id=1, source_target_pairs={{0,1},{1,0},{2,3},{3,2},{4,5},{5,4},{6,7},{7,6},{8,9},{9,8},{10,11... | collective-permute-start | bytes 1769480 | tf_op jit(solution)/shard_map/ppermute | solution.py:400
  458.9 23.9 %collective-permute-start.54 = (bf16[192,768]{1,0:T(8,128)(2,1)S(1)}, bf16[192,768]{1,0:T(8,128)(2,1)S(1)}, u32[]{:S(2)}, u32[]{:S(2)}) collective-permute-start(bf16[192,768]{1,0:T(8,128)(2,1)S(1)} %broadcast_select_fusion.8), channel_id=1, source_target_pairs={{0,16},{16,0},{1,17},{17,1},{2,18},{18,2},{3,19},{19,3},{4,20},{20... | collective-permute-start | bytes 884744 | tf_op jit(solution)/shard_map/ppermute | solution.py:400
  491.2 23.6 %collective-permute-start.56 = (bf16[1,192,768]{2,1,0:T(8,128)(2,1)S(1)}, bf16[1,192,768]{2,1,0:T(8,128)(2,1)S(1)}, u32[]{:S(2)}, u32[]{:S(2)}) collective-permute-start(bf16[1,192,768]{2,1,0:T(8,128)(2,1)S(1)} %bitcast.203), channel_id=1, source_target_pairs={{0,2},{1,3},{2,0},{3,1},{4,6},{5,7},{6,4},{7,5},{8,10},{9,11},{10,... | collective-permute-start | bytes 884744 | tf_op jit(solution)/shard_map/ppermute | solution.py:400
  492.9 26.2 %collective-permute-start.55 = (bf16[1,192,768]{2,1,0:T(8,128)(2,1)S(1)}, bf16[1,192,768]{2,1,0:T(8,128)(2,1)S(1)}, u32[]{:S(2)}, u32[]{:S(2)}) collective-permute-start(bf16[1,192,768]{2,1,0:T(8,128)(2,1)S(1)} %constant_dynamic-slice_fusion), channel_id=1, source_target_pairs={{0,2},{1,3},{2,0},{3,1},{4,6},{5,7},{6,4},{7,5},{8,10},{9,11},{10,... | collective-permute-start | bytes 884744 | tf_op jit(solution)/shard_map/ppermute | solution.py:400
  537.5 21.9 %collective-permute-start.60 = (bf16[1,192,768]{2,1,0:T(8,128)(2,1)S(1)}, bf16[1,192,768]{2,1,0:T(8,128)(2,1)S(1)}, u32[]{:S(2)}, u32[]{:S(2)}) collective-permute-start(bf16[1,192,768]{2,1,0:T(8,128)(2,1)S(1)} %fusion.14), channel_id=1, source_target_pairs={{0,2},{1,3},{2,0},{3,1},{4,6},{5,7},{6,4},{7,5},{8,10},{9,11},{10,... | collective-permute-start | bytes 884744 | tf_op jit(solution)/shard_map/ppermute | solution.py:400
  540.9 24.4 %collective-permute-start.61 = (bf16[1,192,768]{2,1,0:T(8,128)(2,1)S(1)}, bf16[1,192,768]{2,1,0:T(8,128)(2,1)S(1)}, u32[]{:S(2)}, u32[]{:S(2)}) collective-permute-start(bf16[1,192,768]{2,1,0:T(8,128)(2,1)S(1)} %fusion.15), channel_id=1, source_target_pairs={{0,2},{1,3},{2,0},{3,1},{4,6},{5,7},{6,4},{7,5},{8,10},{9,11},{10,... | collective-permute-start | bytes 884744 | tf_op jit(solution)/shard_map/ppermute | solution.py:400
  566.2 17.8 %collective-permute-start.64 = (bf16[2,192,768]{2,1,0:T(8,128)(2,1)}, bf16[2,192,768]{2,1,0:T(8,128)(2,1)}, u32[]{:S(2)}, u32[]{:S(2)}) collective-permute-start(bf16[2,192,768]{2,1,0:T(8,128)(2,1)} %maximum_select_fusion.5), channel_id=1, source_target_pairs={{0,1},{1,0},{2,3},{3,2},{4,5},{5,4},{6,7},{7,6},{8,9},{9,8},{10,11... | collective-permute-start | bytes 1769480 | tf_op jit(solution)/shard_map/ppermute | solution.py:400
  569.5 25.6 %collective-permute-start.65 = (bf16[2,192,768]{2,1,0:T(8,128)(2,1)}, bf16[2,192,768]{2,1,0:T(8,128)(2,1)}, u32[]{:S(2)}, u32[]{:S(2)}) collective-permute-start(bf16[2,192,768]{2,1,0:T(8,128)(2,1)} %maximum_select_fusion.4), channel_id=1, source_target_pairs={{0,1},{1,0},{2,3},{3,2},{4,5},{5,4},{6,7},{7,6},{8,9},{9,8},{10,11... | collective-permute-start | bytes 1769480 | tf_op jit(solution)/shard_map/ppermute | solution.py:400
  (143 other events, 1433.2 us)
Sparse Core Ops, SparseCore 0:
  263.6 47.9 reduce-scatter.5
  317.9 29.8 reduce-scatter.7
  367.4 29.0 reduce-scatter.9
  422.4 28.9 reduce-scatter.11
  453.5 40.1 reduce-scatter.13

commit v7 on v6

--- a/solution.py
+++ b/solution.py
@@ -49,10 +49,11 @@
     return jnp.sum(values, axis=1, keepdims=True)
 
 
-def columns(parts, lanes):
-    lane = lax.broadcasted_iota(jnp.int32, (parts[0].shape[0], lanes), 1)
-    total = jnp.zeros((parts[0].shape[0], lanes), F32)
-    for index, part in enumerate(parts):
+def columns(parts):
+    rows = next(iter(parts.values())).shape[0]
+    lane = lax.broadcasted_iota(jnp.int32, (rows, 8), 1)
+    total = jnp.zeros((rows, 8), F32)
+    for index, part in parts.items():
         total = jnp.where(lane == index, part, total)
     return total
 
@@ -93,7 +94,7 @@
 
 
 def attention_forward_kernel(
-    count, info, x_ref, col_ref, bqv_ref, *refs
+    count, info, x_ref, col_ref, *refs
 ):
     step = pl.program_id(0)
     pieces, (a1_ref, p_ref, soft_ref, o_ref, h_ref, held, sems) = refs[:count], refs[count:]
@@ -110,11 +111,11 @@
         ).astype(BF16)
         h_ref[...] = values + col[:, BIAS_OUT : BIAS_OUT + 1]
 
-    bias = bqv_ref[step]
+    bias = col_ref[info[step]]
     projected = matmul(held[step, :QKV], a1_ref[...])
-    queries = (projected[:FEATS] + bias[:, 0:1]).astype(BF16)
+    queries = (projected[:FEATS] + bias[:, BIAS_Q : BIAS_Q + 1]).astype(BF16)
     keys = projected[FEATS : 2 * FEATS].astype(BF16)
-    values = (projected[2 * FEATS :] + bias[:, 1:2]).astype(BF16)
+    values = (projected[2 * FEATS :] + bias[:, BIAS_V : BIAS_V + 1]).astype(BF16)
     p_ref[0, :FEATS] = queries
     p_ref[0, FEATS : 2 * FEATS] = keys
     p_ref[0, 2 * FEATS :] = values
@@ -149,7 +150,7 @@
         a2_rows[...] = scaled.T.astype(BF16)
         total[...] = jnp.zeros_like(total)
 
-    inner = matmul(a2_rows[...], held_one[step]) + b1_ref[step]
+    inner = matmul(a2_rows[...], held_one[step]) + b1_ref[info[step]]
     phi = 0.5 + 0.5 * lax.erf(inner * 0.7071067811865476)
     density = 0.3989422804014327 * jnp.exp(-0.5 * inner * inner)
     active = (inner * phi).astype(BF16)
@@ -182,13 +183,14 @@
     @pl.when(step == 0)
     def first():
         gy_rows[...] = gy_ref[...].astype(F32).T.astype(BF16)
+        db1_ref[...] = jnp.zeros_like(db1_ref)
         total[...] = before_ref[...] if last else jnp.zeros_like(total)
 
     slot = info[(7 if last else 5) + step]
     d_active = matmul(gy_rows[...], held_two[slot], 1, 1)
     d_inner = d_active * slope_ref[0].astype(F32)
     rounded = d_inner.astype(BF16)
-    db1_ref[step] = jnp.sum(rounded.astype(F32), axis=0, keepdims=True)
+    db1_ref[info[slot]] = jnp.sum(rounded.astype(F32), axis=0, keepdims=True)
     grad_two[0] = matmul(u_ref[0], gy_rows[...], 0, 0).astype(BF16)
     grad_one[0] = matmul(a2_ref[...], rounded).astype(BF16)
     total[...] += matmul(rounded, held_one[slot], 1, 1)
@@ -205,8 +207,13 @@
         d_hidden = upstream + norm_backward(d_mid, normed, inv_std, col[:, GAIN2 : GAIN2 + 1])
         gh_ref[...] = d_hidden
         dcol_ref[...] = columns(
-            [row_sums(d_mid * normed), row_sums(d_mid), row_sums(d_hidden), row_sums(upstream)], 8
-        )
+            {
+                GAIN2: row_sums(d_mid * normed),
+                SHIFT2: row_sums(d_mid),
+                BIAS_OUT: row_sums(d_hidden),
+                BIAS_FC2: row_sums(upstream),
+            }
+        ).reshape(COLS)
 
 
 def attention_backward_kernel(
@@ -227,6 +234,7 @@
     @pl.when(step == 0)
     def first():
         gh_rounded[...] = gh_ref[...].astype(BF16)
+        dbqv_ref[...] = jnp.zeros_like(dbqv_ref)
         total[...] = before_ref[...] if last else jnp.zeros_like(total)
 
     slot = info[(7 if last else 5) + step]
@@ -254,9 +262,11 @@
     d_projected = g_p[...]
     grad_ref[0, :QKV] = matmul(d_projected, a1_ref[...], 1, 1).astype(BF16)
     total[...] += matmul(d_projected, held[slot, :QKV], 0, 0)
-    dbqv_ref[step] = columns(
-        [row_sums(d_projected[:FEATS].astype(F32)), row_sums(d_projected[2 * FEATS :].astype(F32))],
-        8,
+    dbqv_ref[info[slot]] = columns(
+        {
+            BIAS_Q: row_sums(d_projected[:FEATS].astype(F32)),
+            BIAS_V: row_sums(d_projected[2 * FEATS :].astype(F32)),
+        }
     )
 
     @pl.when(step == 1)
@@ -270,7 +280,9 @@
         gx_ref[...] = gh_ref[...] + norm_backward(
             d_first, normed, inv_std, col[:, GAIN1 : GAIN1 + 1]
         )
-        dcol_ref[...] = columns([row_sums(d_first * normed), row_sums(d_first)], 8)
+        dcol_ref[...] = columns(
+            {GAIN1: row_sums(d_first * normed), SHIFT1: row_sums(d_first)}
+        ).reshape(COLS)
 
 
 def whole(shape):
@@ -321,10 +333,10 @@
 MLP_FLOPS = 4 * FRAMES * D * SHARDS * FF_SHARD
 
 
-def attention_forward(info, x, col, bqv, chunk):
+def attention_forward(info, x, col, chunk):
     return run(
-        functools.partial(attention_forward_kernel, len(chunk)), "attention_forward", SHARDS, info, (x, col, bqv, *chunk),
-        [whole(STREAM), whole(COLS), whole((SHARDS, FEATS, 2))] + PIECE * len(chunk),
+        functools.partial(attention_forward_kernel, len(chunk)), "attention_forward", SHARDS, info, (x, col, *chunk),
+        [whole(STREAM), whole(COLS)] + PIECE * len(chunk),
         [
             of(STREAM), of((SHARDS, QKV, FRAMES)), of((SHARDS, HEADS_SHARD, FRAMES, FRAMES)),
             of((SHARDS, FEATS, FRAMES)), of(STREAM, F32),
@@ -352,7 +364,7 @@
 def mlp_backward(info, gy, h, a2, col, u, slope, before, chunk_one, chunk_two):
     last = before is not None
     carried = (before,) if last else ()
-    ends = [of(STREAM, F32), of((D, 8), F32)] if last else [of(ROWS, F32)]
+    ends = [of(STREAM, F32), of(COLS, F32)] if last else [of(ROWS, F32)]
     return run(
         functools.partial(mlp_backward_kernel, last, (len(chunk_one), len(chunk_two))), "mlp_backward", 2, info,
         (gy, h, a2, col, u, slope, *carried, *chunk_one, *chunk_two),
@@ -362,9 +374,9 @@
         ]
         + [whole(ROWS)] * len(carried)
         + PIECE * len(chunk_one + chunk_two),
-        ends + [of((2, D, D)), of((2, D, D)), of((2, 1, FF_SHARD), F32)],
+        ends + [of((2, D, D)), of((2, D, D)), of((SHARDS, 1, FF_SHARD), F32)],
         [whole(end.shape) for end in ends]
-        + [by_step((D, D)), by_step((D, D)), whole((2, 1, FF_SHARD))],
+        + [by_step((D, D)), by_step((D, D)), whole((SHARDS, 1, FF_SHARD))],
         [HELD, HELD, pltpu.VMEM(ROWS, BF16), pltpu.VMEM(ROWS, F32), COPY_SEMS, COPY_SEMS],
         MLP_FLOPS,
     )
@@ -373,7 +385,7 @@
 def attention_backward(info, gh, x, a1, col, p, soft, o, before, chunk):
     last = before is not None
     carried = (before,) if last else ()
-    ends = [of(STREAM, F32), of((D, 8), F32)] if last else [of(ROWS, F32)]
+    ends = [of(STREAM, F32), of(COLS, F32)] if last else [of(ROWS, F32)]
     return run(
         functools.partial(attention_backward_kernel, last, len(chunk)), "attention_backward", 2, info,
         (gh, x, a1, col, p, soft, o, *carried, *chunk),
@@ -384,8 +396,8 @@
         ]
         + [whole(ROWS)] * len(carried)
         + PIECE * len(chunk),
-        ends + [of((2, D, D)), of((2, FEATS, 8), F32)],
-        [whole(end.shape) for end in ends] + [by_step((D, D)), whole((2, FEATS, 8))],
+        ends + [of((2, D, D)), of(COLS, F32)],
+        [whole(end.shape) for end in ends] + [by_step((D, D)), whole(COLS)],
         [HELD, pltpu.VMEM(STREAM, BF16), pltpu.VMEM((QKV, FRAMES), BF16), pltpu.VMEM(ROWS, F32), COPY_SEMS],
         ATT_FLOPS,
     )
@@ -404,25 +416,34 @@
     return (left.astype(F32) + right.astype(F32)).astype(BF16)
 
 
+def sum_kernel(left_ref, right_ref, *out_refs):
+    for index, out_ref in enumerate(out_refs):
+        place = index if len(out_refs) > 1 else Ellipsis
+        out_ref[...] = added(left_ref[place], right_ref[place])
+
+
+def summed(left, right, outs):
+    rows = left.shape[-2]
+    block = 384 if rows % 384 == 0 else rows
+    spec = pl.BlockSpec((block, D), lambda i: (i, 0))
+    pair = pl.BlockSpec((2, block, D), lambda i: (0, i, 0))
+    return pl.pallas_call(
+        sum_kernel,
+        name="row_sums",
+        grid=(rows // block,),
+        in_specs=[pair if outs == 2 else spec] * 2,
+        out_specs=[spec] * outs,
+        out_shape=[jax.ShapeDtypeStruct((rows, D), BF16)] * outs,
+        compiler_params=pltpu.CompilerParams(vmem_limit_bytes=VMEM_LIMIT),
+        cost_estimate=pl.CostEstimate(flops=2**36, bytes_accessed=2**28, transcendentals=0),
+    )(left, right)
+
+
 def with_rows(blocks, small):
     pad = ((0, 0), (0, 16 - small.shape[1]), (0, blocks.shape[2] - small.shape[2]))
     return jnp.concatenate([blocks, jnp.pad(small.astype(BF16), pad)], axis=1)
 
 
-def by_bits(slots, shard):
-    odd = shard % 2 == 1
-    high = shard >= 2
-    first, second, third, fourth = slots
-    first, second = jnp.where(odd, second, first), jnp.where(odd, first, second)
-    third, fourth = jnp.where(odd, fourth, third), jnp.where(odd, third, fourth)
-    return jnp.stack(
-        [
-            jnp.where(high, third, first), jnp.where(high, fourth, second),
-            jnp.where(high, first, third), jnp.where(high, second, fourth),
-        ]
-    )
-
-
 def rows_of(value, place, parts):
     size = value.shape[-2] // parts
     return lax.dynamic_slice_in_dim(value, place * size, size, axis=value.ndim - 2)
@@ -433,18 +454,22 @@
         self.arrived = flip(send, "tensor", 1)
 
     def cores(self, keep):
-        self.value = added(keep, self.arrived)
+        self.value = summed(keep, self.arrived, 2)
 
     def scatter(self):
         parts = lax.axis_size("dp")
-        rows = self.value.shape[-2] // parts
-        split = self.value.reshape(-1, parts, rows, D)
-        split = jnp.swapaxes(split, 0, 1)
+        both = self.value if isinstance(self.value, (list, tuple)) else [self.value]
+        split = jnp.stack([value.reshape(parts, -1, D) for value in both], axis=1)
         total = lax.psum_scatter(split, "dp", scatter_dimension=0, tiled=False)
-        self.value = total if self.value.ndim == 3 else total[0]
+        self.value = total if len(both) == 2 else total[0]
 
     def send_y(self):
         self.kept, self.arrived = self.value[1], flip(self.value[0], "tensor", 2)
+
+    def fold_rows(self):
+        rows = self.kept.shape
+        (total,) = summed(self.kept.reshape(-1, D), self.arrived.reshape(-1, D), 1)
+        self.value = total.reshape(rows)
 
     def send_x(self, first, second):
         section = lax.axis_index("section")
@@ -509,12 +534,10 @@
     ends = ends_in[0].T.reshape(FEATS, clips, FRAMES).transpose(1, 0, 2)
     ends = with_rows(ends, jnp.broadcast_to(small, (clips,) + small.shape))
     ends = lax.all_to_all(ends, ("section", "tensor"), split_axis=0, concat_axis=0, tiled=True)
-    small = ends[:, FEATS : FEATS + 12, :FEATS].reshape(2, SHARDS, 12, FEATS).astype(F32)
+    small = ends[:, FEATS : FEATS + 12, :FEATS].astype(F32)
+    cols = jnp.swapaxes(small[:, :8], 1, 2).reshape(2, SHARDS, FEATS, 8)
+    b1s = small[:, 8:].reshape(2, SHARDS, 1, FF_SHARD)
     ends = ends[:, :FEATS].reshape(2, D, FRAMES)
-    cols = jnp.transpose(small[:, :, :8], (0, 1, 3, 2))
-    slots = by_bits([small[:, index] for index in range(SHARDS)], shard)
-    bqvs = jnp.transpose(slots[:, :, 4:6], (1, 0, 3, 2))
-    b1s = jnp.transpose(slots[:, :, 8:], (1, 0, 2, 3)).reshape(2, SHARDS, 1, FF_SHARD)
 
     def layers(own, other):
         return jnp.where(section == 0, own, other), jnp.where(section == 0, other, own)
@@ -542,24 +565,24 @@
     there_one = over_y(near_one[0])
 
     def attend(layer, stream, chunk):
-        return attention_forward(info, stream, cols[layer], bqvs[layer], chunk)
+        return attention_forward(info, stream, cols[layer], chunk)
 
     def feed(layer, h, chunk_one, chunk_two):
         return mlp_forward(info, h, cols[layer], b1s[layer], chunk_one, chunk_two)
 
+    there_one, beyond_two = tie((there_one, beyond_two))
+    away_one = flip(there_one, "dp", 1)
+    near_two = layers(nears[2], rows_of(beyond_two, zhalf, 2))
+    far_two = layers(fars[2], rows_of(beyond_two, 1 - zhalf, 2))
+    there_two = over_y(near_two[0])
     chunks = [[chunk_of((near_a[0], far_a[0]), (there_a, away_a))], []]
     stream = ends[0]
     a1, p, soft, o, h = attend(0, stream, chunks[0][0])
-    h, beyond_two, there_one, beyond_far_one, late_a, late_far_a, late_one = tie(
-        (h, beyond_two, there_one, beyond_far_one, near_a[1], far_a[1], near_one[1])
-    )
-    near_two = layers(nears[2], rows_of(beyond_two, zhalf, 2))
-    far_two = layers(fars[2], rows_of(beyond_two, 1 - zhalf, 2))
-    there_two = over_y(near_two[0])
+    h, away_one, there_two, beyond_far_one, late_a, late_far_a, late_one, late_two = tie(
+        (h, away_one, there_two, beyond_far_one, near_a[1], far_a[1], near_one[1], near_two[1])
+    )
     far_one = layers(fars[1], beyond_far_one)
-    away_one = flip(there_one, "dp", 1)
     chunks[0].append(chunk_of((near_one[0], far_one[0]), (there_one, away_one)))
-    there_two, late_a, late_one, late_two = tie((there_two, late_a, late_one, near_two[1]))
     chunks[0].append(chunk_of((near_two[0], far_two[0]), (there_two, flip(there_two, "dp", 1))))
     there_a, there_one, there_two = over_y(late_a), over_y(late_one), over_y(late_two)
     away_a = flip(there_a, "dp", 1)
@@ -604,7 +627,7 @@
         chain_two.cores(keep_two)
         chain_one.cores(keep_one)
         if layer == 0:
-            late_a.fold()
+            late_a.fold_rows()
             (gh,) = tied((late_a, last_two, last_one, late_one), gh)
             late_a.scatter()
             last_two.send_y()
@@ -622,99 +645,98 @@
         )
         chain_a.cores(keep_a)
         if layer == 1:
-            late_two.fold()
+            late_two.fold_rows()
             (upstream,) = tied((late_two, late_a), upstream)
             late_two.scatter()
             late_a.send_y()
         else:
-            last_two.fold()
+            last_two.fold_rows()
             (upstream,) = tied((last_two, last_a, late_two), upstream)
             last_two.scatter()
             last_a.send_y()
-        ends_of[layer] = (db1_kept, db1_sent, dbqv_kept, dbqv_sent, dcol_one, dcol_two)
-
-    upstream, ends_of = tie((upstream, ends_of))
+            late_one.send_y()
+        ends_of[layer] = (db1_kept, db1_sent, (dbqv_kept, dbqv_sent, dcol_one, dcol_two))
+
+    bits = [1 << k for k in range(n_dp.bit_length() - 1)]
+    pair_two, pair_one, pair_a = Chain(), Chain(), Chain()
+
+    def start_far(pair):
+        pair.value = pair.value[None]
+        pair.send_back(bits[-1])
+
+    def finish_far(pair):
+        pair.join(bits[-1])
+        for bit in bits[-2:0:-1]:
+            pair.send_back(bit)
+            pair.join(bit)
+
+    last_one.fold_rows()
+    tied((last_one, late_a))
+    last_one.scatter()
+
+    tied((last_two, late_two))
+    pair_two.send_x(last_two, late_two)
+
+    pair_two.fold()
+    upstream, ends_of = tied((pair_two,), upstream, ends_of)
+    start_far(pair_two)
     for layer in range(2):
-        db1_kept, db1_sent, dbqv_kept, dbqv_sent, dcol_one, dcol_two = ends_of[layer]
-        db1 = by_bits([db1_kept[1], db1_sent[1], db1_kept[0], db1_sent[0]], shard)
-        dbqv = by_bits([dbqv_kept[1], dbqv_sent[1], dbqv_kept[0], dbqv_sent[0]], shard)
-        dcol = jnp.concatenate(
+        db1_kept, db1_sent, dcols = ends_of[layer]
+        smalls[layer] = jnp.concatenate(
             [
-                dcol_one[:, 0:1], dcol_two[:, 0:1], dcol_one[:, 1:2], dcol_two[:, 1:2],
-                dbqv[:, :, 0:2].reshape(D, 2), dcol_two[:, 2:4],
+                jnp.swapaxes(sum(dcols), 1, 2),
+                (db1_kept + db1_sent).reshape(SHARDS, SHARDS, FEATS),
             ],
             axis=1,
         )
-        smalls[layer] = jnp.concatenate(
-            [
-                dcol.reshape(SHARDS, FEATS, 8).transpose(0, 2, 1),
-                db1.reshape(SHARDS, SHARDS, FEATS),
-            ],
-            axis=1,
-        )
-
     result = jnp.stack([upstream.astype(BF16), stream.astype(BF16)])
     result = with_rows(
         result.reshape(2 * SHARDS, FEATS, FRAMES), jnp.stack(smalls).reshape(-1, 12, FEATS)
     )
-
-    late_one.send_y()
-    bits = [1 << k for k in range(n_dp.bit_length() - 1)]
-
-    last_one.fold()
-    result, last_a.arrived = tied((last_one, late_a), result, last_a.arrived)
-    last_one.scatter()
     result = lax.all_to_all(result, ("section", "tensor"), split_axis=0, concat_axis=0, tiled=True)
+
+    last_a.fold_rows()
+    finish_far(pair_two)
+    tied((last_a, pair_two))
+    last_a.split()
+    last_a.send_half(bits[0])
+    pair_two.send_back(bits[0])
 
     last_a.fold()
     late_one.fold()
-    tied((last_a, late_one, last_two))
-    last_a.split()
-    last_a.send_half(bits[0])
-    pair_two, pair_one, pair_a = Chain(), Chain(), Chain()
-    pair_two.send_x(last_two, late_two)
-
-    last_a.fold()
-    pair_two.fold()
-    (result,) = tied((last_a, pair_two), result)
-    pair_two.value = pair_two.value[None]
+    tied((last_a, late_one, last_one))
     for bit in bits[1:]:
         last_a.send_half(bit)
         if bit != bits[-1]:
             last_a.fold()
-    pair_two.send_back(bits[-1])
+    pair_one.send_x(last_one, late_one)
+
+    pair_one.fold()
+    pair_two.join(bits[0])
+    (result,) = tied((pair_one, pair_two), result)
+    start_far(pair_one)
+    small_sum = result[:, FEATS : FEATS + 12, :FEATS].astype(F32).sum(axis=0)
+    result = result[:, :FEATS].transpose(1, 0, 2).reshape(FEATS, clips * FRAMES).T.astype(F32)
 
     last_a.fold()
     last_a.value = last_a.value[0]
-    pair_two.join(bits[-1])
-    for bit in bits[-2:0:-1]:
-        pair_two.send_back(bit)
-        pair_two.join(bit)
-    (result,) = tied((last_a, pair_two, last_one), result)
-    pair_one.send_x(last_one, late_one)
+    (small_sum,) = tied((last_a,), small_sum)
     pair_a.send_x(last_a, late_a)
-    pair_two.send_back(bits[0])
-    small_sum = result[:, FEATS : FEATS + 12, :FEATS].astype(F32).sum(axis=0)
-
-    for pair in (pair_one, pair_a):
-        pair.fold()
-        pair.value = pair.value[None]
-    pair_two.join(bits[0])
-    result, small_sum = tied((pair_one, pair_a, pair_two), result, small_sum)
+    finish_far(pair_one)
     small_sum += flip(small_sum, "dp", bits[0])
-    for bit in bits[:0:-1]:
-        for pair in (pair_one, pair_a):
-            pair.send_back(bit)
-        for pair in (pair_one, pair_a):
-            pair.join(bit)
-    result, small_sum = tied((pair_one, pair_a), result, small_sum)
+
+    pair_a.fold()
+    (small_sum,) = tied((pair_a, pair_one), small_sum)
+    start_far(pair_a)
+    pair_one.send_back(bits[0])
     for bit in bits[1:]:
         small_sum += flip(small_sum, "dp", bit)
-    for pair in (pair_one, pair_a):
-        pair.send_back(bits[0])
-    result = result[:, :FEATS].transpose(1, 0, 2).reshape(FEATS, clips * FRAMES).T.astype(F32)
-    for pair in (pair_one, pair_a):
-        pair.join(bits[0])
+
+    finish_far(pair_a)
+    pair_one.join(bits[0])
+    (small_sum,) = tied((pair_a, pair_one), small_sum)
+    pair_a.send_back(bits[0])
+    pair_a.join(bits[0])
     for pair in (pair_two, pair_one, pair_a):
         pair.value = pair.value.reshape(D, D)
 

time: 612 us -> 574 us (0.938)
  waiting for transfers between devices: 214 us -> 184 us
  other arithmetic: 61.5 us -> 37 us
  Pallas kernels: 168 us -> 192 us
  local copies, waits for them, and re-layouts: 84.1 us -> 74.3 us
    ppermute x66, waiting for transfers between devices: 214 us -> 170 us  [flip(): return lax.ppermute(block, axis, [(i, i ^ bit) for i in range(size)])]
    convert_element_type x14 -> x5, other arithmetic: 31.5 us -> 5.63 us  [added(): return (left.astype(F32) + right.astype(F32)).astype(BF16)]
    pallas_call x0 -> x11, Pallas kernels: none -> 24 us  [summed(): pl.pallas_call(sum_kernel, name='row_sums', grid=(rows // block,), in_spe...]
    unnamed x237 -> x233, local copies, waits for them, and re-layouts: 27.6 us -> 44 us
    reduce_scatter x5, waiting for transfers between devices: 0.05 us -> 13.5 us  [scatter(): total = lax.psum_scatter(split, 'dp', scatter_dimension=0, tiled=False)]
    squeeze x6 -> x1, local copies, waits for them, and re-layouts: 10 us -> 1.7 us  [send_y(): self.kept, self.arrived = (self.value[1], flip(self.value[0], 'tensor', 2))]
    select_n x12 -> x1, local copies, waits for them, and re-layouts: 7.17 us -> 0.08 us  [join(): jnp.where(upper, jnp.stack([self.arrived, self.value], axis=1), jnp.stack...]
  transfers between devices with their start and end apart: 73 -> 73, of which waited for: 27 -> 30; matrix products, arithmetic and copies ran while one was open for 18% -> 10% of each run, Pallas kernels for 24% -> 29%
where the time goes in v7:
time: 574 us; the launch traced here: 566 us
  Pallas kernels  192 us (33%)
  waiting for transfers between devices  184 us (32%)
  local copies, waits for them, and re-layouts  74.3 us (13%)
  starting transfers between devices  63.9 us (11%)
  other arithmetic  37 us (6%)
  between operations  15.6 us (3%)
    ppermute x66, waiting for transfers between devices, flip(): return lax.ppermute(block, axis, [(i, i ^ bit) for i in range(size)])  170 us
    pallas_call x12, Pallas kernels, run(): pl.pallas_call(kernel, name=name, out_shape=outs, grid_spec=pltpu.Prefetc...  168 us
    ppermute x66, starting transfers between devices, flip(): return lax.ppermute(block, axis, [(i, i ^ bit) for i in range(size)])  55.3 us
    unnamed x233, local copies, waits for them, and re-layouts  44 us
    pallas_call x11, Pallas kernels, summed(): pl.pallas_call(sum_kernel, name='row_sums', grid=(rows // block,), in_spe...  24 us
    reduce_scatter x5, waiting for transfers between devices, scatter(): total = lax.psum_scatter(split, 'dp', scatter_dimension=0, tiled=False)  13.5 us
  transfers between devices with their start and end apart: 73, of which 30 were waited for; matrix products, arithmetic and copies ran while one was open for 10% of the time, Pallas kernels for 29%

profile of v7, /device:TPU:0, one launch (start us, length us, event | category | flops | bytes accessed | tf_op | source)
XLA Modules:
  0.0 566.5 jit_solution(12501817278863752638)
XLA Ops:
  8.7 3.0 collective-permute-start
  16.5 4.4 all-to-all-start
  21.1 4.9 collective-permute-done
  32.9 22.2 %collective-permute-done.4.refs_4_.refs_5_ = bf16[384,768]{1,0:T(8,128)(2,1)} collective-permute-done((bf16[384,768]{1,0:T(8,128)(2,1)S(1)}, bf16[384,768]{1,0:T(8,128)(2,1)}, u32[]{:S(2)}, u32[]{:S(2)}) %collective-permute-start.4) | collective-permute-done | bytes 589856 | tf_op jit(solution)/shard_map/ppermute | solution.py:412
  68.5 2.3 collective-permute-done.6.refs_5_.refs_6_
  73.7 2.8 fusion.10
  76.4 4.9 collective-permute-done.10
  83.2 3.0 bitcast_select_fusion
  88.8 15.4 %attention_forward.2 = (bf16[768,448]{1,0:T(8,128)(2,1)S(1)}, bf16[4,576,448]{2,1,0:T(8,128)(2,1)}, bf16[4,3,448,448]{3,2,1,0:T(8,128)(2,1)}, bf16[4,192,448]{2,1,0:T(8,128)(2,1)}, f32[768,448]{1,0:T(8,128)}) custom-call(s32[9]{0:T(128)S(1)} %stack.113.info, bf16[768,448]{1,0:T(8,128)(2,1)} %bitcast.157, f32[4,192,8]{2,1,0:T(8,128)S(1)} %get-tuple-element.322.col_ref, ...), custom_call_target="tpu_custom_call" | custom-call | flops 43687870464 | bytes 268435456 | tf_op jit(solution)/shard_map/attention_forward/pallas_call | solution.py:311
  104.3 4.4 collective-permute-done.11.refs_5_.refs_6_
  115.3 9.4 %collective-permute-done.20.refs_13_.refs_14_ = bf16[384,768]{1,0:T(8,128)(2,1)} collective-permute-done((bf16[384,768]{1,0:T(8,128)(2,1)}, bf16[384,768]{1,0:T(8,128)(2,1)}, u32[]{:S(2)}, u32[]{:S(2)}) %collective-permute-start.20) | collective-permute-done | bytes 589856 | tf_op jit(solution)/shard_map/ppermute | solution.py:412
  136.2 13.5 %mlp_forward.2 = (bf16[768,448]{1,0:T(8,128)(2,1)}, bf16[4,448,768]{2,1,0:T(8,128)(2,1)}, bf16[4,448,768]{2,1,0:T(8,128)(2,1)}, f32[768,448]{1,0:T(8,128)}) custom-call(s32[9]{0:T(128)S(1)} %stack.113.info, f32[768,448]{1,0:T(8,128)} %get-tuple-element.167.h_ref, f32[4,192,8]{2,1,0:T(8,128)S(1)} %copy-done.16, f32[4,1,768]{2,1,0:T(1,128)S(1)} %squeeze.78.b1_ref, ...), custom_call_target="tpu_custom_call" | custom-call | flops 67645734912 | bytes 268435456 | tf_op jit(solution)/shard_map/mlp_forward/pallas_call | solution.py:311
  149.7 7.4 %collective-permute-done.26.refs_12_.refs_13_ = bf16[384,768]{1,0:T(8,128)(2,1)} collective-permute-done((bf16[384,768]{1,0:T(8,128)(2,1)}, bf16[384,768]{1,0:T(8,128)(2,1)}, u32[]{:S(2)}, u32[]{:S(2)}) %collective-permute-start.26) | collective-permute-done | bytes 589856 | tf_op jit(solution)/shard_map/ppermute | solution.py:412
  161.7 16.1 %attention_forward.3 = (bf16[768,448]{1,0:T(8,128)(2,1)S(1)}, bf16[4,576,448]{2,1,0:T(8,128)(2,1)}, bf16[4,3,448,448]{3,2,1,0:T(8,128)(2,1)}, bf16[4,192,448]{2,1,0:T(8,128)(2,1)}, f32[768,448]{1,0:T(8,128)}) custom-call(s32[9]{0:T(128)S(1)} %stack.113.info, f32[768,448]{1,0:T(8,128)} %get-tuple-element.176.x_ref, f32[4,192,8]{2,1,0:T(8,128)S(1)} %copy-done.18, ...), custom_call_target="tpu_custom_call" | custom-call | flops 43687870464 | bytes 268435456 | tf_op jit(solution)/shard_map/attention_forward/pallas_call | solution.py:311
  178.8 7.4 %collective-permute-done.32.refs_13_.refs_14_ = bf16[384,768]{1,0:T(8,128)(2,1)} collective-permute-done((bf16[384,768]{1,0:T(8,128)(2,1)}, bf16[384,768]{1,0:T(8,128)(2,1)}, u32[]{:S(2)}, u32[]{:S(2)}) %collective-permute-start.32) | collective-permute-done | bytes 589856 | tf_op jit(solution)/shard_map/ppermute | solution.py:412
  202.6 13.6 %mlp_forward.3 = (bf16[768,448]{1,0:T(8,128)(2,1)}, bf16[4,448,768]{2,1,0:T(8,128)(2,1)}, bf16[4,448,768]{2,1,0:T(8,128)(2,1)}, f32[768,448]{1,0:T(8,128)}) custom-call(s32[9]{0:T(128)S(1)} %stack.113.info, f32[768,448]{1,0:T(8,128)} %get-tuple-element.184.h_ref, f32[4,192,8]{2,1,0:T(8,128)S(1)} %copy-done.19, f32[4,1,768]{2,1,0:T(1,128)S(1)} %squeeze.79.b1_ref, ...), custom_call_target="tpu_custom_call" | custom-call | flops 67645734912 | bytes 268435456 | tf_op jit(solution)/shard_map/mlp_forward/pallas_call | solution.py:311
  216.3 12.1 %mlp_backward.4 = (f32[448,768]{1,0:T(8,128)}, bf16[2,768,768]{2,1,0:T(8,128)(2,1)}, bf16[2,768,768]{2,1,0:T(8,128)(2,1)}, f32[4,1,768]{2,1,0:T(1,128)S(1)}) custom-call(s32[9]{0:T(128)S(1)} %stack.113.info, bf16[768,448]{1,0:T(8,128)(2,1)} %bitcast.160, f32[768,448]{1,0:T(8,128)} %get-tuple-element.184.h_ref, bf16[768,448]{1,0:T(8,128)(2,1)} %get-tuple-element.193.a2_ref, ...), custom_call_target="tpu_custom_call" | custom-call | flops 67645734912 | bytes 268435456 | tf_op jit(solution)/shard_map/mlp_backward/pallas_call | solution.py:311
  229.0 14.2 %mlp_backward.5 = (f32[768,448]{1,0:T(8,128)}, f32[4,192,8]{2,1,0:T(8,128)S(1)}, bf16[2,768,768]{2,1,0:T(8,128)(2,1)}, bf16[2,768,768]{2,1,0:T(8,128)(2,1)}, f32[4,1,768]{2,1,0:T(1,128)S(1)}) custom-call(s32[9]{0:T(128)S(1)} %stack.113.info, bf16[768,448]{1,0:T(8,128)(2,1)} %bitcast.161, f32[768,448]{1,0:T(8,128)} %get-tuple-element.184.h_ref, ...), custom_call_target="tpu_custom_call" | custom-call | flops 67645734912 | bytes 268435456 | tf_op jit(solution)/shard_map/mlp_backward/pallas_call | solution.py:311
  245.4 2.9 row_sums.11
  261.6 12.5 %attention_backward.4 = (f32[448,768]{1,0:T(8,128)}, bf16[2,768,768]{2,1,0:T(8,128)(2,1)}, f32[4,192,8]{2,1,0:T(8,128)S(1)}) custom-call(s32[9]{0:T(128)S(1)} %stack.113.info, f32[768,448]{1,0:T(8,128)} %get-tuple-element.208.gh_ref, f32[768,448]{1,0:T(8,128)} %get-tuple-element.176.x_ref, bf16[768,448]{1,0:T(8,128)(2,1)} %copy-done.78, ...), custom_call_target="tpu_custom_call" | custom-call | flops 43687870464 | bytes 268435456 | tf_op jit(solution)/shard_map/attention_backward/pallas_call | solution.py:311
  275.1 15.5 %attention_backward.5 = (f32[768,448]{1,0:T(8,128)}, f32[4,192,8]{2,1,0:T(8,128)S(1)}, bf16[2,768,768]{2,1,0:T(8,128)(2,1)}, f32[4,192,8]{2,1,0:T(8,128)S(1)}) custom-call(s32[9]{0:T(128)S(1)} %stack.113.info, f32[768,448]{1,0:T(8,128)} %get-tuple-element.208.gh_ref, f32[768,448]{1,0:T(8,128)} %get-tuple-element.176.x_ref, bf16[768,448]{1,0:T(8,128)(2,1)} %copy-done.78, ...), custom_call_target="tpu_custom_call" | custom-call | flops 43687870464 | bytes 268435456 | tf_op jit(solution)/shard_map/attention_backward/pallas_call | solution.py:311
  290.6 2.6 row_sums.13
  294.6 2.9 row_sums.14
  298.3 12.3 %mlp_backward.6 = (f32[448,768]{1,0:T(8,128)}, bf16[2,768,768]{2,1,0:T(8,128)(2,1)}, bf16[2,768,768]{2,1,0:T(8,128)(2,1)}, f32[4,1,768]{2,1,0:T(1,128)S(1)}) custom-call(s32[9]{0:T(128)S(1)} %stack.113.info, f32[768,448]{1,0:T(8,128)} %get-tuple-element.221.gy_ref, f32[768,448]{1,0:T(8,128)} %get-tuple-element.167.h_ref, ...), custom_call_target="tpu_custom_call" | custom-call | flops 67645734912 | bytes 268435456 | tf_op jit(solution)/shard_map/mlp_backward/pallas_call | solution.py:311
  314.5 14.4 %mlp_backward.7 = (f32[768,448]{1,0:T(8,128)}, f32[4,192,8]{2,1,0:T(8,128)S(1)}, bf16[2,768,768]{2,1,0:T(8,128)(2,1)}, bf16[2,768,768]{2,1,0:T(8,128)(2,1)}, f32[4,1,768]{2,1,0:T(1,128)S(1)}) custom-call(s32[9]{0:T(128)S(1)} %stack.113.info, f32[768,448]{1,0:T(8,128)} %get-tuple-element.221.gy_ref, f32[768,448]{1,0:T(8,128)} %get-tuple-element.167.h_ref, ...), custom_call_target="tpu_custom_call" | custom-call | flops 67645734912 | bytes 268435456 | tf_op jit(solution)/shard_map/mlp_backward/pallas_call | solution.py:311
  329.0 2.4 row_sums.15
  346.0 12.7 %attention_backward.6 = (f32[448,768]{1,0:T(8,128)}, bf16[2,768,768]{2,1,0:T(8,128)(2,1)}, f32[4,192,8]{2,1,0:T(8,128)S(1)}) custom-call(s32[9]{0:T(128)S(1)} %stack.113.info, f32[768,448]{1,0:T(8,128)} %get-tuple-element.239.gh_ref, bf16[768,448]{1,0:T(8,128)(2,1)} %bitcast.158, bf16[768,448]{1,0:T(8,128)(2,1)} %copy-done.79, f32[4,192,8]{2,1,0:T(8,128)S(1)} %copy-done.17, ...), custom_call_target="tpu_custom_call" | custom-call | flops 43687870464 | bytes 268435456 | tf_op jit(solution)/shard_map/attention_backward/pallas_call | solution.py:311
  360.5 15.6 %attention_backward.7 = (f32[768,448]{1,0:T(8,128)}, f32[4,192,8]{2,1,0:T(8,128)S(1)}, bf16[2,768,768]{2,1,0:T(8,128)(2,1)}, f32[4,192,8]{2,1,0:T(8,128)S(1)}) custom-call(s32[9]{0:T(128)S(1)} %stack.113.info, f32[768,448]{1,0:T(8,128)} %get-tuple-element.239.gh_ref, bf16[768,448]{1,0:T(8,128)(2,1)} %bitcast.159, bf16[768,448]{1,0:T(8,128)(2,1)} %copy-done.79, ...), custom_call_target="tpu_custom_call" | custom-call | flops 43687870464 | bytes 268435456 | tf_op jit(solution)/shard_map/attention_backward/pallas_call | solution.py:311
  377.0 2.3 row_sums.18
  383.7 18.6 %collective-permute-done.55.right_ref = bf16[768,768]{1,0:T(8,128)(2,1)} collective-permute-done((bf16[768,768]{1,0:T(8,128)(2,1)}, bf16[768,768]{1,0:T(8,128)(2,1)}, u32[]{:S(2)}, u32[]{:S(2)}) %collective-permute-start.55) | collective-permute-done | bytes 1179680 | tf_op jit(solution)/shard_map/ppermute | solution.py:412
  403.6 2.2 row_sums.21
  405.8 13.5 %reduce-scatter.10.cloned.1.call-done = bf16[1,1,192,768]{3,2,1,0:T(8,128)(2,1)} async-done(((bf16[4,1,192,768]{3,2,1,0:T(8,128)(2,1)}), bf16[1,1,192,768]{3,2,1,0:T(8,128)(2,1)}) %reduce-scatter.10.cloned.1.call-update) | async-done | bytes 294928 | tf_op jit(solution)/shard_map/reduce_scatter | solution.py:463
  419.3 2.6 collective-permute-start.51
  421.9 4.8 collective-permute-done.50.right_ref
  431.7 2.6 collective-permute-start.52
  437.6 23.7 %collective-permute-done.52 = bf16[1,192,768]{2,1,0:T(8,128)(2,1)} collective-permute-done((bf16[1,192,768]{2,1,0:T(8,128)(2,1)}, bf16[1,192,768]{2,1,0:T(8,128)(2,1)}, u32[]{:S(2)}, u32[]{:S(2)}) %collective-permute-start.52) | collective-permute-done | bytes 294944 | tf_op jit(solution)/shard_map/ppermute | solution.py:412
  465.8 3.9 all-to-all-start.1
  472.9 7.7 %collective-permute-done.53 = bf16[2,192,768]{2,1,0:T(8,128)(2,1)} collective-permute-done((bf16[2,192,768]{2,1,0:T(8,128)(2,1)}, bf16[2,192,768]{2,1,0:T(8,128)(2,1)}, u32[]{:S(2)}, u32[]{:S(2)}) %collective-permute-start.53) | collective-permute-done | bytes 589856 | tf_op jit(solution)/shard_map/ppermute | solution.py:412
  483.8 2.5 collective-permute-start.56
  486.3 11.9 %collective-permute-done.57 = bf16[2,192,768]{2,1,0:T(8,128)(2,1)} collective-permute-done((bf16[2,192,768]{2,1,0:T(8,128)(2,1)}, bf16[2,192,768]{2,1,0:T(8,128)(2,1)}, u32[]{:S(2)}, u32[]{:S(2)}) %collective-permute-start.57) | collective-permute-done | bytes 589856 | tf_op jit(solution)/shard_map/ppermute | solution.py:412
  502.7 2.5 collective-permute-start.61
  505.2 3.4 collective-permute-done.61
  510.6 6.6 %collective-permute-done.60 = bf16[1,192,768]{2,1,0:T(8,128)(2,1)S(1)} collective-permute-done((bf16[1,192,768]{2,1,0:T(8,128)(2,1)}, bf16[1,192,768]{2,1,0:T(8,128)(2,1)S(1)}, u32[]{:S(2)}, u32[]{:S(2)}) %collective-permute-start.60) | collective-permute-done | bytes 294944 | tf_op jit(solution)/shard_map/ppermute | solution.py:412
  518.5 2.2 collective-permute-start.64
  524.9 2.4 reshape.217
  527.3 5.0 collective-permute-done.64
  532.3 5.8 %collective-permute-done.62 = bf16[1,192,768]{2,1,0:T(8,128)(2,1)S(1)} collective-permute-done((bf16[1,192,768]{2,1,0:T(8,128)(2,1)}, bf16[1,192,768]{2,1,0:T(8,128)(2,1)S(1)}, u32[]{:S(2)}, u32[]{:S(2)}) %collective-permute-start.62) | collective-permute-done | bytes 294944 | tf_op jit(solution)/shard_map/ppermute | solution.py:412
  547.3 9.6 %collective-permute-done.65 = bf16[2,192,768]{2,1,0:T(8,128)(2,1)S(1)} collective-permute-done((bf16[2,192,768]{2,1,0:T(8,128)(2,1)S(1)}, bf16[2,192,768]{2,1,0:T(8,128)(2,1)S(1)}, u32[]{:S(2)}, u32[]{:S(2)}) %collective-permute-start.65) | collective-permute-done | bytes 589856 | tf_op jit(solution)/shard_map/ppermute | solution.py:412
  (436 shorter events, 162.2 us)
Async XLA Ops:
  8.7 17.3 %collective-permute-start = (bf16[384,768]{1,0:T(8,128)(2,1)S(1)}, bf16[384,768]{1,0:T(8,128)(2,1)}, u32[]{:S(2)}, u32[]{:S(2)}) collective-permute-start(bf16[384,768]{1,0:T(8,128)(2,1)S(1)} %fusion.5), channel_id=1, source_target_pairs={{0,16},{16,0},{1,17},{17,1},{2,18},{18,2},{3,19},{19,3},{4,20},{20... | collective-permute-start | bytes 1769480 | tf_op jit(solution)/shard_map/ppermute | solution.py:412
  16.5 47.6 %all-to-all-start = ((bf16[8,208,448]{2,1,0:T(8,128)(2,1)}), bf16[8,208,448]{2,1,0:T(8,128)(2,1)}, u32[]{:S(2)}, u32[]{:S(2)}) async-start(bf16[8,208,448]{2,1,0:T(8,128)(2,1)} %copy.111), calls=%async_computation | async-start | bytes 3407872 | tf_op jit(solution)/shard_map/all_to_all | solution.py:536
  21.0 318.9 %reduce-scatter.6.cloned.1.call-start = ((), (), s32[]{:S(2)}) async-start(), calls=%async_computation.7 | async-start | bytes 2949120 | tf_op jit(solution)/shard_map/reduce_scatter | solution.py:463
  27.1 27.9 %collective-permute-start.4 = (bf16[384,768]{1,0:T(8,128)(2,1)S(1)}, bf16[384,768]{1,0:T(8,128)(2,1)}, u32[]{:S(2)}, u32[]{:S(2)}) collective-permute-start(bf16[384,768]{1,0:T(8,128)(2,1)S(1)} %get-tuple-element.320.refs_0_.refs_1_), channel_id=1, source_target_pairs={{0,8},{4,12},{8,0},{12,4},{1,9},{5,13},{9,1},{13,5},{2,10},{6,14},... | collective-permute-start | bytes 1769480 | tf_op jit(solution)/shard_map/ppermute | solution.py:412
  29.3 27.5 %collective-permute-start.5 = (bf16[384,768]{1,0:T(8,128)(2,1)S(1)}, bf16[384,768]{1,0:T(8,128)(2,1)S(1)}, u32[]{:S(2)}, u32[]{:S(2)}) collective-permute-start(bf16[384,768]{1,0:T(8,128)(2,1)S(1)} %dynamic-slice_bitcast_fusion.1), channel_id=1, source_target_pairs={{0,16},{16,0},{1,17},{17,1},{2,18},{18,2},{3,19},{19,3},{4,20},{20... | collective-permute-start | bytes 1769480 | tf_op jit(solution)/shard_map/ppermute | solution.py:412
  30.8 30.8 %collective-permute-start.1 = (bf16[384,768]{1,0:T(8,128)(2,1)}, bf16[384,768]{1,0:T(8,128)(2,1)}, u32[]{:S(2)}, u32[]{:S(2)}) collective-permute-start(bf16[384,768]{1,0:T(8,128)(2,1)} %collective-permute-done), channel_id=1, source_target_pairs={{0,1},{1,0},{2,3},{3,2},{4,5},{5,4},{6,7},{7,6},{8,9},{9,8},{10,11... | collective-permute-start | bytes 1769480 | tf_op jit(solution)/shard_map/ppermute | solution.py:412
  32.3 49.0 %collective-permute-start.10 = (bf16[768,768]{1,0:T(8,128)(2,1)}, bf16[768,768]{1,0:T(8,128)(2,1)}, u32[]{:S(2)}, u32[]{:S(2)}) collective-permute-start(bf16[768,768]{1,0:T(8,128)(2,1)} %bitcast.19), channel_id=1, source_target_pairs={{0,16},{16,0},{1,17},{17,1},{2,18},{18,2},{3,19},{19,3},{4,20},{20... | collective-permute-start | bytes 3538952 | tf_op jit(solution)/shard_map/ppermute | solution.py:412
  61.6 24.7 %collective-permute-start.2 = (bf16[384,768]{1,0:T(8,128)(2,1)S(1)}, bf16[384,768]{1,0:T(8,128)(2,1)}, u32[]{:S(2)}, u32[]{:S(2)}) collective-permute-start(bf16[384,768]{1,0:T(8,128)(2,1)S(1)} %get-tuple-element.320.refs_0_.refs_1_), channel_id=1, source_target_pairs={{0,4},{4,0},{8,12},{12,8},{1,5},{5,1},{9,13},{13,9},{2,6},{6,2},{1... | collective-permute-start | bytes 1769480 | tf_op jit(solution)/shard_map/ppermute | solution.py:412
  61.6 24.6 %collective-permute-start.7 = (bf16[384,768]{1,0:T(8,128)(2,1)}, bf16[384,768]{1,0:T(8,128)(2,1)}, u32[]{:S(2)}, u32[]{:S(2)}) collective-permute-start(bf16[384,768]{1,0:T(8,128)(2,1)} %collective-permute-done.4.refs_4_.refs_5_), channel_id=1, source_target_pairs={{0,4},{4,0},{8,12},{12,8},{1,5},{5,1},{9,13},{13,9},{2,6},{6,2},{1... | collective-permute-start | bytes 1769480 | tf_op jit(solution)/shard_map/ppermute | solution.py:412
  70.8 15.9 %collective-permute-start.3 = (bf16[384,768]{1,0:T(8,128)(2,1)S(1)}, bf16[384,768]{1,0:T(8,128)(2,1)S(1)}, u32[]{:S(2)}, u32[]{:S(2)}) collective-permute-start(bf16[384,768]{1,0:T(8,128)(2,1)S(1)} %get-tuple-element.314.refs_1_.refs_2_), channel_id=1, source_target_pairs={{0,4},{4,0},{8,12},{12,8},{1,5},{5,1},{9,13},{13,9},{2,6},{6,2},{1... | collective-permute-start | bytes 1769480 | tf_op jit(solution)/shard_map/ppermute | solution.py:412
  81.4 22.8 %collective-permute-start.13 = (bf16[384,768]{1,0:T(8,128)(2,1)S(1)}, bf16[384,768]{1,0:T(8,128)(2,1)S(1)}, u32[]{:S(2)}, u32[]{:S(2)}) collective-permute-start(bf16[384,768]{1,0:T(8,128)(2,1)S(1)} %copy-done.107), channel_id=1, source_target_pairs={{0,1},{1,0},{2,3},{3,2},{4,5},{5,4},{6,7},{7,6},{8,9},{9,8},{10,11... | collective-permute-start | bytes 1769480 | tf_op jit(solution)/shard_map/ppermute | solution.py:412
  86.2 25.2 %collective-permute-start.14 = (bf16[384,768]{1,0:T(8,128)(2,1)S(1)}, bf16[384,768]{1,0:T(8,128)(2,1)S(1)}, u32[]{:S(2)}, u32[]{:S(2)}) collective-permute-start(bf16[384,768]{1,0:T(8,128)(2,1)S(1)} %get-tuple-element.318.refs_0_.refs_1_), channel_id=1, source_target_pairs={{0,4},{4,0},{8,12},{12,8},{1,5},{5,1},{9,13},{13,9},{2,6},{6,2},{1... | collective-permute-start | bytes 1769480 | tf_op jit(solution)/shard_map/ppermute | solution.py:412
  86.3 26.2 %collective-permute-start.16 = (bf16[384,768]{1,0:T(8,128)(2,1)S(1)}, bf16[384,768]{1,0:T(8,128)(2,1)S(1)}, u32[]{:S(2)}, u32[]{:S(2)}) collective-permute-start(bf16[384,768]{1,0:T(8,128)(2,1)S(1)} %copy-done.35), channel_id=1, source_target_pairs={{0,4},{4,0},{8,12},{12,8},{1,5},{5,1},{9,13},{13,9},{2,6},{6,2},{1... | collective-permute-start | bytes 1769480 | tf_op jit(solution)/shard_map/ppermute | solution.py:412
  86.8 21.9 %collective-permute-start.11 = (bf16[384,768]{1,0:T(8,128)(2,1)S(1)}, bf16[384,768]{1,0:T(8,128)(2,1)}, u32[]{:S(2)}, u32[]{:S(2)}) collective-permute-start(bf16[384,768]{1,0:T(8,128)(2,1)S(1)} %copy-done.35), channel_id=1, source_target_pairs={{0,1},{1,0},{2,3},{3,2},{4,5},{5,4},{6,7},{7,6},{8,9},{9,8},{10,11... | collective-permute-start | bytes 1769480 | tf_op jit(solution)/shard_map/ppermute | solution.py:412
  87.0 21.7 %collective-permute-start.12 = (bf16[384,768]{1,0:T(8,128)(2,1)S(1)}, bf16[384,768]{1,0:T(8,128)(2,1)}, u32[]{:S(2)}, u32[]{:S(2)}) collective-permute-start(bf16[384,768]{1,0:T(8,128)(2,1)S(1)} %get-tuple-element.308.refs_8_.refs_9_), channel_id=1, source_target_pairs={{0,8},{4,12},{8,0},{12,4},{1,9},{5,13},{9,1},{13,5},{2,10},{6,14},... | collective-permute-start | bytes 1769480 | tf_op jit(solution)/shard_map/ppermute | solution.py:412
  108.7 16.1 %collective-permute-start.20 = (bf16[384,768]{1,0:T(8,128)(2,1)}, bf16[384,768]{1,0:T(8,128)(2,1)}, u32[]{:S(2)}, u32[]{:S(2)}) collective-permute-start(bf16[384,768]{1,0:T(8,128)(2,1)} %collective-permute-done.12.refs_12_.refs_13_), channel_id=1, source_target_pairs={{0,1},{1,0},{2,3},{3,2},{4,5},{5,4},{6,7},{7,6},{8,9},{9,8},{10,11... | collective-permute-start | bytes 1769480 | tf_op jit(solution)/shard_map/ppermute | solution.py:412
  112.3 16.1 %collective-permute-start.15 = (bf16[384,768]{1,0:T(8,128)(2,1)}, bf16[384,768]{1,0:T(8,128)(2,1)}, u32[]{:S(2)}, u32[]{:S(2)}) collective-permute-start(bf16[384,768]{1,0:T(8,128)(2,1)} %get-tuple-element.312.refs_1_.refs_2_), channel_id=1, source_target_pairs={{0,4},{4,0},{8,12},{12,8},{1,5},{5,1},{9,13},{13,9},{2,6},{6,2},{1... | collective-permute-start | bytes 1769480 | tf_op jit(solution)/shard_map/ppermute | solution.py:412
  113.3 16.6 %collective-permute-start.23 = (bf16[384,768]{1,0:T(8,128)(2,1)S(1)}, bf16[384,768]{1,0:T(8,128)(2,1)}, u32[]{:S(2)}, u32[]{:S(2)}) collective-permute-start(bf16[384,768]{1,0:T(8,128)(2,1)S(1)} %get-tuple-element.177.refs_0_.refs_1_), channel_id=1, source_target_pairs={{0,8},{4,12},{8,0},{12,4},{1,9},{5,13},{9,1},{13,5},{2,10},{6,14},... | collective-permute-start | bytes 1769480 | tf_op jit(solution)/shard_map/ppermute | solution.py:412
  114.9 17.1 %collective-permute-start.21 = (bf16[384,768]{1,0:T(8,128)(2,1)}, bf16[384,768]{1,0:T(8,128)(2,1)}, u32[]{:S(2)}, u32[]{:S(2)}) collective-permute-start(bf16[384,768]{1,0:T(8,128)(2,1)} %collective-permute-done.12.refs_12_.refs_13_), channel_id=1, source_target_pairs={{0,4},{4,0},{8,12},{12,8},{1,5},{5,1},{9,13},{13,9},{2,6},{6,2},{1... | collective-permute-start | bytes 1769480 | tf_op jit(solution)/shard_map/ppermute | solution.py:412
  128.4 21.3 %collective-permute-start.25 = (bf16[384,768]{1,0:T(8,128)(2,1)}, bf16[384,768]{1,0:T(8,128)(2,1)S(1)}, u32[]{:S(2)}, u32[]{:S(2)}) collective-permute-start(bf16[384,768]{1,0:T(8,128)(2,1)} %get-tuple-element.185.refs_0_.refs_1_), channel_id=1, source_target_pairs={{0,8},{4,12},{8,0},{12,4},{1,9},{5,13},{9,1},{13,5},{2,10},{6,14},... | collective-permute-start | bytes 1769480 | tf_op jit(solution)/shard_map/ppermute | solution.py:412
  129.9 27.2 %collective-permute-start.26 = (bf16[384,768]{1,0:T(8,128)(2,1)}, bf16[384,768]{1,0:T(8,128)(2,1)}, u32[]{:S(2)}, u32[]{:S(2)}) collective-permute-start(bf16[384,768]{1,0:T(8,128)(2,1)} %get-tuple-element.189.refs_8_.refs_9_), channel_id=1, source_target_pairs={{0,8},{4,12},{8,0},{12,4},{1,9},{5,13},{9,1},{13,5},{2,10},{6,14},... | collective-permute-start | bytes 1769480 | tf_op jit(solution)/shard_map/ppermute | solution.py:412
  130.5 26.7 %collective-permute-start.24 = (bf16[384,768]{1,0:T(8,128)(2,1)}, bf16[384,768]{1,0:T(8,128)(2,1)S(1)}, u32[]{:S(2)}, u32[]{:S(2)}) collective-permute-start(bf16[384,768]{1,0:T(8,128)(2,1)} %collective-permute-done.23.refs_4_.refs_5_), channel_id=1, source_target_pairs={{0,1},{1,0},{2,3},{3,2},{4,5},{5,4},{6,7},{7,6},{8,9},{9,8},{10,11... | collective-permute-start | bytes 1769480 | tf_op jit(solution)/shard_map/ppermute | solution.py:412
  158.2 20.6 %collective-permute-start.31 = (bf16[384,768]{1,0:T(8,128)(2,1)S(1)}, bf16[384,768]{1,0:T(8,128)(2,1)}, u32[]{:S(2)}, u32[]{:S(2)}) collective-permute-start(bf16[384,768]{1,0:T(8,128)(2,1)S(1)} %collective-permute-done.25.refs_4_.refs_5_), channel_id=1, source_target_pairs={{0,1},{1,0},{2,3},{3,2},{4,5},{5,4},{6,7},{7,6},{8,9},{9,8},{10,11... | collective-permute-start | bytes 1769480 | tf_op jit(solution)/shard_map/ppermute | solution.py:412
  159.7 26.6 %collective-permute-start.32 = (bf16[384,768]{1,0:T(8,128)(2,1)}, bf16[384,768]{1,0:T(8,128)(2,1)}, u32[]{:S(2)}, u32[]{:S(2)}) collective-permute-start(bf16[384,768]{1,0:T(8,128)(2,1)} %collective-permute-done.26.refs_12_.refs_13_), channel_id=1, source_target_pairs={{0,1},{1,0},{2,3},{3,2},{4,5},{5,4},{6,7},{7,6},{8,9},{9,8},{10,11... | collective-permute-start | bytes 1769480 | tf_op jit(solution)/shard_map/ppermute | solution.py:412
  228.4 15.9 %collective-permute-start.41 = (bf16[2,768,768]{2,1,0:T(8,128)(2,1)}, bf16[2,768,768]{2,1,0:T(8,128)(2,1)}, u32[]{:S(2)}, u32[]{:S(2)}) collective-permute-start(bf16[2,768,768]{2,1,0:T(8,128)(2,1)} %get-tuple-element.198), channel_id=1, source_target_pairs={{0,4},{4,0},{8,12},{12,8},{1,5},{5,1},{9,13},{13,9},{2,6},{6,2},{1... | collective-permute-start | bytes 7077896 | tf_op jit(solution)/shard_map/ppermute | solution.py:412
  228.8 19.4 %collective-permute-start.42 = (bf16[2,768,768]{2,1,0:T(8,128)(2,1)}, bf16[2,768,768]{2,1,0:T(8,128)(2,1)S(1)}, u32[]{:S(2)}, u32[]{:S(2)}) collective-permute-start(bf16[2,768,768]{2,1,0:T(8,128)(2,1)} %get-tuple-element.202), channel_id=1, source_target_pairs={{0,4},{4,0},{8,12},{12,8},{1,5},{5,1},{9,13},{13,9},{2,6},{6,2},{1... | collective-permute-start | bytes 7077896 | tf_op jit(solution)/shard_map/ppermute | solution.py:412
  252.0 38.6 %collective-permute-start.43 = (bf16[768,768]{1,0:T(8,128)(2,1)}, bf16[768,768]{1,0:T(8,128)(2,1)}, u32[]{:S(2)}, u32[]{:S(2)}) collective-permute-start(bf16[768,768]{1,0:T(8,128)(2,1)} %get-tuple-element.207), channel_id=1, source_target_pairs={{0,8},{4,12},{8,0},{12,4},{1,9},{5,13},{9,1},{13,5},{2,10},{6,14},... | collective-permute-start | bytes 3538952 | tf_op jit(solution)/shard_map/ppermute | solution.py:412
  255.1 127.3 %reduce-scatter.8.cloned.1.call-start = ((), (), s32[]{:S(2)}) async-start(), calls=%async_computation.8 | async-start | bytes 1474560 | tf_op jit(solution)/shard_map/reduce_scatter | solution.py:463
  274.9 18.3 %collective-permute-start.44 = (bf16[2,768,768]{2,1,0:T(8,128)(2,1)}, bf16[2,768,768]{2,1,0:T(8,128)(2,1)S(1)}, u32[]{:S(2)}, u32[]{:S(2)}) collective-permute-start(bf16[2,768,768]{2,1,0:T(8,128)(2,1)} %get-tuple-element.215), channel_id=1, source_target_pairs={{0,4},{4,0},{8,12},{12,8},{1,5},{5,1},{9,13},{13,9},{2,6},{6,2},{1... | collective-permute-start | bytes 7077896 | tf_op jit(solution)/shard_map/ppermute | solution.py:412
  297.5 31.4 %collective-permute-start.45 = (bf16[768,768]{1,0:T(8,128)(2,1)}, bf16[768,768]{1,0:T(8,128)(2,1)}, u32[]{:S(2)}, u32[]{:S(2)}) collective-permute-start(bf16[768,768]{1,0:T(8,128)(2,1)} %get-tuple-element.220), channel_id=1, source_target_pairs={{0,8},{4,12},{8,0},{12,4},{1,9},{5,13},{9,1},{13,5},{2,10},{6,14},... | collective-permute-start | bytes 3538952 | tf_op jit(solution)/shard_map/ppermute | solution.py:412
  310.7 20.7 %collective-permute-start.46 = (bf16[2,768,768]{2,1,0:T(8,128)(2,1)}, bf16[2,768,768]{2,1,0:T(8,128)(2,1)}, u32[]{:S(2)}, u32[]{:S(2)}) collective-permute-start(bf16[2,768,768]{2,1,0:T(8,128)(2,1)} %get-tuple-element.227), channel_id=1, source_target_pairs={{0,4},{4,0},{8,12},{12,8},{1,5},{5,1},{9,13},{13,9},{2,6},{6,2},{1... | collective-permute-start | bytes 7077896 | tf_op jit(solution)/shard_map/ppermute | solution.py:412
  310.9 24.7 %collective-permute-start.47 = (bf16[2,768,768]{2,1,0:T(8,128)(2,1)}, bf16[2,768,768]{2,1,0:T(8,128)(2,1)}, u32[]{:S(2)}, u32[]{:S(2)}) collective-permute-start(bf16[2,768,768]{2,1,0:T(8,128)(2,1)} %get-tuple-element.231), channel_id=1, source_target_pairs={{0,4},{4,0},{8,12},{12,8},{1,5},{5,1},{9,13},{13,9},{2,6},{6,2},{1... | collective-permute-start | bytes 7077896 | tf_op jit(solution)/shard_map/ppermute | solution.py:412
  311.3 94.5 %reduce-scatter.12.cloned.1.call-start = ((), (), s32[]{:S(2)}) async-start(), calls=%async_computation.10 | async-start | bytes 1474560 | tf_op jit(solution)/shard_map/reduce_scatter | solution.py:463
  341.6 128.2 %collective-permute-start.54 = (bf16[192,768]{1,0:T(8,128)(2,1)}, bf16[192,768]{1,0:T(8,128)(2,1)}, u32[]{:S(2)}, u32[]{:S(2)}) collective-permute-start(bf16[192,768]{1,0:T(8,128)(2,1)} %slice_bitcast_fusion.2), channel_id=1, source_target_pairs={{0,8},{4,12},{8,0},{12,4},{1,9},{5,13},{9,1},{13,5},{2,10},{6,14},... | collective-permute-start | bytes 884744 | tf_op jit(solution)/shard_map/ppermute | solution.py:412
  342.9 34.1 %collective-permute-start.48 = (bf16[768,768]{1,0:T(8,128)(2,1)}, bf16[768,768]{1,0:T(8,128)(2,1)}, u32[]{:S(2)}, u32[]{:S(2)}) collective-permute-start(bf16[768,768]{1,0:T(8,128)(2,1)} %copy-done.26), channel_id=1, source_target_pairs={{0,8},{4,12},{8,0},{12,4},{1,9},{5,13},{9,1},{13,5},{2,10},{6,14},... | collective-permute-start | bytes 3538952 | tf_op jit(solution)/shard_map/ppermute | solution.py:412
  343.6 58.7 %collective-permute-start.55 = (bf16[768,768]{1,0:T(8,128)(2,1)}, bf16[768,768]{1,0:T(8,128)(2,1)}, u32[]{:S(2)}, u32[]{:S(2)}) collective-permute-start(bf16[768,768]{1,0:T(8,128)(2,1)} %copy-done.25), channel_id=1, source_target_pairs={{0,8},{4,12},{8,0},{12,4},{1,9},{5,13},{9,1},{13,5},{2,10},{6,14},... | collective-permute-start | bytes 3538952 | tf_op jit(solution)/shard_map/ppermute | solution.py:412
  359.4 19.9 %collective-permute-start.49 = (bf16[2,768,768]{2,1,0:T(8,128)(2,1)}, bf16[2,768,768]{2,1,0:T(8,128)(2,1)}, u32[]{:S(2)}, u32[]{:S(2)}) collective-permute-start(bf16[2,768,768]{2,1,0:T(8,128)(2,1)} %get-tuple-element.246), channel_id=1, source_target_pairs={{0,4},{4,0},{8,12},{12,8},{1,5},{5,1},{9,13},{13,9},{2,6},{6,2},{1... | collective-permute-start | bytes 7077896 | tf_op jit(solution)/shard_map/ppermute | solution.py:412
  359.4 59.9 %reduce-scatter.10.cloned.1.call-start = ((), (), s32[]{:S(2)}) async-start(), calls=%async_computation.9 | async-start | bytes 1474560 | tf_op jit(solution)/shard_map/reduce_scatter | solution.py:463
  382.4 44.3 %collective-permute-start.50 = (bf16[768,768]{1,0:T(8,128)(2,1)S(1)}, bf16[768,768]{1,0:T(8,128)(2,1)S(1)}, u32[]{:S(2)}, u32[]{:S(2)}) collective-permute-start(bf16[768,768]{1,0:T(8,128)(2,1)S(1)} %get-tuple-element.252), channel_id=1, source_target_pairs={{0,8},{4,12},{8,0},{12,4},{1,9},{5,13},{9,1},{13,5},{2,10},{6,14},... | collective-permute-start | bytes 3538952 | tf_op jit(solution)/shard_map/ppermute | solution.py:412
  383.6 99.0 %reduce-scatter.14.cloned.1.call-start = ((), (), s32[]{:S(2)}) async-start(), calls=%async_computation.11 | async-start | bytes 1474560 | tf_op jit(solution)/shard_map/reduce_scatter | solution.py:463
  431.7 29.6 %collective-permute-start.52 = (bf16[1,192,768]{2,1,0:T(8,128)(2,1)}, bf16[1,192,768]{2,1,0:T(8,128)(2,1)}, u32[]{:S(2)}, u32[]{:S(2)}) collective-permute-start(bf16[1,192,768]{2,1,0:T(8,128)(2,1)} %bitcast.153), channel_id=1, source_target_pairs={{0,2},{1,3},{2,0},{3,1},{4,6},{5,7},{6,4},{7,5},{8,10},{9,11},{10,... | collective-permute-start | bytes 884744 | tf_op jit(solution)/shard_map/ppermute | solution.py:412
  464.1 16.6 %collective-permute-start.53 = (bf16[2,192,768]{2,1,0:T(8,128)(2,1)}, bf16[2,192,768]{2,1,0:T(8,128)(2,1)}, u32[]{:S(2)}, u32[]{:S(2)}) collective-permute-start(bf16[2,192,768]{2,1,0:T(8,128)(2,1)} %dynamic-slice_bitcast_fusion), channel_id=1, source_target_pairs={{0,1},{1,0},{2,3},{3,2},{4,5},{5,4},{6,7},{7,6},{8,9},{9,8},{10,11... | collective-permute-start | bytes 1769480 | tf_op jit(solution)/shard_map/ppermute | solution.py:412
  465.8 35.3 %all-to-all-start.1 = ((bf16[8,208,448]{2,1,0:T(8,128)(2,1)}), bf16[8,208,448]{2,1,0:T(8,128)(2,1)S(1)}, u32[]{:S(2)}, u32[]{:S(2)}) async-start(bf16[8,208,448]{2,1,0:T(8,128)(2,1)} %fusion.1), calls=%async_computation.6 | async-start | bytes 3407872 | tf_op jit(solution)/shard_map/all_to_all | solution.py:696
  470.9 27.3 %collective-permute-start.57 = (bf16[2,192,768]{2,1,0:T(8,128)(2,1)}, bf16[2,192,768]{2,1,0:T(8,128)(2,1)}, u32[]{:S(2)}, u32[]{:S(2)}) collective-permute-start(bf16[2,192,768]{2,1,0:T(8,128)(2,1)} %maximum_select_fusion.3), channel_id=1, source_target_pairs={{0,1},{1,0},{2,3},{3,2},{4,5},{5,4},{6,7},{7,6},{8,9},{9,8},{10,11... | collective-permute-start | bytes 1769480 | tf_op jit(solution)/shard_map/ppermute | solution.py:412
  483.7 16.4 %collective-permute-start.58 = (bf16[1,192,768]{2,1,0:T(8,128)(2,1)S(1)}, bf16[1,192,768]{2,1,0:T(8,128)(2,1)S(1)}, u32[]{:S(2)}, u32[]{:S(2)}) collective-permute-start(bf16[1,192,768]{2,1,0:T(8,128)(2,1)S(1)} %constant_dynamic-slice_fusion), channel_id=1, source_target_pairs={{0,2},{1,3},{2,0},{3,1},{4,6},{5,7},{6,4},{7,5},{8,10},{9,11},{10,... | collective-permute-start | bytes 884744 | tf_op jit(solution)/shard_map/ppermute | solution.py:412
  483.8 16.4 %collective-permute-start.56 = (bf16[192,768]{1,0:T(8,128)(2,1)S(1)}, bf16[192,768]{1,0:T(8,128)(2,1)S(1)}, u32[]{:S(2)}, u32[]{:S(2)}) collective-permute-start(bf16[192,768]{1,0:T(8,128)(2,1)S(1)} %broadcast_select_fusion.7), channel_id=1, source_target_pairs={{0,16},{16,0},{1,17},{17,1},{2,18},{18,2},{3,19},{19,3},{4,20},{20... | collective-permute-start | bytes 884744 | tf_op jit(solution)/shard_map/ppermute | solution.py:412
  518.1 22.2 %collective-permute-start.63 = (bf16[2,192,768]{2,1,0:T(8,128)(2,1)}, bf16[2,192,768]{2,1,0:T(8,128)(2,1)}, u32[]{:S(2)}, u32[]{:S(2)}) collective-permute-start(bf16[2,192,768]{2,1,0:T(8,128)(2,1)} %maximum_select_fusion.4), channel_id=1, source_target_pairs={{0,1},{1,0},{2,3},{3,2},{4,5},{5,4},{6,7},{7,6},{8,9},{9,8},{10,11... | collective-permute-start | bytes 1769480 | tf_op jit(solution)/shard_map/ppermute | solution.py:412
  520.8 17.3 %collective-permute-start.62 = (bf16[1,192,768]{2,1,0:T(8,128)(2,1)}, bf16[1,192,768]{2,1,0:T(8,128)(2,1)S(1)}, u32[]{:S(2)}, u32[]{:S(2)}) collective-permute-start(bf16[1,192,768]{2,1,0:T(8,128)(2,1)} %bitcast.61), channel_id=1, source_target_pairs={{0,2},{1,3},{2,0},{3,1},{4,6},{5,7},{6,4},{7,5},{8,10},{9,11},{10,... | collective-permute-start | bytes 884744 | tf_op jit(solution)/shard_map/ppermute | solution.py:412
  (141 other events, 1066.3 us)
Sparse Core Ops, SparseCore 0:
  255.3 48.3 reduce-scatter.5
  311.4 30.0 reduce-scatter.7
  359.5 29.6 reduce-scatter.11
  391.4 27.8 reduce-scatter.9
  422.0 37.5 reduce-scatter.13

commit v8 on v7

--- a/solution.py
+++ b/solution.py
@@ -18,7 +18,7 @@
 HALF = D // 2
 EPSILON = 1e-05
 SCALE = float(HD) ** (-0.5)
-VMEM_LIMIT = 48 * 1024 * 1024
+VMEM_LIMIT = 60 * 1024 * 1024
 GAIN1, GAIN2, SHIFT1, SHIFT2, BIAS_Q, BIAS_V, BIAS_OUT, BIAS_FC2 = range(8)
 BACK_ORDER = (3, 1, 2, 0)
 F32 = jnp.float32
@@ -434,7 +434,7 @@
         in_specs=[pair if outs == 2 else spec] * 2,
         out_specs=[spec] * outs,
         out_shape=[jax.ShapeDtypeStruct((rows, D), BF16)] * outs,
-        compiler_params=pltpu.CompilerParams(vmem_limit_bytes=VMEM_LIMIT),
+        compiler_params=pltpu.CompilerParams(vmem_limit_bytes=VMEM_LIMIT // 4),
         cost_estimate=pl.CostEstimate(flops=2**36, bytes_accessed=2**28, transcendentals=0),
     )(left, right)
 
@@ -533,6 +533,7 @@
     )
     ends = ends_in[0].T.reshape(FEATS, clips, FRAMES).transpose(1, 0, 2)
     ends = with_rows(ends, jnp.broadcast_to(small, (clips,) + small.shape))
+    beyond_a, near_one, own_two, ends = tie((beyond_a, nears[1], owned[2], ends))
     ends = lax.all_to_all(ends, ("section", "tensor"), split_axis=0, concat_axis=0, tiled=True)
     small = ends[:, FEATS : FEATS + 12, :FEATS].astype(F32)
     cols = jnp.swapaxes(small[:, :8], 1, 2).reshape(2, SHARDS, FEATS, 8)
@@ -552,7 +553,6 @@
         )
 
     n_dp = lax.axis_size("dp")
-    beyond_a, near_one, own_two = tie((beyond_a, nears[1], owned[2]))
     beyond_one = flip(near_one, "section", 1)
     beyond_two = flip(own_two, "section", 1)
     near_a = layers(nears[0], beyond_a)
@@ -579,25 +579,26 @@
     stream = ends[0]
     a1, p, soft, o, h = attend(0, stream, chunks[0][0])
     h, away_one, there_two, beyond_far_one, late_a, late_far_a, late_one, late_two = tie(
-        (h, away_one, there_two, beyond_far_one, near_a[1], far_a[1], near_one[1], near_two[1])
+        (h, away_one, there_two, beyond_far_one, near_a[1], far_a[1], near_one[1], (near_two[1], far_two[1]))
     )
     far_one = layers(fars[1], beyond_far_one)
     chunks[0].append(chunk_of((near_one[0], far_one[0]), (there_one, away_one)))
     chunks[0].append(chunk_of((near_two[0], far_two[0]), (there_two, flip(there_two, "dp", 1))))
-    there_a, there_one, there_two = over_y(late_a), over_y(late_one), over_y(late_two)
+    there_a, there_one = over_y(late_a), over_y(late_one)
+    there_two, away_two = over_y(late_two[0]), over_y(late_two[1])
     away_a = flip(there_a, "dp", 1)
     a2, u, slope, y = feed(0, h, *chunks[0][1:])
     stored = [(stream, a1, p, soft, o, h, a2, u, slope)]
-    stream, there_a, away_a, there_one, there_two, late_a, late_far_a = tie(
-        (y, there_a, away_a, there_one, there_two, late_a, late_far_a)
+    stream, there_a, away_a, there_one, late_a, late_far_a = tie(
+        (y, there_a, away_a, there_one, late_a, late_far_a)
     )
     chunks[1].append(chunk_of((late_a, late_far_a), (there_a, away_a)))
-    away_one, away_two = flip(there_one, "dp", 1), flip(there_two, "dp", 1)
+    away_one = flip(there_one, "dp", 1)
     a1, p, soft, o, h = attend(1, stream, chunks[1][0])
     h, late = tie(
         (
             h,
-            (late_one, far_one[1], there_one, away_one, late_two, far_two[1], there_two, away_two),
+            (late_one, far_one[1], there_one, away_one, *late_two, there_two, away_two),
         )
     )
     chunks[1].append(chunk_of(late[0:2], late[2:4]))
@@ -607,6 +608,7 @@
     stream = y
 
     upstream = ends[1]
+    bits = [1 << k for k in range(n_dp.bit_length() - 1)]
     chains = [[Chain() for _ in range(3)] for _ in range(2)]
     smalls = [None, None]
     ends_of = [None, None]
@@ -629,7 +631,8 @@
         if layer == 0:
             late_a.fold_rows()
             (gh,) = tied((late_a, last_two, last_one, late_one), gh)
-            late_a.scatter()
+            late_a.split()
+            late_a.send_half(bits[0])
             last_two.send_y()
             last_one.send_y()
         else:
@@ -651,13 +654,17 @@
             late_a.send_y()
         else:
             last_two.fold_rows()
-            (upstream,) = tied((last_two, last_a, late_two), upstream)
+            late_a.fold()
+            (upstream,) = tied((last_two, last_a, late_two, late_a), upstream)
+            for bit in bits[1:]:
+                late_a.send_half(bit)
+                if bit != bits[-1]:
+                    late_a.fold()
             last_two.scatter()
             last_a.send_y()
             late_one.send_y()
         ends_of[layer] = (db1_kept, db1_sent, (dbqv_kept, dbqv_sent, dcol_one, dcol_two))
 
-    bits = [1 << k for k in range(n_dp.bit_length() - 1)]
     pair_two, pair_one, pair_a = Chain(), Chain(), Chain()
 
     def start_far(pair):
@@ -671,15 +678,15 @@
             pair.join(bit)
 
     last_one.fold_rows()
+    late_a.fold()
+    late_a.value = late_a.value[0]
     tied((last_one, late_a))
     last_one.scatter()
-
     tied((last_two, late_two))
     pair_two.send_x(last_two, late_two)
 
     pair_two.fold()
     upstream, ends_of = tied((pair_two,), upstream, ends_of)
-    start_far(pair_two)
     for layer in range(2):
         db1_kept, db1_sent, dcols = ends_of[layer]
         smalls[layer] = jnp.concatenate(
@@ -696,46 +703,49 @@
     result = lax.all_to_all(result, ("section", "tensor"), split_axis=0, concat_axis=0, tiled=True)
 
     last_a.fold_rows()
-    finish_far(pair_two)
     tied((last_a, pair_two))
     last_a.split()
     last_a.send_half(bits[0])
-    pair_two.send_back(bits[0])
+    start_far(pair_two)
 
     last_a.fold()
-    late_one.fold()
-    tied((last_a, late_one, last_one))
+    tied((last_a,))
     for bit in bits[1:]:
         last_a.send_half(bit)
         if bit != bits[-1]:
             last_a.fold()
+
+    late_one.fold()
+    finish_far(pair_two)
+    (result,) = tied((pair_two, last_one, late_one), result)
     pair_one.send_x(last_one, late_one)
-
-    pair_one.fold()
-    pair_two.join(bits[0])
-    (result,) = tied((pair_one, pair_two), result)
-    start_far(pair_one)
+    pair_two.send_back(bits[0])
     small_sum = result[:, FEATS : FEATS + 12, :FEATS].astype(F32).sum(axis=0)
-    result = result[:, :FEATS].transpose(1, 0, 2).reshape(FEATS, clips * FRAMES).T.astype(F32)
 
     last_a.fold()
     last_a.value = last_a.value[0]
-    (small_sum,) = tied((last_a,), small_sum)
+    pair_one.fold()
+    result, small_sum = tied((last_a, pair_one), result, small_sum)
     pair_a.send_x(last_a, late_a)
-    finish_far(pair_one)
+    start_far(pair_one)
     small_sum += flip(small_sum, "dp", bits[0])
 
     pair_a.fold()
-    (small_sum,) = tied((pair_a, pair_one), small_sum)
+    pair_two.join(bits[0])
+    result, small_sum = tied((pair_a, pair_two), result, small_sum)
     start_far(pair_a)
-    pair_one.send_back(bits[0])
     for bit in bits[1:]:
         small_sum += flip(small_sum, "dp", bit)
 
+    finish_far(pair_one)
+    (result,) = tied((pair_one,), result)
+    pair_one.send_back(bits[0])
+    result = result[:, :FEATS].transpose(1, 0, 2).reshape(FEATS, clips * FRAMES).T.astype(F32)
+
     finish_far(pair_a)
+    (small_sum,) = tied((pair_a,), small_sum)
+    pair_a.send_back(bits[0])
     pair_one.join(bits[0])
-    (small_sum,) = tied((pair_a, pair_one), small_sum)
-    pair_a.send_back(bits[0])
     pair_a.join(bits[0])
     for pair in (pair_two, pair_one, pair_a):
         pair.value = pair.value.reshape(D, D)

time: 574 us -> 539 us (0.939)
  local copies, waits for them, and re-layouts: 74.3 us -> 41.2 us
    unnamed x233 -> x145, local copies, waits for them, and re-layouts: 44 us -> 16.9 us
    all_to_all x1, waiting for transfers between devices: 0.01 us -> 12 us  [body(): lax.all_to_all(ends, ('section', 'tensor'), split_axis=0, concat_axis=0,...]
    reduce_scatter x5 -> x4, waiting for transfers between devices: 13.5 us -> 4.09 us  [scatter(): total = lax.psum_scatter(split, 'dp', scatter_dimension=0, tiled=False)]
    pallas_call x12, Pallas kernels: 168 us -> 177 us  [run(): pl.pallas_call(kernel, name=name, out_shape=outs, grid_spec=pltpu.Prefetc...]
    pallas_call x11, Pallas kernels: 24 us -> 17.5 us  [summed(): pl.pallas_call(sum_kernel, name='row_sums', grid=(rows // block,), in_spe...]
    ppermute x66 -> x68, starting transfers between devices: 55.3 us -> 57.7 us  [flip(): return lax.ppermute(block, axis, [(i, i ^ bit) for i in range(size)])]
    ppermute x66 -> x68, waiting for transfers between devices: 170 us -> 169 us  [flip(): return lax.ppermute(block, axis, [(i, i ^ bit) for i in range(size)])]
  transfers between devices with their start and end apart: 73 -> 74, of which waited for: 30 -> 30; matrix products, arithmetic and copies ran while one was open for 10% -> 8% of each run, Pallas kernels for 29% -> 31%
where the time goes in v8:
time: 539 us; the launch traced here: 533 us
  Pallas kernels  194 us (36%)
  waiting for transfers between devices  185 us (34%)
  starting transfers between devices  65.5 us (12%)
  local copies, waits for them, and re-layouts  41.2 us (8%)
  other arithmetic  31.6 us (6%)
  between operations  15.4 us (3%)
    pallas_call x12, Pallas kernels, run(): pl.pallas_call(kernel, name=name, out_shape=outs, grid_spec=pltpu.Prefetc...  177 us
    ppermute x68, waiting for transfers between devices, flip(): return lax.ppermute(block, axis, [(i, i ^ bit) for i in range(size)])  169 us
    ppermute x68, starting transfers between devices, flip(): return lax.ppermute(block, axis, [(i, i ^ bit) for i in range(size)])  57.7 us
    pallas_call x11, Pallas kernels, summed(): pl.pallas_call(sum_kernel, name='row_sums', grid=(rows // block,), in_spe...  17.5 us
    unnamed x145, local copies, waits for them, and re-layouts  16.9 us
    all_to_all x1, waiting for transfers between devices, body(): lax.all_to_all(ends, ('section', 'tensor'), split_axis=0, concat_axis=0,...  12 us
  transfers between devices with their start and end apart: 74, of which 30 were waited for; matrix products, arithmetic and copies ran while one was open for 8% of the time, Pallas kernels for 31%

profile of v8, /device:TPU:0, one launch (start us, length us, event | category | flops | bytes accessed | tf_op | source)
XLA Modules:
  0.0 533.0 jit_solution(12137176031041911653)
XLA Ops:
  8.6 3.0 collective-permute-start
  11.7 3.3 reshape.221
  16.2 8.8 %collective-permute-done = bf16[384,768]{1,0:T(8,128)(2,1)} collective-permute-done((bf16[384,768]{1,0:T(8,128)(2,1)S(1)}, bf16[384,768]{1,0:T(8,128)(2,1)}, u32[]{:S(2)}, u32[]{:S(2)}) %collective-permute-start) | collective-permute-done | bytes 589856 | tf_op jit(solution)/shard_map/ppermute | solution.py:412
  32.7 3.6 all-to-all-start
  38.1 5.7 %collective-permute-done.4.refs_4_.refs_5_ = bf16[384,768]{1,0:T(8,128)(2,1)} collective-permute-done((bf16[384,768]{1,0:T(8,128)(2,1)}, bf16[384,768]{1,0:T(8,128)(2,1)}, u32[]{:S(2)}, u32[]{:S(2)}) %collective-permute-start.4) | collective-permute-done | bytes 589856 | tf_op jit(solution)/shard_map/ppermute | solution.py:412
  45.5 2.5 broadcast_select_fusion
  55.2 2.6 broadcast_select_fusion.1
  57.8 6.0 %collective-permute-done.9.refs_4_.refs_5_ = bf16[384,768]{1,0:T(8,128)(2,1)} collective-permute-done((bf16[384,768]{1,0:T(8,128)(2,1)}, bf16[384,768]{1,0:T(8,128)(2,1)}, u32[]{:S(2)}, u32[]{:S(2)}) %collective-permute-start.9) | collective-permute-done | bytes 589856 | tf_op jit(solution)/shard_map/ppermute | solution.py:412
  63.8 7.0 %collective-permute-done.10 = bf16[768,768]{1,0:T(8,128)(2,1)} collective-permute-done((bf16[768,768]{1,0:T(8,128)(2,1)}, bf16[768,768]{1,0:T(8,128)(2,1)}, u32[]{:S(2)}, u32[]{:S(2)}) %collective-permute-start.10) | collective-permute-done | bytes 1179680 | tf_op jit(solution)/shard_map/ppermute | solution.py:412
  71.3 3.3 bitcast_select_fusion.2
  74.7 12.0 %all-to-all-done = bf16[8,208,448]{2,1,0:T(8,128)(2,1)S(1)} async-done(((bf16[8,208,448]{2,1,0:T(8,128)(2,1)}), bf16[8,208,448]{2,1,0:T(8,128)(2,1)S(1)}, u32[]{:S(2)}, u32[]{:S(2)}) %all-to-all-start) | async-done | bytes 1490976 | tf_op jit(solution)/shard_map/all_to_all | solution.py:537
  91.9 17.0 %attention_forward.2 = (bf16[768,448]{1,0:T(8,128)(2,1)}, bf16[4,576,448]{2,1,0:T(8,128)(2,1)}, bf16[4,3,448,448]{3,2,1,0:T(8,128)(2,1)}, bf16[4,192,448]{2,1,0:T(8,128)(2,1)}, f32[768,448]{1,0:T(8,128)}) custom-call(s32[9]{0:T(128)} %stack.113.info, bf16[768,448]{1,0:T(8,128)(2,1)} %bitcast.160, f32[4,192,8]{2,1,0:T(8,128)} %get-tuple-element.330.col_ref, ...), custom_call_target="tpu_custom_call" | custom-call | flops 43687870464 | bytes 268435456 | tf_op jit(solution)/shard_map/attention_forward/pallas_call | solution.py:311
  110.1 2.3 bitcast_select_fusion
  114.4 10.8 %collective-permute-done.20.refs_13_.refs_14_ = bf16[384,768]{1,0:T(8,128)(2,1)} collective-permute-done((bf16[384,768]{1,0:T(8,128)(2,1)}, bf16[384,768]{1,0:T(8,128)(2,1)}, u32[]{:S(2)}, u32[]{:S(2)}) %collective-permute-start.20) | collective-permute-done | bytes 589856 | tf_op jit(solution)/shard_map/ppermute | solution.py:412
  129.9 14.1 %mlp_forward.2 = (bf16[768,448]{1,0:T(8,128)(2,1)}, bf16[4,448,768]{2,1,0:T(8,128)(2,1)}, bf16[4,448,768]{2,1,0:T(8,128)(2,1)}, f32[768,448]{1,0:T(8,128)}) custom-call(s32[9]{0:T(128)} %stack.113.info, f32[768,448]{1,0:T(8,128)} %get-tuple-element.172.h_ref, f32[4,192,8]{2,1,0:T(8,128)} %get-tuple-element.330.col_ref, f32[4,1,768]{2,1,0:T(1,128)} %squeeze.92.b1_ref, ...), custom_call_target="tpu_custom_call" | custom-call | flops 67645734912 | bytes 268435456 | tf_op jit(solution)/shard_map/mlp_forward/pallas_call | solution.py:311
  150.1 17.0 %attention_forward.3 = (bf16[768,448]{1,0:T(8,128)(2,1)}, bf16[4,576,448]{2,1,0:T(8,128)(2,1)}, bf16[4,3,448,448]{3,2,1,0:T(8,128)(2,1)}, bf16[4,192,448]{2,1,0:T(8,128)(2,1)}, f32[768,448]{1,0:T(8,128)}) custom-call(s32[9]{0:T(128)} %stack.113.info, f32[768,448]{1,0:T(8,128)} %get-tuple-element.180.x_ref, f32[4,192,8]{2,1,0:T(8,128)} %get-tuple-element.329.col_ref, ...), custom_call_target="tpu_custom_call" | custom-call | flops 43687870464 | bytes 268435456 | tf_op jit(solution)/shard_map/attention_forward/pallas_call | solution.py:311
  167.1 6.0 %collective-permute-done.32.refs_13_.refs_14_ = bf16[384,768]{1,0:T(8,128)(2,1)} collective-permute-done((bf16[384,768]{1,0:T(8,128)(2,1)}, bf16[384,768]{1,0:T(8,128)(2,1)}, u32[]{:S(2)}, u32[]{:S(2)}) %collective-permute-start.32) | collective-permute-done | bytes 589856 | tf_op jit(solution)/shard_map/ppermute | solution.py:412
  175.3 2.4 collective-permute-done.34.refs_3_.refs_4_
  181.6 14.5 %mlp_forward.3 = (bf16[768,448]{1,0:T(8,128)(2,1)}, bf16[4,448,768]{2,1,0:T(8,128)(2,1)}, bf16[4,448,768]{2,1,0:T(8,128)(2,1)}, f32[768,448]{1,0:T(8,128)}) custom-call(s32[9]{0:T(128)} %stack.113.info, f32[768,448]{1,0:T(8,128)} %get-tuple-element.189.h_ref, f32[4,192,8]{2,1,0:T(8,128)} %get-tuple-element.329.col_ref, f32[4,1,768]{2,1,0:T(1,128)} %squeeze.93.b1_ref, ...), custom_call_target="tpu_custom_call" | custom-call | flops 67645734912 | bytes 268435456 | tf_op jit(solution)/shard_map/mlp_forward/pallas_call | solution.py:311
  196.1 12.4 %mlp_backward.4 = (f32[448,768]{1,0:T(8,128)}, bf16[2,768,768]{2,1,0:T(8,128)(2,1)}, bf16[2,768,768]{2,1,0:T(8,128)(2,1)}, f32[4,1,768]{2,1,0:T(1,128)}) custom-call(s32[9]{0:T(128)} %stack.113.info, bf16[768,448]{1,0:T(8,128)(2,1)} %bitcast.163, f32[768,448]{1,0:T(8,128)} %get-tuple-element.189.h_ref, bf16[768,448]{1,0:T(8,128)(2,1)} %get-tuple-element.198.a2_ref, ...), custom_call_target="tpu_custom_call" | custom-call | flops 67645734912 | bytes 268435456 | tf_op jit(solution)/shard_map/mlp_backward/pallas_call | solution.py:311
  209.1 14.6 %mlp_backward.5 = (f32[768,448]{1,0:T(8,128)}, f32[4,192,8]{2,1,0:T(8,128)}, bf16[2,768,768]{2,1,0:T(8,128)(2,1)}, bf16[2,768,768]{2,1,0:T(8,128)(2,1)}, f32[4,1,768]{2,1,0:T(1,128)}) custom-call(s32[9]{0:T(128)} %stack.113.info, bf16[768,448]{1,0:T(8,128)(2,1)} %bitcast.164, f32[768,448]{1,0:T(8,128)} %get-tuple-element.189.h_ref, ...), custom_call_target="tpu_custom_call" | custom-call | flops 67645734912 | bytes 268435456 | tf_op jit(solution)/shard_map/mlp_backward/pallas_call | solution.py:311
  232.2 13.9 %attention_backward.4 = (f32[448,768]{1,0:T(8,128)}, bf16[2,768,768]{2,1,0:T(8,128)(2,1)}, f32[4,192,8]{2,1,0:T(8,128)}) custom-call(s32[9]{0:T(128)} %stack.113.info, f32[768,448]{1,0:T(8,128)} %get-tuple-element.213.gh_ref, f32[768,448]{1,0:T(8,128)} %get-tuple-element.180.x_ref, bf16[768,448]{1,0:T(8,128)(2,1)} %get-tuple-element.214.a1_ref, ...), custom_call_target="tpu_custom_call" | custom-call | flops 43687870464 | bytes 268435456 | tf_op jit(solution)/shard_map/attention_backward/pallas_call | solution.py:311
  246.2 16.2 %attention_backward.5 = (f32[768,448]{1,0:T(8,128)}, f32[4,192,8]{2,1,0:T(8,128)}, bf16[2,768,768]{2,1,0:T(8,128)(2,1)}, f32[4,192,8]{2,1,0:T(8,128)}) custom-call(s32[9]{0:T(128)} %stack.113.info, f32[768,448]{1,0:T(8,128)} %get-tuple-element.213.gh_ref, f32[768,448]{1,0:T(8,128)} %get-tuple-element.180.x_ref, bf16[768,448]{1,0:T(8,128)(2,1)} %get-tuple-element.214.a1_ref, ...), custom_call_target="tpu_custom_call" | custom-call | flops 43687870464 | bytes 268435456 | tf_op jit(solution)/shard_map/attention_backward/pallas_call | solution.py:311
  269.3 12.6 %mlp_backward.6 = (f32[448,768]{1,0:T(8,128)}, bf16[2,768,768]{2,1,0:T(8,128)(2,1)}, bf16[2,768,768]{2,1,0:T(8,128)(2,1)}, f32[4,1,768]{2,1,0:T(1,128)}) custom-call(s32[9]{0:T(128)} %stack.113.info, f32[768,448]{1,0:T(8,128)} %get-tuple-element.226.gy_ref, f32[768,448]{1,0:T(8,128)} %get-tuple-element.172.h_ref, ...), custom_call_target="tpu_custom_call" | custom-call | flops 67645734912 | bytes 268435456 | tf_op jit(solution)/shard_map/mlp_backward/pallas_call | solution.py:311
  282.5 15.0 %mlp_backward.7 = (f32[768,448]{1,0:T(8,128)}, f32[4,192,8]{2,1,0:T(8,128)}, bf16[2,768,768]{2,1,0:T(8,128)(2,1)}, bf16[2,768,768]{2,1,0:T(8,128)(2,1)}, f32[4,1,768]{2,1,0:T(1,128)}) custom-call(s32[9]{0:T(128)} %stack.113.info, f32[768,448]{1,0:T(8,128)} %get-tuple-element.226.gy_ref, f32[768,448]{1,0:T(8,128)} %get-tuple-element.172.h_ref, ...), custom_call_target="tpu_custom_call" | custom-call | flops 67645734912 | bytes 268435456 | tf_op jit(solution)/shard_map/mlp_backward/pallas_call | solution.py:311
  305.4 2.8 row_sums.17
  312.8 13.5 %attention_backward.6 = (f32[448,768]{1,0:T(8,128)}, bf16[2,768,768]{2,1,0:T(8,128)(2,1)}, f32[4,192,8]{2,1,0:T(8,128)}) custom-call(s32[9]{0:T(128)} %stack.113.info, f32[768,448]{1,0:T(8,128)} %get-tuple-element.244.gh_ref, bf16[768,448]{1,0:T(8,128)(2,1)} %bitcast.161, bf16[768,448]{1,0:T(8,128)(2,1)} %get-tuple-element.245.a1_ref, ...), custom_call_target="tpu_custom_call" | custom-call | flops 43687870464 | bytes 268435456 | tf_op jit(solution)/shard_map/attention_backward/pallas_call | solution.py:311
  326.4 16.1 %attention_backward.7 = (f32[768,448]{1,0:T(8,128)}, f32[4,192,8]{2,1,0:T(8,128)}, bf16[2,768,768]{2,1,0:T(8,128)(2,1)}, f32[4,192,8]{2,1,0:T(8,128)}) custom-call(s32[9]{0:T(128)} %stack.113.info, f32[768,448]{1,0:T(8,128)} %get-tuple-element.244.gh_ref, bf16[768,448]{1,0:T(8,128)(2,1)} %bitcast.162, bf16[768,448]{1,0:T(8,128)(2,1)} %get-tuple-element.245.a1_ref, ...), custom_call_target="tpu_custom_call" | custom-call | flops 43687870464 | bytes 268435456 | tf_op jit(solution)/shard_map/attention_backward/pallas_call | solution.py:311
  344.7 2.4 row_sums.18
  350.2 2.7 collective-permute-start.57
  354.2 11.0 %collective-permute-done.56.right_ref = bf16[768,768]{1,0:T(8,128)(2,1)} collective-permute-done((bf16[768,768]{1,0:T(8,128)(2,1)}, bf16[768,768]{1,0:T(8,128)(2,1)}, u32[]{:S(2)}, u32[]{:S(2)}) %collective-permute-start.56) | collective-permute-done | bytes 1179680 | tf_op jit(solution)/shard_map/ppermute | solution.py:412
  367.5 14.0 %collective-permute-done.57 = bf16[1,192,768]{2,1,0:T(8,128)(2,1)S(1)} collective-permute-done((bf16[1,192,768]{2,1,0:T(8,128)(2,1)S(1)}, bf16[1,192,768]{2,1,0:T(8,128)(2,1)S(1)}, u32[]{:S(2)}, u32[]{:S(2)}) %collective-permute-start.57) | collective-permute-done | bytes 294944 | tf_op jit(solution)/shard_map/ppermute | solution.py:412
  382.2 4.1 reduce-scatter.9.cloned.1.call-done
  389.7 6.0 %collective-permute-done.52 = bf16[192,768]{1,0:T(8,128)(2,1)S(1)} collective-permute-done((bf16[192,768]{1,0:T(8,128)(2,1)S(1)}, bf16[192,768]{1,0:T(8,128)(2,1)S(1)}, u32[]{:S(2)}, u32[]{:S(2)}) %collective-permute-start.52) | collective-permute-done | bytes 294944 | tf_op jit(solution)/shard_map/ppermute | solution.py:412
  400.1 4.0 all-to-all-start.1
  404.1 2.4 collective-permute-start.53
  408.6 23.2 %collective-permute-done.58 = bf16[192,768]{1,0:T(8,128)(2,1)S(1)} collective-permute-done((bf16[192,768]{1,0:T(8,128)(2,1)S(1)}, bf16[192,768]{1,0:T(8,128)(2,1)S(1)}, u32[]{:S(2)}, u32[]{:S(2)}) %collective-permute-start.58) | collective-permute-done | bytes 294944 | tf_op jit(solution)/shard_map/ppermute | solution.py:412
  431.9 3.6 collective-permute-start.55
  436.6 19.4 %collective-permute-done.55 = bf16[1,192,768]{2,1,0:T(8,128)(2,1)S(1)} collective-permute-done((bf16[1,192,768]{2,1,0:T(8,128)(2,1)S(1)}, bf16[1,192,768]{2,1,0:T(8,128)(2,1)S(1)}, u32[]{:S(2)}, u32[]{:S(2)}) %collective-permute-start.55) | collective-permute-done | bytes 294944 | tf_op jit(solution)/shard_map/ppermute | solution.py:412
  456.2 2.6 collective-permute-start.59
  458.7 2.7 collective-permute-done.54
  466.3 2.7 collective-permute-start.60
  469.0 14.5 %collective-permute-done.63 = f32[12,192]{1,0:T(8,128)S(1)} collective-permute-done((f32[12,192]{1,0:T(8,128)S(1)}, f32[12,192]{1,0:T(8,128)S(1)}, u32[]{:S(2)}, u32[]{:S(2)}) %collective-permute-start.63) | collective-permute-done | bytes 9248 | tf_op jit(solution)/shard_map/ppermute | solution.py:412
  488.7 3.5 collective-permute-done.65
  492.2 8.2 %collective-permute-done.64 = bf16[1,192,768]{2,1,0:T(8,128)(2,1)S(1)} collective-permute-done((bf16[1,192,768]{2,1,0:T(8,128)(2,1)S(1)}, bf16[1,192,768]{2,1,0:T(8,128)(2,1)S(1)}, u32[]{:S(2)}, u32[]{:S(2)}) %collective-permute-start.64) | collective-permute-done | bytes 294944 | tf_op jit(solution)/shard_map/ppermute | solution.py:412
  504.7 2.4 reshape.235
  509.9 9.4 %collective-permute-done.66 = bf16[2,192,768]{2,1,0:T(8,128)(2,1)} collective-permute-done((bf16[2,192,768]{2,1,0:T(8,128)(2,1)}, bf16[2,192,768]{2,1,0:T(8,128)(2,1)}, u32[]{:S(2)}, u32[]{:S(2)}) %collective-permute-start.66) | collective-permute-done | bytes 589856 | tf_op jit(solution)/shard_map/ppermute | solution.py:412
  519.3 2.8 fusion.2
  (353 shorter events, 117.4 us)
Async XLA Ops:
  8.6 16.4 %collective-permute-start = (bf16[384,768]{1,0:T(8,128)(2,1)S(1)}, bf16[384,768]{1,0:T(8,128)(2,1)}, u32[]{:S(2)}, u32[]{:S(2)}) collective-permute-start(bf16[384,768]{1,0:T(8,128)(2,1)S(1)} %fusion.7), channel_id=1, source_target_pairs={{0,16},{16,0},{1,17},{17,1},{2,18},{18,2},{3,19},{19,3},{4,20},{20... | collective-permute-start | bytes 1769480 | tf_op jit(solution)/shard_map/ppermute | solution.py:412
  27.2 16.6 %collective-permute-start.4 = (bf16[384,768]{1,0:T(8,128)(2,1)}, bf16[384,768]{1,0:T(8,128)(2,1)}, u32[]{:S(2)}, u32[]{:S(2)}) collective-permute-start(bf16[384,768]{1,0:T(8,128)(2,1)} %get-tuple-element.328.refs_0_.refs_1_), channel_id=1, source_target_pairs={{0,8},{4,12},{8,0},{12,4},{1,9},{5,13},{9,1},{13,5},{2,10},{6,14},... | collective-permute-start | bytes 1769480 | tf_op jit(solution)/shard_map/ppermute | solution.py:412
  29.0 16.6 %collective-permute-start.5 = (bf16[384,768]{1,0:T(8,128)(2,1)}, bf16[384,768]{1,0:T(8,128)(2,1)}, u32[]{:S(2)}, u32[]{:S(2)}) collective-permute-start(bf16[384,768]{1,0:T(8,128)(2,1)} %dynamic-slice_bitcast_fusion.2), channel_id=1, source_target_pairs={{0,16},{16,0},{1,17},{17,1},{2,18},{18,2},{3,19},{19,3},{4,20},{20... | collective-permute-start | bytes 1769480 | tf_op jit(solution)/shard_map/ppermute | solution.py:412
  30.5 40.4 %collective-permute-start.10 = (bf16[768,768]{1,0:T(8,128)(2,1)}, bf16[768,768]{1,0:T(8,128)(2,1)}, u32[]{:S(2)}, u32[]{:S(2)}) collective-permute-start(bf16[768,768]{1,0:T(8,128)(2,1)} %bitcast.10), channel_id=1, source_target_pairs={{0,16},{16,0},{1,17},{17,1},{2,18},{18,2},{3,19},{19,3},{4,20},{20... | collective-permute-start | bytes 3538952 | tf_op jit(solution)/shard_map/ppermute | solution.py:412
  32.7 53.9 %all-to-all-start = ((bf16[8,208,448]{2,1,0:T(8,128)(2,1)}), bf16[8,208,448]{2,1,0:T(8,128)(2,1)S(1)}, u32[]{:S(2)}, u32[]{:S(2)}) async-start(bf16[8,208,448]{2,1,0:T(8,128)(2,1)} %copy.111), calls=%async_computation | async-start | bytes 3407872 | tf_op jit(solution)/shard_map/all_to_all | solution.py:537
  36.4 272.9 %reduce-scatter.5.cloned.1.call-start = ((), (), s32[]{:S(2)}) async-start(), calls=%async_computation.6 | async-start | bytes 2949120 | tf_op jit(solution)/shard_map/reduce_scatter | solution.py:463
  36.4 16.4 %collective-permute-start.1 = (bf16[384,768]{1,0:T(8,128)(2,1)}, bf16[384,768]{1,0:T(8,128)(2,1)S(1)}, u32[]{:S(2)}, u32[]{:S(2)}) collective-permute-start(bf16[384,768]{1,0:T(8,128)(2,1)} %collective-permute-done), channel_id=1, source_target_pairs={{0,1},{1,0},{2,3},{3,2},{4,5},{5,4},{6,7},{7,6},{8,9},{9,8},{10,11... | collective-permute-start | bytes 1769480 | tf_op jit(solution)/shard_map/ppermute | solution.py:412
  48.3 22.6 %collective-permute-start.6 = (bf16[384,768]{1,0:T(8,128)(2,1)}, bf16[384,768]{1,0:T(8,128)(2,1)}, u32[]{:S(2)}, u32[]{:S(2)}) collective-permute-start(bf16[384,768]{1,0:T(8,128)(2,1)} %collective-permute-done.4.refs_4_.refs_5_), channel_id=1, source_target_pairs={{0,1},{1,0},{2,3},{3,2},{4,5},{5,4},{6,7},{7,6},{8,9},{9,8},{10,11... | collective-permute-start | bytes 1769480 | tf_op jit(solution)/shard_map/ppermute | solution.py:412
  50.7 38.6 %collective-permute-start.2 = (bf16[384,768]{1,0:T(8,128)(2,1)}, bf16[384,768]{1,0:T(8,128)(2,1)}, u32[]{:S(2)}, u32[]{:S(2)}) collective-permute-start(bf16[384,768]{1,0:T(8,128)(2,1)} %get-tuple-element.328.refs_0_.refs_1_), channel_id=1, source_target_pairs={{0,4},{4,0},{8,12},{12,8},{1,5},{5,1},{9,13},{13,9},{2,6},{6,2},{1... | collective-permute-start | bytes 1769480 | tf_op jit(solution)/shard_map/ppermute | solution.py:412
  53.7 55.2 %collective-permute-start.13 = (bf16[384,768]{1,0:T(8,128)(2,1)}, bf16[384,768]{1,0:T(8,128)(2,1)}, u32[]{:S(2)}, u32[]{:S(2)}) collective-permute-start(bf16[384,768]{1,0:T(8,128)(2,1)} %collective-permute-done.5), channel_id=1, source_target_pairs={{0,1},{1,0},{2,3},{3,2},{4,5},{5,4},{6,7},{7,6},{8,9},{9,8},{10,11... | collective-permute-start | bytes 1769480 | tf_op jit(solution)/shard_map/ppermute | solution.py:412
  63.8 25.5 %collective-permute-start.7 = (bf16[384,768]{1,0:T(8,128)(2,1)}, bf16[384,768]{1,0:T(8,128)(2,1)}, u32[]{:S(2)}, u32[]{:S(2)}) collective-permute-start(bf16[384,768]{1,0:T(8,128)(2,1)} %collective-permute-done.4.refs_4_.refs_5_), channel_id=1, source_target_pairs={{0,4},{4,0},{8,12},{12,8},{1,5},{5,1},{9,13},{13,9},{2,6},{6,2},{1... | collective-permute-start | bytes 1769480 | tf_op jit(solution)/shard_map/ppermute | solution.py:412
  70.8 19.0 %collective-permute-start.3 = (bf16[384,768]{1,0:T(8,128)(2,1)S(1)}, bf16[384,768]{1,0:T(8,128)(2,1)}, u32[]{:S(2)}, u32[]{:S(2)}) collective-permute-start(bf16[384,768]{1,0:T(8,128)(2,1)S(1)} %get-tuple-element.322.refs_1_.refs_2_), channel_id=1, source_target_pairs={{0,4},{4,0},{8,12},{12,8},{1,5},{5,1},{9,13},{13,9},{2,6},{6,2},{1... | collective-permute-start | bytes 1769480 | tf_op jit(solution)/shard_map/ppermute | solution.py:412
  70.8 20.5 %collective-permute-start.8 = (bf16[384,768]{1,0:T(8,128)(2,1)}, bf16[384,768]{1,0:T(8,128)(2,1)}, u32[]{:S(2)}, u32[]{:S(2)}) collective-permute-start(bf16[384,768]{1,0:T(8,128)(2,1)} %collective-permute-done.6.refs_5_.refs_6_), channel_id=1, source_target_pairs={{0,4},{4,0},{8,12},{12,8},{1,5},{5,1},{9,13},{13,9},{2,6},{6,2},{1... | collective-permute-start | bytes 1769480 | tf_op jit(solution)/shard_map/ppermute | solution.py:412
  89.3 23.1 %collective-permute-start.14 = (bf16[384,768]{1,0:T(8,128)(2,1)}, bf16[384,768]{1,0:T(8,128)(2,1)}, u32[]{:S(2)}, u32[]{:S(2)}) collective-permute-start(bf16[384,768]{1,0:T(8,128)(2,1)} %get-tuple-element.326.refs_0_.refs_1_), channel_id=1, source_target_pairs={{0,4},{4,0},{8,12},{12,8},{1,5},{5,1},{9,13},{13,9},{2,6},{6,2},{1... | collective-permute-start | bytes 1769480 | tf_op jit(solution)/shard_map/ppermute | solution.py:412
  89.3 23.3 %collective-permute-start.16 = (bf16[384,768]{1,0:T(8,128)(2,1)}, bf16[384,768]{1,0:T(8,128)(2,1)}, u32[]{:S(2)}, u32[]{:S(2)}) collective-permute-start(bf16[384,768]{1,0:T(8,128)(2,1)} %collective-permute-done.9.refs_4_.refs_5_), channel_id=1, source_target_pairs={{0,4},{4,0},{8,12},{12,8},{1,5},{5,1},{9,13},{13,9},{2,6},{6,2},{1... | collective-permute-start | bytes 1769480 | tf_op jit(solution)/shard_map/ppermute | solution.py:412
  89.8 19.2 %collective-permute-start.11 = (bf16[384,768]{1,0:T(8,128)(2,1)}, bf16[384,768]{1,0:T(8,128)(2,1)S(1)}, u32[]{:S(2)}, u32[]{:S(2)}) collective-permute-start(bf16[384,768]{1,0:T(8,128)(2,1)} %collective-permute-done.9.refs_4_.refs_5_), channel_id=1, source_target_pairs={{0,1},{1,0},{2,3},{3,2},{4,5},{5,4},{6,7},{7,6},{8,9},{9,8},{10,11... | collective-permute-start | bytes 1769480 | tf_op jit(solution)/shard_map/ppermute | solution.py:412
  91.4 18.2 %collective-permute-start.12 = (bf16[384,768]{1,0:T(8,128)(2,1)}, bf16[384,768]{1,0:T(8,128)(2,1)}, u32[]{:S(2)}, u32[]{:S(2)}) collective-permute-start(bf16[384,768]{1,0:T(8,128)(2,1)} %get-tuple-element.316.refs_8_.refs_9_), channel_id=1, source_target_pairs={{0,8},{4,12},{8,0},{12,4},{1,9},{5,13},{9,1},{13,5},{2,10},{6,14},... | collective-permute-start | bytes 1769480 | tf_op jit(solution)/shard_map/ppermute | solution.py:412
  112.4 17.5 %collective-permute-start.21 = (bf16[384,768]{1,0:T(8,128)(2,1)}, bf16[384,768]{1,0:T(8,128)(2,1)}, u32[]{:S(2)}, u32[]{:S(2)}) collective-permute-start(bf16[384,768]{1,0:T(8,128)(2,1)} %collective-permute-done.12.refs_12_.refs_13_), channel_id=1, source_target_pairs={{0,4},{4,0},{8,12},{12,8},{1,5},{5,1},{9,13},{13,9},{2,6},{6,2},{1... | collective-permute-start | bytes 1769480 | tf_op jit(solution)/shard_map/ppermute | solution.py:412
  126.3 17.7 %collective-permute-start.25 = (bf16[384,768]{1,0:T(8,128)(2,1)S(1)}, bf16[384,768]{1,0:T(8,128)(2,1)}, u32[]{:S(2)}, u32[]{:S(2)}) collective-permute-start(bf16[384,768]{1,0:T(8,128)(2,1)S(1)} %copy-done.37), channel_id=1, source_target_pairs={{0,8},{4,12},{8,0},{12,4},{1,9},{5,13},{9,1},{13,5},{2,10},{6,14},... | collective-permute-start | bytes 1769480 | tf_op jit(solution)/shard_map/ppermute | solution.py:412
  145.1 22.0 %collective-permute-start.31 = (bf16[384,768]{1,0:T(8,128)(2,1)S(1)}, bf16[384,768]{1,0:T(8,128)(2,1)}, u32[]{:S(2)}, u32[]{:S(2)}) collective-permute-start(bf16[384,768]{1,0:T(8,128)(2,1)S(1)} %copy-done.38), channel_id=1, source_target_pairs={{0,8},{4,12},{8,0},{12,4},{1,9},{5,13},{9,1},{13,5},{2,10},{6,14},... | collective-permute-start | bytes 1769480 | tf_op jit(solution)/shard_map/ppermute | solution.py:412
  146.6 26.5 %collective-permute-start.32 = (bf16[384,768]{1,0:T(8,128)(2,1)}, bf16[384,768]{1,0:T(8,128)(2,1)}, u32[]{:S(2)}, u32[]{:S(2)}) collective-permute-start(bf16[384,768]{1,0:T(8,128)(2,1)} %get-tuple-element.195.refs_9_.refs_10_), channel_id=1, source_target_pairs={{0,8},{4,12},{8,0},{12,4},{1,9},{5,13},{9,1},{13,5},{2,10},{6,14},... | collective-permute-start | bytes 1769480 | tf_op jit(solution)/shard_map/ppermute | solution.py:412
  147.7 25.4 %collective-permute-start.30 = (bf16[384,768]{1,0:T(8,128)(2,1)}, bf16[384,768]{1,0:T(8,128)(2,1)}, u32[]{:S(2)}, u32[]{:S(2)}) collective-permute-start(bf16[384,768]{1,0:T(8,128)(2,1)} %collective-permute-done.25.refs_4_.refs_5_), channel_id=1, source_target_pairs={{0,1},{1,0},{2,3},{3,2},{4,5},{5,4},{6,7},{7,6},{8,9},{9,8},{10,11... | collective-permute-start | bytes 1769480 | tf_op jit(solution)/shard_map/ppermute | solution.py:412
  208.7 19.2 %collective-permute-start.42 = (bf16[2,768,768]{2,1,0:T(8,128)(2,1)}, bf16[2,768,768]{2,1,0:T(8,128)(2,1)S(1)}, u32[]{:S(2)}, u32[]{:S(2)}) collective-permute-start(bf16[2,768,768]{2,1,0:T(8,128)(2,1)} %get-tuple-element.207), channel_id=1, source_target_pairs={{0,4},{4,0},{8,12},{12,8},{1,5},{5,1},{9,13},{13,9},{2,6},{6,2},{1... | collective-permute-start | bytes 7077896 | tf_op jit(solution)/shard_map/ppermute | solution.py:412
  229.0 33.5 %collective-permute-start.43 = (bf16[768,768]{1,0:T(8,128)(2,1)S(1)}, bf16[768,768]{1,0:T(8,128)(2,1)}, u32[]{:S(2)}, u32[]{:S(2)}) collective-permute-start(bf16[768,768]{1,0:T(8,128)(2,1)S(1)} %get-tuple-element.212), channel_id=1, source_target_pairs={{0,8},{4,12},{8,0},{12,4},{1,9},{5,13},{9,1},{13,5},{2,10},{6,14},... | collective-permute-start | bytes 3538952 | tf_op jit(solution)/shard_map/ppermute | solution.py:412
  232.2 116.8 %reduce-scatter.7.cloned.1.call-start = ((), (), s32[]{:S(2)}) async-start(), calls=%async_computation.7 | async-start | bytes 1474560 | tf_op jit(solution)/shard_map/reduce_scatter | solution.py:463
  246.1 19.9 %collective-permute-start.44 = (bf16[2,768,768]{2,1,0:T(8,128)(2,1)}, bf16[2,768,768]{2,1,0:T(8,128)(2,1)S(1)}, u32[]{:S(2)}, u32[]{:S(2)}) collective-permute-start(bf16[2,768,768]{2,1,0:T(8,128)(2,1)} %get-tuple-element.220), channel_id=1, source_target_pairs={{0,4},{4,0},{8,12},{12,8},{1,5},{5,1},{9,13},{13,9},{2,6},{6,2},{1... | collective-permute-start | bytes 7077896 | tf_op jit(solution)/shard_map/ppermute | solution.py:412
  268.8 28.7 %collective-permute-start.45 = (bf16[768,768]{1,0:T(8,128)(2,1)}, bf16[768,768]{1,0:T(8,128)(2,1)S(1)}, u32[]{:S(2)}, u32[]{:S(2)}) collective-permute-start(bf16[768,768]{1,0:T(8,128)(2,1)} %get-tuple-element.225), channel_id=1, source_target_pairs={{0,8},{4,12},{8,0},{12,4},{1,9},{5,13},{9,1},{13,5},{2,10},{6,14},... | collective-permute-start | bytes 3538952 | tf_op jit(solution)/shard_map/ppermute | solution.py:412
  281.9 19.5 %collective-permute-start.46 = (bf16[2,768,768]{2,1,0:T(8,128)(2,1)}, bf16[2,768,768]{2,1,0:T(8,128)(2,1)S(1)}, u32[]{:S(2)}, u32[]{:S(2)}) collective-permute-start(bf16[2,768,768]{2,1,0:T(8,128)(2,1)} %get-tuple-element.232), channel_id=1, source_target_pairs={{0,4},{4,0},{8,12},{12,8},{1,5},{5,1},{9,13},{13,9},{2,6},{6,2},{1... | collective-permute-start | bytes 7077896 | tf_op jit(solution)/shard_map/ppermute | solution.py:412
  282.1 23.3 %collective-permute-start.47 = (bf16[2,768,768]{2,1,0:T(8,128)(2,1)}, bf16[2,768,768]{2,1,0:T(8,128)(2,1)}, u32[]{:S(2)}, u32[]{:S(2)}) collective-permute-start(bf16[2,768,768]{2,1,0:T(8,128)(2,1)} %get-tuple-element.236), channel_id=1, source_target_pairs={{0,4},{4,0},{8,12},{12,8},{1,5},{5,1},{9,13},{13,9},{2,6},{6,2},{1... | collective-permute-start | bytes 7077896 | tf_op jit(solution)/shard_map/ppermute | solution.py:412
  282.5 103.8 %reduce-scatter.9.cloned.1.call-start = ((), (), s32[]{:S(2)}) async-start(), calls=%async_computation.8 | async-start | bytes 1474560 | tf_op jit(solution)/shard_map/reduce_scatter | solution.py:463
  310.1 32.4 %collective-permute-start.50 = (bf16[2,192,768]{2,1,0:T(8,128)(2,1)}, bf16[2,192,768]{2,1,0:T(8,128)(2,1)}, u32[]{:S(2)}, u32[]{:S(2)}) collective-permute-start(bf16[2,192,768]{2,1,0:T(8,128)(2,1)} %dynamic-slice_bitcast_fusion.1), channel_id=1, source_target_pairs={{0,1},{1,0},{2,3},{3,2},{4,5},{5,4},{6,7},{7,6},{8,9},{9,8},{10,11... | collective-permute-start | bytes 1769480 | tf_op jit(solution)/shard_map/ppermute | solution.py:412
  310.8 33.9 %collective-permute-start.48 = (bf16[768,768]{1,0:T(8,128)(2,1)}, bf16[768,768]{1,0:T(8,128)(2,1)}, u32[]{:S(2)}, u32[]{:S(2)}) collective-permute-start(bf16[768,768]{1,0:T(8,128)(2,1)} %get-tuple-element.243), channel_id=1, source_target_pairs={{0,8},{4,12},{8,0},{12,4},{1,9},{5,13},{9,1},{13,5},{2,10},{6,14},... | collective-permute-start | bytes 3538952 | tf_op jit(solution)/shard_map/ppermute | solution.py:412
  312.4 52.9 %collective-permute-start.56 = (bf16[768,768]{1,0:T(8,128)(2,1)}, bf16[768,768]{1,0:T(8,128)(2,1)}, u32[]{:S(2)}, u32[]{:S(2)}) collective-permute-start(bf16[768,768]{1,0:T(8,128)(2,1)} %get-tuple-element.280), channel_id=1, source_target_pairs={{0,8},{4,12},{8,0},{12,4},{1,9},{5,13},{9,1},{13,5},{2,10},{6,14},... | collective-permute-start | bytes 3538952 | tf_op jit(solution)/shard_map/ppermute | solution.py:412
  326.3 20.7 %collective-permute-start.49 = (bf16[2,768,768]{2,1,0:T(8,128)(2,1)}, bf16[2,768,768]{2,1,0:T(8,128)(2,1)S(1)}, u32[]{:S(2)}, u32[]{:S(2)}) collective-permute-start(bf16[2,768,768]{2,1,0:T(8,128)(2,1)} %get-tuple-element.251), channel_id=1, source_target_pairs={{0,4},{4,0},{8,12},{12,8},{1,5},{5,1},{9,13},{13,9},{2,6},{6,2},{1... | collective-permute-start | bytes 7077896 | tf_op jit(solution)/shard_map/ppermute | solution.py:412
  349.0 107.0 %reduce-scatter.11.cloned.1.call-start = ((), (), s32[]{:S(2)}) async-start(), calls=%async_computation.9 | async-start | bytes 1474560 | tf_op jit(solution)/shard_map/reduce_scatter | solution.py:463
  350.2 31.3 %collective-permute-start.57 = (bf16[1,192,768]{2,1,0:T(8,128)(2,1)S(1)}, bf16[1,192,768]{2,1,0:T(8,128)(2,1)S(1)}, u32[]{:S(2)}, u32[]{:S(2)}) collective-permute-start(bf16[1,192,768]{2,1,0:T(8,128)(2,1)S(1)} %constant_dynamic-slice_fusion), channel_id=1, source_target_pairs={{0,2},{1,3},{2,0},{3,1},{4,6},{5,7},{6,4},{7,5},{8,10},{9,11},{10,... | collective-permute-start | bytes 884744 | tf_op jit(solution)/shard_map/ppermute | solution.py:412
  352.8 36.5 %collective-permute-start.51 = (bf16[768,768]{1,0:T(8,128)(2,1)S(1)}, bf16[768,768]{1,0:T(8,128)(2,1)S(1)}, u32[]{:S(2)}, u32[]{:S(2)}) collective-permute-start(bf16[768,768]{1,0:T(8,128)(2,1)S(1)} %get-tuple-element.258), channel_id=1, source_target_pairs={{0,8},{4,12},{8,0},{12,4},{1,9},{5,13},{9,1},{13,5},{2,10},{6,14},... | collective-permute-start | bytes 3538952 | tf_op jit(solution)/shard_map/ppermute | solution.py:412
  400.1 56.0 %all-to-all-start.1 = ((bf16[8,208,448]{2,1,0:T(8,128)(2,1)}), bf16[8,208,448]{2,1,0:T(8,128)(2,1)S(1)}, u32[]{:S(2)}, u32[]{:S(2)}) async-start(bf16[8,208,448]{2,1,0:T(8,128)(2,1)} %fusion.1), calls=%async_computation.5 | async-start | bytes 3407872 | tf_op jit(solution)/shard_map/all_to_all | solution.py:703
  404.1 31.4 %collective-permute-start.53 = (bf16[2,192,768]{2,1,0:T(8,128)(2,1)S(1)}, bf16[2,192,768]{2,1,0:T(8,128)(2,1)S(1)}, u32[]{:S(2)}, u32[]{:S(2)}) collective-permute-start(bf16[2,192,768]{2,1,0:T(8,128)(2,1)S(1)} %dynamic-slice_bitcast_fusion), channel_id=1, source_target_pairs={{0,1},{1,0},{2,3},{3,2},{4,5},{5,4},{6,7},{7,6},{8,9},{9,8},{10,11... | collective-permute-start | bytes 1769480 | tf_op jit(solution)/shard_map/ppermute | solution.py:412
  406.6 25.2 %collective-permute-start.58 = (bf16[192,768]{1,0:T(8,128)(2,1)S(1)}, bf16[192,768]{1,0:T(8,128)(2,1)S(1)}, u32[]{:S(2)}, u32[]{:S(2)}) collective-permute-start(bf16[192,768]{1,0:T(8,128)(2,1)S(1)} %slice_bitcast_fusion.2), channel_id=1, source_target_pairs={{0,8},{4,12},{8,0},{12,4},{1,9},{5,13},{9,1},{13,5},{2,10},{6,14},... | collective-permute-start | bytes 884744 | tf_op jit(solution)/shard_map/ppermute | solution.py:412
  431.9 24.1 %collective-permute-start.55 = (bf16[1,192,768]{2,1,0:T(8,128)(2,1)S(1)}, bf16[1,192,768]{2,1,0:T(8,128)(2,1)S(1)}, u32[]{:S(2)}, u32[]{:S(2)}) collective-permute-start(bf16[1,192,768]{2,1,0:T(8,128)(2,1)S(1)} %bitcast.154), channel_id=1, source_target_pairs={{0,2},{1,3},{2,0},{3,1},{4,6},{5,7},{6,4},{7,5},{8,10},{9,11},{10,... | collective-permute-start | bytes 884744 | tf_op jit(solution)/shard_map/ppermute | solution.py:412
  436.4 24.9 %collective-permute-start.54 = (bf16[1,192,768]{2,1,0:T(8,128)(2,1)}, bf16[1,192,768]{2,1,0:T(8,128)(2,1)}, u32[]{:S(2)}, u32[]{:S(2)}) collective-permute-start(bf16[1,192,768]{2,1,0:T(8,128)(2,1)} %constant_dynamic-slice_fusion.1), channel_id=1, source_target_pairs={{0,2},{1,3},{2,0},{3,1},{4,6},{5,7},{6,4},{7,5},{8,10},{9,11},{10,... | collective-permute-start | bytes 884744 | tf_op jit(solution)/shard_map/ppermute | solution.py:412
  462.4 21.1 %collective-permute-start.62 = (bf16[2,192,768]{2,1,0:T(8,128)(2,1)S(1)}, bf16[2,192,768]{2,1,0:T(8,128)(2,1)S(1)}, u32[]{:S(2)}, u32[]{:S(2)}) collective-permute-start(bf16[2,192,768]{2,1,0:T(8,128)(2,1)S(1)} %maximum_select_fusion.3), channel_id=1, source_target_pairs={{0,1},{1,0},{2,3},{3,2},{4,5},{5,4},{6,7},{7,6},{8,9},{9,8},{10,11... | collective-permute-start | bytes 1769480 | tf_op jit(solution)/shard_map/ppermute | solution.py:412
  464.2 19.5 %collective-permute-start.61 = (bf16[192,768]{1,0:T(8,128)(2,1)S(1)}, bf16[192,768]{1,0:T(8,128)(2,1)S(1)}, u32[]{:S(2)}, u32[]{:S(2)}) collective-permute-start(bf16[192,768]{1,0:T(8,128)(2,1)S(1)} %broadcast_select_fusion.6), channel_id=1, source_target_pairs={{0,16},{16,0},{1,17},{17,1},{2,18},{18,2},{3,19},{19,3},{4,20},{20... | collective-permute-start | bytes 884744 | tf_op jit(solution)/shard_map/ppermute | solution.py:412
  466.0 17.5 %collective-permute-start.63 = (f32[12,192]{1,0:T(8,128)S(1)}, f32[12,192]{1,0:T(8,128)S(1)}, u32[]{:S(2)}, u32[]{:S(2)}) collective-permute-start(f32[12,192]{1,0:T(8,128)S(1)} %convert_reduce_fusion), channel_id=1, source_target_pairs={{0,1},{1,0},{2,3},{3,2},{4,5},{5,4},{6,7},{7,6},{8,9},{9,8},{10,11... | collective-permute-start | bytes 27656 | tf_op jit(solution)/shard_map/ppermute | solution.py:412
  466.3 17.6 %collective-permute-start.60 = (bf16[1,192,768]{2,1,0:T(8,128)(2,1)S(1)}, bf16[1,192,768]{2,1,0:T(8,128)(2,1)S(1)}, u32[]{:S(2)}, u32[]{:S(2)}) collective-permute-start(bf16[1,192,768]{2,1,0:T(8,128)(2,1)S(1)} %bitcast.156), channel_id=1, source_target_pairs={{0,2},{1,3},{2,0},{3,1},{4,6},{5,7},{6,4},{7,5},{8,10},{9,11},{10,... | collective-permute-start | bytes 884744 | tf_op jit(solution)/shard_map/ppermute | solution.py:412
  487.7 22.2 %collective-permute-start.67 = (bf16[2,192,768]{2,1,0:T(8,128)(2,1)}, bf16[2,192,768]{2,1,0:T(8,128)(2,1)}, u32[]{:S(2)}, u32[]{:S(2)}) collective-permute-start(bf16[2,192,768]{2,1,0:T(8,128)(2,1)} %maximum_select_fusion.4), channel_id=1, source_target_pairs={{0,1},{1,0},{2,3},{3,2},{4,5},{5,4},{6,7},{7,6},{8,9},{9,8},{10,11... | collective-permute-start | bytes 1769480 | tf_op jit(solution)/shard_map/ppermute | solution.py:412
  501.3 18.0 %collective-permute-start.66 = (bf16[2,192,768]{2,1,0:T(8,128)(2,1)}, bf16[2,192,768]{2,1,0:T(8,128)(2,1)}, u32[]{:S(2)}, u32[]{:S(2)}) collective-permute-start(bf16[2,192,768]{2,1,0:T(8,128)(2,1)} %maximum_select_fusion.5), channel_id=1, source_target_pairs={{0,1},{1,0},{2,3},{3,2},{4,5},{5,4},{6,7},{7,6},{8,9},{9,8},{10,11... | collective-permute-start | bytes 1769480 | tf_op jit(solution)/shard_map/ppermute | solution.py:412
  (98 other events, 707.3 us)
Sparse Core Ops, SparseCore 0:
  232.3 47.4 reduce-scatter.4
  282.6 29.3 reduce-scatter.6
  349.1 37.0 reduce-scatter.8
  389.0 37.7 reduce-scatter.10

commit v9 on v8

--- a/solution.py
+++ b/solution.py
@@ -495,12 +495,10 @@
 
     def join(self, bit):
         upper = (lax.axis_index("dp") & bit) != 0
-        value = jnp.where(
-            upper,
-            jnp.stack([self.arrived, self.value], axis=1),
-            jnp.stack([self.value, self.arrived], axis=1),
-        )
-        self.value = value.reshape(-1, *value.shape[2:])
+        rows = []
+        for arrived, value in zip(self.arrived, self.value):
+            rows += [jnp.where(upper, arrived, value), jnp.where(upper, value, arrived)]
+        self.value = jnp.concatenate(rows, axis=0).reshape(len(rows), -1, D)
 
 
 def tied(chains, *others):
@@ -533,7 +531,7 @@
     )
     ends = ends_in[0].T.reshape(FEATS, clips, FRAMES).transpose(1, 0, 2)
     ends = with_rows(ends, jnp.broadcast_to(small, (clips,) + small.shape))
-    beyond_a, near_one, own_two, ends = tie((beyond_a, nears[1], owned[2], ends))
+    beyond_a, near_one, ends = tie((beyond_a, nears[1], ends))
     ends = lax.all_to_all(ends, ("section", "tensor"), split_axis=0, concat_axis=0, tiled=True)
     small = ends[:, FEATS : FEATS + 12, :FEATS].astype(F32)
     cols = jnp.swapaxes(small[:, :8], 1, 2).reshape(2, SHARDS, FEATS, 8)
@@ -554,11 +552,11 @@
 
     n_dp = lax.axis_size("dp")
     beyond_one = flip(near_one, "section", 1)
-    beyond_two = flip(own_two, "section", 1)
     near_a = layers(nears[0], beyond_a)
     far_a = layers(fars[0], flip(beyond_a, "dp", 1))
     there_a = over_y(near_a[0])
-    there_a, beyond_one = tie((there_a, beyond_one))
+    there_a, beyond_one, own_two = tie((there_a, beyond_one, owned[2]))
+    beyond_two = flip(own_two, "section", 1)
     away_a = flip(there_a, "dp", 1)
     near_one = layers(nears[1], beyond_one)
     beyond_far_one = flip(beyond_one, "dp", 1)
@@ -647,6 +645,7 @@
             info, gh, x, a1, cols[layer], p, soft, o, after, chunk_a
         )
         chain_a.cores(keep_a)
+        ends_of[layer] = (db1_kept, db1_sent, (dbqv_kept, dbqv_sent, dcol_one, dcol_two))
         if layer == 1:
             late_two.fold_rows()
             (upstream,) = tied((late_two, late_a), upstream)
@@ -655,7 +654,7 @@
         else:
             last_two.fold_rows()
             late_a.fold()
-            (upstream,) = tied((last_two, last_a, late_two, late_a), upstream)
+            upstream, ends_of = tied((last_two, last_a, late_two, late_a), upstream, ends_of)
             for bit in bits[1:]:
                 late_a.send_half(bit)
                 if bit != bits[-1]:
@@ -663,7 +662,6 @@
             last_two.scatter()
             last_a.send_y()
             late_one.send_y()
-        ends_of[layer] = (db1_kept, db1_sent, (dbqv_kept, dbqv_sent, dcol_one, dcol_two))
 
     pair_two, pair_one, pair_a = Chain(), Chain(), Chain()
 
@@ -677,16 +675,6 @@
             pair.send_back(bit)
             pair.join(bit)
 
-    last_one.fold_rows()
-    late_a.fold()
-    late_a.value = late_a.value[0]
-    tied((last_one, late_a))
-    last_one.scatter()
-    tied((last_two, late_two))
-    pair_two.send_x(last_two, late_two)
-
-    pair_two.fold()
-    upstream, ends_of = tied((pair_two,), upstream, ends_of)
     for layer in range(2):
         db1_kept, db1_sent, dcols = ends_of[layer]
         smalls[layer] = jnp.concatenate(
@@ -700,53 +688,60 @@
     result = with_rows(
         result.reshape(2 * SHARDS, FEATS, FRAMES), jnp.stack(smalls).reshape(-1, 12, FEATS)
     )
+    late_a.fold()
+    late_a.value = late_a.value[0]
+    result, last_one.arrived = tied((last_two, late_two, late_a), result, last_one.arrived)
+    last_one.fold_rows()
+    late_one.fold()
+    tied((last_one, late_one, last_two, late_two))
+    last_one.scatter()
+    pair_two.send_x(last_two, late_two)
     result = lax.all_to_all(result, ("section", "tensor"), split_axis=0, concat_axis=0, tiled=True)
 
     last_a.fold_rows()
-    tied((last_a, pair_two))
+    tied((last_a,))
     last_a.split()
     last_a.send_half(bits[0])
+    pair_two.fold()
     start_far(pair_two)
 
     last_a.fold()
-    tied((last_a,))
+    (pair_two.arrived,) = tied((last_a,), pair_two.arrived)
     for bit in bits[1:]:
         last_a.send_half(bit)
         if bit != bits[-1]:
             last_a.fold()
-
-    late_one.fold()
     finish_far(pair_two)
-    (result,) = tied((pair_two, last_one, late_one), result)
-    pair_one.send_x(last_one, late_one)
+    (result,) = tied((pair_two,), result)
     pair_two.send_back(bits[0])
-    small_sum = result[:, FEATS : FEATS + 12, :FEATS].astype(F32).sum(axis=0)
 
     last_a.fold()
     last_a.value = last_a.value[0]
+    pair_a.send_x(last_a, late_a)
+    pair_one.send_x(last_one, late_one)
+    pair_a.fold()
     pair_one.fold()
-    result, small_sum = tied((last_a, pair_one), result, small_sum)
-    pair_a.send_x(last_a, late_a)
+    result, pair_two.arrived = tied((pair_a, pair_one), result, pair_two.arrived)
+    start_far(pair_a)
     start_far(pair_one)
-    small_sum += flip(small_sum, "dp", bits[0])
-
-    pair_a.fold()
+    small_sum = result[:, FEATS : FEATS + 12, :FEATS].astype(F32).sum(axis=0)
+    small_parts = [flip(small_sum, "dp", k) for k in range(1, n_dp)] if n_dp <= 4 else None
     pair_two.join(bits[0])
-    result, small_sum = tied((pair_a, pair_two), result, small_sum)
-    start_far(pair_a)
-    for bit in bits[1:]:
-        small_sum += flip(small_sum, "dp", bit)
-
+
+    finish_far(pair_a)
+    (pair_one.arrived,) = tied((pair_a,), pair_one.arrived)
+    pair_a.send_back(bits[0])
     finish_far(pair_one)
     (result,) = tied((pair_one,), result)
     pair_one.send_back(bits[0])
     result = result[:, :FEATS].transpose(1, 0, 2).reshape(FEATS, clips * FRAMES).T.astype(F32)
-
-    finish_far(pair_a)
-    (small_sum,) = tied((pair_a,), small_sum)
-    pair_a.send_back(bits[0])
+    pair_a.join(bits[0])
+    if small_parts is None:
+        small_sum = lax.psum(small_sum, "dp")
+    else:
+        small_parts, pair_a.value = tie((small_parts, pair_a.value))
+        small_sum = sum(small_parts, small_sum)
     pair_one.join(bits[0])
-    pair_a.join(bits[0])
     for pair in (pair_two, pair_one, pair_a):
         pair.value = pair.value.reshape(D, D)
 

time: 539 us -> 560 us (1.039)
  other arithmetic: 31.6 us -> 45.8 us
  local copies, waits for them, and re-layouts: 41.2 us -> 48.8 us
    ppermute x68 -> x69, waiting for transfers between devices: 169 us -> 188 us  [flip(): return lax.ppermute(block, axis, [(i, i ^ bit) for i in range(size)])]
    all_to_all x1, waiting for transfers between devices: 12 us -> 0.01 us  [body(): lax.all_to_all(ends, ('section', 'tensor'), split_axis=0, concat_axis=0,...]
    unnamed x145 -> x147, local copies, waits for them, and re-layouts: 16.9 us -> 21.1 us
    ppermute x68 -> x69, starting transfers between devices: 57.7 us -> 54.4 us  [flip(): return lax.ppermute(block, axis, [(i, i ^ bit) for i in range(size)])]
  transfers between devices with their start and end apart: 74 -> 75, of which waited for: 30 -> 27; matrix products, arithmetic and copies ran while one was open for 8% -> 12% of each run, Pallas kernels for 31% -> 30%
where the time goes in v9:
time: 560 us; the launch traced here: 554 us
  Pallas kernels  193 us (34%)
  waiting for transfers between devices  188 us (34%)
  starting transfers between devices  62.4 us (11%)
  local copies, waits for them, and re-layouts  48.8 us (9%)
  other arithmetic  45.8 us (8%)
  between operations  15.3 us (3%)
    ppermute x69, waiting for transfers between devices, flip(): return lax.ppermute(block, axis, [(i, i ^ bit) for i in range(size)])  188 us
    pallas_call x12, Pallas kernels, run(): pl.pallas_call(kernel, name=name, out_shape=outs, grid_spec=pltpu.Prefetc...  176 us
    ppermute x69, starting transfers between devices, flip(): return lax.ppermute(block, axis, [(i, i ^ bit) for i in range(size)])  54.4 us
    unnamed x147, local copies, waits for them, and re-layouts  21.1 us
    pallas_call x11, Pallas kernels, summed(): pl.pallas_call(sum_kernel, name='row_sums', grid=(rows // block,), in_spe...  16.9 us
  transfers between devices with their start and end apart: 75, of which 27 were waited for; matrix products, arithmetic and copies ran while one was open for 12% of the time, Pallas kernels for 30%

profile of v9, /device:TPU:0, one launch (start us, length us, event | category | flops | bytes accessed | tf_op | source)
XLA Modules:
  0.0 553.8 jit_solution(12405917272945063653)
XLA Ops:
  8.7 3.0 collective-permute-start
  11.8 3.2 reshape.203
  16.2 8.9 %collective-permute-done = bf16[384,768]{1,0:T(8,128)(2,1)} collective-permute-done((bf16[384,768]{1,0:T(8,128)(2,1)S(1)}, bf16[384,768]{1,0:T(8,128)(2,1)}, u32[]{:S(2)}, u32[]{:S(2)}) %collective-permute-start) | collective-permute-done | bytes 589856 | tf_op jit(solution)/shard_map/ppermute | solution.py:412
  26.9 4.0 all-to-all-start
  38.0 27.1 %collective-permute-done.4.refs_4_.refs_5_ = bf16[384,768]{1,0:T(8,128)(2,1)} collective-permute-done((bf16[384,768]{1,0:T(8,128)(2,1)S(1)}, bf16[384,768]{1,0:T(8,128)(2,1)}, u32[]{:S(2)}, u32[]{:S(2)}) %collective-permute-start.4) | collective-permute-done | bytes 589856 | tf_op jit(solution)/shard_map/ppermute | solution.py:412
  68.1 2.3 broadcast_select_fusion
  72.9 2.6 broadcast_select_fusion.1
  75.9 4.4 collective-permute-done.6.refs_5_.refs_6_
  80.3 4.8 collective-permute-done.9.refs_4_.refs_5_
  87.3 6.9 %collective-permute-done.10 = bf16[768,768]{1,0:T(8,128)(2,1)} collective-permute-done((bf16[768,768]{1,0:T(8,128)(2,1)}, bf16[768,768]{1,0:T(8,128)(2,1)}, u32[]{:S(2)}, u32[]{:S(2)}) %collective-permute-start.10) | collective-permute-done | bytes 1179680 | tf_op jit(solution)/shard_map/ppermute | solution.py:412
  94.6 3.3 bitcast_select_fusion.2
  101.5 17.0 %attention_forward.2 = (bf16[768,448]{1,0:T(8,128)(2,1)}, bf16[4,576,448]{2,1,0:T(8,128)(2,1)}, bf16[4,3,448,448]{3,2,1,0:T(8,128)(2,1)}, bf16[4,192,448]{2,1,0:T(8,128)(2,1)}, f32[768,448]{1,0:T(8,128)}) custom-call(s32[9]{0:T(128)} %stack.47.info, bf16[768,448]{1,0:T(8,128)(2,1)} %bitcast.164, f32[4,192,8]{2,1,0:T(8,128)} %get-tuple-element.344.col_ref, ...), custom_call_target="tpu_custom_call" | custom-call | flops 43687870464 | bytes 268435456 | tf_op jit(solution)/shard_map/attention_forward/pallas_call | solution.py:311
  121.5 2.3 bitcast_select_fusion
  125.9 10.9 %collective-permute-done.20.refs_13_.refs_14_ = bf16[384,768]{1,0:T(8,128)(2,1)} collective-permute-done((bf16[384,768]{1,0:T(8,128)(2,1)}, bf16[384,768]{1,0:T(8,128)(2,1)}, u32[]{:S(2)}, u32[]{:S(2)}) %collective-permute-start.20) | collective-permute-done | bytes 589856 | tf_op jit(solution)/shard_map/ppermute | solution.py:412
  141.2 14.0 %mlp_forward.2 = (bf16[768,448]{1,0:T(8,128)(2,1)}, bf16[4,448,768]{2,1,0:T(8,128)(2,1)}, bf16[4,448,768]{2,1,0:T(8,128)(2,1)}, f32[768,448]{1,0:T(8,128)}) custom-call(s32[9]{0:T(128)} %stack.47.info, f32[768,448]{1,0:T(8,128)} %get-tuple-element.173.h_ref, f32[4,192,8]{2,1,0:T(8,128)} %get-tuple-element.344.col_ref, f32[4,1,768]{2,1,0:T(1,128)} %squeeze.92.b1_ref, ...), custom_call_target="tpu_custom_call" | custom-call | flops 67645734912 | bytes 268435456 | tf_op jit(solution)/shard_map/mlp_forward/pallas_call | solution.py:311
  161.5 17.0 %attention_forward.3 = (bf16[768,448]{1,0:T(8,128)(2,1)}, bf16[4,576,448]{2,1,0:T(8,128)(2,1)}, bf16[4,3,448,448]{3,2,1,0:T(8,128)(2,1)}, bf16[4,192,448]{2,1,0:T(8,128)(2,1)}, f32[768,448]{1,0:T(8,128)}) custom-call(s32[9]{0:T(128)} %stack.47.info, f32[768,448]{1,0:T(8,128)} %get-tuple-element.181.x_ref, f32[4,192,8]{2,1,0:T(8,128)} %get-tuple-element.343.col_ref, ...), custom_call_target="tpu_custom_call" | custom-call | flops 43687870464 | bytes 268435456 | tf_op jit(solution)/shard_map/attention_forward/pallas_call | solution.py:311
  178.5 6.0 %collective-permute-done.32.refs_13_.refs_14_ = bf16[384,768]{1,0:T(8,128)(2,1)} collective-permute-done((bf16[384,768]{1,0:T(8,128)(2,1)}, bf16[384,768]{1,0:T(8,128)(2,1)}, u32[]{:S(2)}, u32[]{:S(2)}) %collective-permute-start.32) | collective-permute-done | bytes 589856 | tf_op jit(solution)/shard_map/ppermute | solution.py:412
  186.6 2.4 collective-permute-done.34.refs_3_.refs_4_
  193.0 14.4 %mlp_forward.3 = (bf16[768,448]{1,0:T(8,128)(2,1)}, bf16[4,448,768]{2,1,0:T(8,128)(2,1)}, bf16[4,448,768]{2,1,0:T(8,128)(2,1)}, f32[768,448]{1,0:T(8,128)}) custom-call(s32[9]{0:T(128)} %stack.47.info, f32[768,448]{1,0:T(8,128)} %get-tuple-element.190.h_ref, f32[4,192,8]{2,1,0:T(8,128)} %get-tuple-element.343.col_ref, f32[4,1,768]{2,1,0:T(1,128)} %squeeze.93.b1_ref, ...), custom_call_target="tpu_custom_call" | custom-call | flops 67645734912 | bytes 268435456 | tf_op jit(solution)/shard_map/mlp_forward/pallas_call | solution.py:311
  207.4 12.3 %mlp_backward.4 = (f32[448,768]{1,0:T(8,128)}, bf16[2,768,768]{2,1,0:T(8,128)(2,1)}, bf16[2,768,768]{2,1,0:T(8,128)(2,1)}, f32[4,1,768]{2,1,0:T(1,128)}) custom-call(s32[9]{0:T(128)} %stack.47.info, bf16[768,448]{1,0:T(8,128)(2,1)} %bitcast.167, f32[768,448]{1,0:T(8,128)} %get-tuple-element.190.h_ref, bf16[768,448]{1,0:T(8,128)(2,1)} %get-tuple-element.199.a2_ref, ...), custom_call_target="tpu_custom_call" | custom-call | flops 67645734912 | bytes 268435456 | tf_op jit(solution)/shard_map/mlp_backward/pallas_call | solution.py:311
  220.4 14.5 %mlp_backward.5 = (f32[768,448]{1,0:T(8,128)}, f32[4,192,8]{2,1,0:T(8,128)}, bf16[2,768,768]{2,1,0:T(8,128)(2,1)}, bf16[2,768,768]{2,1,0:T(8,128)(2,1)}, f32[4,1,768]{2,1,0:T(1,128)}) custom-call(s32[9]{0:T(128)} %stack.47.info, bf16[768,448]{1,0:T(8,128)(2,1)} %bitcast.168, f32[768,448]{1,0:T(8,128)} %get-tuple-element.190.h_ref, ...), custom_call_target="tpu_custom_call" | custom-call | flops 67645734912 | bytes 268435456 | tf_op jit(solution)/shard_map/mlp_backward/pallas_call | solution.py:311
  236.6 2.1 row_sums.11
  243.1 14.0 %attention_backward.4 = (f32[448,768]{1,0:T(8,128)}, bf16[2,768,768]{2,1,0:T(8,128)(2,1)}, f32[4,192,8]{2,1,0:T(8,128)}) custom-call(s32[9]{0:T(128)} %stack.47.info, f32[768,448]{1,0:T(8,128)} %get-tuple-element.214.gh_ref, f32[768,448]{1,0:T(8,128)} %get-tuple-element.181.x_ref, bf16[768,448]{1,0:T(8,128)(2,1)} %get-tuple-element.215.a1_ref, ...), custom_call_target="tpu_custom_call" | custom-call | flops 43687870464 | bytes 268435456 | tf_op jit(solution)/shard_map/attention_backward/pallas_call | solution.py:311
  257.1 16.1 %attention_backward.5 = (f32[768,448]{1,0:T(8,128)}, f32[4,192,8]{2,1,0:T(8,128)}, bf16[2,768,768]{2,1,0:T(8,128)(2,1)}, f32[4,192,8]{2,1,0:T(8,128)}) custom-call(s32[9]{0:T(128)} %stack.47.info, f32[768,448]{1,0:T(8,128)} %get-tuple-element.214.gh_ref, f32[768,448]{1,0:T(8,128)} %get-tuple-element.181.x_ref, bf16[768,448]{1,0:T(8,128)(2,1)} %get-tuple-element.215.a1_ref, ...), custom_call_target="tpu_custom_call" | custom-call | flops 43687870464 | bytes 268435456 | tf_op jit(solution)/shard_map/attention_backward/pallas_call | solution.py:311
  274.7 2.2 row_sums.13
  280.2 12.6 %mlp_backward.6 = (f32[448,768]{1,0:T(8,128)}, bf16[2,768,768]{2,1,0:T(8,128)(2,1)}, bf16[2,768,768]{2,1,0:T(8,128)(2,1)}, f32[4,1,768]{2,1,0:T(1,128)}) custom-call(s32[9]{0:T(128)} %stack.47.info, f32[768,448]{1,0:T(8,128)} %get-tuple-element.227.gy_ref, f32[768,448]{1,0:T(8,128)} %get-tuple-element.173.h_ref, bf16[768,448]{1,0:T(8,128)(2,1)} %get-tuple-element.228.a2_ref, ...), custom_call_target="tpu_custom_call" | custom-call | flops 67645734912 | bytes 268435456 | tf_op jit(solution)/shard_map/mlp_backward/pallas_call | solution.py:311
  293.4 14.9 %mlp_backward.7 = (f32[768,448]{1,0:T(8,128)}, f32[4,192,8]{2,1,0:T(8,128)}, bf16[2,768,768]{2,1,0:T(8,128)(2,1)}, bf16[2,768,768]{2,1,0:T(8,128)(2,1)}, f32[4,1,768]{2,1,0:T(1,128)}) custom-call(s32[9]{0:T(128)} %stack.47.info, f32[768,448]{1,0:T(8,128)} %get-tuple-element.227.gy_ref, f32[768,448]{1,0:T(8,128)} %get-tuple-element.173.h_ref, ...), custom_call_target="tpu_custom_call" | custom-call | flops 67645734912 | bytes 268435456 | tf_op jit(solution)/shard_map/mlp_backward/pallas_call | solution.py:311
  323.5 13.5 %attention_backward.6 = (f32[448,768]{1,0:T(8,128)}, bf16[2,768,768]{2,1,0:T(8,128)(2,1)}, f32[4,192,8]{2,1,0:T(8,128)}) custom-call(s32[9]{0:T(128)} %stack.47.info, f32[768,448]{1,0:T(8,128)} %get-tuple-element.245.gh_ref, bf16[768,448]{1,0:T(8,128)(2,1)} %bitcast.165, bf16[768,448]{1,0:T(8,128)(2,1)} %get-tuple-element.246.a1_ref, ...), custom_call_target="tpu_custom_call" | custom-call | flops 43687870464 | bytes 268435456 | tf_op jit(solution)/shard_map/attention_backward/pallas_call | solution.py:311
  337.1 16.1 %attention_backward.7 = (f32[768,448]{1,0:T(8,128)}, f32[4,192,8]{2,1,0:T(8,128)}, bf16[2,768,768]{2,1,0:T(8,128)(2,1)}, f32[4,192,8]{2,1,0:T(8,128)}) custom-call(s32[9]{0:T(128)} %stack.47.info, f32[768,448]{1,0:T(8,128)} %get-tuple-element.245.gh_ref, bf16[768,448]{1,0:T(8,128)(2,1)} %bitcast.166, bf16[768,448]{1,0:T(8,128)(2,1)} %get-tuple-element.246.a1_ref, ...), custom_call_target="tpu_custom_call" | custom-call | flops 43687870464 | bytes 268435456 | tf_op jit(solution)/shard_map/attention_backward/pallas_call | solution.py:311
  355.3 2.5 row_sums.18
  365.7 7.1 %collective-permute-done.55 = bf16[192,768]{1,0:T(8,128)(2,1)} collective-permute-done((bf16[192,768]{1,0:T(8,128)(2,1)}, bf16[192,768]{1,0:T(8,128)(2,1)}, u32[]{:S(2)}, u32[]{:S(2)}) %collective-permute-start.55) | collective-permute-done | bytes 294944 | tf_op jit(solution)/shard_map/ppermute | solution.py:412
  376.8 2.4 collective-permute-start.53
  379.2 2.8 fusion.9
  390.2 11.4 %collective-permute-done.53 = bf16[1,192,768]{2,1,0:T(8,128)(2,1)} collective-permute-done((bf16[1,192,768]{2,1,0:T(8,128)(2,1)}, bf16[1,192,768]{2,1,0:T(8,128)(2,1)}, u32[]{:S(2)}, u32[]{:S(2)}) %collective-permute-start.53) | collective-permute-done | bytes 294944 | tf_op jit(solution)/shard_map/ppermute | solution.py:412
  405.8 17.1 %collective-permute-done.51.right_ref = bf16[768,768]{1,0:T(8,128)(2,1)} collective-permute-done((bf16[768,768]{1,0:T(8,128)(2,1)S(1)}, bf16[768,768]{1,0:T(8,128)(2,1)}, u32[]{:S(2)}, u32[]{:S(2)}) %collective-permute-start.51) | collective-permute-done | bytes 1179680 | tf_op jit(solution)/shard_map/ppermute | solution.py:412
  429.5 3.9 all-to-all-start.1
  436.5 2.5 collective-permute-start.57
  438.9 12.1 %collective-permute-done.52 = bf16[2,192,768]{2,1,0:T(8,128)(2,1)} collective-permute-done((bf16[2,192,768]{2,1,0:T(8,128)(2,1)}, bf16[2,192,768]{2,1,0:T(8,128)(2,1)}, u32[]{:S(2)}, u32[]{:S(2)}) %collective-permute-start.52) | collective-permute-done | bytes 589856 | tf_op jit(solution)/shard_map/ppermute | solution.py:412
  452.4 15.3 %collective-permute-done.58 = bf16[1,192,768]{2,1,0:T(8,128)(2,1)S(1)} collective-permute-done((bf16[1,192,768]{2,1,0:T(8,128)(2,1)S(1)}, bf16[1,192,768]{2,1,0:T(8,128)(2,1)S(1)}, u32[]{:S(2)}, u32[]{:S(2)}) %collective-permute-start.58) | collective-permute-done | bytes 294944 | tf_op jit(solution)/shard_map/ppermute | solution.py:412
  471.9 6.9 %collective-permute-done.59 = bf16[192,768]{1,0:T(8,128)(2,1)} collective-permute-done((bf16[192,768]{1,0:T(8,128)(2,1)}, bf16[192,768]{1,0:T(8,128)(2,1)}, u32[]{:S(2)}, u32[]{:S(2)}) %collective-permute-start.59) | collective-permute-done | bytes 294944 | tf_op jit(solution)/shard_map/ppermute | solution.py:412
  480.1 3.2 collective-permute-done.60
  486.7 2.6 collective-permute-start.64
  490.8 2.6 collective-permute-start.63
  495.0 14.9 %collective-permute-done.62 = bf16[1,192,768]{2,1,0:T(8,128)(2,1)S(1)} collective-permute-done((bf16[1,192,768]{2,1,0:T(8,128)(2,1)S(1)}, bf16[1,192,768]{2,1,0:T(8,128)(2,1)S(1)}, u32[]{:S(2)}, u32[]{:S(2)}) %collective-permute-start.62) | collective-permute-done | bytes 294944 | tf_op jit(solution)/shard_map/ppermute | solution.py:412
  510.8 5.1 collective-permute-done.63
  521.1 2.4 reshape.217
  523.5 9.0 %collective-permute-done.67 = bf16[2,192,768]{2,1,0:T(8,128)(2,1)} collective-permute-done((bf16[2,192,768]{2,1,0:T(8,128)(2,1)}, bf16[2,192,768]{2,1,0:T(8,128)(2,1)}, u32[]{:S(2)}, u32[]{:S(2)}) %collective-permute-start.67) | collective-permute-done | bytes 589856 | tf_op jit(solution)/shard_map/ppermute | solution.py:412
  538.1 5.8 %collective-permute-done.68 = bf16[2,192,768]{2,1,0:T(8,128)(2,1)} collective-permute-done((bf16[2,192,768]{2,1,0:T(8,128)(2,1)}, bf16[2,192,768]{2,1,0:T(8,128)(2,1)}, u32[]{:S(2)}, u32[]{:S(2)}) %collective-permute-start.68) | collective-permute-done | bytes 589856 | tf_op jit(solution)/shard_map/ppermute | solution.py:412
  (358 shorter events, 136.1 us)
Async XLA Ops:
  8.7 16.4 %collective-permute-start = (bf16[384,768]{1,0:T(8,128)(2,1)S(1)}, bf16[384,768]{1,0:T(8,128)(2,1)}, u32[]{:S(2)}, u32[]{:S(2)}) collective-permute-start(bf16[384,768]{1,0:T(8,128)(2,1)S(1)} %fusion.5), channel_id=1, source_target_pairs={{0,16},{16,0},{1,17},{17,1},{2,18},{18,2},{3,19},{19,3},{4,20},{20... | collective-permute-start | bytes 1769480 | tf_op jit(solution)/shard_map/ppermute | solution.py:412
  26.9 48.6 %all-to-all-start = ((bf16[8,208,448]{2,1,0:T(8,128)(2,1)}), bf16[8,208,448]{2,1,0:T(8,128)(2,1)S(1)}, u32[]{:S(2)}, u32[]{:S(2)}) async-start(bf16[8,208,448]{2,1,0:T(8,128)(2,1)} %copy.76), calls=%async_computation | async-start | bytes 3407872 | tf_op jit(solution)/shard_map/all_to_all | solution.py:535
  30.8 289.6 %reduce-scatter.5.cloned.1.call-start = ((), (), s32[]{:S(2)}) async-start(), calls=%async_computation.6 | async-start | bytes 2949120 | tf_op jit(solution)/shard_map/reduce_scatter | solution.py:463
  33.0 32.1 %collective-permute-start.4 = (bf16[384,768]{1,0:T(8,128)(2,1)S(1)}, bf16[384,768]{1,0:T(8,128)(2,1)}, u32[]{:S(2)}, u32[]{:S(2)}) collective-permute-start(bf16[384,768]{1,0:T(8,128)(2,1)S(1)} %get-tuple-element.342.refs_0_.refs_1_), channel_id=1, source_target_pairs={{0,8},{4,12},{8,0},{12,4},{1,9},{5,13},{9,1},{13,5},{2,10},{6,14},... | collective-permute-start | bytes 1769480 | tf_op jit(solution)/shard_map/ppermute | solution.py:412
  35.0 30.1 %collective-permute-start.5 = (bf16[384,768]{1,0:T(8,128)(2,1)S(1)}, bf16[384,768]{1,0:T(8,128)(2,1)}, u32[]{:S(2)}, u32[]{:S(2)}) collective-permute-start(bf16[384,768]{1,0:T(8,128)(2,1)S(1)} %copy-done.40), channel_id=1, source_target_pairs={{0,16},{16,0},{1,17},{17,1},{2,18},{18,2},{3,19},{19,3},{4,20},{20... | collective-permute-start | bytes 1769480 | tf_op jit(solution)/shard_map/ppermute | solution.py:412
  36.4 35.1 %collective-permute-start.1 = (bf16[384,768]{1,0:T(8,128)(2,1)}, bf16[384,768]{1,0:T(8,128)(2,1)S(1)}, u32[]{:S(2)}, u32[]{:S(2)}) collective-permute-start(bf16[384,768]{1,0:T(8,128)(2,1)} %collective-permute-done), channel_id=1, source_target_pairs={{0,1},{1,0},{2,3},{3,2},{4,5},{5,4},{6,7},{7,6},{8,9},{9,8},{10,11... | collective-permute-start | bytes 1769480 | tf_op jit(solution)/shard_map/ppermute | solution.py:412
  66.6 27.5 %collective-permute-start.10 = (bf16[768,768]{1,0:T(8,128)(2,1)}, bf16[768,768]{1,0:T(8,128)(2,1)}, u32[]{:S(2)}, u32[]{:S(2)}) collective-permute-start(bf16[768,768]{1,0:T(8,128)(2,1)} %bitcast.19), channel_id=1, source_target_pairs={{0,16},{16,0},{1,17},{17,1},{2,18},{18,2},{3,19},{19,3},{4,20},{20... | collective-permute-start | bytes 3538952 | tf_op jit(solution)/shard_map/ppermute | solution.py:412
  71.5 26.4 %collective-permute-start.2 = (bf16[384,768]{1,0:T(8,128)(2,1)}, bf16[384,768]{1,0:T(8,128)(2,1)}, u32[]{:S(2)}, u32[]{:S(2)}) collective-permute-start(bf16[384,768]{1,0:T(8,128)(2,1)} %copy-done.38), channel_id=1, source_target_pairs={{0,4},{4,0},{8,12},{12,8},{1,5},{5,1},{9,13},{13,9},{2,6},{6,2},{1... | collective-permute-start | bytes 1769480 | tf_op jit(solution)/shard_map/ppermute | solution.py:412
  72.4 25.6 %collective-permute-start.7 = (bf16[384,768]{1,0:T(8,128)(2,1)}, bf16[384,768]{1,0:T(8,128)(2,1)}, u32[]{:S(2)}, u32[]{:S(2)}) collective-permute-start(bf16[384,768]{1,0:T(8,128)(2,1)} %collective-permute-done.4.refs_4_.refs_5_), channel_id=1, source_target_pairs={{0,4},{4,0},{8,12},{12,8},{1,5},{5,1},{9,13},{13,9},{2,6},{6,2},{1... | collective-permute-start | bytes 1769480 | tf_op jit(solution)/shard_map/ppermute | solution.py:412
  80.2 18.2 %collective-permute-start.3 = (bf16[384,768]{1,0:T(8,128)(2,1)S(1)}, bf16[384,768]{1,0:T(8,128)(2,1)S(1)}, u32[]{:S(2)}, u32[]{:S(2)}) collective-permute-start(bf16[384,768]{1,0:T(8,128)(2,1)S(1)} %get-tuple-element.324.refs_1_.refs_2_), channel_id=1, source_target_pairs={{0,4},{4,0},{8,12},{12,8},{1,5},{5,1},{9,13},{13,9},{2,6},{6,2},{1... | collective-permute-start | bytes 1769480 | tf_op jit(solution)/shard_map/ppermute | solution.py:412
  94.2 24.4 %collective-permute-start.13 = (bf16[384,768]{1,0:T(8,128)(2,1)}, bf16[384,768]{1,0:T(8,128)(2,1)}, u32[]{:S(2)}, u32[]{:S(2)}) collective-permute-start(bf16[384,768]{1,0:T(8,128)(2,1)} %collective-permute-done.5), channel_id=1, source_target_pairs={{0,1},{1,0},{2,3},{3,2},{4,5},{5,4},{6,7},{7,6},{8,9},{9,8},{10,11... | collective-permute-start | bytes 1769480 | tf_op jit(solution)/shard_map/ppermute | solution.py:412
  98.0 25.9 %collective-permute-start.14 = (bf16[384,768]{1,0:T(8,128)(2,1)}, bf16[384,768]{1,0:T(8,128)(2,1)}, u32[]{:S(2)}, u32[]{:S(2)}) collective-permute-start(bf16[384,768]{1,0:T(8,128)(2,1)} %get-tuple-element.340.refs_0_.refs_1_), channel_id=1, source_target_pairs={{0,4},{4,0},{8,12},{12,8},{1,5},{5,1},{9,13},{13,9},{2,6},{6,2},{1... | collective-permute-start | bytes 1769480 | tf_op jit(solution)/shard_map/ppermute | solution.py:412
  98.0 25.9 %collective-permute-start.16 = (bf16[384,768]{1,0:T(8,128)(2,1)}, bf16[384,768]{1,0:T(8,128)(2,1)}, u32[]{:S(2)}, u32[]{:S(2)}) collective-permute-start(bf16[384,768]{1,0:T(8,128)(2,1)} %collective-permute-done.9.refs_4_.refs_5_), channel_id=1, source_target_pairs={{0,4},{4,0},{8,12},{12,8},{1,5},{5,1},{9,13},{13,9},{2,6},{6,2},{1... | collective-permute-start | bytes 1769480 | tf_op jit(solution)/shard_map/ppermute | solution.py:412
  98.5 22.2 %collective-permute-start.11 = (bf16[384,768]{1,0:T(8,128)(2,1)}, bf16[384,768]{1,0:T(8,128)(2,1)S(1)}, u32[]{:S(2)}, u32[]{:S(2)}) collective-permute-start(bf16[384,768]{1,0:T(8,128)(2,1)} %collective-permute-done.9.refs_4_.refs_5_), channel_id=1, source_target_pairs={{0,1},{1,0},{2,3},{3,2},{4,5},{5,4},{6,7},{7,6},{8,9},{9,8},{10,11... | collective-permute-start | bytes 1769480 | tf_op jit(solution)/shard_map/ppermute | solution.py:412
  100.1 20.6 %collective-permute-start.12 = (bf16[384,768]{1,0:T(8,128)(2,1)}, bf16[384,768]{1,0:T(8,128)(2,1)}, u32[]{:S(2)}, u32[]{:S(2)}) collective-permute-start(bf16[384,768]{1,0:T(8,128)(2,1)} %get-tuple-element.318.refs_8_.refs_9_), channel_id=1, source_target_pairs={{0,8},{4,12},{8,0},{12,4},{1,9},{5,13},{9,1},{13,5},{2,10},{6,14},... | collective-permute-start | bytes 1769480 | tf_op jit(solution)/shard_map/ppermute | solution.py:412
  120.7 16.1 %collective-permute-start.20 = (bf16[384,768]{1,0:T(8,128)(2,1)}, bf16[384,768]{1,0:T(8,128)(2,1)}, u32[]{:S(2)}, u32[]{:S(2)}) collective-permute-start(bf16[384,768]{1,0:T(8,128)(2,1)} %collective-permute-done.12.refs_12_.refs_13_), channel_id=1, source_target_pairs={{0,1},{1,0},{2,3},{3,2},{4,5},{5,4},{6,7},{7,6},{8,9},{9,8},{10,11... | collective-permute-start | bytes 1769480 | tf_op jit(solution)/shard_map/ppermute | solution.py:412
  123.8 17.4 %collective-permute-start.21 = (bf16[384,768]{1,0:T(8,128)(2,1)}, bf16[384,768]{1,0:T(8,128)(2,1)}, u32[]{:S(2)}, u32[]{:S(2)}) collective-permute-start(bf16[384,768]{1,0:T(8,128)(2,1)} %collective-permute-done.12.refs_12_.refs_13_), channel_id=1, source_target_pairs={{0,4},{4,0},{8,12},{12,8},{1,5},{5,1},{9,13},{13,9},{2,6},{6,2},{1... | collective-permute-start | bytes 1769480 | tf_op jit(solution)/shard_map/ppermute | solution.py:412
  124.4 15.5 %collective-permute-start.23 = (bf16[384,768]{1,0:T(8,128)(2,1)S(1)}, bf16[384,768]{1,0:T(8,128)(2,1)}, u32[]{:S(2)}, u32[]{:S(2)}) collective-permute-start(bf16[384,768]{1,0:T(8,128)(2,1)S(1)} %copy-done.39), channel_id=1, source_target_pairs={{0,8},{4,12},{8,0},{12,4},{1,9},{5,13},{9,1},{13,5},{2,10},{6,14},... | collective-permute-start | bytes 1769480 | tf_op jit(solution)/shard_map/ppermute | solution.py:412
  137.9 17.4 %collective-permute-start.25 = (bf16[384,768]{1,0:T(8,128)(2,1)S(1)}, bf16[384,768]{1,0:T(8,128)(2,1)}, u32[]{:S(2)}, u32[]{:S(2)}) collective-permute-start(bf16[384,768]{1,0:T(8,128)(2,1)S(1)} %copy-done.44), channel_id=1, source_target_pairs={{0,8},{4,12},{8,0},{12,4},{1,9},{5,13},{9,1},{13,5},{2,10},{6,14},... | collective-permute-start | bytes 1769480 | tf_op jit(solution)/shard_map/ppermute | solution.py:412
  156.4 22.1 %collective-permute-start.31 = (bf16[384,768]{1,0:T(8,128)(2,1)S(1)}, bf16[384,768]{1,0:T(8,128)(2,1)}, u32[]{:S(2)}, u32[]{:S(2)}) collective-permute-start(bf16[384,768]{1,0:T(8,128)(2,1)S(1)} %copy-done.45), channel_id=1, source_target_pairs={{0,8},{4,12},{8,0},{12,4},{1,9},{5,13},{9,1},{13,5},{2,10},{6,14},... | collective-permute-start | bytes 1769480 | tf_op jit(solution)/shard_map/ppermute | solution.py:412
  157.9 26.6 %collective-permute-start.32 = (bf16[384,768]{1,0:T(8,128)(2,1)}, bf16[384,768]{1,0:T(8,128)(2,1)}, u32[]{:S(2)}, u32[]{:S(2)}) collective-permute-start(bf16[384,768]{1,0:T(8,128)(2,1)} %get-tuple-element.196.refs_9_.refs_10_), channel_id=1, source_target_pairs={{0,8},{4,12},{8,0},{12,4},{1,9},{5,13},{9,1},{13,5},{2,10},{6,14},... | collective-permute-start | bytes 1769480 | tf_op jit(solution)/shard_map/ppermute | solution.py:412
  159.1 25.4 %collective-permute-start.30 = (bf16[384,768]{1,0:T(8,128)(2,1)}, bf16[384,768]{1,0:T(8,128)(2,1)}, u32[]{:S(2)}, u32[]{:S(2)}) collective-permute-start(bf16[384,768]{1,0:T(8,128)(2,1)} %collective-permute-done.25.refs_4_.refs_5_), channel_id=1, source_target_pairs={{0,1},{1,0},{2,3},{3,2},{4,5},{5,4},{6,7},{7,6},{8,9},{9,8},{10,11... | collective-permute-start | bytes 1769480 | tf_op jit(solution)/shard_map/ppermute | solution.py:412
  220.0 18.7 %collective-permute-start.42 = (bf16[2,768,768]{2,1,0:T(8,128)(2,1)}, bf16[2,768,768]{2,1,0:T(8,128)(2,1)S(1)}, u32[]{:S(2)}, u32[]{:S(2)}) collective-permute-start(bf16[2,768,768]{2,1,0:T(8,128)(2,1)} %get-tuple-element.208), channel_id=1, source_target_pairs={{0,4},{4,0},{8,12},{12,8},{1,5},{5,1},{9,13},{13,9},{2,6},{6,2},{1... | collective-permute-start | bytes 7077896 | tf_op jit(solution)/shard_map/ppermute | solution.py:412
  239.8 33.4 %collective-permute-start.43 = (bf16[768,768]{1,0:T(8,128)(2,1)S(1)}, bf16[768,768]{1,0:T(8,128)(2,1)}, u32[]{:S(2)}, u32[]{:S(2)}) collective-permute-start(bf16[768,768]{1,0:T(8,128)(2,1)S(1)} %get-tuple-element.213), channel_id=1, source_target_pairs={{0,8},{4,12},{8,0},{12,4},{1,9},{5,13},{9,1},{13,5},{2,10},{6,14},... | collective-permute-start | bytes 3538952 | tf_op jit(solution)/shard_map/ppermute | solution.py:412
  243.0 117.7 %reduce-scatter.7.cloned.1.call-start = ((), (), s32[]{:S(2)}) async-start(), calls=%async_computation.7 | async-start | bytes 1474560 | tf_op jit(solution)/shard_map/reduce_scatter | solution.py:463
  257.1 19.9 %collective-permute-start.44 = (bf16[2,768,768]{2,1,0:T(8,128)(2,1)}, bf16[2,768,768]{2,1,0:T(8,128)(2,1)S(1)}, u32[]{:S(2)}, u32[]{:S(2)}) collective-permute-start(bf16[2,768,768]{2,1,0:T(8,128)(2,1)} %get-tuple-element.221), channel_id=1, source_target_pairs={{0,4},{4,0},{8,12},{12,8},{1,5},{5,1},{9,13},{13,9},{2,6},{6,2},{1... | collective-permute-start | bytes 7077896 | tf_op jit(solution)/shard_map/ppermute | solution.py:412
  279.6 28.7 %collective-permute-start.45 = (bf16[768,768]{1,0:T(8,128)(2,1)}, bf16[768,768]{1,0:T(8,128)(2,1)S(1)}, u32[]{:S(2)}, u32[]{:S(2)}) collective-permute-start(bf16[768,768]{1,0:T(8,128)(2,1)} %get-tuple-element.226), channel_id=1, source_target_pairs={{0,8},{4,12},{8,0},{12,4},{1,9},{5,13},{9,1},{13,5},{2,10},{6,14},... | collective-permute-start | bytes 3538952 | tf_op jit(solution)/shard_map/ppermute | solution.py:412
  292.8 19.5 %collective-permute-start.46 = (bf16[2,768,768]{2,1,0:T(8,128)(2,1)}, bf16[2,768,768]{2,1,0:T(8,128)(2,1)S(1)}, u32[]{:S(2)}, u32[]{:S(2)}) collective-permute-start(bf16[2,768,768]{2,1,0:T(8,128)(2,1)} %get-tuple-element.233), channel_id=1, source_target_pairs={{0,4},{4,0},{8,12},{12,8},{1,5},{5,1},{9,13},{13,9},{2,6},{6,2},{1... | collective-permute-start | bytes 7077896 | tf_op jit(solution)/shard_map/ppermute | solution.py:412
  293.0 23.3 %collective-permute-start.47 = (bf16[2,768,768]{2,1,0:T(8,128)(2,1)}, bf16[2,768,768]{2,1,0:T(8,128)(2,1)}, u32[]{:S(2)}, u32[]{:S(2)}) collective-permute-start(bf16[2,768,768]{2,1,0:T(8,128)(2,1)} %get-tuple-element.237), channel_id=1, source_target_pairs={{0,4},{4,0},{8,12},{12,8},{1,5},{5,1},{9,13},{13,9},{2,6},{6,2},{1... | collective-permute-start | bytes 7077896 | tf_op jit(solution)/shard_map/ppermute | solution.py:412
  293.4 110.0 %reduce-scatter.9.cloned.1.call-start = ((), (), s32[]{:S(2)}) async-start(), calls=%async_computation.8 | async-start | bytes 1474560 | tf_op jit(solution)/shard_map/reduce_scatter | solution.py:463
  321.3 31.9 %collective-permute-start.50 = (bf16[2,192,768]{2,1,0:T(8,128)(2,1)}, bf16[2,192,768]{2,1,0:T(8,128)(2,1)}, u32[]{:S(2)}, u32[]{:S(2)}) collective-permute-start(bf16[2,192,768]{2,1,0:T(8,128)(2,1)} %dynamic-slice_bitcast_fusion.1), channel_id=1, source_target_pairs={{0,1},{1,0},{2,3},{3,2},{4,5},{5,4},{6,7},{7,6},{8,9},{9,8},{10,11... | collective-permute-start | bytes 1769480 | tf_op jit(solution)/shard_map/ppermute | solution.py:412
  322.0 33.3 %collective-permute-start.48 = (bf16[768,768]{1,0:T(8,128)(2,1)}, bf16[768,768]{1,0:T(8,128)(2,1)}, u32[]{:S(2)}, u32[]{:S(2)}) collective-permute-start(bf16[768,768]{1,0:T(8,128)(2,1)} %get-tuple-element.244), channel_id=1, source_target_pairs={{0,8},{4,12},{8,0},{12,4},{1,9},{5,13},{9,1},{13,5},{2,10},{6,14},... | collective-permute-start | bytes 3538952 | tf_op jit(solution)/shard_map/ppermute | solution.py:412
  337.0 20.8 %collective-permute-start.49 = (bf16[2,768,768]{2,1,0:T(8,128)(2,1)}, bf16[2,768,768]{2,1,0:T(8,128)(2,1)S(1)}, u32[]{:S(2)}, u32[]{:S(2)}) collective-permute-start(bf16[2,768,768]{2,1,0:T(8,128)(2,1)} %get-tuple-element.252), channel_id=1, source_target_pairs={{0,4},{4,0},{8,12},{12,8},{1,5},{5,1},{9,13},{13,9},{2,6},{6,2},{1... | collective-permute-start | bytes 7077896 | tf_op jit(solution)/shard_map/ppermute | solution.py:412
  360.8 109.6 %reduce-scatter.11.cloned.1.call-start = ((), (), s32[]{:S(2)}) async-start(), calls=%async_computation.9 | async-start | bytes 1474560 | tf_op jit(solution)/shard_map/reduce_scatter | solution.py:463
  364.2 39.1 %collective-permute-start.54 = (bf16[768,768]{1,0:T(8,128)(2,1)S(1)}, bf16[768,768]{1,0:T(8,128)(2,1)S(1)}, u32[]{:S(2)}, u32[]{:S(2)}) collective-permute-start(bf16[768,768]{1,0:T(8,128)(2,1)S(1)} %copy-done.1), channel_id=1, source_target_pairs={{0,8},{4,12},{8,0},{12,4},{1,9},{5,13},{9,1},{13,5},{2,10},{6,14},... | collective-permute-start | bytes 3538952 | tf_op jit(solution)/shard_map/ppermute | solution.py:412
  376.8 24.8 %collective-permute-start.53 = (bf16[1,192,768]{2,1,0:T(8,128)(2,1)}, bf16[1,192,768]{2,1,0:T(8,128)(2,1)}, u32[]{:S(2)}, u32[]{:S(2)}) collective-permute-start(bf16[1,192,768]{2,1,0:T(8,128)(2,1)} %constant_dynamic-slice_fusion.1), channel_id=1, source_target_pairs={{0,2},{1,3},{2,0},{3,1},{4,6},{5,7},{6,4},{7,5},{8,10},{9,11},{10,... | collective-permute-start | bytes 884744 | tf_op jit(solution)/shard_map/ppermute | solution.py:412
  386.3 36.6 %collective-permute-start.51 = (bf16[768,768]{1,0:T(8,128)(2,1)S(1)}, bf16[768,768]{1,0:T(8,128)(2,1)}, u32[]{:S(2)}, u32[]{:S(2)}) collective-permute-start(bf16[768,768]{1,0:T(8,128)(2,1)S(1)} %copy-done.3), channel_id=1, source_target_pairs={{0,8},{4,12},{8,0},{12,4},{1,9},{5,13},{9,1},{13,5},{2,10},{6,14},... | collective-permute-start | bytes 3538952 | tf_op jit(solution)/shard_map/ppermute | solution.py:412
  428.2 22.8 %collective-permute-start.52 = (bf16[2,192,768]{2,1,0:T(8,128)(2,1)}, bf16[2,192,768]{2,1,0:T(8,128)(2,1)}, u32[]{:S(2)}, u32[]{:S(2)}) collective-permute-start(bf16[2,192,768]{2,1,0:T(8,128)(2,1)} %dynamic-slice_bitcast_fusion), channel_id=1, source_target_pairs={{0,1},{1,0},{2,3},{3,2},{4,5},{5,4},{6,7},{7,6},{8,9},{9,8},{10,11... | collective-permute-start | bytes 1769480 | tf_op jit(solution)/shard_map/ppermute | solution.py:412
  429.5 40.8 %all-to-all-start.1 = ((bf16[8,208,448]{2,1,0:T(8,128)(2,1)}), bf16[8,208,448]{2,1,0:T(8,128)(2,1)S(1)}, u32[]{:S(2)}, u32[]{:S(2)}) async-start(bf16[8,208,448]{2,1,0:T(8,128)(2,1)} %fusion.1), calls=%async_computation.5 | async-start | bytes 3407872 | tf_op jit(solution)/shard_map/all_to_all | solution.py:699
  436.5 15.8 %collective-permute-start.57 = (bf16[1,192,768]{2,1,0:T(8,128)(2,1)S(1)}, bf16[1,192,768]{2,1,0:T(8,128)(2,1)S(1)}, u32[]{:S(2)}, u32[]{:S(2)}) collective-permute-start(bf16[1,192,768]{2,1,0:T(8,128)(2,1)S(1)} %bitcast.163), channel_id=1, source_target_pairs={{0,2},{1,3},{2,0},{3,1},{4,6},{5,7},{6,4},{7,5},{8,10},{9,11},{10,... | collective-permute-start | bytes 884744 | tf_op jit(solution)/shard_map/ppermute | solution.py:412
  452.3 15.5 %collective-permute-start.58 = (bf16[1,192,768]{2,1,0:T(8,128)(2,1)S(1)}, bf16[1,192,768]{2,1,0:T(8,128)(2,1)S(1)}, u32[]{:S(2)}, u32[]{:S(2)}) collective-permute-start(bf16[1,192,768]{2,1,0:T(8,128)(2,1)S(1)} %constant_dynamic-slice_fusion), channel_id=1, source_target_pairs={{0,2},{1,3},{2,0},{3,1},{4,6},{5,7},{6,4},{7,5},{8,10},{9,11},{10,... | collective-permute-start | bytes 884744 | tf_op jit(solution)/shard_map/ppermute | solution.py:412
  484.8 49.0 %collective-permute-start.66 = (f32[12,192]{1,0:T(8,128)S(1)}, f32[12,192]{1,0:T(8,128)S(1)}, u32[]{:S(2)}, u32[]{:S(2)}) collective-permute-start(f32[12,192]{1,0:T(8,128)S(1)} %convert_reduce_fusion), channel_id=1, source_target_pairs={{0,3},{1,2},{2,1},{3,0},{4,7},{5,6},{6,5},{7,4},{8,11},{9,10},{10,... | collective-permute-start | bytes 27656 | tf_op jit(solution)/shard_map/ppermute | solution.py:412
  486.7 47.1 %collective-permute-start.65 = (f32[12,192]{1,0:T(8,128)S(1)}, f32[12,192]{1,0:T(8,128)S(1)}, u32[]{:S(2)}, u32[]{:S(2)}) collective-permute-start(f32[12,192]{1,0:T(8,128)S(1)} %convert_reduce_fusion), channel_id=1, source_target_pairs={{0,2},{1,3},{2,0},{3,1},{4,6},{5,7},{6,4},{7,5},{8,10},{9,11},{10,... | collective-permute-start | bytes 27656 | tf_op jit(solution)/shard_map/ppermute | solution.py:412
  486.7 47.1 %collective-permute-start.64 = (f32[12,192]{1,0:T(8,128)S(1)}, f32[12,192]{1,0:T(8,128)S(1)}, u32[]{:S(2)}, u32[]{:S(2)}) collective-permute-start(f32[12,192]{1,0:T(8,128)S(1)} %convert_reduce_fusion), channel_id=1, source_target_pairs={{0,1},{1,0},{2,3},{3,2},{4,5},{5,4},{6,7},{7,6},{8,9},{9,8},{10,11... | collective-permute-start | bytes 27656 | tf_op jit(solution)/shard_map/ppermute | solution.py:412
  489.3 20.6 %collective-permute-start.62 = (bf16[1,192,768]{2,1,0:T(8,128)(2,1)S(1)}, bf16[1,192,768]{2,1,0:T(8,128)(2,1)S(1)}, u32[]{:S(2)}, u32[]{:S(2)}) collective-permute-start(bf16[1,192,768]{2,1,0:T(8,128)(2,1)S(1)} %bitcast.159), channel_id=1, source_target_pairs={{0,2},{1,3},{2,0},{3,1},{4,6},{5,7},{6,4},{7,5},{8,10},{9,11},{10,... | collective-permute-start | bytes 884744 | tf_op jit(solution)/shard_map/ppermute | solution.py:412
  490.8 25.1 %collective-permute-start.63 = (bf16[1,192,768]{2,1,0:T(8,128)(2,1)S(1)}, bf16[1,192,768]{2,1,0:T(8,128)(2,1)S(1)}, u32[]{:S(2)}, u32[]{:S(2)}) collective-permute-start(bf16[1,192,768]{2,1,0:T(8,128)(2,1)S(1)} %bitcast.162), channel_id=1, source_target_pairs={{0,2},{1,3},{2,0},{3,1},{4,6},{5,7},{6,4},{7,5},{8,10},{9,11},{10,... | collective-permute-start | bytes 884744 | tf_op jit(solution)/shard_map/ppermute | solution.py:412
  515.9 16.5 %collective-permute-start.67 = (bf16[2,192,768]{2,1,0:T(8,128)(2,1)}, bf16[2,192,768]{2,1,0:T(8,128)(2,1)}, u32[]{:S(2)}, u32[]{:S(2)}) collective-permute-start(bf16[2,192,768]{2,1,0:T(8,128)(2,1)} %bitcast.58), channel_id=1, source_target_pairs={{0,1},{1,0},{2,3},{3,2},{4,5},{5,4},{6,7},{7,6},{8,9},{9,8},{10,11... | collective-permute-start | bytes 1769480 | tf_op jit(solution)/shard_map/ppermute | solution.py:412
  516.8 27.1 %collective-permute-start.68 = (bf16[2,192,768]{2,1,0:T(8,128)(2,1)}, bf16[2,192,768]{2,1,0:T(8,128)(2,1)}, u32[]{:S(2)}, u32[]{:S(2)}) collective-permute-start(bf16[2,192,768]{2,1,0:T(8,128)(2,1)} %bitcast.61), channel_id=1, source_target_pairs={{0,1},{1,0},{2,3},{3,2},{4,5},{5,4},{6,7},{7,6},{8,9},{9,8},{10,11... | collective-permute-start | bytes 1769480 | tf_op jit(solution)/shard_map/ppermute | solution.py:412
  (100 other events, 835.5 us)
Sparse Core Ops, SparseCore 0:
  243.1 47.3 reduce-scatter.4
  293.5 28.9 reduce-scatter.6
  360.9 35.5 reduce-scatter.8
  405.9 28.4 reduce-scatter.10

commit v10 on v8

--- a/solution.py
+++ b/solution.py
@@ -634,6 +634,7 @@
             late_a.split()
             late_a.send_half(bits[0])
             last_two.send_y()
+            late_one.send_y()
             last_one.send_y()
         else:
             (gh,) = tied((late_two, late_one), gh)
@@ -655,14 +656,14 @@
         else:
             last_two.fold_rows()
             late_a.fold()
-            (upstream,) = tied((last_two, last_a, late_two, late_a), upstream)
+            late_one.fold()
+            (upstream,) = tied((last_two, last_a, late_two, late_a, late_one), upstream)
             for bit in bits[1:]:
                 late_a.send_half(bit)
                 if bit != bits[-1]:
                     late_a.fold()
             last_two.scatter()
             last_a.send_y()
-            late_one.send_y()
         ends_of[layer] = (db1_kept, db1_sent, (dbqv_kept, dbqv_sent, dcol_one, dcol_two))
 
     pair_two, pair_one, pair_a = Chain(), Chain(), Chain()
@@ -709,15 +710,14 @@
     start_far(pair_two)
 
     last_a.fold()
-    tied((last_a,))
+    (pair_two.arrived,) = tied((last_a,), pair_two.arrived)
     for bit in bits[1:]:
         last_a.send_half(bit)
         if bit != bits[-1]:
             last_a.fold()
 
-    late_one.fold()
     finish_far(pair_two)
-    (result,) = tied((pair_two, last_one, late_one), result)
+    (result,) = tied((pair_two, last_one), result)
     pair_one.send_x(last_one, late_one)
     pair_two.send_back(bits[0])
     small_sum = result[:, FEATS : FEATS + 12, :FEATS].astype(F32).sum(axis=0)
@@ -728,14 +728,12 @@
     result, small_sum = tied((last_a, pair_one), result, small_sum)
     pair_a.send_x(last_a, late_a)
     start_far(pair_one)
-    small_sum += flip(small_sum, "dp", bits[0])
+    small_parts = [flip(small_sum, "dp", k) for k in range(1, n_dp)] if n_dp <= 4 else None
 
     pair_a.fold()
     pair_two.join(bits[0])
-    result, small_sum = tied((pair_a, pair_two), result, small_sum)
+    (result,) = tied((pair_a, pair_two), result)
     start_far(pair_a)
-    for bit in bits[1:]:
-        small_sum += flip(small_sum, "dp", bit)
 
     finish_far(pair_one)
     (result,) = tied((pair_one,), result)
@@ -743,9 +741,14 @@
     result = result[:, :FEATS].transpose(1, 0, 2).reshape(FEATS, clips * FRAMES).T.astype(F32)
 
     finish_far(pair_a)
-    (small_sum,) = tied((pair_a,), small_sum)
+    tied((pair_a,))
     pair_a.send_back(bits[0])
     pair_one.join(bits[0])
+    if small_parts is None:
+        small_sum = lax.psum(small_sum, "dp")
+    else:
+        small_parts, pair_one.value = tie((small_parts, pair_one.value))
+        small_sum = sum(small_parts, small_sum)
     pair_a.join(bits[0])
     for pair in (pair_two, pair_one, pair_a):
         pair.value = pair.value.reshape(D, D)

time: 539 us -> 550 us (1.020)
  other arithmetic: 31.6 us -> 45.9 us
    ppermute x68 -> x69, waiting for transfers between devices: 169 us -> 136 us  [flip(): return lax.ppermute(block, axis, [(i, i ^ bit) for i in range(size)])]
    reduce_scatter x4, waiting for transfers between devices: 4.09 us -> 33.5 us  [scatter(): total = lax.psum_scatter(split, 'dp', scatter_dimension=0, tiled=False)]
    ppermute x68 -> x69, starting transfers between devices: 57.7 us -> 58.1 us  [flip(): return lax.ppermute(block, axis, [(i, i ^ bit) for i in range(size)])]
    unnamed x145 -> x127, local copies, waits for them, and re-layouts: 16.9 us -> 17.2 us
  transfers between devices with their start and end apart: 74 -> 75, of which waited for: 30 -> 25; matrix products, arithmetic and copies ran while one was open for 8% -> 12% of each run, Pallas kernels for 31% -> 30%
where the time goes in v10:
time: 550 us; the launch traced here: 543 us
  Pallas kernels  192 us (35%)
  waiting for transfers between devices  181 us (33%)
  starting transfers between devices  66.6 us (12%)
  other arithmetic  45.9 us (8%)
  local copies, waits for them, and re-layouts  41.6 us (8%)
  between operations  15.3 us (3%)
    pallas_call x12, Pallas kernels, run(): pl.pallas_call(kernel, name=name, out_shape=outs, grid_spec=pltpu.Prefetc...  177 us
    ppermute x69, waiting for transfers between devices, flip(): return lax.ppermute(block, axis, [(i, i ^ bit) for i in range(size)])  136 us
    ppermute x69, starting transfers between devices, flip(): return lax.ppermute(block, axis, [(i, i ^ bit) for i in range(size)])  58.1 us
    reduce_scatter x4, waiting for transfers between devices, scatter(): total = lax.psum_scatter(split, 'dp', scatter_dimension=0, tiled=False)  33.5 us
    unnamed x127, local copies, waits for them, and re-layouts  17.2 us
    pallas_call x11, Pallas kernels, summed(): pl.pallas_call(sum_kernel, name='row_sums', grid=(rows // block,), in_spe...  15.7 us
    all_to_all x1, waiting for transfers between devices, body(): lax.all_to_all(ends, ('section', 'tensor'), split_axis=0, concat_axis=0,...  12 us
  transfers between devices with their start and end apart: 75, of which 25 were waited for; matrix products, arithmetic and copies ran while one was open for 12% of the time, Pallas kernels for 30%

profile of v10, /device:TPU:0, one launch (start us, length us, event | category | flops | bytes accessed | tf_op | source)
XLA Modules:
  0.0 543.1 jit_solution(8003746856323208970)
XLA Ops:
  8.6 3.0 collective-permute-start
  11.7 3.3 reshape.213
  16.2 8.8 %collective-permute-done = bf16[384,768]{1,0:T(8,128)(2,1)} collective-permute-done((bf16[384,768]{1,0:T(8,128)(2,1)S(1)}, bf16[384,768]{1,0:T(8,128)(2,1)}, u32[]{:S(2)}, u32[]{:S(2)}) %collective-permute-start) | collective-permute-done | bytes 589856 | tf_op jit(solution)/shard_map/ppermute | solution.py:412
  25.0 2.2 broadcast_select_fusion.2
  32.7 3.6 all-to-all-start
  38.1 5.7 %collective-permute-done.4.refs_4_.refs_5_ = bf16[384,768]{1,0:T(8,128)(2,1)} collective-permute-done((bf16[384,768]{1,0:T(8,128)(2,1)}, bf16[384,768]{1,0:T(8,128)(2,1)}, u32[]{:S(2)}, u32[]{:S(2)}) %collective-permute-start.4) | collective-permute-done | bytes 589856 | tf_op jit(solution)/shard_map/ppermute | solution.py:412
  45.6 2.5 broadcast_select_fusion
  55.2 2.6 broadcast_select_fusion.1
  57.8 6.0 %collective-permute-done.9.refs_4_.refs_5_ = bf16[384,768]{1,0:T(8,128)(2,1)} collective-permute-done((bf16[384,768]{1,0:T(8,128)(2,1)}, bf16[384,768]{1,0:T(8,128)(2,1)}, u32[]{:S(2)}, u32[]{:S(2)}) %collective-permute-start.9) | collective-permute-done | bytes 589856 | tf_op jit(solution)/shard_map/ppermute | solution.py:412
  63.8 7.0 %collective-permute-done.10 = bf16[768,768]{1,0:T(8,128)(2,1)} collective-permute-done((bf16[768,768]{1,0:T(8,128)(2,1)}, bf16[768,768]{1,0:T(8,128)(2,1)}, u32[]{:S(2)}, u32[]{:S(2)}) %collective-permute-start.10) | collective-permute-done | bytes 1179680 | tf_op jit(solution)/shard_map/ppermute | solution.py:412
  71.3 3.3 bitcast_select_fusion.2
  74.7 12.0 %all-to-all-done = bf16[8,208,448]{2,1,0:T(8,128)(2,1)S(1)} async-done(((bf16[8,208,448]{2,1,0:T(8,128)(2,1)}), bf16[8,208,448]{2,1,0:T(8,128)(2,1)S(1)}, u32[]{:S(2)}, u32[]{:S(2)}) %all-to-all-start) | async-done | bytes 1490976 | tf_op jit(solution)/shard_map/all_to_all | solution.py:537
  91.9 17.0 %attention_forward.2 = (bf16[768,448]{1,0:T(8,128)(2,1)}, bf16[4,576,448]{2,1,0:T(8,128)(2,1)}, bf16[4,3,448,448]{3,2,1,0:T(8,128)(2,1)}, bf16[4,192,448]{2,1,0:T(8,128)(2,1)}, f32[768,448]{1,0:T(8,128)}) custom-call(s32[9]{0:T(128)} %stack.113.info, bf16[768,448]{1,0:T(8,128)(2,1)} %bitcast.165, f32[4,192,8]{2,1,0:T(8,128)} %get-tuple-element.336.col_ref, ...), custom_call_target="tpu_custom_call" | custom-call | flops 43687870464 | bytes 268435456 | tf_op jit(solution)/shard_map/attention_forward/pallas_call | solution.py:311
  110.1 2.3 bitcast_select_fusion
  114.4 10.8 %collective-permute-done.20.refs_13_.refs_14_ = bf16[384,768]{1,0:T(8,128)(2,1)} collective-permute-done((bf16[384,768]{1,0:T(8,128)(2,1)}, bf16[384,768]{1,0:T(8,128)(2,1)}, u32[]{:S(2)}, u32[]{:S(2)}) %collective-permute-start.20) | collective-permute-done | bytes 589856 | tf_op jit(solution)/shard_map/ppermute | solution.py:412
  129.9 14.0 %mlp_forward.2 = (bf16[768,448]{1,0:T(8,128)(2,1)}, bf16[4,448,768]{2,1,0:T(8,128)(2,1)}, bf16[4,448,768]{2,1,0:T(8,128)(2,1)}, f32[768,448]{1,0:T(8,128)}) custom-call(s32[9]{0:T(128)} %stack.113.info, f32[768,448]{1,0:T(8,128)} %get-tuple-element.175.h_ref, f32[4,192,8]{2,1,0:T(8,128)} %get-tuple-element.336.col_ref, f32[4,1,768]{2,1,0:T(1,128)} %squeeze.92.b1_ref, ...), custom_call_target="tpu_custom_call" | custom-call | flops 67645734912 | bytes 268435456 | tf_op jit(solution)/shard_map/mlp_forward/pallas_call | solution.py:311
  150.0 17.0 %attention_forward.3 = (bf16[768,448]{1,0:T(8,128)(2,1)}, bf16[4,576,448]{2,1,0:T(8,128)(2,1)}, bf16[4,3,448,448]{3,2,1,0:T(8,128)(2,1)}, bf16[4,192,448]{2,1,0:T(8,128)(2,1)}, f32[768,448]{1,0:T(8,128)}) custom-call(s32[9]{0:T(128)} %stack.113.info, f32[768,448]{1,0:T(8,128)} %get-tuple-element.183.x_ref, f32[4,192,8]{2,1,0:T(8,128)} %get-tuple-element.335.col_ref, ...), custom_call_target="tpu_custom_call" | custom-call | flops 43687870464 | bytes 268435456 | tf_op jit(solution)/shard_map/attention_forward/pallas_call | solution.py:311
  167.0 6.1 %collective-permute-done.32.refs_13_.refs_14_ = bf16[384,768]{1,0:T(8,128)(2,1)} collective-permute-done((bf16[384,768]{1,0:T(8,128)(2,1)}, bf16[384,768]{1,0:T(8,128)(2,1)}, u32[]{:S(2)}, u32[]{:S(2)}) %collective-permute-start.32) | collective-permute-done | bytes 589856 | tf_op jit(solution)/shard_map/ppermute | solution.py:412
  175.2 2.4 collective-permute-done.34.refs_3_.refs_4_
  181.7 14.4 %mlp_forward.3 = (bf16[768,448]{1,0:T(8,128)(2,1)}, bf16[4,448,768]{2,1,0:T(8,128)(2,1)}, bf16[4,448,768]{2,1,0:T(8,128)(2,1)}, f32[768,448]{1,0:T(8,128)}) custom-call(s32[9]{0:T(128)} %stack.113.info, f32[768,448]{1,0:T(8,128)} %get-tuple-element.192.h_ref, f32[4,192,8]{2,1,0:T(8,128)} %get-tuple-element.335.col_ref, f32[4,1,768]{2,1,0:T(1,128)} %squeeze.93.b1_ref, ...), custom_call_target="tpu_custom_call" | custom-call | flops 67645734912 | bytes 268435456 | tf_op jit(solution)/shard_map/mlp_forward/pallas_call | solution.py:311
  196.1 12.3 %mlp_backward.4 = (f32[448,768]{1,0:T(8,128)}, bf16[2,768,768]{2,1,0:T(8,128)(2,1)}, bf16[2,768,768]{2,1,0:T(8,128)(2,1)}, f32[4,1,768]{2,1,0:T(1,128)}) custom-call(s32[9]{0:T(128)} %stack.113.info, bf16[768,448]{1,0:T(8,128)(2,1)} %bitcast.168, f32[768,448]{1,0:T(8,128)} %get-tuple-element.192.h_ref, bf16[768,448]{1,0:T(8,128)(2,1)} %get-tuple-element.201.a2_ref, ...), custom_call_target="tpu_custom_call" | custom-call | flops 67645734912 | bytes 268435456 | tf_op jit(solution)/shard_map/mlp_backward/pallas_call | solution.py:311
  209.0 14.6 %mlp_backward.5 = (f32[768,448]{1,0:T(8,128)}, f32[4,192,8]{2,1,0:T(8,128)}, bf16[2,768,768]{2,1,0:T(8,128)(2,1)}, bf16[2,768,768]{2,1,0:T(8,128)(2,1)}, f32[4,1,768]{2,1,0:T(1,128)}) custom-call(s32[9]{0:T(128)} %stack.113.info, bf16[768,448]{1,0:T(8,128)(2,1)} %bitcast.169, f32[768,448]{1,0:T(8,128)} %get-tuple-element.192.h_ref, ...), custom_call_target="tpu_custom_call" | custom-call | flops 67645734912 | bytes 268435456 | tf_op jit(solution)/shard_map/mlp_backward/pallas_call | solution.py:311
  231.9 13.9 %attention_backward.4 = (f32[448,768]{1,0:T(8,128)}, bf16[2,768,768]{2,1,0:T(8,128)(2,1)}, f32[4,192,8]{2,1,0:T(8,128)}) custom-call(s32[9]{0:T(128)} %stack.113.info, f32[768,448]{1,0:T(8,128)} %get-tuple-element.216.gh_ref, f32[768,448]{1,0:T(8,128)} %get-tuple-element.183.x_ref, bf16[768,448]{1,0:T(8,128)(2,1)} %get-tuple-element.217.a1_ref, ...), custom_call_target="tpu_custom_call" | custom-call | flops 43687870464 | bytes 268435456 | tf_op jit(solution)/shard_map/attention_backward/pallas_call | solution.py:311
  245.8 16.2 %attention_backward.5 = (f32[768,448]{1,0:T(8,128)}, f32[4,192,8]{2,1,0:T(8,128)}, bf16[2,768,768]{2,1,0:T(8,128)(2,1)}, f32[4,192,8]{2,1,0:T(8,128)}) custom-call(s32[9]{0:T(128)} %stack.113.info, f32[768,448]{1,0:T(8,128)} %get-tuple-element.216.gh_ref, f32[768,448]{1,0:T(8,128)} %get-tuple-element.183.x_ref, bf16[768,448]{1,0:T(8,128)(2,1)} %get-tuple-element.217.a1_ref, ...), custom_call_target="tpu_custom_call" | custom-call | flops 43687870464 | bytes 268435456 | tf_op jit(solution)/shard_map/attention_backward/pallas_call | solution.py:311
  263.5 2.2 row_sums.13
  269.0 12.6 %mlp_backward.6 = (f32[448,768]{1,0:T(8,128)}, bf16[2,768,768]{2,1,0:T(8,128)(2,1)}, bf16[2,768,768]{2,1,0:T(8,128)(2,1)}, f32[4,1,768]{2,1,0:T(1,128)}) custom-call(s32[9]{0:T(128)} %stack.113.info, f32[768,448]{1,0:T(8,128)} %get-tuple-element.229.gy_ref, f32[768,448]{1,0:T(8,128)} %get-tuple-element.175.h_ref, ...), custom_call_target="tpu_custom_call" | custom-call | flops 67645734912 | bytes 268435456 | tf_op jit(solution)/shard_map/mlp_backward/pallas_call | solution.py:311
  282.2 14.9 %mlp_backward.7 = (f32[768,448]{1,0:T(8,128)}, f32[4,192,8]{2,1,0:T(8,128)}, bf16[2,768,768]{2,1,0:T(8,128)(2,1)}, bf16[2,768,768]{2,1,0:T(8,128)(2,1)}, f32[4,1,768]{2,1,0:T(1,128)}) custom-call(s32[9]{0:T(128)} %stack.113.info, f32[768,448]{1,0:T(8,128)} %get-tuple-element.229.gy_ref, f32[768,448]{1,0:T(8,128)} %get-tuple-element.175.h_ref, ...), custom_call_target="tpu_custom_call" | custom-call | flops 67645734912 | bytes 268435456 | tf_op jit(solution)/shard_map/mlp_backward/pallas_call | solution.py:311
  314.5 13.6 %attention_backward.6 = (f32[448,768]{1,0:T(8,128)}, bf16[2,768,768]{2,1,0:T(8,128)(2,1)}, f32[4,192,8]{2,1,0:T(8,128)}) custom-call(s32[9]{0:T(128)} %stack.113.info, f32[768,448]{1,0:T(8,128)} %get-tuple-element.247.gh_ref, bf16[768,448]{1,0:T(8,128)(2,1)} %bitcast.166, bf16[768,448]{1,0:T(8,128)(2,1)} %get-tuple-element.248.a1_ref, ...), custom_call_target="tpu_custom_call" | custom-call | flops 43687870464 | bytes 268435456 | tf_op jit(solution)/shard_map/attention_backward/pallas_call | solution.py:311
  328.1 16.1 %attention_backward.7 = (f32[768,448]{1,0:T(8,128)}, f32[4,192,8]{2,1,0:T(8,128)}, bf16[2,768,768]{2,1,0:T(8,128)(2,1)}, f32[4,192,8]{2,1,0:T(8,128)}) custom-call(s32[9]{0:T(128)} %stack.113.info, f32[768,448]{1,0:T(8,128)} %get-tuple-element.247.gh_ref, bf16[768,448]{1,0:T(8,128)(2,1)} %bitcast.167, bf16[768,448]{1,0:T(8,128)(2,1)} %get-tuple-element.248.a1_ref, ...), custom_call_target="tpu_custom_call" | custom-call | flops 43687870464 | bytes 268435456 | tf_op jit(solution)/shard_map/attention_backward/pallas_call | solution.py:311
  348.1 2.4 row_sums.18
  354.2 2.5 convert_bitcast_fusion.1
  358.3 2.5 collective-permute-start.58
  360.8 33.5 %reduce-scatter.9.cloned.1.call-done = bf16[1,1,192,768]{3,2,1,0:T(8,128)(2,1)} async-done(((bf16[4,1,192,768]{3,2,1,0:T(8,128)(2,1)}), bf16[1,1,192,768]{3,2,1,0:T(8,128)(2,1)}) %reduce-scatter.9.cloned.1.call-update) | async-done | bytes 294928 | tf_op jit(solution)/shard_map/reduce_scatter | solution.py:463
  400.9 3.5 collective-permute-done.53
  412.0 4.7 all-to-all-start.1
  416.8 19.9 %collective-permute-done.52.right_ref = bf16[768,768]{1,0:T(8,128)(2,1)S(1)} collective-permute-done((bf16[768,768]{1,0:T(8,128)(2,1)S(1)}, bf16[768,768]{1,0:T(8,128)(2,1)S(1)}, u32[]{:S(2)}, u32[]{:S(2)}) %collective-permute-start.52) | collective-permute-done | bytes 1179680 | tf_op jit(solution)/shard_map/ppermute | solution.py:412
  439.0 16.2 %collective-permute-done.54 = bf16[2,192,768]{2,1,0:T(8,128)(2,1)S(1)} collective-permute-done((bf16[2,192,768]{2,1,0:T(8,128)(2,1)S(1)}, bf16[2,192,768]{2,1,0:T(8,128)(2,1)S(1)}, u32[]{:S(2)}, u32[]{:S(2)}) %collective-permute-start.54) | collective-permute-done | bytes 589856 | tf_op jit(solution)/shard_map/ppermute | solution.py:412
  455.4 2.9 collective-permute-start.56
  460.2 8.1 %collective-permute-done.56 = bf16[1,192,768]{2,1,0:T(8,128)(2,1)S(1)} collective-permute-done((bf16[1,192,768]{2,1,0:T(8,128)(2,1)S(1)}, bf16[1,192,768]{2,1,0:T(8,128)(2,1)S(1)}, u32[]{:S(2)}, u32[]{:S(2)}) %collective-permute-start.56) | collective-permute-done | bytes 294944 | tf_op jit(solution)/shard_map/ppermute | solution.py:412
  470.4 2.8 collective-permute-start.65
  474.8 8.3 %collective-permute-done.62 = bf16[2,192,768]{2,1,0:T(8,128)(2,1)S(1)} collective-permute-done((bf16[2,192,768]{2,1,0:T(8,128)(2,1)S(1)}, bf16[2,192,768]{2,1,0:T(8,128)(2,1)S(1)}, u32[]{:S(2)}, u32[]{:S(2)}) %collective-permute-start.62) | collective-permute-done | bytes 589856 | tf_op jit(solution)/shard_map/ppermute | solution.py:412
  483.1 3.1 collective-permute-start.60
  487.5 11.1 %collective-permute-done.60 = bf16[1,192,768]{2,1,0:T(8,128)(2,1)S(1)} collective-permute-done((bf16[1,192,768]{2,1,0:T(8,128)(2,1)S(1)}, bf16[1,192,768]{2,1,0:T(8,128)(2,1)S(1)}, u32[]{:S(2)}, u32[]{:S(2)}) %collective-permute-start.60) | collective-permute-done | bytes 294944 | tf_op jit(solution)/shard_map/ppermute | solution.py:412
  499.5 4.1 collective-permute-start.66
  507.3 2.4 reshape.227
  509.7 2.8 bitcast_convert_fusion
  515.6 6.3 %collective-permute-done.66 = bf16[2,192,768]{2,1,0:T(8,128)(2,1)} collective-permute-done((bf16[2,192,768]{2,1,0:T(8,128)(2,1)}, bf16[2,192,768]{2,1,0:T(8,128)(2,1)}, u32[]{:S(2)}, u32[]{:S(2)}) %collective-permute-start.66) | collective-permute-done | bytes 589856 | tf_op jit(solution)/shard_map/ppermute | solution.py:412
  527.3 6.2 %collective-permute-done.68 = bf16[2,192,768]{2,1,0:T(8,128)(2,1)S(1)} collective-permute-done((bf16[2,192,768]{2,1,0:T(8,128)(2,1)S(1)}, bf16[2,192,768]{2,1,0:T(8,128)(2,1)S(1)}, u32[]{:S(2)}, u32[]{:S(2)}) %collective-permute-start.68) | collective-permute-done | bytes 589856 | tf_op jit(solution)/shard_map/ppermute | solution.py:412
  (336 shorter events, 124.0 us)
Async XLA Ops:
  8.6 16.4 %collective-permute-start = (bf16[384,768]{1,0:T(8,128)(2,1)S(1)}, bf16[384,768]{1,0:T(8,128)(2,1)}, u32[]{:S(2)}, u32[]{:S(2)}) collective-permute-start(bf16[384,768]{1,0:T(8,128)(2,1)S(1)} %fusion.6), channel_id=1, source_target_pairs={{0,16},{16,0},{1,17},{17,1},{2,18},{18,2},{3,19},{19,3},{4,20},{20... | collective-permute-start | bytes 1769480 | tf_op jit(solution)/shard_map/ppermute | solution.py:412
  27.2 16.6 %collective-permute-start.4 = (bf16[384,768]{1,0:T(8,128)(2,1)}, bf16[384,768]{1,0:T(8,128)(2,1)}, u32[]{:S(2)}, u32[]{:S(2)}) collective-permute-start(bf16[384,768]{1,0:T(8,128)(2,1)} %get-tuple-element.334.refs_0_.refs_1_), channel_id=1, source_target_pairs={{0,8},{4,12},{8,0},{12,4},{1,9},{5,13},{9,1},{13,5},{2,10},{6,14},... | collective-permute-start | bytes 1769480 | tf_op jit(solution)/shard_map/ppermute | solution.py:412
  29.0 16.6 %collective-permute-start.5 = (bf16[384,768]{1,0:T(8,128)(2,1)}, bf16[384,768]{1,0:T(8,128)(2,1)}, u32[]{:S(2)}, u32[]{:S(2)}) collective-permute-start(bf16[384,768]{1,0:T(8,128)(2,1)} %dynamic-slice_bitcast_fusion.2), channel_id=1, source_target_pairs={{0,16},{16,0},{1,17},{17,1},{2,18},{18,2},{3,19},{19,3},{4,20},{20... | collective-permute-start | bytes 1769480 | tf_op jit(solution)/shard_map/ppermute | solution.py:412
  30.5 40.4 %collective-permute-start.10 = (bf16[768,768]{1,0:T(8,128)(2,1)}, bf16[768,768]{1,0:T(8,128)(2,1)}, u32[]{:S(2)}, u32[]{:S(2)}) collective-permute-start(bf16[768,768]{1,0:T(8,128)(2,1)} %bitcast.10), channel_id=1, source_target_pairs={{0,16},{16,0},{1,17},{17,1},{2,18},{18,2},{3,19},{19,3},{4,20},{20... | collective-permute-start | bytes 3538952 | tf_op jit(solution)/shard_map/ppermute | solution.py:412
  32.7 53.9 %all-to-all-start = ((bf16[8,208,448]{2,1,0:T(8,128)(2,1)}), bf16[8,208,448]{2,1,0:T(8,128)(2,1)S(1)}, u32[]{:S(2)}, u32[]{:S(2)}) async-start(bf16[8,208,448]{2,1,0:T(8,128)(2,1)} %copy.111), calls=%async_computation | async-start | bytes 3407872 | tf_op jit(solution)/shard_map/all_to_all | solution.py:537
  36.4 272.8 %reduce-scatter.5.cloned.1.call-start = ((), (), s32[]{:S(2)}) async-start(), calls=%async_computation.6 | async-start | bytes 2949120 | tf_op jit(solution)/shard_map/reduce_scatter | solution.py:463
  36.4 16.4 %collective-permute-start.1 = (bf16[384,768]{1,0:T(8,128)(2,1)}, bf16[384,768]{1,0:T(8,128)(2,1)S(1)}, u32[]{:S(2)}, u32[]{:S(2)}) collective-permute-start(bf16[384,768]{1,0:T(8,128)(2,1)} %collective-permute-done), channel_id=1, source_target_pairs={{0,1},{1,0},{2,3},{3,2},{4,5},{5,4},{6,7},{7,6},{8,9},{9,8},{10,11... | collective-permute-start | bytes 1769480 | tf_op jit(solution)/shard_map/ppermute | solution.py:412
  48.0 15.8 %collective-permute-start.9 = (bf16[384,768]{1,0:T(8,128)(2,1)}, bf16[384,768]{1,0:T(8,128)(2,1)}, u32[]{:S(2)}, u32[]{:S(2)}) collective-permute-start(bf16[384,768]{1,0:T(8,128)(2,1)} %get-tuple-element.332.refs_0_.refs_1_), channel_id=1, source_target_pairs={{0,8},{4,12},{8,0},{12,4},{1,9},{5,13},{9,1},{13,5},{2,10},{6,14},... | collective-permute-start | bytes 1769480 | tf_op jit(solution)/shard_map/ppermute | solution.py:412
  48.3 22.5 %collective-permute-start.6 = (bf16[384,768]{1,0:T(8,128)(2,1)}, bf16[384,768]{1,0:T(8,128)(2,1)}, u32[]{:S(2)}, u32[]{:S(2)}) collective-permute-start(bf16[384,768]{1,0:T(8,128)(2,1)} %collective-permute-done.4.refs_4_.refs_5_), channel_id=1, source_target_pairs={{0,1},{1,0},{2,3},{3,2},{4,5},{5,4},{6,7},{7,6},{8,9},{9,8},{10,11... | collective-permute-start | bytes 1769480 | tf_op jit(solution)/shard_map/ppermute | solution.py:412
  50.7 38.6 %collective-permute-start.2 = (bf16[384,768]{1,0:T(8,128)(2,1)}, bf16[384,768]{1,0:T(8,128)(2,1)}, u32[]{:S(2)}, u32[]{:S(2)}) collective-permute-start(bf16[384,768]{1,0:T(8,128)(2,1)} %get-tuple-element.334.refs_0_.refs_1_), channel_id=1, source_target_pairs={{0,4},{4,0},{8,12},{12,8},{1,5},{5,1},{9,13},{13,9},{2,6},{6,2},{1... | collective-permute-start | bytes 1769480 | tf_op jit(solution)/shard_map/ppermute | solution.py:412
  53.7 55.2 %collective-permute-start.13 = (bf16[384,768]{1,0:T(8,128)(2,1)}, bf16[384,768]{1,0:T(8,128)(2,1)}, u32[]{:S(2)}, u32[]{:S(2)}) collective-permute-start(bf16[384,768]{1,0:T(8,128)(2,1)} %collective-permute-done.5), channel_id=1, source_target_pairs={{0,1},{1,0},{2,3},{3,2},{4,5},{5,4},{6,7},{7,6},{8,9},{9,8},{10,11... | collective-permute-start | bytes 1769480 | tf_op jit(solution)/shard_map/ppermute | solution.py:412
  63.8 25.5 %collective-permute-start.7 = (bf16[384,768]{1,0:T(8,128)(2,1)}, bf16[384,768]{1,0:T(8,128)(2,1)}, u32[]{:S(2)}, u32[]{:S(2)}) collective-permute-start(bf16[384,768]{1,0:T(8,128)(2,1)} %collective-permute-done.4.refs_4_.refs_5_), channel_id=1, source_target_pairs={{0,4},{4,0},{8,12},{12,8},{1,5},{5,1},{9,13},{13,9},{2,6},{6,2},{1... | collective-permute-start | bytes 1769480 | tf_op jit(solution)/shard_map/ppermute | solution.py:412
  70.8 19.0 %collective-permute-start.3 = (bf16[384,768]{1,0:T(8,128)(2,1)S(1)}, bf16[384,768]{1,0:T(8,128)(2,1)}, u32[]{:S(2)}, u32[]{:S(2)}) collective-permute-start(bf16[384,768]{1,0:T(8,128)(2,1)S(1)} %get-tuple-element.328.refs_1_.refs_2_), channel_id=1, source_target_pairs={{0,4},{4,0},{8,12},{12,8},{1,5},{5,1},{9,13},{13,9},{2,6},{6,2},{1... | collective-permute-start | bytes 1769480 | tf_op jit(solution)/shard_map/ppermute | solution.py:412
  70.8 20.5 %collective-permute-start.8 = (bf16[384,768]{1,0:T(8,128)(2,1)}, bf16[384,768]{1,0:T(8,128)(2,1)}, u32[]{:S(2)}, u32[]{:S(2)}) collective-permute-start(bf16[384,768]{1,0:T(8,128)(2,1)} %collective-permute-done.6.refs_5_.refs_6_), channel_id=1, source_target_pairs={{0,4},{4,0},{8,12},{12,8},{1,5},{5,1},{9,13},{13,9},{2,6},{6,2},{1... | collective-permute-start | bytes 1769480 | tf_op jit(solution)/shard_map/ppermute | solution.py:412
  89.3 23.1 %collective-permute-start.14 = (bf16[384,768]{1,0:T(8,128)(2,1)}, bf16[384,768]{1,0:T(8,128)(2,1)}, u32[]{:S(2)}, u32[]{:S(2)}) collective-permute-start(bf16[384,768]{1,0:T(8,128)(2,1)} %get-tuple-element.332.refs_0_.refs_1_), channel_id=1, source_target_pairs={{0,4},{4,0},{8,12},{12,8},{1,5},{5,1},{9,13},{13,9},{2,6},{6,2},{1... | collective-permute-start | bytes 1769480 | tf_op jit(solution)/shard_map/ppermute | solution.py:412
  89.3 23.3 %collective-permute-start.16 = (bf16[384,768]{1,0:T(8,128)(2,1)}, bf16[384,768]{1,0:T(8,128)(2,1)}, u32[]{:S(2)}, u32[]{:S(2)}) collective-permute-start(bf16[384,768]{1,0:T(8,128)(2,1)} %collective-permute-done.9.refs_4_.refs_5_), channel_id=1, source_target_pairs={{0,4},{4,0},{8,12},{12,8},{1,5},{5,1},{9,13},{13,9},{2,6},{6,2},{1... | collective-permute-start | bytes 1769480 | tf_op jit(solution)/shard_map/ppermute | solution.py:412
  89.8 19.2 %collective-permute-start.11 = (bf16[384,768]{1,0:T(8,128)(2,1)}, bf16[384,768]{1,0:T(8,128)(2,1)S(1)}, u32[]{:S(2)}, u32[]{:S(2)}) collective-permute-start(bf16[384,768]{1,0:T(8,128)(2,1)} %collective-permute-done.9.refs_4_.refs_5_), channel_id=1, source_target_pairs={{0,1},{1,0},{2,3},{3,2},{4,5},{5,4},{6,7},{7,6},{8,9},{9,8},{10,11... | collective-permute-start | bytes 1769480 | tf_op jit(solution)/shard_map/ppermute | solution.py:412
  91.4 18.2 %collective-permute-start.12 = (bf16[384,768]{1,0:T(8,128)(2,1)}, bf16[384,768]{1,0:T(8,128)(2,1)}, u32[]{:S(2)}, u32[]{:S(2)}) collective-permute-start(bf16[384,768]{1,0:T(8,128)(2,1)} %get-tuple-element.322.refs_8_.refs_9_), channel_id=1, source_target_pairs={{0,8},{4,12},{8,0},{12,4},{1,9},{5,13},{9,1},{13,5},{2,10},{6,14},... | collective-permute-start | bytes 1769480 | tf_op jit(solution)/shard_map/ppermute | solution.py:412
  112.4 17.5 %collective-permute-start.21 = (bf16[384,768]{1,0:T(8,128)(2,1)}, bf16[384,768]{1,0:T(8,128)(2,1)}, u32[]{:S(2)}, u32[]{:S(2)}) collective-permute-start(bf16[384,768]{1,0:T(8,128)(2,1)} %collective-permute-done.12.refs_12_.refs_13_), channel_id=1, source_target_pairs={{0,4},{4,0},{8,12},{12,8},{1,5},{5,1},{9,13},{13,9},{2,6},{6,2},{1... | collective-permute-start | bytes 1769480 | tf_op jit(solution)/shard_map/ppermute | solution.py:412
  126.3 17.6 %collective-permute-start.25 = (bf16[384,768]{1,0:T(8,128)(2,1)S(1)}, bf16[384,768]{1,0:T(8,128)(2,1)}, u32[]{:S(2)}, u32[]{:S(2)}) collective-permute-start(bf16[384,768]{1,0:T(8,128)(2,1)S(1)} %copy-done.35), channel_id=1, source_target_pairs={{0,8},{4,12},{8,0},{12,4},{1,9},{5,13},{9,1},{13,5},{2,10},{6,14},... | collective-permute-start | bytes 1769480 | tf_op jit(solution)/shard_map/ppermute | solution.py:412
  145.0 22.0 %collective-permute-start.31 = (bf16[384,768]{1,0:T(8,128)(2,1)S(1)}, bf16[384,768]{1,0:T(8,128)(2,1)}, u32[]{:S(2)}, u32[]{:S(2)}) collective-permute-start(bf16[384,768]{1,0:T(8,128)(2,1)S(1)} %copy-done.36), channel_id=1, source_target_pairs={{0,8},{4,12},{8,0},{12,4},{1,9},{5,13},{9,1},{13,5},{2,10},{6,14},... | collective-permute-start | bytes 1769480 | tf_op jit(solution)/shard_map/ppermute | solution.py:412
  146.6 26.5 %collective-permute-start.32 = (bf16[384,768]{1,0:T(8,128)(2,1)}, bf16[384,768]{1,0:T(8,128)(2,1)}, u32[]{:S(2)}, u32[]{:S(2)}) collective-permute-start(bf16[384,768]{1,0:T(8,128)(2,1)} %get-tuple-element.198.refs_9_.refs_10_), channel_id=1, source_target_pairs={{0,8},{4,12},{8,0},{12,4},{1,9},{5,13},{9,1},{13,5},{2,10},{6,14},... | collective-permute-start | bytes 1769480 | tf_op jit(solution)/shard_map/ppermute | solution.py:412
  147.7 25.4 %collective-permute-start.30 = (bf16[384,768]{1,0:T(8,128)(2,1)}, bf16[384,768]{1,0:T(8,128)(2,1)}, u32[]{:S(2)}, u32[]{:S(2)}) collective-permute-start(bf16[384,768]{1,0:T(8,128)(2,1)} %collective-permute-done.25.refs_4_.refs_5_), channel_id=1, source_target_pairs={{0,1},{1,0},{2,3},{3,2},{4,5},{5,4},{6,7},{7,6},{8,9},{9,8},{10,11... | collective-permute-start | bytes 1769480 | tf_op jit(solution)/shard_map/ppermute | solution.py:412
  208.7 18.8 %collective-permute-start.42 = (bf16[2,768,768]{2,1,0:T(8,128)(2,1)}, bf16[2,768,768]{2,1,0:T(8,128)(2,1)S(1)}, u32[]{:S(2)}, u32[]{:S(2)}) collective-permute-start(bf16[2,768,768]{2,1,0:T(8,128)(2,1)} %get-tuple-element.210), channel_id=1, source_target_pairs={{0,4},{4,0},{8,12},{12,8},{1,5},{5,1},{9,13},{13,9},{2,6},{6,2},{1... | collective-permute-start | bytes 7077896 | tf_op jit(solution)/shard_map/ppermute | solution.py:412
  228.6 33.5 %collective-permute-start.43 = (bf16[768,768]{1,0:T(8,128)(2,1)S(1)}, bf16[768,768]{1,0:T(8,128)(2,1)}, u32[]{:S(2)}, u32[]{:S(2)}) collective-permute-start(bf16[768,768]{1,0:T(8,128)(2,1)S(1)} %get-tuple-element.215), channel_id=1, source_target_pairs={{0,8},{4,12},{8,0},{12,4},{1,9},{5,13},{9,1},{13,5},{2,10},{6,14},... | collective-permute-start | bytes 3538952 | tf_op jit(solution)/shard_map/ppermute | solution.py:412
  231.8 120.6 %reduce-scatter.7.cloned.1.call-start = ((), (), s32[]{:S(2)}) async-start(), calls=%async_computation.7 | async-start | bytes 1474560 | tf_op jit(solution)/shard_map/reduce_scatter | solution.py:463
  245.8 20.0 %collective-permute-start.44 = (bf16[2,768,768]{2,1,0:T(8,128)(2,1)}, bf16[2,768,768]{2,1,0:T(8,128)(2,1)S(1)}, u32[]{:S(2)}, u32[]{:S(2)}) collective-permute-start(bf16[2,768,768]{2,1,0:T(8,128)(2,1)} %get-tuple-element.223), channel_id=1, source_target_pairs={{0,4},{4,0},{8,12},{12,8},{1,5},{5,1},{9,13},{13,9},{2,6},{6,2},{1... | collective-permute-start | bytes 7077896 | tf_op jit(solution)/shard_map/ppermute | solution.py:412
  268.5 28.7 %collective-permute-start.45 = (bf16[768,768]{1,0:T(8,128)(2,1)}, bf16[768,768]{1,0:T(8,128)(2,1)S(1)}, u32[]{:S(2)}, u32[]{:S(2)}) collective-permute-start(bf16[768,768]{1,0:T(8,128)(2,1)} %get-tuple-element.228), channel_id=1, source_target_pairs={{0,8},{4,12},{8,0},{12,4},{1,9},{5,13},{9,1},{13,5},{2,10},{6,14},... | collective-permute-start | bytes 3538952 | tf_op jit(solution)/shard_map/ppermute | solution.py:412
  281.5 19.5 %collective-permute-start.46 = (bf16[2,768,768]{2,1,0:T(8,128)(2,1)}, bf16[2,768,768]{2,1,0:T(8,128)(2,1)S(1)}, u32[]{:S(2)}, u32[]{:S(2)}) collective-permute-start(bf16[2,768,768]{2,1,0:T(8,128)(2,1)} %get-tuple-element.235), channel_id=1, source_target_pairs={{0,4},{4,0},{8,12},{12,8},{1,5},{5,1},{9,13},{13,9},{2,6},{6,2},{1... | collective-permute-start | bytes 7077896 | tf_op jit(solution)/shard_map/ppermute | solution.py:412
  281.8 23.3 %collective-permute-start.47 = (bf16[2,768,768]{2,1,0:T(8,128)(2,1)}, bf16[2,768,768]{2,1,0:T(8,128)(2,1)}, u32[]{:S(2)}, u32[]{:S(2)}) collective-permute-start(bf16[2,768,768]{2,1,0:T(8,128)(2,1)} %get-tuple-element.239), channel_id=1, source_target_pairs={{0,4},{4,0},{8,12},{12,8},{1,5},{5,1},{9,13},{13,9},{2,6},{6,2},{1... | collective-permute-start | bytes 7077896 | tf_op jit(solution)/shard_map/ppermute | solution.py:412
  282.1 112.2 %reduce-scatter.9.cloned.1.call-start = ((), (), s32[]{:S(2)}) async-start(), calls=%async_computation.8 | async-start | bytes 1474560 | tf_op jit(solution)/shard_map/reduce_scatter | solution.py:463
  310.9 33.3 %collective-permute-start.51 = (bf16[192,768]{1,0:T(8,128)(2,1)}, bf16[192,768]{1,0:T(8,128)(2,1)S(1)}, u32[]{:S(2)}, u32[]{:S(2)}) collective-permute-start(bf16[192,768]{1,0:T(8,128)(2,1)} %slice_bitcast_fusion.2), channel_id=1, source_target_pairs={{0,8},{4,12},{8,0},{12,4},{1,9},{5,13},{9,1},{13,5},{2,10},{6,14},... | collective-permute-start | bytes 884744 | tf_op jit(solution)/shard_map/ppermute | solution.py:412
  313.3 32.8 %collective-permute-start.50 = (bf16[2,192,768]{2,1,0:T(8,128)(2,1)}, bf16[2,192,768]{2,1,0:T(8,128)(2,1)}, u32[]{:S(2)}, u32[]{:S(2)}) collective-permute-start(bf16[2,192,768]{2,1,0:T(8,128)(2,1)} %dynamic-slice_bitcast_fusion.1), channel_id=1, source_target_pairs={{0,1},{1,0},{2,3},{3,2},{4,5},{5,4},{6,7},{7,6},{8,9},{9,8},{10,11... | collective-permute-start | bytes 1769480 | tf_op jit(solution)/shard_map/ppermute | solution.py:412
  314.0 34.1 %collective-permute-start.48 = (bf16[768,768]{1,0:T(8,128)(2,1)}, bf16[768,768]{1,0:T(8,128)(2,1)}, u32[]{:S(2)}, u32[]{:S(2)}) collective-permute-start(bf16[768,768]{1,0:T(8,128)(2,1)} %get-tuple-element.246), channel_id=1, source_target_pairs={{0,8},{4,12},{8,0},{12,4},{1,9},{5,13},{9,1},{13,5},{2,10},{6,14},... | collective-permute-start | bytes 3538952 | tf_op jit(solution)/shard_map/ppermute | solution.py:412
  328.0 22.5 %collective-permute-start.49 = (bf16[2,768,768]{2,1,0:T(8,128)(2,1)}, bf16[2,768,768]{2,1,0:T(8,128)(2,1)S(1)}, u32[]{:S(2)}, u32[]{:S(2)}) collective-permute-start(bf16[2,768,768]{2,1,0:T(8,128)(2,1)} %get-tuple-element.254), channel_id=1, source_target_pairs={{0,4},{4,0},{8,12},{12,8},{1,5},{5,1},{9,13},{13,9},{2,6},{6,2},{1... | collective-permute-start | bytes 7077896 | tf_op jit(solution)/shard_map/ppermute | solution.py:412
  352.5 106.0 %reduce-scatter.11.cloned.1.call-start = ((), (), s32[]{:S(2)}) async-start(), calls=%async_computation.9 | async-start | bytes 1474560 | tf_op jit(solution)/shard_map/reduce_scatter | solution.py:463
  352.5 45.0 %collective-permute-start.57 = (bf16[768,768]{1,0:T(8,128)(2,1)}, bf16[768,768]{1,0:T(8,128)(2,1)S(1)}, u32[]{:S(2)}, u32[]{:S(2)}) collective-permute-start(bf16[768,768]{1,0:T(8,128)(2,1)} %copy-done), channel_id=1, source_target_pairs={{0,8},{4,12},{8,0},{12,4},{1,9},{5,13},{9,1},{13,5},{2,10},{6,14},... | collective-permute-start | bytes 3538952 | tf_op jit(solution)/shard_map/ppermute | solution.py:412
  358.3 40.8 %collective-permute-start.58 = (bf16[1,192,768]{2,1,0:T(8,128)(2,1)}, bf16[1,192,768]{2,1,0:T(8,128)(2,1)}, u32[]{:S(2)}, u32[]{:S(2)}) collective-permute-start(bf16[1,192,768]{2,1,0:T(8,128)(2,1)} %constant_dynamic-slice_fusion), channel_id=1, source_target_pairs={{0,2},{1,3},{2,0},{3,1},{4,6},{5,7},{6,4},{7,5},{8,10},{9,11},{10,... | collective-permute-start | bytes 884744 | tf_op jit(solution)/shard_map/ppermute | solution.py:412
  398.7 38.0 %collective-permute-start.52 = (bf16[768,768]{1,0:T(8,128)(2,1)S(1)}, bf16[768,768]{1,0:T(8,128)(2,1)S(1)}, u32[]{:S(2)}, u32[]{:S(2)}) collective-permute-start(bf16[768,768]{1,0:T(8,128)(2,1)S(1)} %get-tuple-element.262), channel_id=1, source_target_pairs={{0,8},{4,12},{8,0},{12,4},{1,9},{5,13},{9,1},{13,5},{2,10},{6,14},... | collective-permute-start | bytes 3538952 | tf_op jit(solution)/shard_map/ppermute | solution.py:412
  412.0 46.4 %all-to-all-start.1 = ((bf16[8,208,448]{2,1,0:T(8,128)(2,1)}), bf16[8,208,448]{2,1,0:T(8,128)(2,1)}, u32[]{:S(2)}, u32[]{:S(2)}) async-start(bf16[8,208,448]{2,1,0:T(8,128)(2,1)} %fusion.1), calls=%async_computation.5 | async-start | bytes 3407872 | tf_op jit(solution)/shard_map/all_to_all | solution.py:704
  437.1 18.1 %collective-permute-start.54 = (bf16[2,192,768]{2,1,0:T(8,128)(2,1)S(1)}, bf16[2,192,768]{2,1,0:T(8,128)(2,1)S(1)}, u32[]{:S(2)}, u32[]{:S(2)}) collective-permute-start(bf16[2,192,768]{2,1,0:T(8,128)(2,1)S(1)} %dynamic-slice_bitcast_fusion), channel_id=1, source_target_pairs={{0,1},{1,0},{2,3},{3,2},{4,5},{5,4},{6,7},{7,6},{8,9},{9,8},{10,11... | collective-permute-start | bytes 1769480 | tf_op jit(solution)/shard_map/ppermute | solution.py:412
  438.1 17.3 %collective-permute-start.55 = (bf16[1,192,768]{2,1,0:T(8,128)(2,1)S(1)}, bf16[1,192,768]{2,1,0:T(8,128)(2,1)S(1)}, u32[]{:S(2)}, u32[]{:S(2)}) collective-permute-start(bf16[1,192,768]{2,1,0:T(8,128)(2,1)S(1)} %bitcast.159), channel_id=1, source_target_pairs={{0,2},{1,3},{2,0},{3,1},{4,6},{5,7},{6,4},{7,5},{8,10},{9,11},{10,... | collective-permute-start | bytes 884744 | tf_op jit(solution)/shard_map/ppermute | solution.py:412
  469.8 17.6 %collective-permute-start.61 = (bf16[192,768]{1,0:T(8,128)(2,1)S(1)}, bf16[192,768]{1,0:T(8,128)(2,1)S(1)}, u32[]{:S(2)}, u32[]{:S(2)}) collective-permute-start(bf16[192,768]{1,0:T(8,128)(2,1)S(1)} %broadcast_select_fusion.6), channel_id=1, source_target_pairs={{0,16},{16,0},{1,17},{17,1},{2,18},{18,2},{3,19},{19,3},{4,20},{20... | collective-permute-start | bytes 884744 | tf_op jit(solution)/shard_map/ppermute | solution.py:412
  470.4 53.5 %collective-permute-start.65 = (f32[12,192]{1,0:T(8,128)S(1)}, f32[12,192]{1,0:T(8,128)S(1)}, u32[]{:S(2)}, u32[]{:S(2)}) collective-permute-start(f32[12,192]{1,0:T(8,128)S(1)} %convert_reduce_fusion), channel_id=1, source_target_pairs={{0,3},{1,2},{2,1},{3,0},{4,7},{5,6},{6,5},{7,4},{8,11},{9,10},{10,... | collective-permute-start | bytes 27656 | tf_op jit(solution)/shard_map/ppermute | solution.py:412
  473.2 50.7 %collective-permute-start.64 = (f32[12,192]{1,0:T(8,128)S(1)}, f32[12,192]{1,0:T(8,128)S(1)}, u32[]{:S(2)}, u32[]{:S(2)}) collective-permute-start(f32[12,192]{1,0:T(8,128)S(1)} %convert_reduce_fusion), channel_id=1, source_target_pairs={{0,2},{1,3},{2,0},{3,1},{4,6},{5,7},{6,4},{7,5},{8,10},{9,11},{10,... | collective-permute-start | bytes 27656 | tf_op jit(solution)/shard_map/ppermute | solution.py:412
  473.8 50.2 %collective-permute-start.63 = (f32[12,192]{1,0:T(8,128)S(1)}, f32[12,192]{1,0:T(8,128)S(1)}, u32[]{:S(2)}, u32[]{:S(2)}) collective-permute-start(f32[12,192]{1,0:T(8,128)S(1)} %convert_reduce_fusion), channel_id=1, source_target_pairs={{0,1},{1,0},{2,3},{3,2},{4,5},{5,4},{6,7},{7,6},{8,9},{9,8},{10,11... | collective-permute-start | bytes 27656 | tf_op jit(solution)/shard_map/ppermute | solution.py:412
  499.5 22.4 %collective-permute-start.66 = (bf16[2,192,768]{2,1,0:T(8,128)(2,1)}, bf16[2,192,768]{2,1,0:T(8,128)(2,1)}, u32[]{:S(2)}, u32[]{:S(2)}) collective-permute-start(bf16[2,192,768]{2,1,0:T(8,128)(2,1)} %maximum_select_fusion.4), channel_id=1, source_target_pairs={{0,1},{1,0},{2,3},{3,2},{4,5},{5,4},{6,7},{7,6},{8,9},{9,8},{10,11... | collective-permute-start | bytes 1769480 | tf_op jit(solution)/shard_map/ppermute | solution.py:412
  515.6 18.0 %collective-permute-start.68 = (bf16[2,192,768]{2,1,0:T(8,128)(2,1)S(1)}, bf16[2,192,768]{2,1,0:T(8,128)(2,1)S(1)}, u32[]{:S(2)}, u32[]{:S(2)}) collective-permute-start(bf16[2,192,768]{2,1,0:T(8,128)(2,1)S(1)} %maximum_select_fusion.5), channel_id=1, source_target_pairs={{0,1},{1,0},{2,3},{3,2},{4,5},{5,4},{6,7},{7,6},{8,9},{9,8},{10,11... | collective-permute-start | bytes 1769480 | tf_op jit(solution)/shard_map/ppermute | solution.py:412
  (90 other events, 708.6 us)
Sparse Core Ops, SparseCore 0:
  231.9 47.4 reduce-scatter.4
  282.3 29.4 reduce-scatter.6
  352.6 41.6 reduce-scatter.8
  401.0 27.8 reduce-scatter.10
